TPU v7x, 32 devices: a whole 2x2x4 slice. The times are simulated.
32 devices in a mesh: fs: 8 (over y, x, core), sp: 4 (over z).
Axes of the slice: x: 2, y: 2, z: 4, core: 2. Of those that a mesh axis runs over, the one named last changes fastest.
Arguments:
- hidden: bfloat16 [6, 4096, 1536], P(None, ('fs', 'sp')), may hold values from -6 to 6
- norm_gain: bfloat16 [1536], P('fs'), may hold values from 0.5 to 1.5
- w_z: bfloat16 [1536, 3072], P('fs'), may hold values from -0.15625 to 0.15625
- w_x: bfloat16 [1536, 3072], P('fs'), may hold values from -0.15625 to 0.15625
- w_bc: bfloat16 [1536, 256], P('fs'), may hold values from -0.15625 to 0.15625
- w_dt: bfloat16 [1536, 48], P('fs'), may hold values from -0.15625 to 0.15625
- w_out: bfloat16 [1536, 3072], P('fs'), may hold values from -0.109375 to 0.109375
- conv_x: bfloat16 [3072, 4], P('fs'), may hold values from -3 to 3
- conv_x_bias: bfloat16 [3072], P('fs'), may hold values from -0.5 to 0.5
- conv_bc: bfloat16 [256, 4], P('fs'), may hold values from -3 to 3
- conv_bc_bias: bfloat16 [256], P('fs'), may hold values from -0.5 to 0.5
- dt_bias: bfloat16 [48], P('fs'), may hold values from -7 to -2.296875
- a_log: bfloat16 [48], P('fs'), may hold values from -2.6875 to -1.59375
- skip_d: bfloat16 [48], P('fs'), may hold values from 0.5 to 4
- gate_gain: bfloat16 [3072], P('fs'), may hold values from 0.5 to 1.5
- cotangent: bfloat16 [6, 4096, 1536], P(None, ('fs', 'sp')), may hold values from -6 to 6
Outputs:
- output: bfloat16 [6, 4096, 1536], P(None, ('fs', 'sp'))
- grad_hidden: float32 [6, 4096, 1536], P(None, ('fs', 'sp'))
- grad_norm_gain: float32 [1536], P('fs')
- grad_w_z: float32 [1536, 3072], P('fs')
- grad_w_x: float32 [1536, 3072], P('fs')
- grad_w_bc: float32 [1536, 256], P('fs')
- grad_w_dt: float32 [1536, 48], P('fs')
- grad_w_out: float32 [1536, 3072], P('fs')
- grad_conv_x: float32 [3072, 4], P('fs')
- grad_conv_x_bias: float32 [3072], P('fs')
- grad_conv_bc: float32 [256, 4], P('fs')
- grad_conv_bc_bias: float32 [256], P('fs')
- grad_dt_bias: float32 [48], P('fs')
- grad_a_log: float32 [48], P('fs')
- grad_skip_d: float32 [48], P('fs')
- grad_gate_gain: float32 [3072], P('fs')
All inputs are finite; a program needn't handle non-finite values.
Results may differ from a plain program's by a relative error of at most 0.035.
Values may be sent and summed in bfloat16 or wider, within the bound.
A program may use at most 384 MiB of HBM per device.

v0:
```python
import jax
import jax.numpy as jnp
from jax import lax
from jax.sharding import PartitionSpec as P

SPAN = 256


EPSILON = 1e-05
HIGHEST = lax.Precision.HIGHEST


def passed_along(x, axis, by):
    size = lax.axis_size(axis)
    pairs = [(i, i + by) for i in range(size) if 0 <= i + by < size]
    return lax.ppermute(x, axis, pairs)


def prefix(part, axis, combine, identity):
    place = lax.axis_index(axis)
    gathered = jax.tree.map(lambda a: lax.all_gather(a, axis), part)
    state = jax.tree.map(lambda a, e: jnp.zeros_like(a) + jnp.asarray(e, a.dtype), part, identity)

    def one(hop, state):
        return combine(
            state, jax.tree.map(lambda a: lax.dynamic_index_in_dim(a, hop, 0, False), gathered)
        )

    return lax.fori_loop(0, place, one, state)


def carried_in(x, axis, combine, identity):
    size, place = (lax.axis_size(axis), lax.axis_index(axis))
    everything = jax.tree.map(
        lambda part, kind: lax.all_gather(part.astype(kind), axis), x, (jnp.bfloat16, jnp.bfloat16)
    )
    start = jax.tree.map(
        lambda part, zero: jnp.broadcast_to(jnp.asarray(zero, part.dtype), part.shape), x, identity
    )

    def hop(k, before):
        at = size - 1 - k
        reached = at > place
        new = combine(
            before, jax.tree.map(lambda part, own: part[at].astype(own.dtype), everything, x)
        )
        return jax.tree.map(lambda a, b: jnp.where(reached, a, b), new, before)

    return lax.fori_loop(0, size, hop, start)


def for_sending(x):

    def short(part):
        return part.astype(jnp.bfloat16) if part.dtype == jnp.float32 else part

    return jax.tree.map(short, x)


def row_scale(values):
    return lax.rsqrt(jnp.mean(values * values, axis=-1, keepdims=True) + EPSILON)


def norm_backward(grad_unit, unit_rows, scale_rows):
    return scale_rows * (
        grad_unit - unit_rows * jnp.mean(grad_unit * unit_rows, axis=-1, keepdims=True)
    )


def run_conv(extended, kernel, offset):
    tap_count = kernel.shape[1]
    length = extended.shape[1] - tap_count + 1
    summed = offset[None, None, :]
    for position in range(tap_count):
        summed = (
            summed + extended[:, position : position + length] * kernel[:, position][None, None, :]
        )
    return summed


def decay_terms(dt_raw, dt_shift, decay_log):
    step_size = jax.nn.softplus(dt_raw + dt_shift[None, None, :])
    return (step_size, -step_size * jnp.exp(decay_log)[None, None, :])


def span_update(carry_state, pieces):
    weighted, log_decay, key_rows, read_rows = pieces
    length = log_decay.shape[1]
    running = jnp.cumsum(log_decay, axis=1)
    indices = jnp.arange(length)
    causal = (indices[:, None] >= indices[None, :])[None, :, :, None]
    log_gaps = running[:, :, None, :] - running[:, None, :, :]
    decay_mix = jnp.where(causal, jnp.exp(jnp.where(causal, log_gaps, 0.0)), 0.0)
    scores = jnp.einsum("btn,bsn->bts", read_rows, key_rows, precision=HIGHEST)
    within = jnp.einsum(
        "btsh,bshp->bthp", scores[..., None] * decay_mix, weighted, precision=HIGHEST
    )
    carried = (
        jnp.einsum("btn,bhpn->bthp", read_rows, carry_state, precision=HIGHEST)
        * jnp.exp(running)[..., None]
    )
    tail_decay = jnp.exp(running[:, -1:, :] - running)
    fresh_terms = jnp.einsum(
        "bsh,bshp,bsn->bhpn", tail_decay, weighted, key_rows, precision=HIGHEST
    )
    new_state = jnp.exp(running[:, -1])[..., None, None] * carry_state + fresh_terms
    return (new_state, within + carried)


def mix_heads(
    x_ext,
    bc_ext,
    dt_raw,
    gate_raw,
    kernel_local,
    local_offset_part,
    kernel_shared,
    offset_shared,
    dt_shift,
    decay_log,
    skip_local,
    start,
):
    features = jax.nn.silu(run_conv(x_ext, kernel_local, local_offset_part))
    shared = jax.nn.silu(run_conv(bc_ext, kernel_shared, offset_shared))
    state_size = shared.shape[2] // 2
    step_size, log_decay = decay_terms(dt_raw, dt_shift, decay_log)
    batch, segment, local_inner = features.shape
    local_heads = step_size.shape[2]
    head_size = local_inner // local_heads
    blocks_count = segment // SPAN
    head_x = features.reshape(batch, segment, local_heads, head_size)
    weighted = head_x * step_size[..., None]
    blocks = (
        jnp.moveaxis(weighted.reshape(batch, blocks_count, SPAN, local_heads, head_size), 1, 0),
        jnp.moveaxis(log_decay.reshape(batch, blocks_count, SPAN, local_heads), 1, 0),
        jnp.moveaxis(shared[..., :state_size].reshape(batch, blocks_count, SPAN, state_size), 1, 0),
        jnp.moveaxis(shared[..., state_size:].reshape(batch, blocks_count, SPAN, state_size), 1, 0),
    )
    final_state, mixed = lax.scan(jax.checkpoint(span_update), start, blocks)
    result = jnp.moveaxis(mixed, 0, 1).reshape(batch, segment, local_heads, head_size)
    result = result + skip_local[None, None, :, None] * head_x
    gated = result.reshape(batch, segment, local_inner) * jax.nn.silu(gate_raw)
    return (gated, final_state)


def compose(earlier, later):
    return (earlier[0] * later[0], later[0][..., None, None] * earlier[1] + later[1])


def body(
    hidden,
    norm_gain,
    w_z,
    w_x,
    w_bc,
    w_dt,
    w_out,
    conv_x,
    conv_x_bias,
    conv_bc,
    conv_bc_bias,
    dt_bias,
    a_log,
    skip_d,
    gate_gain,
    cotangent,
):
    gathered = (
        lax.all_gather(norm_gain, "fs", axis=0, tiled=True),
        lax.all_gather(w_z, "fs", axis=0, tiled=True),
        lax.all_gather(w_x, "fs", axis=0, tiled=True),
        lax.all_gather(w_bc, "fs", axis=0, tiled=True),
        lax.all_gather(w_dt, "fs", axis=0, tiled=True),
        lax.all_gather(w_out, "fs", axis=0, tiled=True),
        lax.all_gather(conv_x, "fs", axis=0, tiled=True),
        lax.all_gather(conv_x_bias, "fs", axis=0, tiled=True),
        lax.all_gather(conv_bc, "fs", axis=0, tiled=True),
        lax.all_gather(conv_bc_bias, "fs", axis=0, tiled=True),
        lax.all_gather(dt_bias, "fs", axis=0, tiled=True),
        lax.all_gather(a_log, "fs", axis=0, tiled=True),
        lax.all_gather(skip_d, "fs", axis=0, tiled=True),
        lax.all_gather(gate_gain, "fs", axis=0, tiled=True),
    )
    (
        gain_in,
        weight_z,
        weight_x,
        weight_bc,
        weight_dt,
        output_weight,
        kernel_x,
        offset_x,
        kernel_bc,
        offset_bc,
        shift_dt,
        decay_all,
        skip_all,
        gain_out,
    ) = gathered
    groups = lax.axis_size("sp")
    member = lax.axis_index("sp")
    batch = hidden.shape[0]
    inner_width = weight_z.shape[1]
    head_count = weight_dt.shape[1]
    local_inner = inner_width // groups
    local_heads = head_count // groups
    head_size = inner_width // head_count
    margin = kernel_x.shape[1] - 1
    resid = hidden.astype(jnp.float32)
    scale_in = row_scale(resid)
    unit_in = resid * scale_in
    gain_in32 = gain_in.astype(jnp.float32)
    normed = (unit_in * gain_in32).astype(jnp.bfloat16)

    def project(token_rows, weight_matrix):
        return jnp.einsum(
            "rut,to->ruo", token_rows, weight_matrix, preferred_element_type=jnp.float32
        ).astype(jnp.bfloat16)

    gate_in = project(normed, weight_z)
    x_in = project(normed, weight_x)
    bc_in = project(normed, weight_bc)
    dt_in = project(normed, weight_dt)
    x_heads, gate_heads, dt_heads, bc_segment = (
        lax.all_to_all(x_in, "sp", split_axis=2, concat_axis=1, tiled=True),
        lax.all_to_all(gate_in, "sp", split_axis=2, concat_axis=1, tiled=True),
        lax.all_to_all(dt_in, "sp", split_axis=2, concat_axis=1, tiled=True),
        lax.all_to_all(
            jnp.tile(bc_in, (1, 1, groups)), "sp", split_axis=2, concat_axis=1, tiled=True
        ),
    )
    before_x, before_bc = passed_along((x_heads[:, -margin:], bc_segment[:, -margin:]), "fs", 1)
    x_ext = jnp.concatenate([before_x, x_heads], axis=1).astype(jnp.float32)
    bc_ext = jnp.concatenate([before_bc, bc_segment], axis=1).astype(jnp.float32)
    kernel_local = lax.dynamic_slice_in_dim(kernel_x, member * local_inner, local_inner, 0).astype(
        jnp.float32
    )
    local_offset_part = lax.dynamic_slice_in_dim(
        offset_x, member * local_inner, local_inner, 0
    ).astype(jnp.float32)
    shift_local = lax.dynamic_slice_in_dim(shift_dt, member * local_heads, local_heads, 0).astype(
        jnp.float32
    )
    decay_local = lax.dynamic_slice_in_dim(decay_all, member * local_heads, local_heads, 0).astype(
        jnp.float32
    )
    skip_local = lax.dynamic_slice_in_dim(skip_all, member * local_heads, local_heads, 0).astype(
        jnp.float32
    )
    kernel_shared = kernel_bc.astype(jnp.float32)
    offset_shared = offset_bc.astype(jnp.float32)
    dt_local = dt_heads.astype(jnp.float32)
    gate_local = gate_heads.astype(jnp.float32)
    local_args = (
        x_ext,
        bc_ext,
        dt_local,
        gate_local,
        kernel_local,
        local_offset_part,
        kernel_shared,
        offset_shared,
        shift_local,
        decay_local,
        skip_local,
    )
    state_size = bc_segment.shape[2] // 2
    segment = x_heads.shape[1]
    empty_state = jnp.zeros((batch, local_heads, head_size, state_size), jnp.float32)
    gated_zero, own_state = mix_heads(*local_args, empty_state)
    read_rows = jax.nn.silu(run_conv(bc_ext, kernel_shared, offset_shared))[..., state_size:]
    step_size, log_decay = decay_terms(dt_local, shift_local, decay_local)
    reach = jnp.exp(jnp.cumsum(log_decay, axis=1))
    through = reach[:, -1]
    identity = (jnp.ones_like(through), jnp.zeros_like(own_state))
    incoming = prefix((through, own_state), "fs", compose, identity)[1]
    carried = (
        jnp.einsum("btn,bhpn->bthp", read_rows, incoming, precision=HIGHEST) * reach[..., None]
    )
    gate_silu = jax.nn.silu(gate_local)
    gated = gated_zero + carried.reshape(batch, segment, local_inner) * gate_silu
    gated_tokens = lax.all_to_all(
        gated.astype(jnp.bfloat16), "sp", split_axis=1, concat_axis=2, tiled=True
    )
    gated_rows = gated_tokens.astype(jnp.float32)
    scale_out = row_scale(gated_rows)
    unit_out = gated_rows * scale_out
    gain_out32 = gain_out.astype(jnp.float32)
    normalized_output = (unit_out * gain_out32).astype(jnp.bfloat16)
    result = resid + jnp.einsum(
        "zvh,xh->zvx", normalized_output, output_weight, preferred_element_type=jnp.float32
    )
    output = result.astype(jnp.bfloat16)
    grad_out_weight = jnp.einsum(
        "pyw,pyf->wf", cotangent, normalized_output, preferred_element_type=jnp.float32
    )
    grad_normed_out = jnp.einsum(
        "ayg,gp->ayp", cotangent, output_weight, preferred_element_type=jnp.float32
    )
    grad_gain_out = jnp.sum(grad_normed_out * unit_out, axis=(0, 1))
    grad_gated = norm_backward(grad_normed_out * gain_out32, unit_out, scale_out).astype(
        jnp.bfloat16
    )
    grad_local = lax.all_to_all(grad_gated, "sp", split_axis=2, concat_axis=1, tiled=True).astype(
        jnp.float32
    )
    flowing = (grad_local * gate_silu).reshape(batch, segment, local_heads, head_size)
    local_pull = jnp.einsum("btn,bthp,bth->bhpn", read_rows, flowing, reach, precision=HIGHEST)
    after_state = carried_in((through, local_pull), "fs", compose, identity)[1]
    _, pullback = jax.vjp(mix_heads, *local_args, incoming)
    (
        grad_x_ext,
        extended_bc_gradient,
        grad_dt,
        grad_gate,
        grad_kernel,
        grad_offset,
        grad_kernel_bc,
        grad_offset_bc,
        grad_shift,
        grad_decay,
        grad_skip,
        ignored,
    ) = pullback((grad_local, after_state))
    later_x, later_bc = (
        passed_along(grad_x_ext[:, :margin].astype(jnp.bfloat16), "fs", -1).astype(jnp.float32),
        passed_along(extended_bc_gradient[:, :margin].astype(jnp.bfloat16), "fs", -1).astype(
            jnp.float32
        ),
    )
    grad_x = jnp.concatenate(
        [grad_x_ext[:, margin:-margin], grad_x_ext[:, -margin:] + later_x], axis=1
    )
    grad_bc = jnp.concatenate(
        [extended_bc_gradient[:, margin:-margin], extended_bc_gradient[:, -margin:] + later_bc],
        axis=1,
    )
    bc_parts = lax.psum_scatter(grad_bc.astype(jnp.bfloat16), "sp", scatter_dimension=1, tiled=True)
    grad_x_low = grad_x.astype(jnp.bfloat16)
    grad_gate_low = grad_gate.astype(jnp.bfloat16)
    grad_dt_low = grad_dt.astype(jnp.bfloat16)

    def back_project(row_gradients, weight_matrix):
        return jnp.einsum(
            "rxz,wz->rxw", row_gradients, weight_matrix, preferred_element_type=jnp.float32
        )

    def weight_grad(token_rows, row_gradients):
        return jnp.einsum(
            "nwp,nwo->po", token_rows, row_gradients, preferred_element_type=jnp.float32
        )

    grad_x_tok, grad_gate_tok, grad_dt_tok = (
        lax.all_to_all(grad_x_low, "sp", split_axis=1, concat_axis=2, tiled=True),
        lax.all_to_all(grad_gate_low, "sp", split_axis=1, concat_axis=2, tiled=True),
        lax.all_to_all(grad_dt_low, "sp", split_axis=1, concat_axis=2, tiled=True),
    )
    grad_normed = (
        back_project(grad_gate_tok, weight_z)
        + back_project(grad_x_tok, weight_x)
        + back_project(bc_parts, weight_bc)
        + back_project(grad_dt_tok, weight_dt)
    )
    token_grads = (
        weight_grad(normed, grad_gate_tok),
        weight_grad(normed, grad_x_tok),
        weight_grad(normed, grad_dt_tok),
    )
    grad_gain_in = jnp.sum(grad_normed * unit_in, axis=(0, 1))
    grad_hidden = cotangent.astype(jnp.float32) + norm_backward(
        grad_normed * gain_in32, unit_in, scale_in
    )

    def place(local_rows):
        whole = jnp.zeros((local_rows.shape[0] * groups,) + local_rows.shape[1:], jnp.float32)
        return lax.dynamic_update_slice_in_dim(whole, local_rows, member * local_rows.shape[0], 0)

    head_stack = jnp.stack([grad_shift, grad_decay, grad_skip], axis=1)
    leading = (jnp.arange(local_inner) % head_size == 0)[:, None]
    head_rows = jnp.where(leading, jnp.repeat(head_stack, head_size, axis=0), 0.0)
    gradients = (
        grad_gain_in,
        weight_grad(normed, bc_parts),
        grad_out_weight,
        place(grad_kernel),
        place(grad_offset),
        grad_kernel_bc,
        grad_offset_bc,
        place(head_rows),
        grad_gain_out,
    ) + token_grads
    shards = jax.tree.map(
        lambda part: part.astype(jnp.float32),
        lax.psum_scatter(for_sending(gradients), "fs", scatter_dimension=0, tiled=True),
    )
    shards = jax.tree.map(
        lambda part: part.astype(jnp.float32), lax.psum(for_sending(shards), "sp")
    )
    (
        total_gain_in,
        total_bc,
        total_out,
        total_kernel,
        total_offset,
        total_kernel_bc,
        total_offset_bc,
        total_heads,
        total_gain_out,
    ) = shards[:9]
    total_z, total_x, total_dt = (shards[9], shards[10], shards[11])
    head_values = total_heads.reshape(-1, head_size, 3)[:, 0, :]
    return (
        output,
        grad_hidden,
        total_gain_in,
        total_z,
        total_x,
        total_bc,
        total_dt,
        total_out,
        total_kernel,
        total_offset,
        total_kernel_bc,
        total_offset_bc,
        head_values[:, 0],
        head_values[:, 1],
        head_values[:, 2],
        total_gain_out,
    )


def solution(mesh):
    placed = (
        P(None, ("fs", "sp"), None),
        P("fs"),
        P("fs", None),
        P("fs", None),
        P("fs", None),
        P("fs", None),
        P("fs", None),
        P("fs", None),
        P("fs"),
        P("fs", None),
        P("fs"),
        P("fs"),
        P("fs"),
        P("fs"),
        P("fs"),
        P(None, ("fs", "sp"), None),
    )
    return jax.shard_map(
        body,
        mesh=mesh,
        in_specs=placed,
        out_specs=(
            P(None, ("fs", "sp"), None),
            P(None, ("fs", "sp"), None),
            P("fs"),
            P("fs", None),
            P("fs", None),
            P("fs", None),
            P("fs", None),
            P("fs", None),
            P("fs", None),
            P("fs"),
            P("fs", None),
            P("fs"),
            P("fs"),
            P("fs"),
            P("fs"),
            P("fs"),
        ),
        check_vma=False,
    )
```

profile of v0, /device:TPU:0, one launch (start us, length us, event | category | flops | bytes accessed | tf_op | source)
XLA Modules:
  0.0 2440.2 jit_solution(16651629440764122596)
XLA Ops:
  15.6 15.8 all-reduce.30
  51.2 14.1 all_gather.69
  75.1 13.0 fusion.151
  96.6 26.2 %all-to-all-done.2 = bf16[6,128,1024]{1,0,2:T(8,128)(2,1)} async-done(((bf16[6,128,1024]{1,0,2:T(8,128)(2,1)}), bf16[6,128,1024]{1,0,2:T(8,128)(2,1)}, u32[]{:S(2)}, u32[]{:S(2)}) %all-to-all-start.2) | async-done | bytes 1572896 | tf_op jit(solution)/shard_map/all_to_all | solution.py:229
  170.1 95.8 %all-to-all-done.1 = bf16[6,128,3072]{1,0,2:T(8,128)(2,1)} async-done(((bf16[6,128,3072]{1,0,2:T(8,128)(2,1)}), bf16[6,128,3072]{1,0,2:T(8,128)(2,1)}, u32[]{:S(2)}, u32[]{:S(2)}) %all-to-all-start.1) | async-done | bytes 4718624 | tf_op jit(solution)/shard_map/all_to_all | solution.py:226
  299.4 12.0 reshape.507
  327.2 96.6 %while.84 = (s32[]{:T(128)}, f32[6,12,64,128]{3,2,1,0:T(8,128)}, f32[2,6,256,12,64]{2,4,3,1,0:T(8,128)}, f32[2,6,256,12]{2,3,1,0:T(8,128)S(1)}, f32[2,6,256,12,6...) while((s32[]{:T(128)}, f32[6,12,64,128]{3,2,1,0:T(8,128)}, ...), condition=%wide.region_4.5_spmd.clone, body=%wide.region_1.4_spmd.clone.sunk | while | flops 7878952960 | bytes 57628476 | solution.py:140
  334.3 23.7 fusion.326
  382.0 23.7 fusion.326
  423.9 14.4 fusion.154
  462.4 11.3 all-gather
  474.9 116.3 %all-to-all-done.3 = bf16[6,128,3072]{1,0,2:T(8,128)(2,1)} async-done(((bf16[6,128,3072]{1,0,2:T(8,128)(2,1)}), bf16[6,128,3072]{1,0,2:T(8,128)(2,1)}, u32[]{:S(2)}, u32[]{:S(2)}) %all-to-all-start.3) | async-done | bytes 4718624 | tf_op jit(solution)/shard_map/all_to_all | solution.py:227
  601.2 12.1 copy.636
  613.3 17.1 copy.625
  630.4 12.9 reshape.510
  656.6 11.1 broadcast_multiply_fusion
  677.3 14.1 multiply_convert_fusion
  702.3 32.9 %all-gather.7 = bf16[8,1,384]{2,1,0:T(2,128)(2,1)S(1)} all-gather(bf16[1,1,384]{2,1,0:T(2,128)(2,1)S(1)} %reshape.572), channel_id=1, replica_groups=mesh['fs'=8,'sp'=4] {'fs'}, dimensions={0}, use_global_device_ids=true | all-gather | bytes 6912 | tf_op jit(solution)/shard_map/all_gather | solution.py:183
  735.2 105.5 %all-to-all-done.4 = bf16[6,512,768]{2,0,1:T(8,128)(2,1)} async-done(((bf16[6,512,768]{2,0,1:T(8,128)(2,1)}), bf16[6,512,768]{2,0,1:T(8,128)(2,1)}, u32[]{:S(2)}, u32[]{:S(2)}) %all-to-all-start.4) | async-done | bytes 4718624 | tf_op jit(solution)/shard_map/all_to_all | solution.py:283
  850.8 12.3 reshape.530
  867.8 15.5 multiply_reduce_fusion.5
  883.3 11.6 multiply_convert_fusion.1
  908.7 12.4 reshape.533
  921.1 127.0 %all-to-all-done.5 = bf16[6,128,3072]{1,0,2:T(8,128)(2,1)} async-done(((bf16[6,128,3072]{1,0,2:T(8,128)(2,1)}), bf16[6,128,3072]{1,0,2:T(8,128)(2,1)}, u32[]{:S(2)}, u32[]{:S(2)}) %all-to-all-start.5) | async-done | bytes 4718624 | tf_op jit(solution)/shard_map/all_to_all | solution.py:305
  1058.2 12.3 reshape.532
  1070.5 14.7 fusion.176
  1086.0 29.6 %all-gather.3 = bf16[48,1,12]{2,1,0:T(2,128)(2,1)S(1)} all-gather(bf16[6,1,12]{2,1,0:T(2,128)(2,1)S(1)} %copy.649), channel_id=5, replica_groups=mesh['fs'=8,'sp'=4] {'fs'}, dimensions={0}, use_global_device_ids=true | all-gather | bytes 1296 | tf_op jit(solution)/shard_map/all_gather | solution.py:35
  1115.7 13.3 reshape.535
  1133.8 96.4 %while.83 = (s32[]{:T(128)}, f32[6,12,64,128]{3,2,1,0:T(8,128)}, f32[2,6,256,12,64]{2,4,3,1,0:T(8,128)}, f32[2,6,12,64,128]{4,3,2,1,0:T(8,128)}, f32[2,6,256,12]...) while((s32[]{:T(128)}, f32[6,12,64,128]{3,2,1,0:T(8,128)}, ...), condition=%wide.region_14.15_spmd.clone.clone, body=%wide.region_11.14_spmd.clone.clone.sunk | while | flops 7877707776 | bytes 150361072 | solution.py:140
  1144.9 23.2 fusion.317
  1192.7 23.2 fusion.317
  1230.2 13.7 reshape.534
  1243.9 12.6 fusion.146
  1256.5 15.5 while.85
  1280.0 313.1 %while.82 = (s32[]{:T(128)}, f32[6,12,64,128]{3,2,1,0:T(8,128)S(1)}, f32[2,6,256,12,64]{2,4,3,1,0:T(8,128)}, f32[2,6,256,12]{2,0,3,1:T(2,128)}, f32[2,6,256,128]...) while((s32[]{:T(128)}, ...), condition=%wide.region_29.30_spmd, body=%wide.region_18.29_spmd.sunk | while | flops 18208079872 | bytes 301422336 | solution.py:140
  1334.8 10.9 fusion.305
  1348.6 28.1 %fusion.304 = (f32[6,256,12]{1,2,0:T(8,128)}, f32[6,256,12]{1,2,0:T(8,128)}, f32[6,256,256]{2,1,0:T(8,128)}) fusion(f32[6,256,12]{1,2,0:T(8,128)S(1)} %bitcast.567, f32[6,256,256]{2,1,0:T(8,128)S(1)} %fusion.303, pred[256,256]{1,0:T(8,128)(4,1)S(1)} %iota_compare_fusion.5, f32[6,256,12,64]{1,3,2,0:T(8,128)S(1)} %copy-done.1, ...), kind=kOutput, calls=%fused_computation.103.clone.1 | convolution fusion | flops 3675353088 | bytes 12869632 | tf_op jit(solution)/shard_map/transpose(jvp())/while/body/eval_jaxpr/checkpoint/btsh,bshp->bthp/dot_general | solution.py:95
  1391.1 18.7 bitcast_dynamic-update-slice_fusion.8
  1409.9 14.9 reduce-window.96
  1478.7 10.9 fusion.305
  1492.5 28.1 %fusion.304 = (f32[6,256,12]{1,2,0:T(8,128)}, f32[6,256,12]{1,2,0:T(8,128)}, f32[6,256,256]{2,1,0:T(8,128)}) fusion(f32[6,256,12]{1,2,0:T(8,128)S(1)} %bitcast.567, f32[6,256,256]{2,1,0:T(8,128)S(1)} %fusion.303, pred[256,256]{1,0:T(8,128)(4,1)S(1)} %iota_compare_fusion.5, f32[6,256,12,64]{1,3,2,0:T(8,128)S(1)} %copy-done.1, ...), kind=kOutput, calls=%fused_computation.103.clone.1 | convolution fusion | flops 3675353088 | bytes 12869632 | tf_op jit(solution)/shard_map/transpose(jvp())/while/body/eval_jaxpr/checkpoint/btsh,bshp->bthp/dot_general | solution.py:95
  1535.1 18.7 bitcast_dynamic-update-slice_fusion.8
  1553.9 14.9 reduce-window.96
  1607.9 14.0 fusion.115
  1622.0 12.7 copy.696
  1634.7 17.1 copy.642
  1651.7 14.0 reshape.514
  1675.8 12.0 copy.646
  1712.6 17.1 copy.653
  1729.7 12.9 reshape.515
  1766.7 38.2 %multiply_reduce_fusion.10 = (f32[768]{0:T(1024)S(1)}, f32[768]{0:T(1024)S(1)}, f32[768]{0:T(1024)S(1)}, f32[768]{0:T(1024)S(1)}, bf16[768]{0:T(1024)(128)(2,1)}...) fusion(f32[6,515,768]{2,1,0:T(8,128)} %copy-done.4, ...), kind=kLoop, calls=%fused_computation.202 | loop fusion | flops 92007936 | bytes 108547584 | tf_op jit(solution)/shard_map/transpose(jvp())/reduce_sum | solution.py:76
  1829.6 127.3 %all-to-all-done.6 = bf16[6,512,768]{2,0,1:T(8,128)(2,1)} async-done(((bf16[6,512,768]{2,0,1:T(8,128)(2,1)}), bf16[6,512,768]{2,0,1:T(8,128)(2,1)}, u32[]{:S(2)}, u32[]{:S(2)}) %all-to-all-start.6) | async-done | bytes 4718624 | tf_op jit(solution)/shard_map/all_to_all | solution.py:356
  1974.9 12.5 bitcast_convert_fusion.3
  1988.1 11.1 broadcast_multiply_fusion.1
  1999.2 13.8 fusion.211
  2022.7 142.0 %all_to_all.126 = bf16[6,512,768]{2,0,1:T(8,128)(2,1)S(1)} all-to-all(bf16[6,512,768]{2,0,1:T(8,128)(2,1)S(1)} %copy.656), channel_id=1, replica_groups=mesh['fs'=8,'sp'=4] {'sp'}, dimensions={1} | all-to-all | bytes 9437184 | tf_op jit(solution)/shard_map/all_to_all | solution.py:355
  2180.1 12.5 bitcast_convert_fusion.2
  2194.8 14.8 fusion.164
  2222.6 13.2 fusion.129
  2235.7 33.8 %reduce-scatter.24.cloned.1.call-done = bf16[192,3072]{1,0:T(8,128)(2,1)} async-done(((bf16[1536,3072]{1,0:T(8,128)(2,1)}), bf16[192,3072]{1,0:T(8,128)(2,1)}) %reduce-scatter.24.cloned.1.call-update) | async-done | bytes 1179664 | tf_op jit(solution)/shard_map/reduce_scatter | solution.py:395
  2269.6 11.6 fusion.133
  2286.5 24.7 %all-reduce.29 = (bf16[1536]{0:T(1024)(128)(2,1)S(1)}, bf16[3072]{0:T(1024)(128)(2,1)S(1)}, bf16[256]{0:T(256)(128)(2,1)S(1)}, bf16[3072]{0:T(1024)(128)(2,1)S(1)}) all-reduce(bf16[1536]{0:T(1024)(128)(2,1)S(1)} %get-tuple-element.1107, bf16[3072]{0:T(1024)(128)(2,1)S(1)} %copy-done.78, ...), channel_id=7, replica_groups=mesh['fs'=8,'sp'=4] {'fs'}, use_global_device_ids=true, to_apply=%region_34.35.clone | all-reduce | flops 7936 | bytes 31744
  2311.4 21.9 all-reduce.31
  2344.6 80.4 %all-reduce.35.cloned.1.call-done = (bf16[192,3072]{0,1:T(8,128)(2,1)}, bf16[192,3072]{1,0:T(8,128)(2,1)}, bf16[192,3072]{1,0:T(8,128)(2,1)}, bf16[192,256]{1,0:T(8,128)(2,1)}) async-done(((bf16[192,3072]{0,1:T(8,128)(2,1)}, bf16[192,3072]{1,0:T(8,128)(2,1)}, bf16[192,3072]{1,0:T(8,128)(2,1)}, bf16[192,256]{1,0:T(8,128)(2,1)}), (bf16[192,3072]{0,1:T(8,128)(2,1)}, bf16[192,3072]{1,0:T(8,128)(2,1)}, ...) | async-done | bytes 3637264 | tf_op jit(solution)/shard_map/psum | solution.py:398
  (718 shorter events, 696.5 us)
Async XLA Ops:
  7.2 44.0 %copy-start.56 = (bf16[192,256]{1,0:T(8,128)(2,1)S(1)}, bf16[192,256]{1,0:T(8,128)(2,1)}, u32[]{:S(2)}) copy-start(bf16[192,256]{1,0:T(8,128)(2,1)} %param.30) | copy-start | bytes 294916
  7.2 67.9 %all-gather.14.cloned.1.call-start = ((), (), s32[]{:S(2)}) async-start(), calls=%async_computation.18 | async-start | bytes 10616832 | tf_op jit(solution)/shard_map/all_gather | solution.py:172
  7.9 58.4 %copy-start.22 = (bf16[6,128,1536]{2,1,0:T(8,128)(2,1)S(1)}, bf16[6,128,1536]{2,1,0:T(8,128)(2,1)}, u32[]{:S(2)}) copy-start(bf16[6,128,1536]{2,1,0:T(8,128)(2,1)} %param.26) | copy-start | bytes 7077892
  31.4 123.0 %copy-start.104 = (bf16[48]{0:T(256)(128)(2,1)}, bf16[48]{0:T(256)(128)(2,1)S(1)}, u32[]{:S(2)}) copy-start(bf16[48]{0:T(256)(128)(2,1)S(1)} %get-tuple-element.1200) | copy-start | bytes 292
  40.2 34.9 %copy-start.59 = (f32[1536]{0:T(1024)}, f32[1536]{0:T(1024)S(1)}, u32[]{:S(2)}) copy-start(f32[1536]{0:T(1024)S(1)} %convert_element_type.327) | copy-start | bytes 18436
  42.5 32.7 %copy-start.74 = (f32[6,128]{1,0:T(8,128)}, f32[6,128]{1,0:T(8,128)S(1)}, u32[]{:S(2)}) copy-start(f32[6,128]{1,0:T(8,128)S(1)} %add_rsqrt_fusion.1) | copy-start | bytes 9220
  46.4 21.1 all-to-all-start
  69.1 53.7 %all-to-all-start.2 = ((bf16[6,128,1024]{1,0,2:T(8,128)(2,1)}), bf16[6,128,1024]{1,0,2:T(8,128)(2,1)}, u32[]{:S(2)}, u32[]{:S(2)}) async-start(bf16[6,128,1024]{1,0,2:T(8,128)(2,1)} %bitcast.583), calls=%async_computation.2 | async-start | bytes 4194304 | tf_op jit(solution)/shard_map/all_to_all | solution.py:229
  96.6 32.3 %copy-start.102 = (bf16[384]{0:T(512)(128)(2,1)S(1)}, bf16[384]{0:T(512)(128)(2,1)}, u32[]{:S(2)}) copy-start(bf16[384]{0:T(512)(128)(2,1)} %param.34) | copy-start | bytes 2308
  96.6 40.6 %copy-start.101 = (bf16[32,4]{0,1:T(4,128)(2,1)S(1)}, bf16[32,4]{0,1:T(4,128)(2,1)}, u32[]{:S(2)}) copy-start(bf16[32,4]{0,1:T(4,128)(2,1)} %param.35) | copy-start | bytes 772
  96.6 49.3 %copy-start.98 = (bf16[384,4]{0,1:T(4,128)(2,1)S(1)}, bf16[384,4]{0,1:T(4,128)(2,1)}, u32[]{:S(2)}) copy-start(bf16[384,4]{0,1:T(4,128)(2,1)} %param.33) | copy-start | bytes 9220
  122.8 143.1 %all-to-all-start.1 = ((bf16[6,128,3072]{1,0,2:T(8,128)(2,1)}), bf16[6,128,3072]{1,0,2:T(8,128)(2,1)}, u32[]{:S(2)}, u32[]{:S(2)}) async-start(bf16[6,128,3072]{1,0,2:T(8,128)(2,1)} %copy.613), calls=%async_computation.1 | async-start | bytes 12582912 | tf_op jit(solution)/shard_map/all_to_all | solution.py:226
  128.1 295.8 %all-gather.16.cloned.1.call-start = ((), (), s32[]{:S(2)}) async-start(), calls=%async_computation.19 | async-start | bytes 10616832 | tf_op jit(solution)/shard_map/all_gather | solution.py:171
  128.8 524.1 %all-gather.20.cloned.1.call-start = ((), (), s32[]{:S(2)}) async-start(), calls=%async_computation.25 | async-start | bytes 21233664 | tf_op jit(solution)/shard_map/all_gather | solution.py:21
  155.1 124.6 %copy-start.66 = (f32[768]{0:T(1024)}, f32[768]{0:T(1024)S(1)}, u32[]{:S(2)}) copy-start(f32[768]{0:T(1024)S(1)} %get-tuple-element.1116) | copy-start | bytes 9220
  155.2 124.6 %copy-start.68 = (f32[768]{0:T(1024)}, f32[768]{0:T(1024)S(1)}, u32[]{:S(2)}) copy-start(f32[768]{0:T(1024)S(1)} %get-tuple-element.1117) | copy-start | bytes 9220
  155.2 124.6 %copy-start.70 = (f32[768]{0:T(1024)}, f32[768]{0:T(1024)S(1)}, u32[]{:S(2)}) copy-start(f32[768]{0:T(1024)S(1)} %get-tuple-element.1118) | copy-start | bytes 9220
  155.2 124.6 %copy-start.72 = (f32[768]{0:T(1024)}, f32[768]{0:T(1024)S(1)}, u32[]{:S(2)}) copy-start(f32[768]{0:T(1024)S(1)} %get-tuple-element.1119) | copy-start | bytes 9220
  159.0 3.9 collective-permute-start.1
  275.3 3.5 collective-permute-start
  327.2 96.7 %copy-start.60 = (f32[1536]{0:T(1024)S(1)}, f32[1536]{0:T(1024)}, u32[]{:S(2)}) copy-start(f32[1536]{0:T(1024)} %copy-done.59) | copy-start | bytes 18436
  327.2 96.7 %copy-start.75 = (f32[6,128]{1,0:T(8,128)S(1)}, f32[6,128]{1,0:T(8,128)}, u32[]{:S(2)}) copy-start(f32[6,128]{1,0:T(8,128)} %copy-done.74) | copy-start | bytes 9220
  446.9 144.4 %all-to-all-start.3 = ((bf16[6,128,3072]{1,0,2:T(8,128)(2,1)}), bf16[6,128,3072]{1,0,2:T(8,128)(2,1)}, u32[]{:S(2)}, u32[]{:S(2)}) async-start(bf16[6,128,3072]{1,0,2:T(8,128)(2,1)} %copy.634), calls=%async_computation.3 | async-start | bytes 12582912 | tf_op jit(solution)/shard_map/all_to_all | solution.py:227
  452.3 415.5 %all-gather.18.cloned.1.call-start = ((), (), s32[]{:S(2)}) async-start(), calls=%async_computation.20 | async-start | bytes 10616832 | tf_op jit(solution)/shard_map/all_gather | solution.py:175
  453.0 224.3 %copy-start.64 = (f32[768]{0:T(1024)}, f32[768]{0:T(1024)S(1)}, u32[]{:S(2)}) copy-start(f32[768]{0:T(1024)S(1)} %mul.797) | copy-start | bytes 9220
  461.8 139.4 %copy-start.31 = (f32[6,12,4,128]{1,0,3,2:T(8,128)}, f32[6,12,4,128]{1,0,3,2:T(8,128)S(1)}, u32[]{:S(2)}) copy-start(f32[6,12,4,128]{1,0,3,2:T(8,128)S(1)} %copy.691) | copy-start | bytes 442372
  462.4 192.3 %copy-start.49 = (f32[6,512,12]{1,2,0:T(8,128)}, f32[6,512,12]{1,2,0:T(8,128)S(1)}, u32[]{:S(2)}) copy-start(f32[6,512,12]{1,2,0:T(8,128)S(1)} %copy.632) | copy-start | bytes 442372
  696.9 143.9 %all-to-all-start.4 = ((bf16[6,512,768]{2,0,1:T(8,128)(2,1)}), bf16[6,512,768]{2,0,1:T(8,128)(2,1)}, u32[]{:S(2)}, u32[]{:S(2)}) async-start(bf16[6,512,768]{2,0,1:T(8,128)(2,1)} %copy.637), calls=%async_computation.4 | async-start | bytes 12582912 | tf_op jit(solution)/shard_map/all_to_all | solution.py:283
  735.2 148.1 %copy-start.62 = (f32[8,1,384]{2,1,0:T(1,128)}, f32[8,1,384]{2,1,0:T(1,128)S(1)}, u32[]{:S(2)}) copy-start(f32[8,1,384]{2,1,0:T(1,128)S(1)} %convert_element_type.436) | copy-start | bytes 36868
  903.3 144.8 %all-to-all-start.5 = ((bf16[6,128,3072]{1,0,2:T(8,128)(2,1)}), bf16[6,128,3072]{1,0,2:T(8,128)(2,1)}, u32[]{:S(2)}, u32[]{:S(2)}) async-start(bf16[6,128,3072]{1,0,2:T(8,128)(2,1)} %copy.644), calls=%async_computation.5 | async-start | bytes 12582912 | tf_op jit(solution)/shard_map/all_to_all | solution.py:305
  908.6 347.9 %all-gather.22.cloned.1.call-start = ((), (), s32[]{:S(2)}) async-start(), calls=%async_computation.26 | async-start | bytes 10616832 | tf_op jit(solution)/shard_map/all_gather | solution.py:35
  1085.2 741.5 %reduce-scatter.20.cloned.1.call-start = ((), (), s32[]{:S(2)}) async-start(), calls=%async_computation.21 | async-start | bytes 1966080 | tf_op jit(solution)/shard_map/reduce_scatter | solution.py:339
  1141.9 26.5 %slice-start.7 = ((s8[9437184]{0:T(1024)(128)(4,1)}), s8[4194304]{0:T(1024)(128)(4,1)S(1)}, s32[]{:S(2)}) async-start(s8[9437184]{0:T(1024)(128)(4,1)} %bitcast.558), calls=%async_computation.40 | async-start | bytes 8388608 | tf_op jit(solution)/shard_map/jvp()/while
  1141.9 32.9 %slice-start.4 = ((s8[9437184]{0:T(1024)(128)(4,1)}), s8[4194304]{0:T(1024)(128)(4,1)S(1)}, s32[]{:S(2)}) async-start(s8[9437184]{0:T(1024)(128)(4,1)} %bitcast.547), calls=%async_computation.37 | async-start | bytes 8388608 | tf_op jit(solution)/shard_map/jvp()/while
  1144.9 30.0 %slice-start.5 = ((s8[9437184]{0:T(1024)(128)(4,1)}), s8[4194304]{0:T(1024)(128)(4,1)S(1)}, s32[]{:S(2)}) async-start(s8[9437184]{0:T(1024)(128)(4,1)} %bitcast.547), calls=%async_computation.38 | async-start | bytes 8388608 | tf_op jit(solution)/shard_map/jvp()/while
  1144.9 30.0 %slice-start.6 = ((s8[9437184]{0:T(1024)(128)(4,1)}), s8[1048576]{0:T(1024)(128)(4,1)S(1)}, s32[]{:S(2)}) async-start(s8[9437184]{0:T(1024)(128)(4,1)} %bitcast.547), calls=%async_computation.39 | async-start | bytes 2097152 | tf_op jit(solution)/shard_map/jvp()/while
  1189.7 26.5 %slice-start.7 = ((s8[9437184]{0:T(1024)(128)(4,1)}), s8[4194304]{0:T(1024)(128)(4,1)S(1)}, s32[]{:S(2)}) async-start(s8[9437184]{0:T(1024)(128)(4,1)} %bitcast.558), calls=%async_computation.40 | async-start | bytes 8388608 | tf_op jit(solution)/shard_map/jvp()/while
  1189.7 32.9 %slice-start.4 = ((s8[9437184]{0:T(1024)(128)(4,1)}), s8[4194304]{0:T(1024)(128)(4,1)S(1)}, s32[]{:S(2)}) async-start(s8[9437184]{0:T(1024)(128)(4,1)} %bitcast.547), calls=%async_computation.37 | async-start | bytes 8388608 | tf_op jit(solution)/shard_map/jvp()/while
  1192.7 30.0 %slice-start.5 = ((s8[9437184]{0:T(1024)(128)(4,1)}), s8[4194304]{0:T(1024)(128)(4,1)S(1)}, s32[]{:S(2)}) async-start(s8[9437184]{0:T(1024)(128)(4,1)} %bitcast.547), calls=%async_computation.38 | async-start | bytes 8388608 | tf_op jit(solution)/shard_map/jvp()/while
  1192.7 30.0 %slice-start.6 = ((s8[9437184]{0:T(1024)(128)(4,1)}), s8[1048576]{0:T(1024)(128)(4,1)S(1)}, s32[]{:S(2)}) async-start(s8[9437184]{0:T(1024)(128)(4,1)} %bitcast.547), calls=%async_computation.39 | async-start | bytes 2097152 | tf_op jit(solution)/shard_map/jvp()/while
  1348.5 28.3 %copy-start.19 = (f32[6,256,256]{2,1,0:T(8,128)}, f32[6,256,256]{2,1,0:T(8,128)S(1)}, u32[]{:S(2)}) copy-start(f32[6,256,256]{2,1,0:T(8,128)S(1)} %fusion.303) | copy-start | bytes 4718596 | tf_op jit(solution)/shard_map/transpose(jvp())/while
  1348.6 28.2 %copy-start.40 = (pred[256,256]{1,0:T(8,128)(4,1)}, pred[256,256]{1,0:T(8,128)(4,1)S(1)}, u32[]{:S(2)}) copy-start(pred[256,256]{1,0:T(8,128)(4,1)S(1)} %iota_compare_fusion.5) | copy-start | bytes 196612 | tf_op jit(solution)/shard_map/transpose(jvp())/while
  1348.6 28.2 %copy-start.2 = (f32[6,12,64,128]{3,2,1,0:T(8,128)S(1)}, f32[6,12,64,128]{3,2,1,0:T(8,128)}, u32[]{:S(2)}) copy-start(f32[6,12,64,128]{3,2,1,0:T(8,128)} %dynamic-slice_bitcast_fusion.15) | copy-start | bytes 7077892 | tf_op jit(solution)/shard_map/transpose(jvp())/while
  1348.6 28.2 %copy-start.6 = (f32[6,256,128]{2,1,0:T(8,128)S(1)}, f32[6,256,128]{2,1,0:T(8,128)}, u32[]{:S(2)}) copy-start(f32[6,256,128]{2,1,0:T(8,128)} %get-tuple-element.1520) | copy-start | bytes 2359300 | tf_op jit(solution)/shard_map/transpose(jvp())/while
  1492.4 28.3 %copy-start.19 = (f32[6,256,256]{2,1,0:T(8,128)}, f32[6,256,256]{2,1,0:T(8,128)S(1)}, u32[]{:S(2)}) copy-start(f32[6,256,256]{2,1,0:T(8,128)S(1)} %fusion.303) | copy-start | bytes 4718596 | tf_op jit(solution)/shard_map/transpose(jvp())/while
  1492.5 28.2 %copy-start.40 = (pred[256,256]{1,0:T(8,128)(4,1)}, pred[256,256]{1,0:T(8,128)(4,1)S(1)}, u32[]{:S(2)}) copy-start(pred[256,256]{1,0:T(8,128)(4,1)S(1)} %iota_compare_fusion.5) | copy-start | bytes 196612 | tf_op jit(solution)/shard_map/transpose(jvp())/while
  1492.5 28.2 %copy-start.2 = (f32[6,12,64,128]{3,2,1,0:T(8,128)S(1)}, f32[6,12,64,128]{3,2,1,0:T(8,128)}, u32[]{:S(2)}) copy-start(f32[6,12,64,128]{3,2,1,0:T(8,128)} %dynamic-slice_bitcast_fusion.15) | copy-start | bytes 7077892 | tf_op jit(solution)/shard_map/transpose(jvp())/while
  1492.5 28.2 %copy-start.6 = (f32[6,256,128]{2,1,0:T(8,128)S(1)}, f32[6,256,128]{2,1,0:T(8,128)}, u32[]{:S(2)}) copy-start(f32[6,256,128]{2,1,0:T(8,128)} %get-tuple-element.1520) | copy-start | bytes 2359300 | tf_op jit(solution)/shard_map/transpose(jvp())/while
  1603.3 3.2 collective-permute-start.3
  1607.8 601.7 %reduce-scatter.30.cloned.1.call-start = ((), (), s32[]{:S(2)}) async-start(), calls=%async_computation.28 | async-start | bytes 10616832
  1708.9 103.7 %all-to-all-start.8 = ((bf16[4,2,4608]{2,1,0:T(2,128)(2,1)}), bf16[4,2,4608]{2,1,0:T(2,128)(2,1)S(1)}, u32[]{:S(2)}, u32[]{:S(2)}) async-start(bf16[4,2,4608]{2,1,0:T(2,128)(2,1)} %reshape.653), calls=%async_computation.9 | async-start | bytes 147456 | tf_op jit(solution)/shard_map/all_to_all | solution.py:357
  1812.7 144.3 %all-to-all-start.6 = ((bf16[6,512,768]{2,0,1:T(8,128)(2,1)}), bf16[6,512,768]{2,0,1:T(8,128)(2,1)}, u32[]{:S(2)}, u32[]{:S(2)}) async-start(bf16[6,512,768]{2,0,1:T(8,128)(2,1)} %copy.647), calls=%async_computation.6 | async-start | bytes 12582912 | tf_op jit(solution)/shard_map/all_to_all | solution.py:356
  1818.1 396.0 %reduce-scatter.34.cloned.1.call-start = ((), (), s32[]{:S(2)}) async-start(), calls=%async_computation.30 | async-start | bytes 73728
  1820.0 395.4 %reduce-scatter.36.cloned.1.call-start = ((), (), s32[]{:S(2)}) async-start(), calls=%async_computation.31 | async-start | bytes 884736
  1821.6 395.5 %reduce-scatter.32.cloned.1.call-start = ((), (), s32[]{:S(2)}) async-start(), calls=%async_computation.29 | async-start | bytes 884736
  1822.9 395.1 %reduce-scatter.28.cloned.1.call-start = ((), (), s32[]{:S(2)}) async-start(), calls=%async_computation.27 | async-start | bytes 442368
  1826.6 409.2 %reduce-scatter.26.cloned.1.call-start = ((), (), s32[]{:S(2)}) async-start(), calls=%async_computation.24 | async-start | bytes 884736 | tf_op jit(solution)/shard_map/reduce_scatter | solution.py:395
  1829.6 406.1 %reduce-scatter.22.cloned.1.call-start = ((), (), s32[]{:S(2)}) async-start(), calls=%async_computation.22 | async-start | bytes 10616832 | tf_op jit(solution)/shard_map/reduce_scatter | solution.py:395
  1987.4 282.1 %reduce-scatter.24.cloned.1.call-start = ((), (), s32[]{:S(2)}) async-start(), calls=%async_computation.23 | async-start | bytes 10616832 | tf_op jit(solution)/shard_map/reduce_scatter | solution.py:395
  2013.9 4.8 collective-permute-start.2
  2192.6 232.4 %all-reduce.35.cloned.1.call-start = ((), (), s32[]{:S(2)}) async-start(), calls=%async_computation.32 | async-start | bytes 8060928 | tf_op jit(solution)/shard_map/psum | solution.py:398
  2281.3 30.1 %copy-start.57 = (bf16[192,48]{0,1:T(8,128)(2,1)S(1)}, bf16[192,48]{0,1:T(8,128)(2,1)}, u32[]{:S(2)}) copy-start(bf16[192,48]{0,1:T(8,128)(2,1)} %copy.695) | copy-start | bytes 55300
  2281.3 30.1 %copy-start.77 = (bf16[6,64,3]{1,0,2:T(8,128)(2,1)S(1)}, bf16[6,64,3]{1,0,2:T(8,128)(2,1)}, u32[]{:S(2)}) copy-start(bf16[6,64,3]{1,0,2:T(8,128)(2,1)} %copy.704) | copy-start | bytes 6916
  2281.3 30.1 %copy-start.97 = (bf16[32,4]{0,1:T(4,128)(2,1)S(1)}, bf16[32,4]{0,1:T(4,128)(2,1)}, u32[]{:S(2)}) copy-start(bf16[32,4]{0,1:T(4,128)(2,1)} %copy.701) | copy-start | bytes 772
  (111 other events, 966.0 us)
Sparse Core Ops, SparseCore 0:
  9.9 65.1 all-gather.13
  130.8 59.3 all-gather.15
  424.0 99.0 all-gather.19
  524.8 58.8 all-gather.17
  1085.3 78.9 all-gather.21
  1608.0 36.4 reduce-scatter.19
  1648.0 75.4 reduce-scatter.29
  1821.9 36.1 reduce-scatter.33
  1862.1 34.9 reduce-scatter.35
  1901.0 34.9 reduce-scatter.31
  1939.4 33.7 reduce-scatter.27
  1976.5 34.9 reduce-scatter.25
  2015.5 76.4 reduce-scatter.21
  2192.7 76.7 reduce-scatter.23
  2272.8 152.1 all-reduce.34
where the time goes:
time: 2460 us; the launch traced here: 2440 us
  waiting for transfers between devices  717 us (29%)
  local copies, waits for them, and re-layouts  536 us (22%)
  matrix products  514 us (21%)
  blocking collectives  326 us (13%)
  other arithmetic  252 us (10%)
  starting transfers between devices  48.3 us (2%)
  loops' own time  27.7 us (1%)
    dot_general x8, matrix products, span_update(): jnp.einsum('btsh,bshp->bthp', scores[..., None] * decay_mix, weighted, pr...  188 us
    all_to_all x1, blocking collectives, body(): lax.all_to_all(grad_x_low, 'sp', split_axis=1, concat_axis=2, tiled=True)  142 us
    all_to_all x1, waiting for transfers between devices, body(): lax.all_to_all(grad_gate_low, 'sp', split_axis=1, concat_axis=2, tiled=True)  127 us
    all_to_all x1, waiting for transfers between devices, body(): lax.all_to_all(grad_gated, 'sp', split_axis=2, concat_axis=1, tiled=True)  127 us
    all_to_all x1, waiting for transfers between devices, body(): lax.all_to_all(gate_in, 'sp', split_axis=2, concat_axis=1, tiled=True)  116 us
    all_to_all x1, waiting for transfers between devices, body(): lax.all_to_all(gated.astype(jnp.bfloat16), 'sp', split_axis=1, concat_axi...  106 us
    all_to_all x1, waiting for transfers between devices, body(): lax.all_to_all(x_in, 'sp', split_axis=2, concat_axis=1, tiled=True)  95.8 us
    psum x1, waiting for transfers between devices, body(): lax.psum(for_sending(shards), 'sp')  80.4 us
  transfers between devices with their start and end apart: 27, of which 10 were waited for; matrix products, arithmetic and copies ran while one was open for 36% of the time, Pallas kernels for 0%

commit v1 on v0

v1 whole, which is shorter than its diff:
```python
import functools

import jax
import jax.numpy as jnp
from jax import lax
from jax.experimental import pallas as pl
from jax.experimental.pallas import tpu as pltpu
from jax.sharding import PartitionSpec as P

EPSILON = 1e-05
F32, BF16 = jnp.float32, jnp.bfloat16
MESH = pl.DeviceIdType.MESH
CHUNK = 128
LANES = 128
PER_UNIT = 4
VMEM_LIMIT = 56 * 1024 * 1024


def dot(a, b):
    return jnp.dot(a, b, preferred_element_type=F32)


def dot_nt(a, b):
    return lax.dot_general(a, b, (((1,), (1,)), ((), ())), preferred_element_type=F32)


def dot_tn(a, b):
    return lax.dot_general(a, b, (((0,), (0,)), ((), ())), preferred_element_type=F32)


def pieces_of(v):
    high = v.astype(BF16)
    rest = v - high.astype(F32)
    middle = rest.astype(BF16)
    return high, middle, (rest - middle.astype(F32)).astype(BF16)


def exact_left(ones, v):
    return sum(dot(ones, part) for part in pieces_of(v))


def exact_right(v, ones):
    return sum(dot(part, ones) for part in pieces_of(v))


def sigmoid(v):
    return 0.5 * jnp.tanh(0.5 * v) + 0.5


def grid_iotas():
    rows = lax.broadcasted_iota(jnp.int32, (CHUNK, CHUNK), 0)
    columns = lax.broadcasted_iota(jnp.int32, (CHUNK, CHUNK), 1)
    return rows, columns


def two_heads(v, pair, low):
    return jnp.where(low, v[:, 2 * pair : 2 * pair + 1], v[:, 2 * pair + 1 : 2 * pair + 2])


def conv_of(ext, lanes, taps):
    total = taps[4:5, lanes]
    for k in range(4):
        total = total + ext[5 + k : 5 + k + CHUNK, lanes] * taps[k : k + 1, lanes]
    return total


def forward_kernel(
    x_ref, xp_ref, bc_ref, bcp_ref, step_ref, cx_ref, cbc_ref, hp_ref,
    y_ref, st_ref, own_ref, dec_ref, bcs_ref, acum_ref,
    xe, be, state, base,
):
    chunk = pl.program_id(1)
    inner = x_ref.shape[1]

    @pl.when(chunk == 0)
    def _():
        state[...] = jnp.zeros_like(state)
        base[...] = jnp.zeros_like(base)

    xe[0:8] = xp_ref[0]
    xe[8:] = x_ref[...].astype(F32)
    be[0:8] = bcp_ref[0]
    be[8:] = bc_ref[...].astype(F32)
    shared = []
    for k in range(2):
        pre = conv_of(be, slice(k * LANES, (k + 1) * LANES), cbc_ref)
        shared.append(pre * sigmoid(pre))
    keys, reads = shared
    bcs_ref[:, :LANES] = keys.astype(BF16)
    bcs_ref[:, LANES:] = reads.astype(BF16)
    keys_t = keys.T.astype(BF16)
    keys, reads = keys.astype(BF16), reads.astype(BF16)
    rows, columns = grid_iotas()
    causal = rows >= columns
    step = step_ref[...]
    running = exact_left(jnp.where(causal, 1.0, 0.0).astype(BF16), -step * hp_ref[0:1])
    acum_ref[...] = base[0:1] + running
    total = running[CHUNK - 1 : CHUNK]
    base[...] = base[...] + total
    running_t = running.T
    scores = jnp.where(causal, dot_nt(reads, keys), 0.0)
    low = columns < LANES // 2
    low_row = low[0:1]

    for pair in range(inner // LANES):
        lanes = slice(pair * LANES, (pair + 1) * LANES)
        pre = conv_of(xe, lanes, cx_ref)
        xs = pre * sigmoid(pre)
        weighted = xs * two_heads(step, pair, low)
        first = jnp.broadcast_to(running[:, 2 * pair : 2 * pair + 1], (CHUNK, CHUNK))
        second = jnp.broadcast_to(running[:, 2 * pair + 1 : 2 * pair + 2], (CHUNK, CHUNK))
        mix = jnp.concatenate(
            [
                (jnp.exp(jnp.minimum(first - running_t[2 * pair : 2 * pair + 1], 0.0)) * scores).astype(BF16),
                (jnp.exp(jnp.minimum(second - running_t[2 * pair + 1 : 2 * pair + 2], 0.0)) * scores).astype(BF16),
            ],
            axis=1,
        )
        own = weighted.astype(BF16)
        zero = jnp.zeros_like(own)
        stacked = jnp.concatenate([jnp.where(low, own, zero), jnp.where(low, zero, own)], axis=0)
        at = jnp.where(low, first, second)
        at_end = two_heads(total, pair, low_row)
        before = state[:, lanes]
        before_low = before.astype(BF16)
        st_ref[0, :, lanes] = before_low
        y = dot(mix, stacked) + dot(reads, before_low) * jnp.exp(at) + cx_ref[5:6, lanes] * xs
        y_ref[:, lanes] = y.astype(BF16)
        late = (weighted * jnp.exp(at_end - at)).astype(BF16)
        state[:, lanes] = before * jnp.exp(at_end) + dot(keys_t, late)

    @pl.when(chunk == PER_UNIT - 1)
    def _():
        own_ref[0] = state[...].astype(BF16)
        for pair in range(inner // LANES):
            lanes = slice(pair * LANES, (pair + 1) * LANES)
            dec_ref[0, :, lanes] = jnp.broadcast_to(
                jnp.exp(two_heads(base[0:1], pair, low_row)), (8, LANES)
            )


def gate_kernel(y0_ref, gate_ref, bcs_ref, acum_ref, in_ref, y_ref, gated_ref, ss_ref):
    _, columns = grid_iotas()
    low = columns < LANES // 2
    reads = bcs_ref[:, LANES:]
    reach = acum_ref[...]
    squares = jnp.zeros((CHUNK, LANES), F32)
    for pair in range(y0_ref.shape[1] // LANES):
        lanes = slice(pair * LANES, (pair + 1) * LANES)
        y = y0_ref[:, lanes].astype(F32) + dot(reads, in_ref[0, :, lanes]) * jnp.exp(
            two_heads(reach, pair, low)
        )
        y_ref[:, lanes] = y.astype(BF16)
        gate = gate_ref[:, lanes].astype(F32)
        gated = (y * gate * sigmoid(gate)).astype(BF16)
        gated_ref[:, lanes] = gated
        wide = gated.astype(F32)
        squares = squares + wide * wide
    ss_ref[...] = jnp.broadcast_to(jnp.sum(squares, axis=1, keepdims=True), (CHUNK, LANES))


def pull_kernel(
    dno_ref, gated_ref, gate_ref, y_ref, stats_ref, gain_ref, bcs_ref, acum_ref,
    dy_ref, dgate_ref, pull_ref,
    total,
):
    chunk = pl.program_id(1)

    @pl.when(chunk == 0)
    def _():
        total[...] = jnp.zeros_like(total)

    _, columns = grid_iotas()
    low = columns < LANES // 2
    scale = jnp.broadcast_to(stats_ref[:, 0:1], (CHUNK, LANES))
    mean = jnp.broadcast_to(stats_ref[:, 1:2], (CHUNK, LANES))
    reads_t = bcs_ref[:, LANES:].astype(F32).T.astype(BF16)
    reach = acum_ref[...]
    for pair in range(dno_ref.shape[1] // LANES):
        lanes = slice(pair * LANES, (pair + 1) * LANES)
        unit = gated_ref[:, lanes].astype(F32) * scale
        du = dno_ref[:, lanes].astype(F32) * gain_ref[0:1, lanes]
        d_gated = (scale * (du - unit * mean)).astype(BF16).astype(F32)
        gate = gate_ref[:, lanes].astype(F32)
        sg = sigmoid(gate)
        silu = gate * sg
        dy = d_gated * silu
        dy_ref[:, lanes] = dy.astype(BF16)
        dgate = d_gated * y_ref[:, lanes].astype(F32) * (sg + silu * (1.0 - sg))
        dgate_ref[:, lanes] = dgate.astype(BF16)
        total[:, lanes] += dot(reads_t, (dy * jnp.exp(two_heads(reach, pair, low))).astype(BF16))

    @pl.when(chunk == PER_UNIT - 1)
    def _():
        pull_ref[0] = total[...].astype(BF16)


def backward_kernel(
    x_ref, xp_ref, bc_ref, bcp_ref, step_ref, sig_ref, cx_ref, cbc_ref, hp_ref,
    dy_ref, y_ref, st_ref, in_ref, acum_ref, after_ref, pick_ref,
    dall_ref, head_ref, head_bc_ref, gx_ref, gbc_ref, gh_ref,
    xe, be, adjoint, dpx, dpb, ends,
):
    unit, chunk = pl.program_id(0), pl.program_id(1)
    inner = x_ref.shape[1]

    @pl.when((unit == 0) & (chunk == 0))
    def _():
        gx_ref[...] = jnp.zeros_like(gx_ref)
        gbc_ref[...] = jnp.zeros_like(gbc_ref)
        gh_ref[...] = jnp.zeros_like(gh_ref)

    @pl.when(chunk == 0)
    def _():
        adjoint[...] = after_ref[0].astype(F32)
        dpx[CHUNK:] = jnp.zeros((8, inner), F32)
        dpb[CHUNK:] = jnp.zeros((8, 2 * LANES), F32)

    xe[0:8] = xp_ref[0]
    xe[8:] = x_ref[...].astype(F32)
    be[0:8] = bcp_ref[0]
    be[8:] = bc_ref[...].astype(F32)
    shared, slopes = [], []
    for k in range(2):
        pre = conv_of(be, slice(k * LANES, (k + 1) * LANES), cbc_ref)
        sg = sigmoid(pre)
        shared.append(pre * sg)
        slopes.append(sg + pre * sg * (1.0 - sg))
    keys, reads = shared
    reads_t = reads.T.astype(BF16)
    keys, reads = keys.astype(BF16), reads.astype(BF16)
    rows, columns = grid_iotas()
    causal = rows >= columns
    step = step_ref[...]
    rate = hp_ref[0:1]
    log_decay = -step * rate
    running = exact_left(jnp.where(causal, 1.0, 0.0).astype(BF16), log_decay)
    total = running[CHUNK - 1 : CHUNK]
    base = acum_ref[0:1] - running[0:1]
    running_t = running.T
    scores_t = jnp.where(rows <= columns, dot_nt(keys, reads), 0.0)
    low = columns < LANES // 2
    low_row = low[0:1]
    d_scores = jnp.zeros((CHUNK, CHUNK), F32)
    d_reads = jnp.zeros((CHUNK, LANES), F32)
    d_keys = jnp.zeros((CHUNK, LANES), F32)
    sums = jnp.zeros((3 * CHUNK, LANES), F32)

    for pair in range(inner // LANES):
        lanes = slice(pair * LANES, (pair + 1) * LANES)
        shifted = [xe[5 + k : 5 + k + CHUNK, lanes] for k in range(4)]
        pre = cx_ref[4:5, lanes] + sum(shifted[k] * cx_ref[k : k + 1, lanes] for k in range(4))
        sg = sigmoid(pre)
        xs = pre * sg
        slope = sg + xs * (1.0 - sg)
        step_wide = two_heads(step, pair, low)
        weighted = xs * step_wide
        first = jnp.broadcast_to(running[:, 2 * pair : 2 * pair + 1], (CHUNK, CHUNK))
        second = jnp.broadcast_to(running[:, 2 * pair + 1 : 2 * pair + 2], (CHUNK, CHUNK))
        gap0 = first - running_t[2 * pair : 2 * pair + 1]
        gap1 = second - running_t[2 * pair + 1 : 2 * pair + 2]
        mix_t = jnp.concatenate(
            [
                (jnp.exp(jnp.minimum(-gap0, 0.0)) * scores_t).astype(BF16),
                (jnp.exp(jnp.minimum(-gap1, 0.0)) * scores_t).astype(BF16),
            ],
            axis=1,
        )
        dy_low = dy_ref[:, lanes]
        dy = dy_low.astype(F32)
        zero = jnp.zeros_like(dy_low)
        dy_two = jnp.concatenate([jnp.where(low, dy_low, zero), jnp.where(low, zero, dy_low)], axis=0)
        d_mix = dot_nt(dy_two, weighted.astype(BF16))
        d_scores = d_scores + (
            jnp.exp(jnp.minimum(gap0, 0.0)) * d_mix[:CHUNK]
            + jnp.exp(jnp.minimum(gap1, 0.0)) * d_mix[CHUNK:]
        )
        at = jnp.where(low, first, second)
        at_end = two_heads(total, pair, low_row)
        tail = jnp.exp(at_end - at)
        end_decay = jnp.exp(at_end)
        later = adjoint[:, lanes]
        later_low = later.astype(BF16)
        from_state = dot(keys, later_low) * tail
        d_weighted = dot(mix_t, dy_two) + from_state
        before = st_ref[0, :, lanes].astype(F32) + in_ref[0, :, lanes].astype(F32) * jnp.exp(
            two_heads(base, pair, low_row)
        )
        d_read = (dy * jnp.exp(at)).astype(BF16)
        d_reads = d_reads + dot_nt(d_read, before.astype(BF16))
        d_keys = d_keys + dot_nt((weighted * tail).astype(BF16), later_low)
        skip = cx_ref[5:6, lanes]
        y = y_ref[:, lanes].astype(F32) - skip * xs
        d_run = dy * y - weighted * d_weighted
        pick = pick_ref[lanes, :]
        sums = sums + dot(
            jnp.concatenate(
                [d_run.astype(BF16), (xs * d_weighted).astype(BF16), (dy * xs).astype(BF16)], axis=0
            ),
            pick,
        )
        ends[:, lanes] = jnp.broadcast_to(
            jnp.sum(weighted * from_state, axis=0, keepdims=True)
            + end_decay * jnp.sum(later * before, axis=0, keepdims=True),
            (8, LANES),
        )
        d_pre = (step_wide * d_weighted + skip * dy) * slope
        dpx[0:CHUNK, lanes] = d_pre
        adjoint[:, lanes] = later * end_decay + dot(reads_t, d_read)
        d_x = jnp.zeros((CHUNK, LANES), F32)
        for k in range(4):
            d_x = d_x + dpx[3 - k : 3 - k + CHUNK, lanes] * cx_ref[k : k + 1, lanes]
            gx_ref[8 * k : 8 * k + 8, lanes] += jnp.sum(
                (d_pre * shifted[k]).reshape(CHUNK // 8, 8, LANES), axis=0
            )
        gx_ref[32:40, lanes] += jnp.sum(d_pre.reshape(CHUNK // 8, 8, LANES), axis=0)
        dall_ref[:, lanes] = d_x.astype(BF16)

    d_scores_low = jnp.where(causal, d_scores, 0.0)
    d_reads = d_reads + dot(d_scores_low.astype(BF16), keys)
    d_keys = d_keys + dot(d_scores_low.T.astype(BF16), reads)
    for k, part in enumerate((d_keys, d_reads)):
        lanes = slice(k * LANES, (k + 1) * LANES)
        d_pre = part * slopes[k]
        dpb[0:CHUNK, lanes] = d_pre
        d_x = jnp.zeros((CHUNK, LANES), F32)
        for tap in range(4):
            d_x = d_x + dpb[3 - tap : 3 - tap + CHUNK, lanes] * cbc_ref[tap : tap + 1, lanes]
            gbc_ref[8 * tap : 8 * tap + 8, lanes] += jnp.sum(
                (d_pre * be[5 + tap : 5 + tap + CHUNK, lanes]).reshape(CHUNK // 8, 8, LANES), axis=0
            )
        gbc_ref[32:40, lanes] += jnp.sum(d_pre.reshape(CHUNK // 8, 8, LANES), axis=0)
        dall_ref[:, inner + k * LANES : inner + (k + 1) * LANES] = d_x.astype(BF16)

    at_end = exact_right(ends[...], pick_ref[...])[0:1]
    d_log = exact_left(jnp.where(rows <= columns, 1.0, 0.0).astype(BF16), sums[:CHUNK]) + at_end
    d_step = sums[CHUNK : 2 * CHUNK] - d_log * rate
    d_dt = d_step * sig_ref[...]
    dall_ref[:, inner + 2 * LANES :] = d_dt.astype(BF16)
    for k, part in enumerate((d_dt, d_log * log_decay, sums[2 * CHUNK :])):
        gh_ref[8 * k : 8 * k + 8] += jnp.sum(part.reshape(CHUNK // 8, 8, LANES), axis=0)
    dpx[CHUNK:] = dpx[0:8]
    dpb[CHUNK:] = dpb[0:8]

    @pl.when(chunk == PER_UNIT - 1)
    def _():
        head_ref[0] = dpx[0:8]
        head_bc_ref[0] = dpb[0:8]


def exchange_kernel(
    count, joints, back, own_ref, dec_ref, out_ref, dec_out_ref,
    parts, decs, results, sends, receives, dec_sends, dec_receives, back_sends, back_receives,
):
    f, z = lax.axis_index("fs"), lax.axis_index("sp")
    core, group = f % 2, z // joints
    me = (f // 2) * joints + z % joints
    units, share = own_ref.shape[0], parts.shape[2]

    def peer(k):
        other = (me + k) % count
        return other, ((other // joints) * 2 + core, group * joints + other % joints)

    barrier = pltpu.get_barrier_semaphore()
    for k in range(1, count):
        pl.semaphore_signal(barrier, inc=1, device_id=peer(k)[1], device_id_type=MESH)
    pl.semaphore_wait(barrier, count - 1)

    def rows_of(i):
        return pl.ds(pl.multiple_of(i * share, share), share)

    def out_copy(k):
        other, device = peer(k)
        return pltpu.make_async_remote_copy(
            src_ref=own_ref.at[:, rows_of(other)], dst_ref=parts.at[me],
            send_sem=sends.at[k], recv_sem=receives.at[me], device_id=device, device_id_type=MESH,
        )

    def dec_copy(k):
        return pltpu.make_async_remote_copy(
            src_ref=dec_ref, dst_ref=decs.at[me],
            send_sem=dec_sends.at[k], recv_sem=dec_receives.at[me],
            device_id=peer(k)[1], device_id_type=MESH,
        )

    def back_copy(k):
        other, device = peer(k)
        return pltpu.make_async_remote_copy(
            src_ref=results.at[other], dst_ref=out_ref.at[:, rows_of(me)],
            send_sem=back_sends.at[k], recv_sem=back_receives.at[me],
            device_id=device, device_id_type=MESH,
        )

    for k in range(1, count):
        if not back:
            dec_copy(k).start()
        out_copy(k).start()
    parts[me] = own_ref[:, rows_of(me)]
    if not back:
        decs[me] = dec_ref[...]
    else:
        decs[...] = dec_ref[...]
    for k in range(1, count):
        other = (me + k) % count
        if not back:
            pltpu.make_async_remote_copy(
                src_ref=dec_ref, dst_ref=decs.at[other],
                send_sem=dec_sends.at[k], recv_sem=dec_receives.at[other],
                device_id=peer(k)[1], device_id_type=MESH,
            ).wait_recv()
        pltpu.make_async_remote_copy(
            src_ref=own_ref.at[:, rows_of(other)], dst_ref=parts.at[other],
            send_sem=sends.at[k], recv_sem=receives.at[other],
            device_id=peer(k)[1], device_id_type=MESH,
        ).wait_recv()
    if not back:
        dec_out_ref[...] = decs[...]
    order = range(count - 1, -1, -1) if back else range(count)
    width = own_ref.shape[2]
    running = [jnp.zeros((share, width), F32) for _ in range(units)]
    for i in order:
        for u in range(units):
            results[i, u] = running[u].astype(BF16)
            running[u] = running[u] * decs[i, u : u + 1] + parts[i, u].astype(F32)
    out_ref[:, rows_of(me)] = results[me]
    for k in range(1, count):
        back_copy(k).start()
    for k in range(1, count):
        other = (me + k) % count
        pltpu.make_async_remote_copy(
            src_ref=results.at[other], dst_ref=out_ref.at[:, rows_of(other)],
            send_sem=back_sends.at[k], recv_sem=back_receives.at[other],
            device_id=peer(k)[1], device_id_type=MESH,
        ).wait_recv()
    for k in range(1, count):
        if not back:
            dec_copy(k).wait_send()
        out_copy(k).wait_send()
        back_copy(k).wait_send()


class Plan:
    def __init__(self, batch, tokens):
        self.shards, self.members = lax.axis_size("fs"), lax.axis_size("sp")
        self.f, self.z = lax.axis_index("fs"), lax.axis_index("sp")
        self.core = self.f % 2
        self.chips = self.shards // 2
        self.chip = self.f // 2
        self.batch, self.tokens = batch, tokens
        self.units = batch // 2
        self.joints = self.members // 2
        self.count = self.chips * self.joints
        self.group, self.joint = self.z // self.joints, self.z % self.joints
        self.fast = self.chips == 4 and self.members == 4

    def at(self, f, z):
        return f * self.members + z

    def send(self, x, pairs):
        return lax.ppermute(x, ("fs", "sp"), pairs)

    def swap(self, x, df=0, dz=0):
        pairs = [
            (self.at(f, z), self.at(f ^ df, z ^ dz))
            for f in range(self.shards)
            for z in range(self.members)
        ]
        return self.send(x, pairs)

    def along(self, x, by):
        pairs = []
        for f in range(self.shards):
            for z in range(self.members):
                place = (f // 2) * self.joints + z % self.joints + by
                if 0 <= place < self.count:
                    there = (place // self.joints) * 2 + f % 2
                    pairs.append(
                        (self.at(f, z), self.at(there, z - z % self.joints + place % self.joints))
                    )
        return self.send(x, pairs)

    def by_core(self, mine, other):
        first = self.core == 0
        return jnp.where(first, mine, other), jnp.where(first, other, mine)

    def turned(self, blocks):
        if not self.fast:
            return blocks
        x, y = (self.chip % 2) == 1, (self.chip // 2) == 1
        a, b, c, d = blocks
        a, b = jnp.where(x, b, a), jnp.where(x, a, b)
        c, d = jnp.where(x, d, c), jnp.where(x, c, d)
        return [jnp.where(y, c, a), jnp.where(y, d, b), jnp.where(y, a, c), jnp.where(y, b, d)]

    def turn(self, x):
        if not self.fast:
            return x
        return jnp.concatenate(self.turned(jnp.split(x, 4, axis=-1)), axis=-1)

    def gather(self, x):
        if not self.fast:
            groups = [list(range(c, self.shards, 2)) for c in range(2)]
            return lax.all_gather(x, "fs", axis=0, tiled=True, axis_index_groups=groups)
        half = x.shape[0] // 2
        by_x, by_y = self.swap(x, df=2), self.swap(x, df=4)
        top, bottom = self.swap(by_x[:half], df=4), self.swap(by_y[half:], df=2)
        return jnp.concatenate([x, by_x, by_y, top, bottom], axis=0)

    def reduce_chips(self, g):
        if not self.fast:
            groups = [list(range(c, self.shards, 2)) for c in range(2)]
            return lax.psum_scatter(
                g.astype(BF16), "fs", scatter_dimension=0, tiled=True, axis_index_groups=groups
            ).astype(F32)
        rows, width = g.shape[0] // 4, g.shape[1]
        cut = -(-width // (2 * LANES)) * LANES
        blocks = [g[i * rows : (i + 1) * rows] for i in range(4)]
        left, right = [b[:, :cut] for b in blocks], [b[:, cut:] for b in blocks]
        sent_left = self.swap(jnp.concatenate([left[1], left[3]], axis=0).astype(BF16), df=2)
        sent_right = self.swap(jnp.concatenate([right[2], right[3]], axis=0).astype(BF16), df=4)
        next_left = self.swap((left[2] + sent_left[rows:]).astype(BF16), df=4)
        next_right = self.swap((right[1] + sent_right[rows:]).astype(BF16), df=2)
        return jnp.concatenate(
            [left[0] + sent_left[:rows] + next_left, right[0] + sent_right[:rows] + next_right], axis=1
        )

    def reduce_members(self, g):
        if not self.fast:
            return lax.psum(g.astype(BF16), "sp").astype(F32)
        half = g.shape[0] // 2
        first = self.z % 2 == 0
        kept, given = jnp.where(first, g[:half], g[half:]), jnp.where(first, g[half:], g[:half])
        kept = kept + self.swap(given.astype(BF16), dz=1)
        low = kept.astype(BF16)
        kept = (low.astype(F32) + self.swap(low, dz=2)).astype(BF16)
        other = self.swap(kept, dz=1)
        return jnp.concatenate(
            [jnp.where(first, kept, other), jnp.where(first, other, kept)], axis=0
        ).astype(F32)

    def to_units(self, rows):
        half = rows.shape[-1] // 2
        left, right = rows[..., :half], rows[..., half:]
        first = self.core == 0
        mine = jnp.where(first, left, right)
        other = self.swap(jnp.where(first, right, left), df=1)
        both = jnp.stack(self.by_core(mine, other))
        if self.fast:
            parts = [both[t % 2, (t // 2) * self.units : (t // 2 + 1) * self.units] for t in range(4)]
            parts = self.across(parts)
            block = jnp.stack(parts, axis=1)
        else:
            everything = lax.all_gather(both, "sp")
            per_core = self.joints // 2
            block = lax.dynamic_slice(
                everything,
                ((self.joint % per_core) * 4, self.joint // per_core, self.group * self.units, 0, 0),
                (4, 1, self.units) + both.shape[2:],
            )[:, 0]
            block = jnp.moveaxis(block, 0, 1)
        block = block.reshape(self.units * 4 * self.tokens, half)
        pair = self.by_core(block, self.swap(block, df=1))
        return jnp.concatenate(pair, axis=1)

    def across(self, parts):
        low, high = (self.z % 2) == 1, (self.z // 2) == 1
        a, b, c, d = parts
        a, b = jnp.where(low, b, a), jnp.where(low, a, b)
        c, d = jnp.where(low, d, c), jnp.where(low, c, d)
        a, b, c, d = (
            jnp.where(high, c, a),
            jnp.where(high, d, b),
            jnp.where(high, a, c),
            jnp.where(high, b, d),
        )
        d, c, b = self.swap(d, dz=3), self.swap(c, dz=2), self.swap(b, dz=1)
        a, b = jnp.where(low, b, a), jnp.where(low, a, b)
        c, d = jnp.where(low, d, c), jnp.where(low, c, d)
        return [
            jnp.where(high, c, a),
            jnp.where(high, d, b),
            jnp.where(high, a, c),
            jnp.where(high, b, d),
        ]

    def from_units(self, partial):
        half = partial.shape[-1] // 2
        first = self.core == 0
        left, right = partial[:, :half], partial[:, half:]
        mine = jnp.where(first, left, right)
        total = (mine + self.swap(jnp.where(first, right, left).astype(BF16), df=1)).astype(BF16)
        block = total.reshape(self.units, 4, self.tokens, half)
        if self.fast:
            parts = self.across([block[:, t] for t in range(4)])
            both = [jnp.concatenate([parts[c], parts[2 + c]], axis=0) for c in range(2)]
        else:
            per_core = self.joints // 2
            wide = jnp.zeros((self.members, 2, self.batch, self.tokens, half), BF16)
            wide = lax.dynamic_update_slice(
                wide,
                jnp.moveaxis(block, 1, 0)[:, None],
                ((self.joint % per_core) * 4, self.joint // per_core, self.group * self.units, 0, 0),
            )
            summed = lax.psum_scatter(wide, "sp", scatter_dimension=0, tiled=False)
            both = [summed[0], summed[1]]
        mine, other = jnp.where(first, both[0], both[1]), jnp.where(first, both[1], both[0])
        return jnp.concatenate(self.by_core(mine, self.swap(other, df=1)), axis=-1)

    def sum_all(self, x):
        if not self.fast:
            groups = [list(range(c, self.shards, 2)) for c in range(2)]
            return lax.psum(lax.psum(x, "fs", axis_index_groups=groups), "sp")
        for df, dz in ((2, 0), (4, 0), (0, 1), (0, 2)):
            x = x + self.swap(x, df, dz)
        return x


def row_scale(values):
    return lax.rsqrt(jnp.mean(values * values, axis=-1, keepdims=True) + EPSILON)


def rows_spec(width, column=0, back=False):
    def place(u, c):
        return (u * PER_UNIT + (PER_UNIT - 1 - c if back else c), column)

    return pl.BlockSpec((CHUNK, width), place)


def chunk_spec(shape, back=False):
    def place(u, c):
        return (u * PER_UNIT + (PER_UNIT - 1 - c if back else c), 0, 0)

    return pl.BlockSpec((1,) + shape, place)


def unit_spec(shape):
    return pl.BlockSpec((1,) + shape, lambda u, c: (u, 0, 0))


def whole_spec(shape):
    return pl.BlockSpec(shape, lambda u, c: (0,) * len(shape))


def params():
    return pltpu.CompilerParams(
        dimension_semantics=("arbitrary", "arbitrary"), vmem_limit_bytes=VMEM_LIMIT
    )


def exchange(plan, own, decays, back):
    units, depth, width = own.shape
    count = plan.count
    if depth % (16 * count):
        rates, pieces = decays[:units, None], own.astype(F32)

        def hop(_, before):
            return plan.along((before * rates + pieces).astype(BF16), -1 if back else 1).astype(F32)

        found = lax.fori_loop(0, count - 1, hop, jnp.zeros(own.shape, F32))
        return found.astype(BF16), decays
    share = depth // count
    dec_shape = (count, 8, width)
    vmem = pl.BlockSpec(memory_space=pltpu.VMEM)
    scratch = [
        pltpu.VMEM((count, units, share, width), BF16),
        pltpu.VMEM(dec_shape, F32),
        pltpu.VMEM((count, units, share, width), BF16),
    ] + [pltpu.SemaphoreType.DMA((count,))] * 6
    out_shape = [jax.ShapeDtypeStruct(own.shape, BF16)]
    if not back:
        out_shape.append(jax.ShapeDtypeStruct(dec_shape, F32))
        kernel = functools.partial(exchange_kernel, count, plan.joints, False)
    else:

        def kernel(own_ref, dec_ref, out_ref, *rest):
            exchange_kernel(count, plan.joints, True, own_ref, dec_ref, out_ref, None, *rest)

    outs = pl.pallas_call(
        kernel,
        out_shape=out_shape,
        in_specs=[vmem, vmem],
        out_specs=[vmem] * len(out_shape),
        scratch_shapes=scratch,
        compiler_params=pltpu.CompilerParams(
            collective_id=1 if back else 0, has_side_effects=True, vmem_limit_bytes=VMEM_LIMIT
        ),
        name="states_back" if back else "states",
    )(own, decays)
    return (outs[0], decays) if back else (outs[0], outs[1])


def body(
    hidden, norm_gain, w_z, w_x, w_bc, w_dt, w_out, conv_x, conv_x_bias, conv_bc, conv_bc_bias,
    dt_bias, a_log, skip_d, gate_gain, cotangent,
):
    batch, tokens, model = hidden.shape
    plan = Plan(batch, tokens)
    core = plan.core
    inner = w_z.shape[1] // 2
    heads = w_dt.shape[1] // 2
    head_size = inner // heads
    units = plan.units
    rows = units * 4 * tokens
    chunks = rows // CHUNK

    def halves(w):
        half = w.shape[1] // 2
        return jnp.where(core == 0, w[:, :half], w[:, half:]), jnp.where(core == 0, w[:, half:], w[:, :half])

    small = [conv_x, conv_x_bias, conv_bc, conv_bc_bias, dt_bias, a_log, skip_d, gate_gain, norm_gain]
    flat = jnp.concatenate([part.reshape(-1) for part in small])
    length = flat.shape[0]
    padded = -(-length // LANES) * LANES
    flat = jnp.pad(flat, (0, padded - length)).reshape(padded // LANES, LANES)
    everyone = lax.all_gather(flat, "fs").reshape(plan.shards, padded)
    gathered, start = [], 0
    for part in small:
        gathered.append(
            everyone[:, start : start + part.size].reshape((-1,) + part.shape[1:]).astype(F32)
        )
        start += part.size
    taps_x, bias_x, taps_bc, bias_bc, shift, rate_log, skip, gain_out, gain_in = gathered

    x_mine, x_other = halves(w_x)
    dt_mine, dt_other = halves(w_dt)
    z_mine, z_other = halves(w_z)
    o_mine, o_other = halves(w_out)
    fill = jnp.zeros((w_dt.shape[0], LANES - heads), BF16)
    first_mine = jnp.concatenate([x_mine, w_bc, dt_mine, fill], axis=1)
    first_other = jnp.concatenate([x_other, w_bc, dt_other, fill], axis=1)

    def rows_of_chip(mine, other):
        return jnp.concatenate(plan.by_core(mine, plan.swap(other, df=1)), axis=0)

    weight_first = plan.gather(rows_of_chip(first_mine, first_other))
    weight_gate = plan.gather(rows_of_chip(z_mine, z_other))
    weight_out = plan.gather(rows_of_chip(o_mine, o_other))

    def mine_of(v):
        half = v.shape[0] // 2
        return lax.dynamic_slice_in_dim(v, core * half, half, 0)

    gain_in_turned = plan.turn(gain_in[None])
    taps_x, bias_x, gain_out, skip_mine = (mine_of(v) for v in (taps_x, bias_x, gain_out, skip))
    shift, rate_log = mine_of(shift), mine_of(rate_log)
    cx = jnp.concatenate(
        [taps_x.T, bias_x[None], jnp.repeat(skip_mine, head_size)[None], jnp.zeros((2, inner), F32)]
    )
    cbc = jnp.concatenate([taps_bc.T, bias_bc[None], jnp.zeros((3, taps_bc.shape[0]), F32)])
    pad_heads = (0, LANES - heads)
    rate = jnp.pad(jnp.exp(rate_log), pad_heads)
    hp = jnp.concatenate([rate[None], jnp.zeros((7, LANES), F32)])
    pick = (jnp.arange(inner)[:, None] // head_size == jnp.arange(LANES)[None, :]).astype(BF16)

    hidden_rows = plan.to_units(plan.turn(hidden)).astype(F32)
    scale_in = row_scale(hidden_rows)
    unit_in = hidden_rows * scale_in
    normed = (unit_in * gain_in_turned).astype(BF16)
    cot_rows = plan.to_units(plan.turn(cotangent))

    first = dot(normed, weight_first).astype(BF16)
    dt_shifted = first[:, inner + 2 * LANES :].astype(F32) + jnp.pad(shift, pad_heads)[None]
    step = jax.nn.softplus(dt_shifted)
    slope_dt = jax.nn.sigmoid(dt_shifted)

    tails = first[:, : inner + 2 * LANES].reshape(units, PER_UNIT, CHUNK, inner + 2 * LANES)[:, :, CHUNK - 8 :]
    before = plan.along(tails[:, PER_UNIT - 1], 1)
    tails = jnp.concatenate([before[:, None], tails[:, : PER_UNIT - 1]], axis=1).astype(F32)
    tails = tails.reshape(chunks, 8, inner + 2 * LANES)
    tail_x, tail_bc = tails[..., :inner], tails[..., inner:]

    def shaped(*shape, dtype=BF16):
        return jax.ShapeDtypeStruct(shape, dtype)

    states = (LANES, inner)
    y_own, starts, own, decays, shared, reach = pl.pallas_call(
        forward_kernel,
        grid=(units, PER_UNIT),
        in_specs=[
            rows_spec(inner), chunk_spec((8, inner)),
            rows_spec(2 * LANES, inner // (2 * LANES)), chunk_spec((8, 2 * LANES)),
            rows_spec(LANES), whole_spec(cx.shape), whole_spec(cbc.shape), whole_spec(hp.shape),
        ],
        out_specs=[
            rows_spec(inner), chunk_spec(states), unit_spec(states), unit_spec((8, inner)),
            rows_spec(2 * LANES), rows_spec(LANES),
        ],
        out_shape=[
            shaped(rows, inner), shaped(chunks, *states), shaped(units, *states),
            shaped(units, 8, inner, dtype=F32), shaped(rows, 2 * LANES), shaped(rows, LANES, dtype=F32),
        ],
        scratch_shapes=[
            pltpu.VMEM((CHUNK + 8, inner), F32), pltpu.VMEM((CHUNK + 8, 2 * LANES), F32),
            pltpu.VMEM(states, F32), pltpu.VMEM((8, LANES), F32),
        ],
        compiler_params=params(),
        name="scan_forward",
    )(first, tail_x, first, tail_bc, step, cx, cbc, hp)

    decay_rows = jnp.concatenate([decays[:, 0], jnp.zeros((8 - units, inner), F32)])
    incoming, all_decays = exchange(plan, own, decay_rows, False)
    gate_in = dot(normed, weight_gate).astype(BF16)

    y, gated, squares = pl.pallas_call(
        gate_kernel,
        grid=(units, PER_UNIT),
        in_specs=[
            rows_spec(inner), rows_spec(inner), rows_spec(2 * LANES), rows_spec(LANES), unit_spec(states),
        ],
        out_specs=[rows_spec(inner), rows_spec(inner), rows_spec(LANES)],
        out_shape=[shaped(rows, inner), shaped(rows, inner), shaped(rows, LANES, dtype=F32)],
        compiler_params=params(),
        name="gate_forward",
    )(y_own, gate_in, shared, reach, incoming)

    def pair_sum(v):
        return v + plan.swap(v, df=1)

    squares = pair_sum(squares[:, 0].reshape(chunks, CHUNK))
    scale_out = lax.rsqrt(squares / (2 * inner) + EPSILON).reshape(rows, 1)
    unit_out = gated.astype(F32) * scale_out
    normed_out = (unit_out * gain_out[None]).astype(BF16)
    projected = plan.from_units(dot_nt(normed_out, weight_out))
    output = (hidden.astype(F32) + plan.turn(projected).astype(F32)).astype(BF16)

    d_normed_out = dot(cot_rows, weight_out).astype(BF16)
    wide = d_normed_out.astype(F32)
    g_gate_gain = jnp.sum(wide * unit_out, axis=0)
    mean = pair_sum(jnp.sum(wide * gain_out[None] * unit_out, axis=1).reshape(chunks, CHUNK))
    mean = (mean / (2 * inner)).reshape(rows, 1)
    stats = jnp.concatenate([scale_out, mean, jnp.zeros((rows, LANES - 2), F32)], axis=1)
    gain_rows = jnp.broadcast_to(gain_out[None], (8, inner))

    dy, d_gate, pull = pl.pallas_call(
        pull_kernel,
        grid=(units, PER_UNIT),
        in_specs=[
            rows_spec(inner), rows_spec(inner), rows_spec(inner), rows_spec(inner), rows_spec(LANES),
            whole_spec((8, inner)), rows_spec(2 * LANES), rows_spec(LANES),
        ],
        out_specs=[rows_spec(inner), rows_spec(inner), unit_spec(states)],
        out_shape=[shaped(rows, inner), shaped(rows, inner), shaped(units, *states)],
        scratch_shapes=[pltpu.VMEM(states, F32)],
        compiler_params=params(),
        name="gate_backward",
    )(d_normed_out, gated, gate_in, y, stats, gain_rows, shared, reach)

    after, _ = exchange(plan, pull, all_decays, True)

    back = functools.partial(rows_spec, back=True)
    width = inner + 3 * LANES
    d_all, heads_x, heads_bc, g_x, g_bc, g_heads = pl.pallas_call(
        backward_kernel,
        grid=(units, PER_UNIT),
        in_specs=[
            back(inner), chunk_spec((8, inner), True),
            back(2 * LANES, inner // (2 * LANES)), chunk_spec((8, 2 * LANES), True),
            back(LANES), back(LANES), whole_spec(cx.shape), whole_spec(cbc.shape), whole_spec(hp.shape),
            back(inner), back(inner), chunk_spec(states, True), unit_spec(states), back(LANES),
            unit_spec(states), whole_spec(pick.shape),
        ],
        out_specs=[
            back(width), unit_spec((8, inner)), unit_spec((8, 2 * LANES)),
            whole_spec((40, inner)), whole_spec((40, 2 * LANES)), whole_spec((24, LANES)),
        ],
        out_shape=[
            shaped(rows, width), shaped(units, 8, inner, dtype=F32), shaped(units, 8, 2 * LANES, dtype=F32),
            shaped(40, inner, dtype=F32), shaped(40, 2 * LANES, dtype=F32), shaped(24, LANES, dtype=F32),
        ],
        scratch_shapes=[
            pltpu.VMEM((CHUNK + 8, inner), F32), pltpu.VMEM((CHUNK + 8, 2 * LANES), F32),
            pltpu.VMEM(states, F32),
            pltpu.VMEM((CHUNK + 8, inner), F32), pltpu.VMEM((CHUNK + 8, 2 * LANES), F32),
            pltpu.VMEM((8, inner), F32),
        ],
        compiler_params=params(),
        name="scan_backward",
    )(
        first, tail_x, first, tail_bc, step, slope_dt, cx, cbc, hp,
        dy, y, starts, incoming, reach, after, pick,
    )

    later = plan.along(jnp.concatenate([heads_x, heads_bc], axis=2)[:, :3].astype(BF16), -1).astype(F32)
    taps = jnp.concatenate([cx[:4], cbc[:4]], axis=1)
    extra = jnp.stack(
        [sum(taps[k][None] * later[:, i - k] for k in range(i + 1)) for i in range(3)], axis=1
    )
    tail_rows = d_all.reshape(units, 4 * tokens, width)[:, 4 * tokens - 16 :].astype(F32)
    extra = jnp.pad(extra, ((0, 0), (13, 0), (0, width - extra.shape[2])))
    d_all = d_all.reshape(units, 4 * tokens, width)
    d_all = lax.dynamic_update_slice(d_all, (tail_rows + extra).astype(BF16), (0, 4 * tokens - 16, 0))
    d_all = d_all.reshape(rows, width)

    d_normed = dot_nt(d_gate, weight_gate) + dot_nt(d_all, weight_first)
    g_norm_gain = jnp.sum(d_normed * unit_in, axis=0)

    def both_halves(g):
        half = g.shape[0] // 2
        first_core = core == 0
        mine = jnp.where(first_core, g[:half], g[half:])
        other = jnp.where(first_core, g[half:], g[:half]).astype(BF16)
        return mine, plan.swap(other, df=1)

    g_out_mine, g_out_other = both_halves(plan.reduce_chips(dot_tn(cot_rows, normed_out)))
    total_out = plan.reduce_members(jnp.concatenate(plan.by_core(g_out_mine, g_out_other), axis=1))
    g_z_mine, g_z_other = both_halves(plan.reduce_chips(dot_tn(normed, d_gate)))
    total_z = plan.reduce_members(jnp.concatenate(plan.by_core(g_z_mine, g_z_other), axis=1))

    grad_rows = plan.turn(plan.from_units(d_normed)).astype(F32)
    resid = hidden.astype(F32)
    own_scale = row_scale(resid)
    own_unit = resid * own_scale
    dv = grad_rows * gain_in[None, None]
    grad_hidden = cotangent.astype(F32) + own_scale * (
        dv - own_unit * jnp.mean(dv * own_unit, axis=-1, keepdims=True)
    )

    g_mine, g_other = both_halves(plan.reduce_chips(dot_tn(normed, d_all)))
    x_parts = plan.by_core(g_mine[:, :inner], g_other[:, :inner].astype(F32))
    bc_sum = g_mine[:, inner : inner + 2 * LANES] + g_other[:, inner : inner + 2 * LANES]
    dt_parts = plan.by_core(
        g_mine[:, inner + 2 * LANES : inner + 2 * LANES + heads],
        g_other[:, inner + 2 * LANES : inner + 2 * LANES + heads].astype(F32),
    )
    total = plan.reduce_members(
        jnp.concatenate(
            list(x_parts) + [bc_sum] + list(dt_parts) + [jnp.zeros((bc_sum.shape[0], LANES - 2 * heads), F32)],
            axis=1,
        )
    )
    total_x = total[:, : 2 * inner]
    total_bc = total[:, 2 * inner : 2 * inner + 2 * LANES]
    total_dt = total[:, 2 * inner + 2 * LANES : 2 * inner + 2 * LANES + 2 * heads]

    own_x = g_x.reshape(5, 8, inner).sum(axis=1)
    own_bc = g_bc.reshape(5, 8, 2 * LANES).sum(axis=1)
    own_heads = g_heads.reshape(3, 8, LANES).sum(axis=1)[:, :heads]
    norm_gain_sum = plan.turn(g_norm_gain[None])[0]
    half_parts = [own_x, g_gate_gain[None], own_heads]
    sum_parts = [norm_gain_sum, own_bc]
    vector = jnp.concatenate([v.reshape(-1) for v in half_parts + sum_parts])
    size = -(-vector.shape[0] // 1024) * 1024
    vector = jnp.pad(vector, (0, size - vector.shape[0])).reshape(-1, LANES)
    vector = plan.sum_all(vector)
    lower, upper = (v.reshape(-1) for v in plan.by_core(vector, plan.swap(vector, df=1)))

    def pieces(v):
        found, start = [], 0
        for part in half_parts + sum_parts:
            found.append(v[start : start + part.size].reshape(part.shape))
            start += part.size
        return found

    low_parts, high_parts = pieces(lower), pieces(upper)
    whole_x, whole_gain, whole_heads = (
        jnp.concatenate([a, b], axis=1) for a, b in zip(low_parts[:3], high_parts[:3])
    )
    whole_norm, whole_bc = (a + b for a, b in zip(low_parts[3:], high_parts[3:]))

    def shard(v):
        share = v.shape[-1] // plan.shards
        return lax.dynamic_slice_in_dim(v, plan.f * share, share, v.ndim - 1)

    shard_x, shard_bc, shard_heads = shard(whole_x), shard(whole_bc), shard(whole_heads)
    return (
        output,
        grad_hidden,
        shard(whole_norm),
        total_z,
        total_x,
        total_bc,
        total_dt,
        total_out,
        shard_x[:4].T,
        shard_x[4],
        shard_bc[:4].T,
        shard_bc[4],
        shard_heads[0],
        shard_heads[1],
        shard_heads[2],
        shard(whole_gain)[0],
    )


def solution(mesh):
    one, two = P("fs"), P("fs", None)
    tokens = P(None, ("fs", "sp"), None)
    return jax.shard_map(
        body,
        mesh=mesh,
        in_specs=(tokens, one, two, two, two, two, two, two, one, two, one, one, one, one, one, tokens),
        out_specs=(tokens, tokens, one, two, two, two, two, two, two, one, two, one, one, one, one, one),
        check_vma=False,
    )
```

time: 2460 us -> 1010 us (0.41)
  local copies, waits for them, and re-layouts: 536 us -> 72.5 us
  matrix products: 514 us -> 116 us
  waiting for transfers between devices: 717 us -> 340 us
  blocking collectives: 326 us -> 10.4 us
  Pallas kernels: 0 us -> 210 us
  other arithmetic: 252 us -> 115 us
  starting transfers between devices: 48.3 us -> 133 us
  loops' own time: 27.7 us -> 0 us
    all_to_all x8 -> x0, waiting for transfers between devices: 598 us -> none  [the longest x1 127 us: body(): lax.all_to_all(grad_gate_low, 'sp', split_axis=1, concat_axis=2, tiled=True)]
    dot_general x53 -> x9, matrix products: 514 us -> 116 us  [the longest x3 41.3 us: dot_nt(): lax.dot_general(a, b, (((1,), (1,)), ((), ())), preferred_element_type=F32)]
    ppermute x4 -> x68, waiting for transfers between devices: 1.37 us -> 340 us  [send(): return lax.ppermute(x, ('fs', 'sp'), pairs)]
    pallas_call x0 -> x6, Pallas kernels: none -> 210 us  [the longest x2 75.2 us: exchange(): pl.pallas_call(kernel, out_shape=out_shape, in_specs=[vmem, vmem], out_sp...]
    convert_element_type x24 -> x9, local copies, waits for them, and re-layouts: 159 us -> 6.95 us  [body(): everyone[:, start:start + part.size].reshape((-1,) + part.shape[1:])]
    all_to_all x1 -> x0, blocking collectives: 142 us -> none  [body(): lax.all_to_all(grad_x_low, 'sp', split_axis=1, concat_axis=2, tiled=True)]
    ppermute x4 -> x68, starting transfers between devices: 6.89 us -> 133 us  [send(): return lax.ppermute(x, ('fs', 'sp'), pairs)]
    all_gather x8 -> x1, blocking collectives: 122 us -> 10.4 us  [body(): everyone = lax.all_gather(flat, 'fs').reshape(plan.shards, padded)]
  transfers between devices with their start and end apart: 27 -> 68, of which waited for: 10 -> 29; matrix products, arithmetic and copies ran while one was open for 36% -> 25% of each run, Pallas kernels for 0% -> 21%
where the time goes in v1:
time: 1010 us; the launch traced here: 1000 us
  waiting for transfers between devices  340 us (34%)
  Pallas kernels  210 us (21%)
  starting transfers between devices  133 us (13%)
  matrix products  116 us (11%)
  other arithmetic  115 us (11%)
  local copies, waits for them, and re-layouts  72.5 us (7%)
  blocking collectives  10.4 us (1%)
    ppermute x68, waiting for transfers between devices, send(): return lax.ppermute(x, ('fs', 'sp'), pairs)  340 us
    ppermute x68, starting transfers between devices, send(): return lax.ppermute(x, ('fs', 'sp'), pairs)  133 us
    pallas_call x2, Pallas kernels, exchange(): pl.pallas_call(kernel, out_shape=out_shape, in_specs=[vmem, vmem], out_sp...  75.2 us
    pallas_call x1, Pallas kernels, body(): pl.pallas_call(backward_kernel, grid=(units, PER_UNIT), in_specs=[back(in...  70.8 us
    dot_general x3, matrix products, dot_nt(): lax.dot_general(a, b, (((1,), (1,)), ((), ())), preferred_element_type=F32)  41.3 us
    dot_general x3, matrix products, dot_tn(): lax.dot_general(a, b, (((0,), (0,)), ((), ())), preferred_element_type=F32)  39.7 us
    dot_general x3, matrix products, dot(): return jnp.dot(a, b, preferred_element_type=F32)  35.5 us
    pallas_call x1, Pallas kernels, body(): pl.pallas_call(forward_kernel, grid=(units, PER_UNIT), in_specs=[rows_spe...  30.9 us
  transfers between devices with their start and end apart: 68, of which 29 were waited for; matrix products, arithmetic and copies ran while one was open for 25% of the time, Pallas kernels for 21%

profile of v1, /device:TPU:0, one launch (start us, length us, event | category | flops | bytes accessed | tf_op | source)
XLA Modules:
  0.0 1000.6 jit_solution(8588030535976835334)
XLA Ops:
  16.5 4.8 concatenate.162
  21.4 10.4 %all_gather.3 = bf16[8,21,128]{2,1,0:T(8,128)(2,1)S(1)} all-gather(bf16[1,21,128]{2,1,0:T(8,128)(2,1)S(1)} %pad_bitcast_fusion.1), channel_id=1, replica_groups=mesh['fs'=8,'sp'=4] {'fs'}, dimensions={0}, use_global_device_ids=true | all-gather | bytes 48384 | tf_op jit(solution)/shard_map/all_gather | solution.py:715
  35.6 2.4 reshape.375
  59.8 3.7 collective-permute-start.28
  66.3 3.7 collective-permute-start.1
  70.0 8.0 collective-permute-done.28
  78.0 25.9 %collective-permute-start.2 = (bf16[3,128,768]{2,1,0:T(8,128)(2,1)S(1)}, bf16[3,128,768]{2,1,0:T(8,128)(2,1)S(1)}, u32[]{:S(2)}, u32[]{:S(2)}) collective-permute-start(bf16[3,128,768]{2,1,0:T(8,128)(2,1)S(1)} %get-tuple-element.138), channel_id=1, source_target_pairs={{0,2},{1,3},{2,0},{3,1},{4,6},{5,7},{6,4},{7,5},{8,10},{9,11},{10,... | collective-permute-start | bytes 1769480 | tf_op jit(solution)/shard_map/ppermute | solution.py:460
  103.9 36.3 %collective-permute-done.29 = bf16[3,128,768]{2,1,0:T(8,128)(2,1)S(1)} collective-permute-done((bf16[3,128,768]{2,1,0:T(8,128)(2,1)S(1)}, bf16[3,128,768]{2,1,0:T(8,128)(2,1)S(1)}, u32[]{:S(2)}, u32[]{:S(2)}) %collective-permute-start.29) | collective-permute-done | bytes 589856 | tf_op jit(solution)/shard_map/ppermute | solution.py:460
  142.7 21.9 %collective-permute-done.2 = bf16[3,128,768]{2,1,0:T(8,128)(2,1)S(1)} collective-permute-done((bf16[3,128,768]{2,1,0:T(8,128)(2,1)S(1)}, bf16[3,128,768]{2,1,0:T(8,128)(2,1)S(1)}, u32[]{:S(2)}, u32[]{:S(2)}) %collective-permute-start.2) | collective-permute-done | bytes 589856 | tf_op jit(solution)/shard_map/ppermute | solution.py:460
  171.9 21.6 %collective-permute-done.19 = bf16[384,1536]{1,0:T(8,128)(2,1)S(1)} collective-permute-done((bf16[384,1536]{1,0:T(8,128)(2,1)S(1)}, bf16[384,1536]{1,0:T(8,128)(2,1)S(1)}, u32[]{:S(2)}, u32[]{:S(2)}) %collective-permute-start.19) | collective-permute-done | bytes 1179680 | tf_op jit(solution)/shard_map/ppermute | solution.py:460
  194.8 6.7 collective-permute-done.6
  203.5 21.6 %collective-permute-done.7 = bf16[384,1920]{1,0:T(8,128)(2,1)S(1)} collective-permute-done((bf16[384,1920]{1,0:T(8,128)(2,1)S(1)}, bf16[384,1920]{1,0:T(8,128)(2,1)S(1)}, u32[]{:S(2)}, u32[]{:S(2)}) %collective-permute-start.7) | collective-permute-done | bytes 1474592 | tf_op jit(solution)/shard_map/ppermute | solution.py:460
  226.6 11.2 %collective-permute-done.14 = bf16[192,1536]{1,0:T(8,128)(2,1)S(1)} collective-permute-done((bf16[192,1536]{1,0:T(8,128)(2,1)S(1)}, bf16[192,1536]{1,0:T(8,128)(2,1)S(1)}, u32[]{:S(2)}, u32[]{:S(2)}) %collective-permute-start.14) | collective-permute-done | bytes 589856 | tf_op jit(solution)/shard_map/ppermute | solution.py:460
  240.0 10.4 %collective-permute-done.20 = bf16[192,1536]{1,0:T(8,128)(2,1)S(1)} collective-permute-done((bf16[192,1536]{1,0:T(8,128)(2,1)S(1)}, bf16[192,1536]{1,0:T(8,128)(2,1)S(1)}, u32[]{:S(2)}, u32[]{:S(2)}) %collective-permute-start.20) | collective-permute-done | bytes 589856 | tf_op jit(solution)/shard_map/ppermute | solution.py:460
  250.5 13.9 %collective-permute-done.8 = bf16[192,1920]{1,0:T(8,128)(2,1)S(1)} collective-permute-done((bf16[192,1920]{1,0:T(8,128)(2,1)S(1)}, bf16[192,1920]{1,0:T(8,128)(2,1)S(1)}, u32[]{:S(2)}, u32[]{:S(2)}) %collective-permute-start.8) | collective-permute-done | bytes 737312 | tf_op jit(solution)/shard_map/ppermute | solution.py:460
  267.2 10.4 %convolution_convert_fusion.x_ref.bc_ref = bf16[1536,1920]{1,0:T(8,128)(2,1)S(1)} fusion(bf16[1536,1920]{1,0:T(8,128)(2,1)S(1)} %constant_dynamic-update-slice_fusion, f32[1536]{0:T(1024)S(1)} %maximum_reduce_fusion.2, f32[1536]{0:T(1024)S(1)} %add_rsqrt_fusion.1, bf16[1536,768]{1,0:T(8,128)(2,1)S(1)} %get-tuple-element.164, ...), kind=kOutput, calls=%fused_computation.15 | convolution fusion | flops 9079160832 | bytes 16527360 | tf_op jit(solution)/shard_map/dot_general | solution.py:20
  278.0 3.7 collective-permute-start.10
  281.7 12.2 %convolution_convert_fusion.2.gate_ref = bf16[1536,1536]{1,0:T(8,128)(2,1)} fusion(bf16[1536,1536]{1,0:T(8,128)(2,1)} %copy-done.62, f32[1536]{0:T(1024)S(1)} %maximum_reduce_fusion.2, f32[1536]{0:T(1024)S(1)} %add_rsqrt_fusion.1, bf16[1536,768]{1,0:T(8,128)(2,1)S(1)} %get-tuple-element.164, bf16[1536,768]{1,0:T(8,128)(2,1)S(1)} %get-tuple-element.163), kind=kOutput, calls=%fused_computation.17 | convolution fusion | flops 7266631680 | bytes 14168064 | tf_op jit(solution)/shard_map/dot_general | solution.py:20
  297.3 30.9 %scan_forward.1 = (bf16[1536,1536]{1,0:T(8,128)(2,1)}, bf16[12,128,1536]{2,1,0:T(8,128)(2,1)}, bf16[3,128,1536]{2,1,0:T(8,128)(2,1)}, f32[3,8,1536]{2,1,0:T(8,12...) custom-call(bf16[1536,1920]{1,0:T(8,128)(2,1)} %copy-done, f32[12,8,1536]{2,1,0:T(8,128)} %slice.635.xp_ref, ...), custom_call_target="tpu_custom_call" | custom-call | tf_op jit(solution)/shard_map/scan_forward/pallas_call | solution.py:776
  329.9 38.8 %states.1 = (bf16[3,128,1536]{2,1,0:T(8,128)(2,1)}, f32[8,8,1536]{2,1,0:T(8,128)}) custom-call(bf16[3,128,1536]{2,1,0:T(8,128)(2,1)} %get-tuple-element.39.own_ref, f32[8,1536]{1,0:T(8,128)} %concatenate.174.dec_ref), custom_call_target="tpu_custom_call" | custom-call | tf_op jit(solution)/shard_map/states/pallas_call | solution.py:678
  368.7 14.2 %gate_forward.1 = (bf16[1536,1536]{1,0:T(8,128)(2,1)}, bf16[1536,1536]{1,0:T(8,128)(2,1)}, f32[1536,128]{1,0:T(8,128)}) custom-call(bf16[1536,1536]{1,0:T(8,128)(2,1)} %get-tuple-element.36.y0_ref, bf16[1536,1536]{1,0:T(8,128)(2,1)} %convolution_convert_fusion.2.gate_ref, bf16[1536,256]{1,0:T(8,128)(2,1)} %get-tuple-element.37.bcs_ref, ...), custom_call_target="tpu_custom_call" | custom-call | tf_op jit(solution)/shard_map/gate_forward/pallas_call | solution.py:804
  387.3 10.5 %fusion.65 = (bf16[1536,1536]{1,0:T(8,128)(2,1)S(1)}, f32[1536,1536]{1,0:T(8,128)}) fusion(bf16[1536,1536]{1,0:T(8,128)(2,1)S(1)} %bitcast.294, f32[1536]{0:T(1024)S(1)} %dynamic_slice.38, f32[1536]{0:T(1024)S(1)} %get-tuple-element.252, bf16[1536,768]{1,0:T(8,128)(2,1)S(1)} %get-tuple-element.162, bf16[1536,768]{1,0:T(8,128)(2,1)S(1)} %get-tuple-element.161), kind=kOutput, calls=%fused_computation.408 | convolution fusion | flops 7268990976 | bytes 23605248 | tf_op jit(solution)/shard_map/dot_general | solution.py:28
  398.9 12.8 %fusion.7 = (f32[1536]{0:T(1024)}, f32[1536]{0:T(1024)S(1)}, bf16[1536,1536]{1,0:T(8,128)(2,1)}) fusion(bf16[1536,1536]{1,0:T(8,128)(2,1)S(1)} %bitcast.294, f32[1536]{0:T(1024)S(1)} %get-tuple-element.252, f32[1536]{0:T(1024)S(1)} %dynamic_slice.38, bf16[1536,1536]{1,0:T(8,128)(2,1)} %copy-done.63, bf16[1536,768]{1,0:T(8,128)(2,1)S(1)} %get-tuple-element.162, ...), kind=kOutput, calls=%fused_computation.11 | convolution fusion | flops 7278425088 | bytes 18898944 | tf_op jit(solution)/shard_map/dot_general | solution.py:20
  411.8 9.8 fusion.22
  428.2 2.3 maximum_maximum_fusion.stats_ref
  431.2 19.2 %gate_backward.1 = (bf16[1536,1536]{1,0:T(8,128)(2,1)}, bf16[1536,1536]{1,0:T(8,128)(2,1)}, bf16[3,128,1536]{2,1,0:T(8,128)(2,1)}) custom-call(bf16[1536,1536]{1,0:T(8,128)(2,1)} %get-tuple-element.264.dno_ref, bf16[1536,1536]{1,0:T(8,128)(2,1)} %get-tuple-element.42.gated_ref, bf16[1536,1536]{1,0:T(8,128)(2,1)} %convolution_convert_fusion.2.gate_ref, ...), custom_call_target="tpu_custom_call" | custom-call | tf_op jit(solution)/shard_map/gate_backward/pallas_call | solution.py:834
  450.4 36.4 %states_back.1.after_ref = bf16[3,128,1536]{2,1,0:T(8,128)(2,1)} custom-call(bf16[3,128,1536]{2,1,0:T(8,128)(2,1)} %get-tuple-element.48.own_ref, f32[8,8,1536]{2,1,0:T(8,128)} %get-tuple-element.49.dec_ref), custom_call_target="tpu_custom_call" | custom-call | tf_op jit(solution)/shard_map/states_back/pallas_call | solution.py:678
  486.9 70.8 %scan_backward.1 = (bf16[1536,1920]{1,0:T(8,128)(2,1)}, f32[3,8,1536]{2,1,0:T(8,128)}, f32[3,8,256]{2,1,0:T(8,128)}, f32[40,1536]{1,0:T(8,128)}, f32[40,256]{1,0:T(8,128)}, /*index=5*/f32[24,128]{1,0:T(8,128)}) custom-call(bf16[1536,1920]{1,0:T(8,128)(2,1)} %copy-done, f32[12,8,1536]{2,1,0:T(8,128)} %slice.635.xp_ref, bf16[1536,1920]{1,0:T(8,128)(2,1)} %copy-done, ...), custom_call_target="tpu_custom_call" | custom-call | tf_op jit(solution)/shard_map/scan_backward/pallas_call | solution.py:852
  564.3 12.7 %fusion.63 = (bf16[1536,1536]{1,0:T(8,128)(2,1)S(1)}, f32[1536,1536]{1,0:T(8,128)}) fusion(bf16[1536,1536]{1,0:T(8,128)(2,1)} %get-tuple-element.45, f32[1536]{0:T(1024)S(1)} %maximum_reduce_fusion.2, f32[1536]{0:T(1024)S(1)} %add_rsqrt_fusion.1, bf16[1536,768]{1,0:T(8,128)(2,1)S(1)} %copy-done.16, bf16[1536,768]{1,0:T(8,128)(2,1)S(1)} %get-tuple-element.163), kind=kOutput, calls=%fused_computation.406 | convolution fusion | flops 7266631680 | bytes 23605248 | tf_op jit(solution)/shard_map/dot_general | solution.py:28
  577.0 2.2 copy-done.54
  587.1 15.6 %fusion.66 = f32[1536,1536]{1,0:T(8,128)} fusion(bf16[1536,1920]{1,0:T(8,128)(2,1)} %bitcast.321, bf16[1536,1920]{1,0:T(8,128)(2,1)} %copy-done.60), kind=kOutput, calls=%fused_computation.409 | convolution fusion | flops 9059696640 | bytes 21233664 | tf_op jit(solution)/shard_map/dot_general | solution.py:24
  602.7 15.9 %fusion.3 = (f32[1536]{0:T(1024)S(1)}, f32[1536,1536]{1,0:T(8,128)}) fusion(f32[1536]{0:T(1024)S(1)} %copy-done.74, bf16[1536,768]{1,0:T(8,128)(2,1)S(1)} %copy-done.17, bf16[1536,768]{1,0:T(8,128)(2,1)S(1)} %get-tuple-element.163, f32[1536,1536]{1,0:T(8,128)} %fusion.66, bf16[1536,1536]{1,0:T(8,128)(2,1)} %get-tuple-element.45, ...), kind=kOutput, calls=%fused_computation.7 | convolution fusion | flops 7266630144 | bytes 33042432 | tf_op jit(solution)/shard_map/dot_general | solution.py:24
  620.9 2.6 collective-permute-start.39
  624.6 2.4 concatenate.209
  627.1 4.5 collective-permute-start.40
  631.6 16.5 %fusion.64 = (bf16[1536,1920]{1,0:T(8,128)(2,1)}, f32[1536,1920]{1,0:T(8,128)}) fusion(bf16[1536,1920]{1,0:T(8,128)(2,1)} %bitcast.322, f32[1536]{0:T(1024)S(1)} %copy-done.72, f32[1536]{0:T(1024)S(1)} %copy-done.75, bf16[1536,768]{1,0:T(8,128)(2,1)S(1)} %copy-done.18, bf16[1536,768]{1,0:T(8,128)(2,1)S(1)} %get-tuple-element.163), kind=kOutput, calls=%fused_computation.407 | convolution fusion | flops 9079160832 | bytes 28323840 | tf_op jit(solution)/shard_map/dot_general | solution.py:28
  653.8 3.6 collective-permute-done.42
  689.4 3.8 collective-permute-done.54
  699.0 2.7 fusion.17
  701.8 29.3 %collective-permute-done.61 = bf16[384,768]{1,0:T(8,128)(2,1)S(1)} collective-permute-done((bf16[384,768]{1,0:T(8,128)(2,1)S(1)}, bf16[384,768]{1,0:T(8,128)(2,1)S(1)}, u32[]{:S(2)}, u32[]{:S(2)}) %collective-permute-start.61) | collective-permute-done | bytes 589856 | tf_op jit(solution)/shard_map/ppermute | solution.py:460
  731.0 2.4 fusion.30
  733.7 10.0 collective-permute-done.45
  745.7 2.8 fusion.34
  750.6 9.4 collective-permute-done.63
  762.6 2.8 add_convert_fusion.1
  768.7 2.2 collective-permute-done.47
  771.7 2.2 collective-permute-start.24
  776.5 2.2 fusion.18
  778.8 2.7 add_convert_fusion
  784.0 26.0 %collective-permute-done.23 = bf16[3,128,768]{2,1,0:T(8,128)(2,1)} collective-permute-done((bf16[3,128,768]{2,1,0:T(8,128)(2,1)}, bf16[3,128,768]{2,1,0:T(8,128)(2,1)}, u32[]{:S(2)}, u32[]{:S(2)}) %collective-permute-start.23) | collective-permute-done | bytes 589856 | tf_op jit(solution)/shard_map/ppermute | solution.py:460
  811.9 2.4 collective-permute-done.25
  814.3 35.2 %collective-permute-start.37 = (bf16[3,128,768]{2,1,0:T(8,128)(2,1)S(1)}, bf16[3,128,768]{2,1,0:T(8,128)(2,1)S(1)}, u32[]{:S(2)}, u32[]{:S(2)}) collective-permute-start(bf16[3,128,768]{2,1,0:T(8,128)(2,1)S(1)} %get-tuple-element.199), channel_id=1, source_target_pairs={{0,1},{1,0},{2,3},{3,2},{4,5},{5,4},{6,7},{7,6},{8,9},{9,8},{10,11... | collective-permute-start | bytes 1769480 | tf_op jit(solution)/shard_map/ppermute | solution.py:460
  856.0 4.5 collective-permute-done.35
  860.4 12.8 %collective-permute-start.49 = (bf16[96,3072]{1,0:T(8,128)(2,1)}, bf16[96,3072]{1,0:T(8,128)(2,1)}, u32[]{:S(2)}, u32[]{:S(2)}) collective-permute-start(bf16[96,3072]{1,0:T(8,128)(2,1)} %select_convert_fusion.6), channel_id=1, source_target_pairs={{0,1},{1,0},{2,3},{3,2},{4,5},{5,4},{6,7},{7,6},{8,9},{9,8},{10,11... | collective-permute-start | bytes 1769480 | tf_op jit(solution)/shard_map/ppermute | solution.py:460
  877.5 2.7 concatenate.199
  880.5 5.0 collective-permute-done.65
  887.5 23.2 %collective-permute-done.49 = bf16[96,3072]{1,0:T(8,128)(2,1)} collective-permute-done((bf16[96,3072]{1,0:T(8,128)(2,1)}, bf16[96,3072]{1,0:T(8,128)(2,1)}, u32[]{:S(2)}, u32[]{:S(2)}) %collective-permute-start.49) | collective-permute-done | bytes 589856 | tf_op jit(solution)/shard_map/ppermute | solution.py:460
  912.5 12.4 %collective-permute-done.57 = bf16[96,3456]{1,0:T(8,128)(2,1)S(1)} collective-permute-done((bf16[96,3456]{1,0:T(8,128)(2,1)S(1)}, bf16[96,3456]{1,0:T(8,128)(2,1)S(1)}, u32[]{:S(2)}, u32[]{:S(2)}) %collective-permute-start.57) | collective-permute-done | bytes 663584 | tf_op jit(solution)/shard_map/ppermute | solution.py:460
  927.5 2.5 collective-permute-start.67
  930.1 25.6 %collective-permute-done.50 = bf16[96,3072]{1,0:T(8,128)(2,1)S(1)} collective-permute-done((bf16[96,3072]{1,0:T(8,128)(2,1)S(1)}, bf16[96,3072]{1,0:T(8,128)(2,1)S(1)}, u32[]{:S(2)}, u32[]{:S(2)}) %collective-permute-start.50) | collective-permute-done | bytes 589856 | tf_op jit(solution)/shard_map/ppermute | solution.py:460
  960.8 4.2 fusion.13
  965.0 4.8 collective-permute-done.58
  972.0 10.9 %collective-permute-done.51 = bf16[96,3072]{1,0:T(8,128)(2,1)S(1)} collective-permute-done((bf16[96,3072]{1,0:T(8,128)(2,1)S(1)}, bf16[96,3072]{1,0:T(8,128)(2,1)S(1)}, u32[]{:S(2)}, u32[]{:S(2)}) %collective-permute-start.51) | collective-permute-done | bytes 589856 | tf_op jit(solution)/shard_map/ppermute | solution.py:460
  984.7 12.3 %collective-permute-done.59 = bf16[96,3456]{1,0:T(8,128)(2,1)S(1)} collective-permute-done((bf16[96,3456]{1,0:T(8,128)(2,1)S(1)}, bf16[96,3456]{1,0:T(8,128)(2,1)S(1)}, u32[]{:S(2)}, u32[]{:S(2)}) %collective-permute-start.59) | collective-permute-done | bytes 663584 | tf_op jit(solution)/shard_map/ppermute | solution.py:460
  (511 shorter events, 190.4 us)
Async XLA Ops:
  4.8 52.8 %collective-permute-start.27 = (bf16[6,128,768]{2,1,0:T(8,128)(2,1)}, bf16[6,128,768]{2,1,0:T(8,128)(2,1)}, u32[]{:S(2)}, u32[]{:S(2)}) collective-permute-start(bf16[6,128,768]{2,1,0:T(8,128)(2,1)} %broadcast_select_fusion.8), channel_id=1, source_target_pairs={{0,4},{1,5},{2,6},{3,7},{4,0},{5,1},{6,2},{7,3},{8,12},{9,13},{10,... | collective-permute-start | bytes 3538952 | tf_op jit(solution)/shard_map/ppermute | solution.py:460
  9.3 46.5 %collective-permute-start.5 = (bf16[192,1920]{1,0:T(8,128)(2,1)}, bf16[192,1920]{1,0:T(8,128)(2,1)}, u32[]{:S(2)}, u32[]{:S(2)}) collective-permute-start(bf16[192,1920]{1,0:T(8,128)(2,1)} %concatenate.165), channel_id=1, source_target_pairs={{0,4},{1,5},{2,6},{3,7},{4,0},{5,1},{6,2},{7,3},{8,12},{9,13},{10,... | collective-permute-start | bytes 2211848 | tf_op jit(solution)/shard_map/ppermute | solution.py:460
  11.3 52.9 %collective-permute-start = (bf16[6,128,768]{2,1,0:T(8,128)(2,1)}, bf16[6,128,768]{2,1,0:T(8,128)(2,1)}, u32[]{:S(2)}, u32[]{:S(2)}) collective-permute-start(bf16[6,128,768]{2,1,0:T(8,128)(2,1)} %broadcast_select_fusion.14), channel_id=1, source_target_pairs={{0,4},{1,5},{2,6},{3,7},{4,0},{5,1},{6,2},{7,3},{8,12},{9,13},{10,... | collective-permute-start | bytes 3538952 | tf_op jit(solution)/shard_map/ppermute | solution.py:460
  13.0 38.0 %collective-permute-start.11 = (bf16[192,1536]{1,0:T(8,128)(2,1)}, bf16[192,1536]{1,0:T(8,128)(2,1)}, u32[]{:S(2)}, u32[]{:S(2)}) collective-permute-start(bf16[192,1536]{1,0:T(8,128)(2,1)} %broadcast_select_fusion.33), channel_id=1, source_target_pairs={{0,4},{1,5},{2,6},{3,7},{4,0},{5,1},{6,2},{7,3},{8,12},{9,13},{10,... | collective-permute-start | bytes 1769480 | tf_op jit(solution)/shard_map/ppermute | solution.py:460
  14.2 40.0 %collective-permute-start.17 = (bf16[192,1536]{1,0:T(8,128)(2,1)}, bf16[192,1536]{1,0:T(8,128)(2,1)}, u32[]{:S(2)}, u32[]{:S(2)}) collective-permute-start(bf16[192,1536]{1,0:T(8,128)(2,1)} %broadcast_select_fusion.29), channel_id=1, source_target_pairs={{0,4},{1,5},{2,6},{3,7},{4,0},{5,1},{6,2},{7,3},{8,12},{9,13},{10,... | collective-permute-start | bytes 1769480 | tf_op jit(solution)/shard_map/ppermute | solution.py:460
  52.7 116.2 %collective-permute-start.12 = (bf16[384,1536]{1,0:T(8,128)(2,1)S(1)}, bf16[384,1536]{1,0:T(8,128)(2,1)S(1)}, u32[]{:S(2)}, u32[]{:S(2)}) collective-permute-start(bf16[384,1536]{1,0:T(8,128)(2,1)S(1)} %pad_maximum_fusion.16), channel_id=1, source_target_pairs={{0,8},{1,9},{2,10},{3,11},{4,12},{5,13},{6,14},{7,15},{8,0},{9,1},... | collective-permute-start | bytes 3538952 | tf_op jit(solution)/shard_map/ppermute | solution.py:460
  59.8 18.2 %collective-permute-start.28 = (bf16[3,128,768]{2,1,0:T(8,128)(2,1)S(1)}, bf16[3,128,768]{2,1,0:T(8,128)(2,1)S(1)}, u32[]{:S(2)}, u32[]{:S(2)}) collective-permute-start(bf16[3,128,768]{2,1,0:T(8,128)(2,1)S(1)} %get-tuple-element.202), channel_id=1, source_target_pairs={{0,3},{1,2},{2,1},{3,0},{4,7},{5,6},{6,5},{7,4},{8,11},{9,10},{10,... | collective-permute-start | bytes 1769480 | tf_op jit(solution)/shard_map/ppermute | solution.py:460
  63.4 76.7 %collective-permute-start.29 = (bf16[3,128,768]{2,1,0:T(8,128)(2,1)S(1)}, bf16[3,128,768]{2,1,0:T(8,128)(2,1)S(1)}, u32[]{:S(2)}, u32[]{:S(2)}) collective-permute-start(bf16[3,128,768]{2,1,0:T(8,128)(2,1)S(1)} %get-tuple-element.203), channel_id=1, source_target_pairs={{0,2},{1,3},{2,0},{3,1},{4,6},{5,7},{6,4},{7,5},{8,10},{9,11},{10,... | collective-permute-start | bytes 1769480 | tf_op jit(solution)/shard_map/ppermute | solution.py:460
  63.4 76.9 %collective-permute-start.30 = (bf16[3,128,768]{2,1,0:T(8,128)(2,1)S(1)}, bf16[3,128,768]{2,1,0:T(8,128)(2,1)S(1)}, u32[]{:S(2)}, u32[]{:S(2)}) collective-permute-start(bf16[3,128,768]{2,1,0:T(8,128)(2,1)S(1)} %get-tuple-element.201), channel_id=1, source_target_pairs={{0,1},{1,0},{2,3},{3,2},{4,5},{5,4},{6,7},{7,6},{8,9},{9,8},{10,11... | collective-permute-start | bytes 1769480 | tf_op jit(solution)/shard_map/ppermute | solution.py:460
  66.3 74.8 %collective-permute-start.1 = (bf16[3,128,768]{2,1,0:T(8,128)(2,1)S(1)}, bf16[3,128,768]{2,1,0:T(8,128)(2,1)S(1)}, u32[]{:S(2)}, u32[]{:S(2)}) collective-permute-start(bf16[3,128,768]{2,1,0:T(8,128)(2,1)S(1)} %get-tuple-element.220), channel_id=1, source_target_pairs={{0,3},{1,2},{2,1},{3,0},{4,7},{5,6},{6,5},{7,4},{8,11},{9,10},{10,... | collective-permute-start | bytes 1769480 | tf_op jit(solution)/shard_map/ppermute | solution.py:460
  78.0 86.7 %collective-permute-start.2 = (bf16[3,128,768]{2,1,0:T(8,128)(2,1)S(1)}, bf16[3,128,768]{2,1,0:T(8,128)(2,1)S(1)}, u32[]{:S(2)}, u32[]{:S(2)}) collective-permute-start(bf16[3,128,768]{2,1,0:T(8,128)(2,1)S(1)} %get-tuple-element.138), channel_id=1, source_target_pairs={{0,2},{1,3},{2,0},{3,1},{4,6},{5,7},{6,4},{7,5},{8,10},{9,11},{10,... | collective-permute-start | bytes 1769480 | tf_op jit(solution)/shard_map/ppermute | solution.py:460
  140.2 26.1 %collective-permute-start.3 = (bf16[3,128,768]{2,1,0:T(8,128)(2,1)S(1)}, bf16[3,128,768]{2,1,0:T(8,128)(2,1)S(1)}, u32[]{:S(2)}, u32[]{:S(2)}) collective-permute-start(bf16[3,128,768]{2,1,0:T(8,128)(2,1)S(1)} %get-tuple-element.219), channel_id=1, source_target_pairs={{0,1},{1,0},{2,3},{3,2},{4,5},{5,4},{6,7},{7,6},{8,9},{9,8},{10,11... | collective-permute-start | bytes 1769480 | tf_op jit(solution)/shard_map/ppermute | solution.py:460
  140.3 29.5 %collective-permute-start.13 = (bf16[384,1536]{1,0:T(8,128)(2,1)S(1)}, bf16[384,1536]{1,0:T(8,128)(2,1)S(1)}, u32[]{:S(2)}, u32[]{:S(2)}) collective-permute-start(bf16[384,1536]{1,0:T(8,128)(2,1)S(1)} %pad_maximum_fusion.16), channel_id=1, source_target_pairs={{0,16},{1,17},{2,18},{3,19},{4,20},{5,21},{6,22},{7,23},{8,24},{9,... | collective-permute-start | bytes 3538952 | tf_op jit(solution)/shard_map/ppermute | solution.py:460
  141.1 28.8 %collective-permute-start.18 = (bf16[384,1536]{1,0:T(8,128)(2,1)S(1)}, bf16[384,1536]{1,0:T(8,128)(2,1)S(1)}, u32[]{:S(2)}, u32[]{:S(2)}) collective-permute-start(bf16[384,1536]{1,0:T(8,128)(2,1)S(1)} %pad_maximum_fusion.17), channel_id=1, source_target_pairs={{0,8},{1,9},{2,10},{3,11},{4,12},{5,13},{6,14},{7,15},{8,0},{9,1},... | collective-permute-start | bytes 3538952 | tf_op jit(solution)/shard_map/ppermute | solution.py:460
  164.6 28.9 %collective-permute-start.19 = (bf16[384,1536]{1,0:T(8,128)(2,1)S(1)}, bf16[384,1536]{1,0:T(8,128)(2,1)S(1)}, u32[]{:S(2)}, u32[]{:S(2)}) collective-permute-start(bf16[384,1536]{1,0:T(8,128)(2,1)S(1)} %pad_maximum_fusion.17), channel_id=1, source_target_pairs={{0,16},{1,17},{2,18},{3,19},{4,20},{5,21},{6,22},{7,23},{8,24},{9,... | collective-permute-start | bytes 3538952 | tf_op jit(solution)/shard_map/ppermute | solution.py:460
  166.3 35.2 %collective-permute-start.6 = (bf16[384,1920]{1,0:T(8,128)(2,1)S(1)}, bf16[384,1920]{1,0:T(8,128)(2,1)S(1)}, u32[]{:S(2)}, u32[]{:S(2)}) collective-permute-start(bf16[384,1920]{1,0:T(8,128)(2,1)S(1)} %pad_maximum_fusion.9), channel_id=1, source_target_pairs={{0,8},{1,9},{2,10},{3,11},{4,12},{5,13},{6,14},{7,15},{8,0},{9,1},... | collective-permute-start | bytes 4423688 | tf_op jit(solution)/shard_map/ppermute | solution.py:460
  168.9 56.3 %collective-permute-start.7 = (bf16[384,1920]{1,0:T(8,128)(2,1)S(1)}, bf16[384,1920]{1,0:T(8,128)(2,1)S(1)}, u32[]{:S(2)}, u32[]{:S(2)}) collective-permute-start(bf16[384,1920]{1,0:T(8,128)(2,1)S(1)} %pad_maximum_fusion.9), channel_id=1, source_target_pairs={{0,16},{1,17},{2,18},{3,19},{4,20},{5,21},{6,22},{7,23},{8,24},{9,... | collective-permute-start | bytes 4423688 | tf_op jit(solution)/shard_map/ppermute | solution.py:460
  169.8 94.9 %collective-permute-start.4 = (bf16[1536,768]{1,0:T(8,128)(2,1)S(1)}, bf16[1536,768]{1,0:T(8,128)(2,1)S(1)}, u32[]{:S(2)}, u32[]{:S(2)}) collective-permute-start(bf16[1536,768]{1,0:T(8,128)(2,1)S(1)} %bitcast.288), channel_id=1, source_target_pairs={{0,4},{1,5},{2,6},{3,7},{4,0},{5,1},{6,2},{7,3},{8,12},{9,13},{10,... | collective-permute-start | bytes 7077896 | tf_op jit(solution)/shard_map/ppermute | solution.py:460
  170.0 67.8 %collective-permute-start.14 = (bf16[192,1536]{1,0:T(8,128)(2,1)S(1)}, bf16[192,1536]{1,0:T(8,128)(2,1)S(1)}, u32[]{:S(2)}, u32[]{:S(2)}) collective-permute-start(bf16[192,1536]{1,0:T(8,128)(2,1)S(1)} %slice.645), channel_id=1, source_target_pairs={{0,16},{1,17},{2,18},{3,19},{4,20},{5,21},{6,22},{7,23},{8,24},{9,... | collective-permute-start | bytes 1769480 | tf_op jit(solution)/shard_map/ppermute | solution.py:460
  193.5 45.4 %collective-permute-start.15 = (bf16[192,1536]{1,0:T(8,128)(2,1)S(1)}, bf16[192,1536]{1,0:T(8,128)(2,1)S(1)}, u32[]{:S(2)}, u32[]{:S(2)}) collective-permute-start(bf16[192,1536]{1,0:T(8,128)(2,1)S(1)} %slice.646), channel_id=1, source_target_pairs={{0,8},{1,9},{2,10},{3,11},{4,12},{5,13},{6,14},{7,15},{8,0},{9,1},... | collective-permute-start | bytes 1769480 | tf_op jit(solution)/shard_map/ppermute | solution.py:460
  201.5 48.9 %collective-permute-start.20 = (bf16[192,1536]{1,0:T(8,128)(2,1)S(1)}, bf16[192,1536]{1,0:T(8,128)(2,1)S(1)}, u32[]{:S(2)}, u32[]{:S(2)}) collective-permute-start(bf16[192,1536]{1,0:T(8,128)(2,1)S(1)} %slice.649), channel_id=1, source_target_pairs={{0,16},{1,17},{2,18},{3,19},{4,20},{5,21},{6,22},{7,23},{8,24},{9,... | collective-permute-start | bytes 1769480 | tf_op jit(solution)/shard_map/ppermute | solution.py:460
  225.1 25.3 %collective-permute-start.21 = (bf16[192,1536]{1,0:T(8,128)(2,1)S(1)}, bf16[192,1536]{1,0:T(8,128)(2,1)S(1)}, u32[]{:S(2)}, u32[]{:S(2)}) collective-permute-start(bf16[192,1536]{1,0:T(8,128)(2,1)S(1)} %slice.650), channel_id=1, source_target_pairs={{0,8},{1,9},{2,10},{3,11},{4,12},{5,13},{6,14},{7,15},{8,0},{9,1},... | collective-permute-start | bytes 1769480 | tf_op jit(solution)/shard_map/ppermute | solution.py:460
  237.8 26.7 %collective-permute-start.8 = (bf16[192,1920]{1,0:T(8,128)(2,1)S(1)}, bf16[192,1920]{1,0:T(8,128)(2,1)S(1)}, u32[]{:S(2)}, u32[]{:S(2)}) collective-permute-start(bf16[192,1920]{1,0:T(8,128)(2,1)S(1)} %slice.630), channel_id=1, source_target_pairs={{0,16},{1,17},{2,18},{3,19},{4,20},{5,21},{6,22},{7,23},{8,24},{9,... | collective-permute-start | bytes 2211848 | tf_op jit(solution)/shard_map/ppermute | solution.py:460
  238.9 25.6 %collective-permute-start.9 = (bf16[192,1920]{1,0:T(8,128)(2,1)S(1)}, bf16[192,1920]{1,0:T(8,128)(2,1)S(1)}, u32[]{:S(2)}, u32[]{:S(2)}) collective-permute-start(bf16[192,1920]{1,0:T(8,128)(2,1)S(1)} %slice.631), channel_id=1, source_target_pairs={{0,8},{1,9},{2,10},{3,11},{4,12},{5,13},{6,14},{7,15},{8,0},{9,1},... | collective-permute-start | bytes 2211848 | tf_op jit(solution)/shard_map/ppermute | solution.py:460
  250.4 134.0 %collective-permute-start.31 = (bf16[1536,768]{1,0:T(8,128)(2,1)S(1)}, bf16[1536,768]{1,0:T(8,128)(2,1)}, u32[]{:S(2)}, u32[]{:S(2)}) collective-permute-start(bf16[1536,768]{1,0:T(8,128)(2,1)S(1)} %bitcast.287), channel_id=1, source_target_pairs={{0,4},{1,5},{2,6},{3,7},{4,0},{5,1},{6,2},{7,3},{8,12},{9,13},{10,... | collective-permute-start | bytes 7077896 | tf_op jit(solution)/shard_map/ppermute | solution.py:460
  278.0 17.6 %collective-permute-start.10 = (bf16[3,8,1792]{2,1,0:T(8,128)(2,1)S(1)}, bf16[3,8,1792]{2,1,0:T(8,128)(2,1)S(1)}, u32[]{:S(2)}, u32[]{:S(2)}) collective-permute-start(bf16[3,8,1792]{2,1,0:T(8,128)(2,1)S(1)} %slice_bitcast_fusion.8), channel_id=1, source_target_pairs={{0,1},{1,8},{2,3},{3,10},{4,5},{5,12},{6,7},{7,14},{8,9},{9,16},{1... | collective-permute-start | bytes 258056 | tf_op jit(solution)/shard_map/ppermute | solution.py:460
  421.6 5.4 collective-permute-start.32
  423.0 261.3 %collective-permute-start.60 = (bf16[768,768]{1,0:T(8,128)(2,1)}, bf16[768,768]{1,0:T(8,128)(2,1)}, u32[]{:S(2)}, u32[]{:S(2)}) collective-permute-start(bf16[768,768]{1,0:T(8,128)(2,1)} %pad_maximum_fusion.25), channel_id=1, source_target_pairs={{0,8},{1,9},{2,10},{3,11},{4,12},{5,13},{6,14},{7,15},{8,0},{9,1},... | collective-permute-start | bytes 3538952 | tf_op jit(solution)/shard_map/ppermute | solution.py:460
  423.2 271.8 %collective-permute-start.62 = (bf16[768,768]{1,0:T(8,128)(2,1)}, bf16[768,768]{1,0:T(8,128)(2,1)}, u32[]{:S(2)}, u32[]{:S(2)}) collective-permute-start(bf16[768,768]{1,0:T(8,128)(2,1)} %concatenate.211), channel_id=1, source_target_pairs={{0,16},{1,17},{2,18},{3,19},{4,20},{5,21},{6,22},{7,23},{8,24},{9,... | collective-permute-start | bytes 3538952 | tf_op jit(solution)/shard_map/ppermute | solution.py:460
  559.9 23.9 %collective-permute-start.33 = (bf16[3,3,1792]{2,1,0:T(4,128)(2,1)}, bf16[3,3,1792]{2,1,0:T(4,128)(2,1)}, u32[]{:S(2)}, u32[]{:S(2)}) collective-permute-start(bf16[3,3,1792]{2,1,0:T(4,128)(2,1)} %pad_maximum_fusion.27), channel_id=1, source_target_pairs={{1,0},{3,2},{5,4},{7,6},{8,1},{9,8},{10,3},{11,10},{12,5},{13,12},... | collective-permute-start | bytes 96776 | tf_op jit(solution)/shard_map/ppermute | solution.py:460
  620.9 6.1 collective-permute-start.39
  627.0 59.2 %collective-permute-start.44 = (bf16[768,768]{1,0:T(8,128)(2,1)}, bf16[768,768]{1,0:T(8,128)(2,1)S(1)}, u32[]{:S(2)}, u32[]{:S(2)}) collective-permute-start(bf16[768,768]{1,0:T(8,128)(2,1)} %pad_maximum_fusion.24), channel_id=1, source_target_pairs={{0,8},{1,9},{2,10},{3,11},{4,12},{5,13},{6,14},{7,15},{8,0},{9,1},... | collective-permute-start | bytes 3538952 | tf_op jit(solution)/shard_map/ppermute | solution.py:460
  627.1 21.0 %collective-permute-start.40 = (f32[96,128]{1,0:T(8,128)S(1)}, f32[96,128]{1,0:T(8,128)S(1)}, u32[]{:S(2)}, u32[]{:S(2)}) collective-permute-start(f32[96,128]{1,0:T(8,128)S(1)} %fusion.52), channel_id=1, source_target_pairs={{0,16},{1,17},{2,18},{3,19},{4,20},{5,21},{6,22},{7,23},{8,24},{9,... | collective-permute-start | bytes 147464 | tf_op jit(solution)/shard_map/ppermute | solution.py:460
  659.9 37.1 %collective-permute-start.52 = (bf16[768,1024]{1,0:T(8,128)(2,1)}, bf16[768,1024]{1,0:T(8,128)(2,1)}, u32[]{:S(2)}, u32[]{:S(2)}) collective-permute-start(bf16[768,1024]{1,0:T(8,128)(2,1)} %pad_maximum_fusion.7), channel_id=1, source_target_pairs={{0,8},{1,9},{2,10},{3,11},{4,12},{5,13},{6,14},{7,15},{8,0},{9,1},... | collective-permute-start | bytes 4718600 | tf_op jit(solution)/shard_map/ppermute | solution.py:460
  659.9 33.3 %collective-permute-start.54 = (bf16[768,896]{1,0:T(8,128)(2,1)}, bf16[768,896]{1,0:T(8,128)(2,1)}, u32[]{:S(2)}, u32[]{:S(2)}) collective-permute-start(bf16[768,896]{1,0:T(8,128)(2,1)} %concatenate.210), channel_id=1, source_target_pairs={{0,16},{1,17},{2,18},{3,19},{4,20},{5,21},{6,22},{7,23},{8,24},{9,... | collective-permute-start | bytes 4128776 | tf_op jit(solution)/shard_map/ppermute | solution.py:460
  684.3 78.2 %collective-permute-start.22 = (bf16[1536,768]{1,0:T(8,128)(2,1)S(1)}, bf16[1536,768]{1,0:T(8,128)(2,1)}, u32[]{:S(2)}, u32[]{:S(2)}) collective-permute-start(bf16[1536,768]{1,0:T(8,128)(2,1)S(1)} %copy-done.49), channel_id=1, source_target_pairs={{0,4},{1,5},{2,6},{3,7},{4,0},{5,1},{6,2},{7,3},{8,12},{9,13},{10,... | collective-permute-start | bytes 7077896 | tf_op jit(solution)/shard_map/ppermute | solution.py:460
  686.2 47.2 %collective-permute-start.46 = (bf16[768,768]{1,0:T(8,128)(2,1)S(1)}, bf16[768,768]{1,0:T(8,128)(2,1)S(1)}, u32[]{:S(2)}, u32[]{:S(2)}) collective-permute-start(bf16[768,768]{1,0:T(8,128)(2,1)S(1)} %copy-done.55), channel_id=1, source_target_pairs={{0,16},{1,17},{2,18},{3,19},{4,20},{5,21},{6,22},{7,23},{8,24},{9,... | collective-permute-start | bytes 3538952 | tf_op jit(solution)/shard_map/ppermute | solution.py:460
  693.2 37.8 %collective-permute-start.61 = (bf16[384,768]{1,0:T(8,128)(2,1)S(1)}, bf16[384,768]{1,0:T(8,128)(2,1)S(1)}, u32[]{:S(2)}, u32[]{:S(2)}) collective-permute-start(bf16[384,768]{1,0:T(8,128)(2,1)S(1)} %fusion.29), channel_id=1, source_target_pairs={{0,16},{1,17},{2,18},{3,19},{4,20},{5,21},{6,22},{7,23},{8,24},{9,... | collective-permute-start | bytes 1769480 | tf_op jit(solution)/shard_map/ppermute | solution.py:460
  695.1 48.6 %collective-permute-start.45 = (bf16[384,768]{1,0:T(8,128)(2,1)S(1)}, bf16[384,768]{1,0:T(8,128)(2,1)S(1)}, u32[]{:S(2)}, u32[]{:S(2)}) collective-permute-start(bf16[384,768]{1,0:T(8,128)(2,1)S(1)} %fusion.33), channel_id=1, source_target_pairs={{0,16},{1,17},{2,18},{3,19},{4,20},{5,21},{6,22},{7,23},{8,24},{9,... | collective-permute-start | bytes 1769480 | tf_op jit(solution)/shard_map/ppermute | solution.py:460
  697.0 51.5 %collective-permute-start.55 = (bf16[384,896]{1,0:T(8,128)(2,1)S(1)}, bf16[384,896]{1,0:T(8,128)(2,1)S(1)}, u32[]{:S(2)}, u32[]{:S(2)}) collective-permute-start(bf16[384,896]{1,0:T(8,128)(2,1)S(1)} %fusion.20), channel_id=1, source_target_pairs={{0,8},{1,9},{2,10},{3,11},{4,12},{5,13},{6,14},{7,15},{8,0},{9,1},... | collective-permute-start | bytes 2064392 | tf_op jit(solution)/shard_map/ppermute | solution.py:460
  731.0 47.6 %collective-permute-start.34 = (bf16[1536,768]{1,0:T(8,128)(2,1)}, bf16[1536,768]{1,0:T(8,128)(2,1)}, u32[]{:S(2)}, u32[]{:S(2)}) collective-permute-start(bf16[1536,768]{1,0:T(8,128)(2,1)} %select_convert_fusion), channel_id=1, source_target_pairs={{0,4},{1,5},{2,6},{3,7},{4,0},{5,1},{6,2},{7,3},{8,12},{9,13},{10,... | collective-permute-start | bytes 7077896 | tf_op jit(solution)/shard_map/ppermute | solution.py:460
  733.5 43.0 %collective-permute-start.53 = (bf16[384,1024]{1,0:T(8,128)(2,1)}, bf16[384,1024]{1,0:T(8,128)(2,1)}, u32[]{:S(2)}, u32[]{:S(2)}) collective-permute-start(bf16[384,1024]{1,0:T(8,128)(2,1)} %fusion.17), channel_id=1, source_target_pairs={{0,16},{1,17},{2,18},{3,19},{4,20},{5,21},{6,22},{7,23},{8,24},{9,... | collective-permute-start | bytes 2359304 | tf_op jit(solution)/shard_map/ppermute | solution.py:460
  743.7 16.3 %collective-permute-start.63 = (bf16[384,768]{1,0:T(8,128)(2,1)S(1)}, bf16[384,768]{1,0:T(8,128)(2,1)S(1)}, u32[]{:S(2)}, u32[]{:S(2)}) collective-permute-start(bf16[384,768]{1,0:T(8,128)(2,1)S(1)} %get-tuple-element.150), channel_id=1, source_target_pairs={{0,8},{1,9},{2,10},{3,11},{4,12},{5,13},{6,14},{7,15},{8,0},{9,1},... | collective-permute-start | bytes 1769480 | tf_op jit(solution)/shard_map/ppermute | solution.py:460
  748.5 22.3 %collective-permute-start.47 = (bf16[384,768]{1,0:T(8,128)(2,1)}, bf16[384,768]{1,0:T(8,128)(2,1)S(1)}, u32[]{:S(2)}, u32[]{:S(2)}) collective-permute-start(bf16[384,768]{1,0:T(8,128)(2,1)} %get-tuple-element.152), channel_id=1, source_target_pairs={{0,8},{1,9},{2,10},{3,11},{4,12},{5,13},{6,14},{7,15},{8,0},{9,1},... | collective-permute-start | bytes 1769480 | tf_op jit(solution)/shard_map/ppermute | solution.py:460
  762.5 19.5 %collective-permute-start.64 = (bf16[192,1536]{1,0:T(8,128)(2,1)}, bf16[192,1536]{1,0:T(8,128)(2,1)}, u32[]{:S(2)}, u32[]{:S(2)}) collective-permute-start(bf16[192,1536]{1,0:T(8,128)(2,1)} %select_convert_fusion.5), channel_id=1, source_target_pairs={{0,4},{1,5},{2,6},{3,7},{4,0},{5,1},{6,2},{7,3},{8,12},{9,13},{10,... | collective-permute-start | bytes 1769480 | tf_op jit(solution)/shard_map/ppermute | solution.py:460
  767.3 42.7 %collective-permute-start.23 = (bf16[3,128,768]{2,1,0:T(8,128)(2,1)}, bf16[3,128,768]{2,1,0:T(8,128)(2,1)}, u32[]{:S(2)}, u32[]{:S(2)}) collective-permute-start(bf16[3,128,768]{2,1,0:T(8,128)(2,1)} %get-tuple-element.216), channel_id=1, source_target_pairs={{0,2},{1,3},{2,0},{3,1},{4,6},{5,7},{6,4},{7,5},{8,10},{9,11},{10,... | collective-permute-start | bytes 1769480 | tf_op jit(solution)/shard_map/ppermute | solution.py:460
  771.7 38.2 %collective-permute-start.24 = (bf16[3,128,768]{2,1,0:T(8,128)(2,1)}, bf16[3,128,768]{2,1,0:T(8,128)(2,1)}, u32[]{:S(2)}, u32[]{:S(2)}) collective-permute-start(bf16[3,128,768]{2,1,0:T(8,128)(2,1)} %get-tuple-element.215), channel_id=1, source_target_pairs={{0,3},{1,2},{2,1},{3,0},{4,7},{5,6},{6,5},{7,4},{8,11},{9,10},{10,... | collective-permute-start | bytes 1769480 | tf_op jit(solution)/shard_map/ppermute | solution.py:460
  776.5 37.8 %collective-permute-start.25 = (bf16[3,128,768]{2,1,0:T(8,128)(2,1)}, bf16[3,128,768]{2,1,0:T(8,128)(2,1)}, u32[]{:S(2)}, u32[]{:S(2)}) collective-permute-start(bf16[3,128,768]{2,1,0:T(8,128)(2,1)} %get-tuple-element.214), channel_id=1, source_target_pairs={{0,1},{1,0},{2,3},{3,2},{4,5},{5,4},{6,7},{7,6},{8,9},{9,8},{10,11... | collective-permute-start | bytes 1769480 | tf_op jit(solution)/shard_map/ppermute | solution.py:460
  778.7 74.9 %collective-permute-start.48 = (bf16[192,1536]{1,0:T(8,128)(2,1)}, bf16[192,1536]{1,0:T(8,128)(2,1)}, u32[]{:S(2)}, u32[]{:S(2)}) collective-permute-start(bf16[192,1536]{1,0:T(8,128)(2,1)} %select_convert_fusion.7), channel_id=1, source_target_pairs={{0,4},{1,5},{2,6},{3,7},{4,0},{5,1},{6,2},{7,3},{8,12},{9,13},{10,... | collective-permute-start | bytes 1769480 | tf_op jit(solution)/shard_map/ppermute | solution.py:460
  782.0 92.9 %collective-permute-start.56 = (bf16[192,1920]{1,0:T(8,128)(2,1)S(1)}, bf16[192,1920]{1,0:T(8,128)(2,1)S(1)}, u32[]{:S(2)}, u32[]{:S(2)}) collective-permute-start(bf16[192,1920]{1,0:T(8,128)(2,1)S(1)} %select_convert_fusion.2), channel_id=1, source_target_pairs={{0,4},{1,5},{2,6},{3,7},{4,0},{5,1},{6,2},{7,3},{8,12},{9,13},{10,... | collective-permute-start | bytes 2211848 | tf_op jit(solution)/shard_map/ppermute | solution.py:460
  809.9 50.5 %collective-permute-start.35 = (bf16[3,128,768]{2,1,0:T(8,128)(2,1)S(1)}, bf16[3,128,768]{2,1,0:T(8,128)(2,1)S(1)}, u32[]{:S(2)}, u32[]{:S(2)}) collective-permute-start(bf16[3,128,768]{2,1,0:T(8,128)(2,1)S(1)} %get-tuple-element.125), channel_id=1, source_target_pairs={{0,2},{1,3},{2,0},{3,1},{4,6},{5,7},{6,4},{7,5},{8,10},{9,11},{10,... | collective-permute-start | bytes 1769480 | tf_op jit(solution)/shard_map/ppermute | solution.py:460
  809.9 50.5 %collective-permute-start.36 = (bf16[3,128,768]{2,1,0:T(8,128)(2,1)S(1)}, bf16[3,128,768]{2,1,0:T(8,128)(2,1)S(1)}, u32[]{:S(2)}, u32[]{:S(2)}) collective-permute-start(bf16[3,128,768]{2,1,0:T(8,128)(2,1)S(1)} %get-tuple-element.200), channel_id=1, source_target_pairs={{0,3},{1,2},{2,1},{3,0},{4,7},{5,6},{6,5},{7,4},{8,11},{9,10},{10,... | collective-permute-start | bytes 1769480 | tf_op jit(solution)/shard_map/ppermute | solution.py:460
  814.3 58.9 %collective-permute-start.37 = (bf16[3,128,768]{2,1,0:T(8,128)(2,1)S(1)}, bf16[3,128,768]{2,1,0:T(8,128)(2,1)S(1)}, u32[]{:S(2)}, u32[]{:S(2)}) collective-permute-start(bf16[3,128,768]{2,1,0:T(8,128)(2,1)S(1)} %get-tuple-element.199), channel_id=1, source_target_pairs={{0,1},{1,0},{2,3},{3,2},{4,5},{5,4},{6,7},{7,6},{8,9},{9,8},{10,11... | collective-permute-start | bytes 1769480 | tf_op jit(solution)/shard_map/ppermute | solution.py:460
  853.5 31.9 %collective-permute-start.65 = (bf16[96,3072]{1,0:T(8,128)(2,1)}, bf16[96,3072]{1,0:T(8,128)(2,1)}, u32[]{:S(2)}, u32[]{:S(2)}) collective-permute-start(bf16[96,3072]{1,0:T(8,128)(2,1)} %select_convert_fusion.4), channel_id=1, source_target_pairs={{0,1},{1,0},{2,3},{3,2},{4,5},{5,4},{6,7},{7,6},{8,9},{9,8},{10,11... | collective-permute-start | bytes 1769480 | tf_op jit(solution)/shard_map/ppermute | solution.py:460
  860.4 65.0 %collective-permute-start.26 = (bf16[6,128,768]{2,1,0:T(8,128)(2,1)}, bf16[6,128,768]{2,1,0:T(8,128)(2,1)}, u32[]{:S(2)}, u32[]{:S(2)}) collective-permute-start(bf16[6,128,768]{2,1,0:T(8,128)(2,1)} %broadcast_select_fusion.13), channel_id=1, source_target_pairs={{0,4},{1,5},{2,6},{3,7},{4,0},{5,1},{6,2},{7,3},{8,12},{9,13},{10,... | collective-permute-start | bytes 3538952 | tf_op jit(solution)/shard_map/ppermute | solution.py:460
  860.4 50.3 %collective-permute-start.49 = (bf16[96,3072]{1,0:T(8,128)(2,1)}, bf16[96,3072]{1,0:T(8,128)(2,1)}, u32[]{:S(2)}, u32[]{:S(2)}) collective-permute-start(bf16[96,3072]{1,0:T(8,128)(2,1)} %select_convert_fusion.6), channel_id=1, source_target_pairs={{0,1},{1,0},{2,3},{3,2},{4,5},{5,4},{6,7},{7,6},{8,9},{9,8},{10,11... | collective-permute-start | bytes 1769480 | tf_op jit(solution)/shard_map/ppermute | solution.py:460
  875.0 81.0 %collective-permute-start.38 = (bf16[6,128,768]{2,1,0:T(8,128)(2,1)}, bf16[6,128,768]{2,1,0:T(8,128)(2,1)}, u32[]{:S(2)}, u32[]{:S(2)}) collective-permute-start(bf16[6,128,768]{2,1,0:T(8,128)(2,1)} %broadcast_select_fusion.7), channel_id=1, source_target_pairs={{0,4},{1,5},{2,6},{3,7},{4,0},{5,1},{6,2},{7,3},{8,12},{9,13},{10,... | collective-permute-start | bytes 3538952 | tf_op jit(solution)/shard_map/ppermute | solution.py:460
  880.4 44.5 %collective-permute-start.57 = (bf16[96,3456]{1,0:T(8,128)(2,1)S(1)}, bf16[96,3456]{1,0:T(8,128)(2,1)S(1)}, u32[]{:S(2)}, u32[]{:S(2)}) collective-permute-start(bf16[96,3456]{1,0:T(8,128)(2,1)S(1)} %select_convert_fusion.3), channel_id=1, source_target_pairs={{0,1},{1,0},{2,3},{3,2},{4,5},{5,4},{6,7},{7,6},{8,9},{9,8},{10,11... | collective-permute-start | bytes 1990664 | tf_op jit(solution)/shard_map/ppermute | solution.py:460
  887.1 40.3 %collective-permute-start.66 = (bf16[96,3072]{1,0:T(8,128)(2,1)S(1)}, bf16[96,3072]{1,0:T(8,128)(2,1)S(1)}, u32[]{:S(2)}, u32[]{:S(2)}) collective-permute-start(bf16[96,3072]{1,0:T(8,128)(2,1)S(1)} %add_convert_fusion.5), channel_id=1, source_target_pairs={{0,2},{1,3},{2,0},{3,1},{4,6},{5,7},{6,4},{7,5},{8,10},{9,11},{10,... | collective-permute-start | bytes 1769480 | tf_op jit(solution)/shard_map/ppermute | solution.py:460
  912.1 43.6 %collective-permute-start.50 = (bf16[96,3072]{1,0:T(8,128)(2,1)S(1)}, bf16[96,3072]{1,0:T(8,128)(2,1)S(1)}, u32[]{:S(2)}, u32[]{:S(2)}) collective-permute-start(bf16[96,3072]{1,0:T(8,128)(2,1)S(1)} %add_convert_fusion.7), channel_id=1, source_target_pairs={{0,2},{1,3},{2,0},{3,1},{4,6},{5,7},{6,4},{7,5},{8,10},{9,11},{10,... | collective-permute-start | bytes 1769480 | tf_op jit(solution)/shard_map/ppermute | solution.py:460
  925.0 44.8 %collective-permute-start.58 = (bf16[96,3456]{1,0:T(8,128)(2,1)S(1)}, bf16[96,3456]{1,0:T(8,128)(2,1)S(1)}, u32[]{:S(2)}, u32[]{:S(2)}) collective-permute-start(bf16[96,3456]{1,0:T(8,128)(2,1)S(1)} %add_convert_fusion.3), channel_id=1, source_target_pairs={{0,2},{1,3},{2,0},{3,1},{4,6},{5,7},{6,4},{7,5},{8,10},{9,11},{10,... | collective-permute-start | bytes 1990664 | tf_op jit(solution)/shard_map/ppermute | solution.py:460
  927.5 42.7 %collective-permute-start.67 = (bf16[96,3072]{1,0:T(8,128)(2,1)S(1)}, bf16[96,3072]{1,0:T(8,128)(2,1)S(1)}, u32[]{:S(2)}, u32[]{:S(2)}) collective-permute-start(bf16[96,3072]{1,0:T(8,128)(2,1)S(1)} %add_convert_fusion.4), channel_id=1, source_target_pairs={{0,1},{1,0},{2,3},{3,2},{4,5},{5,4},{6,7},{7,6},{8,9},{9,8},{10,11... | collective-permute-start | bytes 1769480 | tf_op jit(solution)/shard_map/ppermute | solution.py:460
  955.8 27.1 %collective-permute-start.51 = (bf16[96,3072]{1,0:T(8,128)(2,1)S(1)}, bf16[96,3072]{1,0:T(8,128)(2,1)S(1)}, u32[]{:S(2)}, u32[]{:S(2)}) collective-permute-start(bf16[96,3072]{1,0:T(8,128)(2,1)S(1)} %add_convert_fusion.6), channel_id=1, source_target_pairs={{0,1},{1,0},{2,3},{3,2},{4,5},{5,4},{6,7},{7,6},{8,9},{9,8},{10,11... | collective-permute-start | bytes 1769480 | tf_op jit(solution)/shard_map/ppermute | solution.py:460
  970.0 27.0 %collective-permute-start.59 = (bf16[96,3456]{1,0:T(8,128)(2,1)S(1)}, bf16[96,3456]{1,0:T(8,128)(2,1)S(1)}, u32[]{:S(2)}, u32[]{:S(2)}) collective-permute-start(bf16[96,3456]{1,0:T(8,128)(2,1)S(1)} %add_convert_fusion.2), channel_id=1, source_target_pairs={{0,1},{1,0},{2,3},{3,2},{4,5},{5,4},{6,7},{7,6},{8,9},{9,8},{10,11... | collective-permute-start | bytes 1990664 | tf_op jit(solution)/shard_map/ppermute | solution.py:460
  (93 other events, 1893.2 us)

commit v2 on v1

--- a/solution.py
+++ b/solution.py
@@ -439,6 +439,442 @@
         back_copy(k).wait_send()
 
 
+def places():
+    f, z = lax.axis_index("fs"), lax.axis_index("sp")
+    core, chip = f % 2, f // 2
+    by_x, by_y = chip + 1 - 2 * (chip % 2), (chip + 2) % 4
+    return f, z, core, chip, by_x, by_y
+
+
+def remote(src, dst, sends, receives, slot, device):
+    return pltpu.make_async_remote_copy(
+        src_ref=src, dst_ref=dst, send_sem=sends.at[slot], recv_sem=receives.at[slot],
+        device_id=device, device_id_type=MESH,
+    )
+
+
+def head_kernel(
+    hidden, mine, other, small, rows_out, first_out, small_out, local, sends, receives, small_sends, small_receives
+):
+    f, z, core, chip, by_x, by_y = places()
+    units = rows_out.shape[0]
+    partner, over_x, over_y = (f + 1 - 2 * core, z), (2 * by_x + core, z), (2 * by_y + core, z)
+    near_group, far_group = z // 2, 1 - z // 2
+    near, far = (2 * chip + z % 2, 2 * near_group + core), (2 * chip + z % 2, 2 * far_group + core)
+    stays = z % 2 == core
+    shards = small_out.shape[0]
+
+    barrier = pltpu.get_barrier_semaphore()
+    for k in range(1, shards):
+        pl.semaphore_signal(barrier, inc=1, device_id=((f + k) % shards, z), device_id_type=MESH)
+    pl.semaphore_signal(barrier, inc=1, device_id=far, device_id_type=MESH)
+
+    @pl.when(jnp.logical_not(stays))
+    def _():
+        pl.semaphore_signal(barrier, inc=1, device_id=near, device_id_type=MESH)
+
+    pl.semaphore_wait(barrier, shards + (z + core) % 2)
+
+    def group_of(g):
+        return hidden.at[pl.ds(g * units, units)]
+
+    def part(chip_at, core_at):
+        return first_out.at[chip_at, core_at]
+
+    def copy(src, dst, slot, device):
+        return remote(src, dst, sends, receives, slot, device)
+
+    to_far = copy(group_of(far_group), rows_out.at[:, z], 0, far)
+    to_far.start()
+    to_partner = copy(other, part(chip, core), 1, partner)
+    to_partner.start()
+    to_x = copy(mine, part(chip, core), 2, over_x)
+    to_x.start()
+    to_y = copy(mine, part(chip, core), 3, over_y)
+    to_y.start()
+    to_near = copy(group_of(near_group), rows_out.at[:, z], 4, near)
+    keep_rows = pltpu.make_async_copy(group_of(near_group), rows_out.at[:, z], local.at[0])
+
+    @pl.when(stays)
+    def _():
+        keep_rows.start()
+
+    @pl.when(jnp.logical_not(stays))
+    def _():
+        to_near.start()
+
+    keep_first = pltpu.make_async_copy(mine, part(chip, core), local.at[1])
+    keep_first.start()
+    keep_small = pltpu.make_async_copy(small, small_out.at[f], local.at[2])
+    keep_small.start()
+
+    def small_copy(k, at):
+        return pltpu.make_async_remote_copy(
+            src_ref=small, dst_ref=small_out.at[at],
+            send_sem=small_sends.at[k], recv_sem=small_receives.at[at],
+            device_id=((f + k) % shards, z), device_id_type=MESH,
+        )
+
+    for k in range(1, shards):
+        small_copy(k, f).start()
+
+    from_partner = copy(other, part(chip, 1 - core), 1, partner)
+    from_partner.wait_recv()
+    again_x = copy(part(chip, 1 - core), part(chip, 1 - core), 5, over_x)
+    again_x.start()
+    again_y = copy(part(chip, 1 - core), part(chip, 1 - core), 6, over_y)
+    again_y.start()
+
+    near_at, far_at = 2 * near_group + core, 2 * far_group + core
+
+    @pl.when(stays)
+    def _():
+        keep_rows.wait()
+
+    @pl.when(jnp.logical_not(stays))
+    def _():
+        copy(group_of(near_group), rows_out.at[:, near_at], 4, near).wait_recv()
+
+    near_on = copy(rows_out.at[:, near_at], rows_out.at[:, near_at], 7, partner)
+    near_on.start()
+
+    copy(mine, part(by_x, core), 2, over_x).wait_recv()
+    on_y = copy(part(by_x, core), part(by_x, core), 8, over_y)
+    on_y.start()
+    copy(mine, part(by_y, core), 3, over_y).wait_recv()
+    copy(mine, part(by_x, 1 - core), 5, over_x).wait_recv()
+    copy(mine, part(by_y, 1 - core), 6, over_y).wait_recv()
+    on_x = copy(part(by_y, 1 - core), part(by_y, 1 - core), 9, over_x)
+    on_x.start()
+
+    copy(group_of(far_group), rows_out.at[:, far_at], 0, far).wait_recv()
+    far_on = copy(rows_out.at[:, far_at], rows_out.at[:, far_at], 10, partner)
+    far_on.start()
+
+    corner = (by_x + 2) % 4
+    for k in range(1, shards):
+        small_copy(k, (f + k) % shards).wait_recv()
+    copy(mine, part(corner, core), 8, over_y).wait_recv()
+    copy(mine, part(corner, 1 - core), 9, over_x).wait_recv()
+    copy(rows_out.at[:, near_at], rows_out.at[:, 2 * near_group + 1 - core], 7, partner).wait_recv()
+    copy(rows_out.at[:, far_at], rows_out.at[:, 2 * far_group + 1 - core], 10, partner).wait_recv()
+    for sent in (to_far, to_partner, to_x, to_y, again_x, again_y, near_on, on_y, on_x, far_on):
+        sent.wait_send()
+
+    @pl.when(jnp.logical_not(stays))
+    def _():
+        to_near.wait_send()
+
+    for k in range(1, shards):
+        small_copy(k, f).wait_send()
+    keep_first.wait()
+    keep_small.wait()
+
+
+PIECES = ((0, 512, "x"), (1024, 512, "y"), (512, 512, "x"), (1536, 384, "y"))
+
+
+def tail_kernel(
+    g, g_x, g_bc, g_heads, g_gate, g_norm, d_part, out_x, out_bc, out_dt, vec_out, d_out,
+    d_came, d_sum, local, r1, s2, r2, sp, rp, total, z1s, z1r, z2s, z2r, z3s, z3r, vs, vr,
+    sends, receives, vec_sends, vec_receives,
+):
+    f, z, core, chip, by_x, by_y = places()
+    corner = (by_x + 2) % 4
+    rows = g.shape[0] // 4
+    half = rows // 2
+    quarter = half // 2
+    inner = out_x.shape[1] // 2
+    bit = z % 2
+    partner = (f + 1 - 2 * core, z)
+    over = {"x": (2 * by_x + core, z), "y": (2 * by_y + core, z)}
+    near, far = (f, z + 1 - 2 * bit), (f, (z + 2) % 4)
+
+    upper, units = z // 2, d_part.shape[0]
+    token_near, token_far = (2 * chip + bit, 2 * upper + core), (2 * chip + bit, 2 * (1 - upper) + core)
+    stays = bit == core
+
+    barrier = pltpu.get_barrier_semaphore()
+    for device in (partner, over["x"], over["y"], near, far, token_far):
+        pl.semaphore_signal(barrier, inc=1, device_id=device, device_id_type=MESH)
+
+    @pl.when(jnp.logical_not(stays))
+    def _():
+        pl.semaphore_signal(barrier, inc=1, device_id=token_near, device_id_type=MESH)
+
+    pl.semaphore_wait(barrier, 6 + (bit + core) % 2)
+
+    slot = 7 * len(PIECES)
+
+    def d_pair(k, n):
+        return remote(d_part.at[:, k, 1 - core], d_came.at[:, k], sends, receives, slot + n, partner)
+
+    def d_trade(k, n, device, group):
+        return remote(
+            d_sum.at[:, k], d_out.at[pl.ds(group * units, units)], sends, receives, slot + 2 + n, device
+        )
+
+    def d_add(k):
+        for u in range(units):
+            d_sum[u, k] = (d_part[u, k, core].astype(F32) + d_came[u, k].astype(F32)).astype(BF16)
+
+    d_pair(1 - upper, 0).start()
+    d_pair(upper, 1).start()
+    d_keep = pltpu.make_async_copy(d_sum.at[:, upper], d_out.at[pl.ds(upper * units, units)], local.at[0])
+
+    def at(i, size):
+        return pl.ds(pl.multiple_of(i * size, size), size)
+
+    vs[0] = jnp.zeros(vs.shape[1:], F32)
+    for k in range(5):
+        vs[0, k : k + 1] = jnp.sum(g_x[8 * k : 8 * k + 8], axis=0, keepdims=True)
+        vs[0, 8 + k : 9 + k, : 2 * LANES] = jnp.sum(g_bc[8 * k : 8 * k + 8], axis=0, keepdims=True)
+    vs[0, 5:6] = g_gate[...]
+    vs[0, 6:7] = g_norm[...]
+    for k in range(3):
+        vs[0, 7:8, k * LANES : (k + 1) * LANES] = jnp.sum(
+            g_heads[8 * k : 8 * k + 8], axis=0, keepdims=True
+        )
+    vec_ways = [over["x"], over["y"], near, far]
+
+    def vec_copy(k):
+        return remote(vs.at[k], vr.at[k], vec_sends, vec_receives, k, vec_ways[k])
+
+    def vec_last(side):
+        return remote(vec_out.at[core], vec_out.at[side], vec_sends, vec_receives, 4, partner)
+
+    layout = []
+    z_start = 0
+    for n, (start, width, way) in enumerate(PIECES):
+        wide = 4 * LANES if start == inner else 2 * width
+        layout.append((n, start, width, way, "y" if way == "x" else "x", z_start, wide))
+        z_start += wide
+
+    def first_copies(piece):
+        n, start, width, way, _, _, _ = piece
+        columns = pl.ds(start, width)
+        to = by_x if way == "x" else by_y
+        return [
+            remote(g.at[at(i, rows), columns], r1.at[k, :, columns], sends, receives, 7 * n + k, over[way])
+            for k, i in enumerate((to, corner))
+        ]
+
+    def second_copy(piece):
+        n, start, width, _, other, _, _ = piece
+        columns = pl.ds(start, width)
+        return remote(s2.at[:, columns], r2.at[:, columns], sends, receives, 7 * n + 2, over[other])
+
+    def pair_copy(piece):
+        n, start, width, _, _, _, _ = piece
+        columns = pl.ds(start, width)
+        return remote(sp.at[:, columns], rp.at[:, columns], sends, receives, 7 * n + 3, partner)
+
+    def z_copy(piece, k):
+        n, _, _, _, _, start, wide = piece
+        columns = pl.ds(start, wide)
+        src, dst, device = ((z1s, z1r, near), (z2s, z2r, far), (z3s, z3r, near))[k]
+        return remote(src.at[:, columns], dst.at[:, columns], sends, receives, 7 * n + 4 + k, device)
+
+    def after_first(piece):
+        _, start, width, way, _, _, _ = piece
+        for copy in first_copies(piece):
+            copy.wait_recv()
+        columns = pl.ds(start, width)
+        to = by_y if way == "x" else by_x
+        s2[:, columns] = (g[at(to, rows), columns].astype(F32) + r1[1, :, columns].astype(F32)).astype(BF16)
+        second_copy(piece).start()
+
+    def chip_sum(piece, side):
+        _, start, width, _, _, _, _ = piece
+        columns = pl.ds(start, width)
+        own = g[pl.ds(pl.multiple_of(chip * rows + side * half, half), half), columns].astype(F32)
+        return own + r1[0, at(side, half), columns].astype(F32) + r2[at(side, half), columns].astype(F32)
+
+    def lanes_at(start, side, width):
+        return pl.ds(pl.multiple_of(start + side * width, LANES), width)
+
+    def after_second(piece):
+        _, start, width, _, _, z_at, _ = piece
+        second_copy(piece).wait_recv()
+        sp[:, pl.ds(start, width)] = chip_sum(piece, 1 - core).astype(BF16)
+        pair_copy(piece).start()
+        own = chip_sum(piece, core)
+        if start == inner:
+            total[:, pl.ds(z_at, 2 * LANES)] = own[:, : 2 * LANES]
+            total[:, lanes_at(z_at + 2 * LANES, core, LANES)] = own[:, 2 * LANES :]
+        else:
+            total[:, lanes_at(z_at, core, width)] = own
+
+    def after_pair(piece):
+        _, start, width, _, _, z_at, wide = piece
+        pair_copy(piece).wait_recv()
+        came = rp[:, pl.ds(start, width)].astype(F32)
+        if start == inner:
+            total[:, pl.ds(z_at, 2 * LANES)] += came[:, : 2 * LANES]
+            total[:, lanes_at(z_at + 2 * LANES, 1 - core, LANES)] = came[:, 2 * LANES :]
+        else:
+            total[:, lanes_at(z_at, 1 - core, width)] = came
+        columns = pl.ds(z_at, wide)
+        z1s[:, columns] = total[at(1 - bit, quarter), columns].astype(BF16)
+        z_copy(piece, 0).start()
+
+    def after_near(piece):
+        columns = pl.ds(piece[5], piece[6])
+        z_copy(piece, 0).wait_recv()
+        z2s[:, columns] = (total[at(bit, quarter), columns] + z1r[:, columns].astype(F32)).astype(BF16)
+        z_copy(piece, 1).start()
+
+    def store(piece, side, values):
+        _, start, width, _, _, _, _ = piece
+        there = at(side, quarter)
+        if start == inner:
+            out_bc[there, :] = values[:, : 2 * LANES]
+            out_dt[there, :] = values[:, 2 * LANES :]
+        else:
+            out_x[there, pl.ds(start, width)] = values[:, :width]
+            out_x[there, pl.ds(inner + start, width)] = values[:, width:]
+
+    def after_far(piece):
+        columns = pl.ds(piece[5], piece[6])
+        z_copy(piece, 1).wait_recv()
+        low = (z2s[:, columns].astype(F32) + z2r[:, columns].astype(F32)).astype(BF16)
+        z3s[:, columns] = low
+        z_copy(piece, 2).start()
+        store(piece, bit, low.astype(F32))
+
+    def after_last(piece):
+        z_copy(piece, 2).wait_recv()
+        store(piece, 1 - bit, z3r[:, pl.ds(piece[5], piece[6])].astype(F32))
+
+    def vec_step(k):
+        if k:
+            vec_copy(k - 1).wait_recv()
+            summed = vs[k - 1] + vr[k - 1]
+            if k < 4:
+                vs[k] = summed
+            else:
+                vec_out[core] = summed
+        if k < 4:
+            vec_copy(k).start()
+        else:
+            vec_last(core).start()
+
+    for piece in layout:
+        for copy in first_copies(piece):
+            copy.start()
+    vec_step(0)
+    d_pair(1 - upper, 0).wait_recv()
+    d_add(1 - upper)
+    d_trade(1 - upper, 0, token_far, upper).start()
+    d_pair(upper, 1).wait_recv()
+    d_add(upper)
+
+    @pl.when(stays)
+    def _():
+        d_keep.start()
+
+    @pl.when(jnp.logical_not(stays))
+    def _():
+        d_trade(upper, 1, token_near, upper).start()
+
+    early, late = layout[:2], layout[2:]
+    order = (
+        (after_first, early), (1, ()), (after_first, late), (2, ()), (after_second, early), (3, ()),
+        (after_pair, early), (after_second, late), (4, ()), (after_near, early), (after_pair, late),
+        (after_far, early), (after_near, late), (after_last, early), (after_far, late), (after_last, late),
+    )
+    for stage, pieces in order:
+        if not pieces:
+            vec_step(stage)
+        for piece in pieces:
+            stage(piece)
+    vec_last(1 - core).wait_recv()
+    d_trade(1 - upper, 0, token_far, 1 - upper).wait_recv()
+
+    @pl.when(stays)
+    def _():
+        d_keep.wait()
+
+    @pl.when(jnp.logical_not(stays))
+    def _():
+        d_trade(upper, 1, token_near, upper).wait()
+
+    d_trade(1 - upper, 0, token_far, upper).wait_send()
+    d_pair(1 - upper, 0).wait_send()
+    d_pair(upper, 1).wait_send()
+    for piece in layout:
+        for copy in first_copies(piece) + [second_copy(piece), pair_copy(piece)]:
+            copy.wait_send()
+        for k in range(3):
+            z_copy(piece, k).wait_send()
+    for k in range(4):
+        vec_copy(k).wait_send()
+    vec_last(core).wait_send()
+
+
+def trade_steps(source, target, local, sends, receives):
+    f, z, core, chip, _, _ = places()
+    units = source.shape[0]
+    bit, upper = z % 2, z // 2
+    near, far = (2 * chip + bit, 2 * upper + core), (2 * chip + bit, 2 * (1 - upper) + core)
+    stays = bit == core
+
+    def copy(k, n, device, group):
+        return remote(source.at[:, k], target.at[pl.ds(group * units, units)], sends, receives, n, device)
+
+    keep = pltpu.make_async_copy(source.at[:, upper], target.at[pl.ds(upper * units, units)], local.at[0])
+
+    def start():
+        barrier = pltpu.get_barrier_semaphore()
+        pl.semaphore_signal(barrier, inc=1, device_id=far, device_id_type=MESH)
+
+        @pl.when(jnp.logical_not(stays))
+        def _():
+            pl.semaphore_signal(barrier, inc=1, device_id=near, device_id_type=MESH)
+
+        pl.semaphore_wait(barrier, 1 + (bit + core) % 2)
+        copy(1 - upper, 0, far, upper).start()
+
+        @pl.when(stays)
+        def _():
+            keep.start()
+
+        @pl.when(jnp.logical_not(stays))
+        def _():
+            copy(upper, 1, near, upper).start()
+
+    def finish():
+        copy(1 - upper, 0, far, 1 - upper).wait_recv()
+        copy(1 - upper, 0, far, upper).wait_send()
+
+        @pl.when(stays)
+        def _():
+            keep.wait()
+
+        @pl.when(jnp.logical_not(stays))
+        def _():
+            copy(upper, 1, near, upper).wait()
+
+    return start, finish
+
+
+def backward_sending_kernel(*refs):
+    inputs, source, outputs, target = refs[:16], refs[16], refs[17:23], refs[23]
+    scratch, sems = refs[24:30], refs[30:]
+    unit, chunk = pl.program_id(0), pl.program_id(1)
+    start, finish = trade_steps(source, target, *sems)
+
+    @pl.when((unit == 0) & (chunk == 0))
+    def _():
+        start()
+
+    backward_kernel(*inputs, *outputs, *scratch)
+
+    @pl.when((unit == pl.num_programs(0) - 1) & (chunk == PER_UNIT - 1))
+    def _():
+        finish()
+
+
 class Plan:
     def __init__(self, batch, tokens):
         self.shards, self.members = lax.axis_size("fs"), lax.axis_size("sp")
@@ -483,128 +919,180 @@
         first = self.core == 0
         return jnp.where(first, mine, other), jnp.where(first, other, mine)
 
-    def turned(self, blocks):
+    def head(self, hidden, mine, other, small):
         if not self.fast:
-            return blocks
-        x, y = (self.chip % 2) == 1, (self.chip // 2) == 1
-        a, b, c, d = blocks
-        a, b = jnp.where(x, b, a), jnp.where(x, a, b)
-        c, d = jnp.where(x, d, c), jnp.where(x, c, d)
-        return [jnp.where(y, c, a), jnp.where(y, d, b), jnp.where(y, a, c), jnp.where(y, b, d)]
-
-    def turn(self, x):
+            both = jnp.concatenate(self.by_core(mine, self.swap(other, df=1)), axis=0)
+            return self.to_units(hidden), self.gather(both), lax.all_gather(small, "fs")
+        anywhere = pl.BlockSpec(memory_space=pl.ANY)
+        rows, first, everyone = pl.pallas_call(
+            head_kernel,
+            out_shape=[
+                jax.ShapeDtypeStruct((self.units, 4, self.tokens, hidden.shape[-1]), BF16),
+                jax.ShapeDtypeStruct((4, 2) + mine.shape, BF16),
+                jax.ShapeDtypeStruct((self.shards,) + small.shape, BF16),
+            ],
+            in_specs=[anywhere] * 4,
+            out_specs=[anywhere] * 3,
+            scratch_shapes=[
+                pltpu.SemaphoreType.DMA((3,)),
+                pltpu.SemaphoreType.DMA((11,)),
+                pltpu.SemaphoreType.DMA((11,)),
+                pltpu.SemaphoreType.DMA((self.shards,)),
+                pltpu.SemaphoreType.DMA((self.shards,)),
+            ],
+            compiler_params=pltpu.CompilerParams(collective_id=2, has_side_effects=True),
+            cost_estimate=cost(55),
+            name="head",
+        )(hidden, mine, other, small)
+        return (
+            rows.reshape(-1, rows.shape[-1]),
+            first.reshape(-1, first.shape[-1]),
+            everyone,
+        )
+
+    def tail(self, g, g_x, g_bc, g_heads, g_gate, g_norm, d_normed):
+        rows, inner = g.shape[0] // self.shards, g_x.shape[1]
         if not self.fast:
-            return x
-        return jnp.concatenate(self.turned(jnp.split(x, 4, axis=-1)), axis=-1)
+            g = self.reduce_chips(g)
+            low = self.core == 0
+            kept, given = jnp.where(low, g[:rows], g[rows:]), jnp.where(low, g[rows:], g[:rows])
+            came = self.swap(given.astype(BF16), df=1).astype(F32)
+            total = self.reduce_members(
+                jnp.concatenate(
+                    list(self.by_core(kept[:, :inner], came[:, :inner]))
+                    + [kept[:, inner : inner + 2 * LANES] + came[:, inner : inner + 2 * LANES]]
+                    + list(self.by_core(kept[:, inner + 2 * LANES :], came[:, inner + 2 * LANES :])),
+                    axis=1,
+                )
+            )
+            wide = ((0, 0), (0, inner - 2 * LANES))
+            heads = g_heads.reshape(3, 8, LANES).sum(axis=1).reshape(1, -1)
+            vec = jnp.concatenate(
+                [
+                    g_x.reshape(5, 8, inner).sum(axis=1), g_gate, g_norm,
+                    jnp.pad(heads, ((0, 0), (0, inner - 3 * LANES))),
+                    jnp.pad(g_bc.reshape(5, 8, 2 * LANES).sum(axis=1), wide),
+                ]
+            )
+            vec = self.sum_all(jnp.pad(vec, ((0, 3), (0, 0))))
+            vec = jnp.stack(self.by_core(vec, self.swap(vec, df=1)))
+            cut = 2 * inner + 2 * LANES
+            d_rows = self.to_tokens(self.cores_sum(d_normed))
+            return total[:, : 2 * inner], total[:, 2 * inner : cut], total[:, cut:], vec, d_rows
+        width = g.shape[1]
+        half, whole = rows // 2, 2 * inner + 4 * LANES
+        vmem = pl.BlockSpec(memory_space=pltpu.VMEM)
+        vec = (16, inner)
+        return pl.pallas_call(
+            tail_kernel,
+            out_shape=[
+                jax.ShapeDtypeStruct((rows, 2 * inner), F32),
+                jax.ShapeDtypeStruct((rows, 2 * LANES), F32),
+                jax.ShapeDtypeStruct((rows, 2 * LANES), F32),
+                jax.ShapeDtypeStruct((2,) + vec, F32),
+                jax.ShapeDtypeStruct((self.batch, self.tokens, d_normed.shape[1]), BF16),
+            ],
+            in_specs=[vmem] * 7,
+            out_specs=[vmem] * 5,
+            scratch_shapes=[
+                pltpu.VMEM((self.units, 2, self.tokens, d_normed.shape[1]), BF16),
+                pltpu.VMEM((self.units, 2, self.tokens, d_normed.shape[1]), BF16),
+                pltpu.SemaphoreType.DMA((1,)),
+                pltpu.VMEM((2, 2 * rows, width), BF16),
+                pltpu.VMEM((2 * rows, width), BF16),
+                pltpu.VMEM((2 * rows, width), BF16),
+                pltpu.VMEM((rows, width), BF16),
+                pltpu.VMEM((rows, width), BF16),
+                pltpu.VMEM((rows, whole), F32),
+            ]
+            + [pltpu.VMEM((half, whole), BF16)] * 6
+            + [pltpu.VMEM((4,) + vec, F32)] * 2
+            + [pltpu.SemaphoreType.DMA((7 * len(PIECES) + 4,))] * 2
+            + [pltpu.SemaphoreType.DMA((5,))] * 2,
+            compiler_params=pltpu.CompilerParams(
+                collective_id=3, has_side_effects=True, vmem_limit_bytes=VMEM_LIMIT
+            ),
+            cost_estimate=cost(90),
+            name="tail",
+        )(
+            g, g_x, g_bc, g_heads, g_gate, g_norm,
+            d_normed.reshape(self.units, 2, 2, self.tokens, d_normed.shape[1]),
+        )
 
     def gather(self, x):
-        if not self.fast:
-            groups = [list(range(c, self.shards, 2)) for c in range(2)]
-            return lax.all_gather(x, "fs", axis=0, tiled=True, axis_index_groups=groups)
-        half = x.shape[0] // 2
-        by_x, by_y = self.swap(x, df=2), self.swap(x, df=4)
-        top, bottom = self.swap(by_x[:half], df=4), self.swap(by_y[half:], df=2)
-        return jnp.concatenate([x, by_x, by_y, top, bottom], axis=0)
+        groups = [list(range(c, self.shards, 2)) for c in range(2)]
+        return lax.all_gather(x, "fs", axis=0, tiled=True, axis_index_groups=groups)
 
     def reduce_chips(self, g):
-        if not self.fast:
-            groups = [list(range(c, self.shards, 2)) for c in range(2)]
-            return lax.psum_scatter(
-                g.astype(BF16), "fs", scatter_dimension=0, tiled=True, axis_index_groups=groups
-            ).astype(F32)
-        rows, width = g.shape[0] // 4, g.shape[1]
-        cut = -(-width // (2 * LANES)) * LANES
-        blocks = [g[i * rows : (i + 1) * rows] for i in range(4)]
-        left, right = [b[:, :cut] for b in blocks], [b[:, cut:] for b in blocks]
-        sent_left = self.swap(jnp.concatenate([left[1], left[3]], axis=0).astype(BF16), df=2)
-        sent_right = self.swap(jnp.concatenate([right[2], right[3]], axis=0).astype(BF16), df=4)
-        next_left = self.swap((left[2] + sent_left[rows:]).astype(BF16), df=4)
-        next_right = self.swap((right[1] + sent_right[rows:]).astype(BF16), df=2)
-        return jnp.concatenate(
-            [left[0] + sent_left[:rows] + next_left, right[0] + sent_right[:rows] + next_right], axis=1
-        )
+        groups = [list(range(c, self.shards, 2)) for c in range(2)]
+        return lax.psum_scatter(
+            g, "fs", scatter_dimension=0, tiled=True, axis_index_groups=groups
+        ).astype(F32)
 
     def reduce_members(self, g):
-        if not self.fast:
-            return lax.psum(g.astype(BF16), "sp").astype(F32)
-        half = g.shape[0] // 2
-        first = self.z % 2 == 0
-        kept, given = jnp.where(first, g[:half], g[half:]), jnp.where(first, g[half:], g[:half])
-        kept = kept + self.swap(given.astype(BF16), dz=1)
-        low = kept.astype(BF16)
-        kept = (low.astype(F32) + self.swap(low, dz=2)).astype(BF16)
-        other = self.swap(kept, dz=1)
-        return jnp.concatenate(
-            [jnp.where(first, kept, other), jnp.where(first, other, kept)], axis=0
-        ).astype(F32)
+        return lax.psum(g.astype(BF16), "sp").astype(F32)
+
+    def traded(self, x, far):
+        pairs = [
+            (self.at(f, z), self.at(f - f % 2 + z % 2, ((z // 2) ^ far) * 2 + f % 2))
+            for f in range(self.shards)
+            for z in range(self.members)
+        ]
+        return self.send(x, pairs)
 
     def to_units(self, rows):
-        half = rows.shape[-1] // 2
-        left, right = rows[..., :half], rows[..., half:]
-        first = self.core == 0
-        mine = jnp.where(first, left, right)
-        other = self.swap(jnp.where(first, right, left), df=1)
-        both = jnp.stack(self.by_core(mine, other))
+        units, width = self.units, rows.shape[-1]
         if self.fast:
-            parts = [both[t % 2, (t // 2) * self.units : (t // 2 + 1) * self.units] for t in range(4)]
-            parts = self.across(parts)
-            block = jnp.stack(parts, axis=1)
+            low, high = rows[:units], rows[units:]
+            upper = self.z // 2 == 1
+            far = self.traded(jnp.where(upper, low, high), 1)
+            near = self.traded(jnp.where(upper, high, low), 0)
+            mine = jnp.stack([jnp.where(upper, far, near), jnp.where(upper, near, far)], axis=1)
+            pair = self.by_core(mine, self.swap(mine, df=1))
+            block = jnp.stack(pair, axis=2)
         else:
-            everything = lax.all_gather(both, "sp")
+            other = self.swap(rows, df=1)
+            everything = lax.all_gather(jnp.stack(self.by_core(rows, other)), "sp")
             per_core = self.joints // 2
             block = lax.dynamic_slice(
                 everything,
-                ((self.joint % per_core) * 4, self.joint // per_core, self.group * self.units, 0, 0),
-                (4, 1, self.units) + both.shape[2:],
+                ((self.joint % per_core) * 4, self.joint // per_core, self.group * units, 0, 0),
+                (4, 1, units) + rows.shape[1:],
             )[:, 0]
             block = jnp.moveaxis(block, 0, 1)
-        block = block.reshape(self.units * 4 * self.tokens, half)
-        pair = self.by_core(block, self.swap(block, df=1))
-        return jnp.concatenate(pair, axis=1)
-
-    def across(self, parts):
-        low, high = (self.z % 2) == 1, (self.z // 2) == 1
-        a, b, c, d = parts
-        a, b = jnp.where(low, b, a), jnp.where(low, a, b)
-        c, d = jnp.where(low, d, c), jnp.where(low, c, d)
-        a, b, c, d = (
-            jnp.where(high, c, a),
-            jnp.where(high, d, b),
-            jnp.where(high, a, c),
-            jnp.where(high, b, d),
-        )
-        d, c, b = self.swap(d, dz=3), self.swap(c, dz=2), self.swap(b, dz=1)
-        a, b = jnp.where(low, b, a), jnp.where(low, a, b)
-        c, d = jnp.where(low, d, c), jnp.where(low, c, d)
-        return [
-            jnp.where(high, c, a),
-            jnp.where(high, d, b),
-            jnp.where(high, a, c),
-            jnp.where(high, b, d),
-        ]
-
-    def from_units(self, partial):
-        half = partial.shape[-1] // 2
+        return block.reshape(units * 4 * self.tokens, width)
+
+    def cores_sum(self, partial):
+        units, width = self.units, partial.shape[-1]
+        if self.fast:
+            block = partial.reshape(units, 2, 2, self.tokens, width)
+            even = self.core == 0
+            mine = jnp.where(even, block[:, :, 0], block[:, :, 1])
+            given = jnp.where(even, block[:, :, 1], block[:, :, 0]).astype(BF16)
+            return (mine.astype(F32) + self.swap(given, df=1).astype(F32)).astype(BF16)
+        return partial.astype(BF16).reshape(units, 4, self.tokens, width)
+
+    def to_tokens(self, total):
+        units, width = self.units, total.shape[-1]
+        if self.fast:
+            upper = self.z // 2 == 1
+            far = self.traded(jnp.where(upper, total[:, 0], total[:, 1]), 1)
+            near = self.traded(jnp.where(upper, total[:, 1], total[:, 0]), 0)
+            return jnp.concatenate(
+                [jnp.where(upper, far, near), jnp.where(upper, near, far)], axis=0
+            )
+        per_core = self.joints // 2
+        block = total
+        wide = jnp.zeros((self.members, 2, self.batch, self.tokens, width), BF16)
+        wide = lax.dynamic_update_slice(
+            wide,
+            jnp.moveaxis(block, 1, 0)[:, None],
+            ((self.joint % per_core) * 4, self.joint // per_core, self.group * units, 0, 0),
+        )
+        summed = lax.psum_scatter(wide, "sp", scatter_dimension=0, tiled=False)
         first = self.core == 0
-        left, right = partial[:, :half], partial[:, half:]
-        mine = jnp.where(first, left, right)
-        total = (mine + self.swap(jnp.where(first, right, left).astype(BF16), df=1)).astype(BF16)
-        block = total.reshape(self.units, 4, self.tokens, half)
-        if self.fast:
-            parts = self.across([block[:, t] for t in range(4)])
-            both = [jnp.concatenate([parts[c], parts[2 + c]], axis=0) for c in range(2)]
-        else:
-            per_core = self.joints // 2
-            wide = jnp.zeros((self.members, 2, self.batch, self.tokens, half), BF16)
-            wide = lax.dynamic_update_slice(
-                wide,
-                jnp.moveaxis(block, 1, 0)[:, None],
-                ((self.joint % per_core) * 4, self.joint // per_core, self.group * self.units, 0, 0),
-            )
-            summed = lax.psum_scatter(wide, "sp", scatter_dimension=0, tiled=False)
-            both = [summed[0], summed[1]]
-        mine, other = jnp.where(first, both[0], both[1]), jnp.where(first, both[1], both[0])
-        return jnp.concatenate(self.by_core(mine, self.swap(other, df=1)), axis=-1)
+        mine, given = jnp.where(first, summed[0], summed[1]), jnp.where(first, summed[1], summed[0])
+        return (mine.astype(F32) + self.swap(given, df=1).astype(F32)).astype(BF16)
 
     def sum_all(self, x):
         if not self.fast:
@@ -639,6 +1127,10 @@
 
 def whole_spec(shape):
     return pl.BlockSpec(shape, lambda u, c: (0,) * len(shape))
+
+
+def cost(microseconds):
+    return pl.CostEstimate(flops=int(microseconds * 1.15e9), bytes_accessed=0, transcendentals=0)
 
 
 def params():
@@ -684,6 +1176,7 @@
         compiler_params=pltpu.CompilerParams(
             collective_id=1 if back else 0, has_side_effects=True, vmem_limit_bytes=VMEM_LIMIT
         ),
+        cost_estimate=cost(35),
         name="states_back" if back else "states",
     )(own, decays)
     return (outs[0], decays) if back else (outs[0], outs[1])
@@ -707,19 +1200,13 @@
         half = w.shape[1] // 2
         return jnp.where(core == 0, w[:, :half], w[:, half:]), jnp.where(core == 0, w[:, half:], w[:, :half])
 
-    small = [conv_x, conv_x_bias, conv_bc, conv_bc_bias, dt_bias, a_log, skip_d, gate_gain, norm_gain]
-    flat = jnp.concatenate([part.reshape(-1) for part in small])
+    misc = jnp.concatenate([conv_bc_bias, dt_bias, a_log, skip_d])
+    flat = jnp.concatenate(
+        [conv_x.T.reshape(-1), conv_x_bias, gate_gain, norm_gain, conv_bc.T.reshape(-1), misc]
+    )
     length = flat.shape[0]
-    padded = -(-length // LANES) * LANES
+    padded = -(-length // (16 * LANES)) * 16 * LANES
     flat = jnp.pad(flat, (0, padded - length)).reshape(padded // LANES, LANES)
-    everyone = lax.all_gather(flat, "fs").reshape(plan.shards, padded)
-    gathered, start = [], 0
-    for part in small:
-        gathered.append(
-            everyone[:, start : start + part.size].reshape((-1,) + part.shape[1:]).astype(F32)
-        )
-        start += part.size
-    taps_x, bias_x, taps_bc, bias_bc, shift, rate_log, skip, gain_out, gain_in = gathered
 
     x_mine, x_other = halves(w_x)
     dt_mine, dt_other = halves(w_dt)
@@ -732,31 +1219,52 @@
     def rows_of_chip(mine, other):
         return jnp.concatenate(plan.by_core(mine, plan.swap(other, df=1)), axis=0)
 
-    weight_first = plan.gather(rows_of_chip(first_mine, first_other))
-    weight_gate = plan.gather(rows_of_chip(z_mine, z_other))
-    weight_out = plan.gather(rows_of_chip(o_mine, o_other))
+    rows_gate, rows_out = rows_of_chip(z_mine, z_other), rows_of_chip(o_mine, o_other)
+    weight_gate, weight_out = plan.gather(rows_gate), plan.gather(rows_out)
+    hidden_rows, weight_first, everyone = plan.head(hidden, first_mine, first_other, flat)
+    everyone = everyone.reshape(plan.shards, padded).astype(F32)
+
+    parts, start = [], 0
+    for shape in (
+        conv_x.shape[::-1], conv_x_bias.shape, gate_gain.shape, norm_gain.shape, conv_bc.shape[::-1],
+        conv_bc_bias.shape, dt_bias.shape, a_log.shape, skip_d.shape,
+    ):
+        size = shape[0] * (shape[1] if len(shape) > 1 else 1)
+        parts.append(everyone[:, start : start + size].reshape((plan.shards,) + shape))
+        start += size
+    taps_x, bias_x, gain_out, gain_in, taps_bc, bias_bc, shift, rate_log, skip = parts
+    gain_in = gain_in.reshape(-1)
 
     def mine_of(v):
         half = v.shape[0] // 2
         return lax.dynamic_slice_in_dim(v, core * half, half, 0)
 
-    gain_in_turned = plan.turn(gain_in[None])
-    taps_x, bias_x, gain_out, skip_mine = (mine_of(v) for v in (taps_x, bias_x, gain_out, skip))
-    shift, rate_log = mine_of(shift), mine_of(rate_log)
+    def flat_taps(v):
+        return jnp.moveaxis(v, 0, 1).reshape(v.shape[1], -1)
+
+    bias_x, gain_out, skip_mine = (mine_of(v).reshape(-1) for v in (bias_x, gain_out, skip))
+    shift, rate_log = mine_of(shift).reshape(-1), mine_of(rate_log).reshape(-1)
     cx = jnp.concatenate(
-        [taps_x.T, bias_x[None], jnp.repeat(skip_mine, head_size)[None], jnp.zeros((2, inner), F32)]
+        [
+            flat_taps(mine_of(taps_x)), bias_x[None],
+            jnp.repeat(skip_mine, head_size)[None], jnp.zeros((2, inner), F32),
+        ]
     )
-    cbc = jnp.concatenate([taps_bc.T, bias_bc[None], jnp.zeros((3, taps_bc.shape[0]), F32)])
+    cbc = jnp.concatenate(
+        [flat_taps(taps_bc), bias_bc.reshape(1, -1), jnp.zeros((3, bias_bc.size), F32)]
+    )
     pad_heads = (0, LANES - heads)
     rate = jnp.pad(jnp.exp(rate_log), pad_heads)
     hp = jnp.concatenate([rate[None], jnp.zeros((7, LANES), F32)])
     pick = (jnp.arange(inner)[:, None] // head_size == jnp.arange(LANES)[None, :]).astype(BF16)
 
-    hidden_rows = plan.to_units(plan.turn(hidden)).astype(F32)
+    hidden_rows, cot_late = lax.optimization_barrier((hidden_rows, cotangent))
+    cot_rows = plan.to_units(cot_late)
+
+    hidden_rows = hidden_rows.astype(F32)
     scale_in = row_scale(hidden_rows)
     unit_in = hidden_rows * scale_in
-    normed = (unit_in * gain_in_turned).astype(BF16)
-    cot_rows = plan.to_units(plan.turn(cotangent))
+    normed = (unit_in * gain_in[None]).astype(BF16)
 
     first = dot(normed, weight_first).astype(BF16)
     dt_shifted = first[:, inner + 2 * LANES :].astype(F32) + jnp.pad(shift, pad_heads)[None]
@@ -794,6 +1302,7 @@
             pltpu.VMEM(states, F32), pltpu.VMEM((8, LANES), F32),
         ],
         compiler_params=params(),
+        cost_estimate=cost(31),
         name="scan_forward",
     )(first, tail_x, first, tail_bc, step, cx, cbc, hp)
 
@@ -810,6 +1319,7 @@
         out_specs=[rows_spec(inner), rows_spec(inner), rows_spec(LANES)],
         out_shape=[shaped(rows, inner), shaped(rows, inner), shaped(rows, LANES, dtype=F32)],
         compiler_params=params(),
+        cost_estimate=cost(14),
         name="gate_forward",
     )(y_own, gate_in, shared, reach, incoming)
 
@@ -820,9 +1330,10 @@
     scale_out = lax.rsqrt(squares / (2 * inner) + EPSILON).reshape(rows, 1)
     unit_out = gated.astype(F32) * scale_out
     normed_out = (unit_out * gain_out[None]).astype(BF16)
-    projected = plan.from_units(dot_nt(normed_out, weight_out))
-    output = (hidden.astype(F32) + plan.turn(projected).astype(F32)).astype(BF16)
-
+    projected = plan.cores_sum(dot_nt(normed_out, weight_out))
+
+    g_out = dot_tn(cot_rows, normed_out).astype(BF16)
+    g_out, weight_out, cot_rows = lax.optimization_barrier((g_out, weight_out, cot_rows))
     d_normed_out = dot(cot_rows, weight_out).astype(BF16)
     wide = d_normed_out.astype(F32)
     g_gate_gain = jnp.sum(wide * unit_out, axis=0)
@@ -842,43 +1353,78 @@
         out_shape=[shaped(rows, inner), shaped(rows, inner), shaped(units, *states)],
         scratch_shapes=[pltpu.VMEM(states, F32)],
         compiler_params=params(),
+        cost_estimate=cost(19),
         name="gate_backward",
     )(d_normed_out, gated, gate_in, y, stats, gain_rows, shared, reach)
 
+    def both_halves(g):
+        half = g.shape[0] // 2
+        first_core = core == 0
+        mine = jnp.where(first_core, g[:half], g[half:])
+        other = jnp.where(first_core, g[half:], g[:half]).astype(BF16)
+        return mine, plan.swap(other, df=1)
+
+    g_z = dot_tn(normed, d_gate).astype(BF16)
+    pull, g_z, g_out = lax.optimization_barrier((pull, g_z, plan.reduce_chips(g_out)))
     after, _ = exchange(plan, pull, all_decays, True)
+    after, projected, g_z, g_out = lax.optimization_barrier((after, projected, plan.reduce_chips(g_z), g_out))
+    g_out_mine, g_out_other = both_halves(g_out)
+    g_out = jnp.concatenate(plan.by_core(g_out_mine, g_out_other), axis=1).astype(BF16)
+    total_out = lax.psum(g_out, "sp")
+    g_z_mine, g_z_other = both_halves(g_z)
+    g_z = jnp.concatenate(plan.by_core(g_z_mine, g_z_other), axis=1).astype(BF16)
 
     back = functools.partial(rows_spec, back=True)
     width = inner + 3 * LANES
-    d_all, heads_x, heads_bc, g_x, g_bc, g_heads = pl.pallas_call(
-        backward_kernel,
-        grid=(units, PER_UNIT),
-        in_specs=[
-            back(inner), chunk_spec((8, inner), True),
-            back(2 * LANES, inner // (2 * LANES)), chunk_spec((8, 2 * LANES), True),
-            back(LANES), back(LANES), whole_spec(cx.shape), whole_spec(cbc.shape), whole_spec(hp.shape),
-            back(inner), back(inner), chunk_spec(states, True), unit_spec(states), back(LANES),
-            unit_spec(states), whole_spec(pick.shape),
-        ],
-        out_specs=[
-            back(width), unit_spec((8, inner)), unit_spec((8, 2 * LANES)),
-            whole_spec((40, inner)), whole_spec((40, 2 * LANES)), whole_spec((24, LANES)),
-        ],
-        out_shape=[
-            shaped(rows, width), shaped(units, 8, inner, dtype=F32), shaped(units, 8, 2 * LANES, dtype=F32),
-            shaped(40, inner, dtype=F32), shaped(40, 2 * LANES, dtype=F32), shaped(24, LANES, dtype=F32),
-        ],
-        scratch_shapes=[
-            pltpu.VMEM((CHUNK + 8, inner), F32), pltpu.VMEM((CHUNK + 8, 2 * LANES), F32),
-            pltpu.VMEM(states, F32),
-            pltpu.VMEM((CHUNK + 8, inner), F32), pltpu.VMEM((CHUNK + 8, 2 * LANES), F32),
-            pltpu.VMEM((8, inner), F32),
-        ],
-        compiler_params=params(),
-        name="scan_backward",
-    )(
+    anywhere = pl.BlockSpec(memory_space=pl.ANY)
+    in_specs = [
+        back(inner), chunk_spec((8, inner), True),
+        back(2 * LANES, inner // (2 * LANES)), chunk_spec((8, 2 * LANES), True),
+        back(LANES), back(LANES), whole_spec(cx.shape), whole_spec(cbc.shape), whole_spec(hp.shape),
+        back(inner), back(inner), chunk_spec(states, True), unit_spec(states), back(LANES),
+        unit_spec(states), whole_spec(pick.shape),
+    ]
+    out_specs = [
+        back(width), unit_spec((8, inner)), unit_spec((8, 2 * LANES)),
+        whole_spec((40, inner)), whole_spec((40, 2 * LANES)), whole_spec((24, LANES)),
+    ]
+    out_shape = [
+        shaped(rows, width), shaped(units, 8, inner, dtype=F32), shaped(units, 8, 2 * LANES, dtype=F32),
+        shaped(40, inner, dtype=F32), shaped(40, 2 * LANES, dtype=F32), shaped(24, LANES, dtype=F32),
+    ]
+    scratch = [
+        pltpu.VMEM((CHUNK + 8, inner), F32), pltpu.VMEM((CHUNK + 8, 2 * LANES), F32),
+        pltpu.VMEM(states, F32),
+        pltpu.VMEM((CHUNK + 8, inner), F32), pltpu.VMEM((CHUNK + 8, 2 * LANES), F32),
+        pltpu.VMEM((8, inner), F32),
+    ]
+    operands = [
         first, tail_x, first, tail_bc, step, slope_dt, cx, cbc, hp,
         dy, y, starts, incoming, reach, after, pick,
-    )
+    ]
+    sending = params()
+    if plan.fast:
+        in_specs, operands = in_specs + [anywhere], operands + [projected]
+        out_specs, out_shape = out_specs + [anywhere], out_shape + [shaped(batch, tokens, model)]
+        scratch = scratch + [
+            pltpu.SemaphoreType.DMA((1,)), pltpu.SemaphoreType.DMA((2,)), pltpu.SemaphoreType.DMA((2,)),
+        ]
+        sending = pltpu.CompilerParams(
+            dimension_semantics=("arbitrary", "arbitrary"), vmem_limit_bytes=VMEM_LIMIT,
+            collective_id=4, has_side_effects=True,
+        )
+    d_all, heads_x, heads_bc, g_x, g_bc, g_heads, *sent = pl.pallas_call(
+        backward_sending_kernel if plan.fast else backward_kernel,
+        grid=(units, PER_UNIT),
+        in_specs=in_specs,
+        out_specs=out_specs,
+        out_shape=out_shape,
+        scratch_shapes=scratch,
+        compiler_params=sending,
+        cost_estimate=cost(70),
+        name="scan_backward",
+    )(*operands)
+    projected = sent[0] if plan.fast else plan.to_tokens(projected)
 
     later = plan.along(jnp.concatenate([heads_x, heads_bc], axis=2)[:, :3].astype(BF16), -1).astype(F32)
     taps = jnp.concatenate([cx[:4], cbc[:4]], axis=1)
@@ -891,22 +1437,16 @@
     d_all = lax.dynamic_update_slice(d_all, (tail_rows + extra).astype(BF16), (0, 4 * tokens - 16, 0))
     d_all = d_all.reshape(rows, width)
 
+    total_z = lax.psum(g_z, "sp")
+    output = (hidden.astype(F32) + projected.astype(F32)).astype(BF16)
+    g_first = dot_tn(normed, d_all).astype(BF16)
     d_normed = dot_nt(d_gate, weight_gate) + dot_nt(d_all, weight_first)
     g_norm_gain = jnp.sum(d_normed * unit_in, axis=0)
 
-    def both_halves(g):
-        half = g.shape[0] // 2
-        first_core = core == 0
-        mine = jnp.where(first_core, g[:half], g[half:])
-        other = jnp.where(first_core, g[half:], g[:half]).astype(BF16)
-        return mine, plan.swap(other, df=1)
-
-    g_out_mine, g_out_other = both_halves(plan.reduce_chips(dot_tn(cot_rows, normed_out)))
-    total_out = plan.reduce_members(jnp.concatenate(plan.by_core(g_out_mine, g_out_other), axis=1))
-    g_z_mine, g_z_other = both_halves(plan.reduce_chips(dot_tn(normed, d_gate)))
-    total_z = plan.reduce_members(jnp.concatenate(plan.by_core(g_z_mine, g_z_other), axis=1))
-
-    grad_rows = plan.turn(plan.from_units(d_normed)).astype(F32)
+    total_x, total_bc, total_dt, vec, grad_rows = plan.tail(
+        g_first, g_x, g_bc, g_heads, g_gate_gain[None], g_norm_gain[None], d_normed.astype(BF16)
+    )
+    grad_rows = grad_rows.astype(F32)
     resid = hidden.astype(F32)
     own_scale = row_scale(resid)
     own_unit = resid * own_scale
@@ -915,47 +1455,12 @@
         dv - own_unit * jnp.mean(dv * own_unit, axis=-1, keepdims=True)
     )
 
-    g_mine, g_other = both_halves(plan.reduce_chips(dot_tn(normed, d_all)))
-    x_parts = plan.by_core(g_mine[:, :inner], g_other[:, :inner].astype(F32))
-    bc_sum = g_mine[:, inner : inner + 2 * LANES] + g_other[:, inner : inner + 2 * LANES]
-    dt_parts = plan.by_core(
-        g_mine[:, inner + 2 * LANES : inner + 2 * LANES + heads],
-        g_other[:, inner + 2 * LANES : inner + 2 * LANES + heads].astype(F32),
-    )
-    total = plan.reduce_members(
-        jnp.concatenate(
-            list(x_parts) + [bc_sum] + list(dt_parts) + [jnp.zeros((bc_sum.shape[0], LANES - 2 * heads), F32)],
-            axis=1,
-        )
-    )
-    total_x = total[:, : 2 * inner]
-    total_bc = total[:, 2 * inner : 2 * inner + 2 * LANES]
-    total_dt = total[:, 2 * inner + 2 * LANES : 2 * inner + 2 * LANES + 2 * heads]
-
-    own_x = g_x.reshape(5, 8, inner).sum(axis=1)
-    own_bc = g_bc.reshape(5, 8, 2 * LANES).sum(axis=1)
-    own_heads = g_heads.reshape(3, 8, LANES).sum(axis=1)[:, :heads]
-    norm_gain_sum = plan.turn(g_norm_gain[None])[0]
-    half_parts = [own_x, g_gate_gain[None], own_heads]
-    sum_parts = [norm_gain_sum, own_bc]
-    vector = jnp.concatenate([v.reshape(-1) for v in half_parts + sum_parts])
-    size = -(-vector.shape[0] // 1024) * 1024
-    vector = jnp.pad(vector, (0, size - vector.shape[0])).reshape(-1, LANES)
-    vector = plan.sum_all(vector)
-    lower, upper = (v.reshape(-1) for v in plan.by_core(vector, plan.swap(vector, df=1)))
-
-    def pieces(v):
-        found, start = [], 0
-        for part in half_parts + sum_parts:
-            found.append(v[start : start + part.size].reshape(part.shape))
-            start += part.size
-        return found
-
-    low_parts, high_parts = pieces(lower), pieces(upper)
-    whole_x, whole_gain, whole_heads = (
-        jnp.concatenate([a, b], axis=1) for a, b in zip(low_parts[:3], high_parts[:3])
-    )
-    whole_norm, whole_bc = (a + b for a, b in zip(low_parts[3:], high_parts[3:]))
+    total_dt = jnp.concatenate([total_dt[:, :heads], total_dt[:, LANES : LANES + heads]], axis=1)
+    whole_x = jnp.moveaxis(vec[:, :6], 0, 1).reshape(6, 2 * inner)
+    whole_heads = jnp.moveaxis(vec[:, 7, : 3 * LANES].reshape(2, 3, LANES)[:, :, :heads], 0, 1)
+    whole_heads = whole_heads.reshape(3, 2 * heads)
+    whole_norm = vec[0, 6] + vec[1, 6]
+    whole_bc = vec[0, 8:13, : 2 * LANES] + vec[1, 8:13, : 2 * LANES]
 
     def shard(v):
         share = v.shape[-1] // plan.shards
@@ -966,11 +1471,11 @@
         output,
         grad_hidden,
         shard(whole_norm),
-        total_z,
+        total_z.astype(F32),
         total_x,
         total_bc,
         total_dt,
-        total_out,
+        total_out.astype(F32),
         shard_x[:4].T,
         shard_x[4],
         shard_bc[:4].T,
@@ -978,7 +1483,7 @@
         shard_heads[0],
         shard_heads[1],
         shard_heads[2],
-        shard(whole_gain)[0],
+        shard_x[5],
     )
 
 

time: 1010 us -> 798 us (0.79)
  waiting for transfers between devices: 340 us -> 118 us
  Pallas kernels: 210 us -> 408 us
  starting transfers between devices: 133 us -> 19.8 us
  other arithmetic: 115 us -> 63 us
  local copies, waits for them, and re-layouts: 72.5 us -> 48 us
  between operations: 2.79 us -> 14.7 us
  blocking collectives: 10.4 us -> 0 us
    ppermute x68 -> x12, waiting for transfers between devices: 340 us -> 6.24 us  [send(): return lax.ppermute(x, ('fs', 'sp'), pairs)]
    pallas_call x1 -> x3, Pallas kernels: 70.8 us -> 247 us  [the longest x1 108 us: tail(): pl.pallas_call(tail_kernel, out_shape=[jax.ShapeDtypeStruct((rows, 2 * in...]
    ppermute x68 -> x12, starting transfers between devices: 133 us -> 19 us  [send(): return lax.ppermute(x, ('fs', 'sp'), pairs)]
    psum x0 -> x1, waiting for transfers between devices: none -> 81 us  [body(): total_z = lax.psum(g_z, 'sp')]
    pallas_call x2, Pallas kernels: 75.2 us -> 95.8 us  [exchange(): pl.pallas_call(kernel, out_shape=out_shape, in_specs=[vmem, vmem], out_sp...]
    reduce_scatter x0 -> x2, waiting for transfers between devices: none -> 19.2 us  [reduce_chips(): lax.psum_scatter(g, 'fs', scatter_dimension=0, tiled=True, axis_index_gro...]
    convert_element_type x25 -> x4, other arithmetic: 27.6 us -> 15.4 us  [the longest x1 7.65 us: cores_sum(): return (mine.astype(F32) + self.swap(given, df=1).astype(F32)).astype(BF16)]
    select_n x20 -> x1, other arithmetic: 13.7 us -> 1.56 us  [to_units(): far = self.traded(jnp.where(upper, low, high), 1)]
  transfers between devices with their start and end apart: 68 -> 17, of which waited for: 29 -> 8; matrix products, arithmetic and copies ran while one was open for 25% -> 26% of each run, Pallas kernels for 21% -> 42%
where the time goes in v2:
time: 798 us; the launch traced here: 788 us
  Pallas kernels  408 us (51%)
  waiting for transfers between devices  118 us (15%)
  matrix products  117 us (15%)
  other arithmetic  63 us (8%)
  local copies, waits for them, and re-layouts  48 us (6%)
  starting transfers between devices  19.8 us (2%)
  between operations  14.7 us (2%)
    pallas_call x1, Pallas kernels, tail(): pl.pallas_call(tail_kernel, out_shape=[jax.ShapeDtypeStruct((rows, 2 * in...  108 us
    pallas_call x2, Pallas kernels, exchange(): pl.pallas_call(kernel, out_shape=out_shape, in_specs=[vmem, vmem], out_sp...  95.8 us
    psum x1, waiting for transfers between devices, body(): total_z = lax.psum(g_z, 'sp')  81 us
    pallas_call x1, Pallas kernels, body(): pl.pallas_call(backward_sending_kernel if plan.fast else backward_kernel,...  75.4 us
    pallas_call x1, Pallas kernels, head(): pl.pallas_call(head_kernel, out_shape=[jax.ShapeDtypeStruct((self.units,...  63.8 us
    dot_general x3, matrix products, dot_nt(): lax.dot_general(a, b, (((1,), (1,)), ((), ())), preferred_element_type=F32)  41.4 us
    dot_general x3, matrix products, dot(): return jnp.dot(a, b, preferred_element_type=F32)  40.2 us
    dot_general x3, matrix products, dot_tn(): lax.dot_general(a, b, (((0,), (0,)), ((), ())), preferred_element_type=F32)  35.9 us
  transfers between devices with their start and end apart: 17, of which 8 were waited for; matrix products, arithmetic and copies ran while one was open for 26% of the time, Pallas kernels for 42%

profile of v2, /device:TPU:0, one launch (start us, length us, event | category | flops | bytes accessed | tf_op | source)
XLA Modules:
  0.0 788.3 jit_solution(17785595711298193389)
XLA Ops:
  7.2 2.1 broadcast_select_fusion.4
  9.8 2.1 broadcast_select_fusion.8
  13.5 4.8 concatenate.53
  19.8 1.3 broadcast_select_fusion.10
  23.3 63.8 %head.1 = (bf16[3,4,128,1536]{3,2,1,0:T(8,128)(2,1)}, bf16[4,2,192,1920]{3,2,1,0:T(8,128)(2,1)}, bf16[8,32,128]{2,1,0:T(8,128)(2,1)}) custom-call(bf16[6,128,1536]{2,1,0:T(8,128)(2,1)} %hidden.1, bf16[192,1920]{1,0:T(8,128)(2,1)} %concatenate.51.mine, bf16[192,1920]{1,0:T(8,128)(2,1)} %concatenate.52.other, bf16[32,128]{1,0:T(8,128)(2,1)} %pad_bitcast_fusion.small), custom_call_target="tpu_custom_call" | custom-call | flops 63250001920 | tf_op jit(solution)/shard_map/head/pallas_call | solution.py:927
  87.1 1.6 broadcast_select_fusion.1
  88.7 2.4 collective-permute-start.1
  91.1 10.3 %collective-permute-start.2 = (bf16[3,128,1536]{2,1,0:T(8,128)(2,1)}, bf16[3,128,1536]{2,1,0:T(8,128)(2,1)}, u32[]{:S(2)}, u32[]{:S(2)}) collective-permute-start(bf16[3,128,1536]{2,1,0:T(8,128)(2,1)} %get-tuple-element.166), channel_id=1, source_target_pairs={{0,0},{1,4},{2,2},{3,6},{4,1},{5,5},{6,3},{7,7},{8,8},{9,12},{10,1... | collective-permute-start | bytes 3538952 | tf_op jit(solution)/shard_map/ppermute | solution.py:896
  102.7 13.8 %convolution_convert_fusion.1.x_ref.bc_ref.refs_0_.refs_2_ = bf16[1536,1920]{1,0:T(8,128)(2,1)S(1)} fusion(bf16[1536,1920]{1,0:T(8,128)(2,1)} %bitcast.170, bf16[1536,1536]{1,0:T(8,128)(2,1)} %bitcast.132, f32[1536]{0:T(1024)S(1)} %mul.163, f32[1536]{0:T(1024)S(1)} %add_rsqrt_fusion.1), kind=kOutput, calls=%fused_computation.16 | convolution fusion | flops 9072082944 | bytes 16527360 | tf_op jit(solution)/shard_map/dot_general | solution.py:20
  116.9 2.1 copy-done.8
  119.0 1.4 collective-permute-start
  122.2 2.7 add_divide_fusion
  130.5 30.9 %scan_forward.1 = (bf16[1536,1536]{1,0:T(8,128)(2,1)}, bf16[12,128,1536]{2,1,0:T(8,128)(2,1)}, bf16[3,128,1536]{2,1,0:T(8,128)(2,1)}, f32[3,8,1536]{2,1,0:T(8,12...) custom-call(bf16[1536,1920]{1,0:T(8,128)(2,1)} %copy-done.8, f32[12,8,1536]{2,1,0:T(8,128)} %slice.274.xp_ref.refs_1_, ...), custom_call_target="tpu_custom_call" | custom-call | flops 35649998848 | tf_op jit(solution)/shard_map/scan_forward/pallas_call | solution.py:1284
  163.1 1.6 select_bitcast_fusion.3
  164.6 1.6 pad_maximum_fusion.1
  166.3 1.7 collective-permute-start.3
  168.0 53.7 %states.1 = (bf16[3,128,1536]{2,1,0:T(8,128)(2,1)}, f32[8,8,1536]{2,1,0:T(8,128)}) custom-call(bf16[3,128,1536]{2,1,0:T(8,128)(2,1)} %get-tuple-element.65.own_ref, f32[8,1536]{1,0:T(8,128)} %concatenate.59.dec_ref), custom_call_target="tpu_custom_call" | custom-call | flops 40249999360 | tf_op jit(solution)/shard_map/states/pallas_call | solution.py:1170
  221.7 1.2 broadcast_select_fusion.3
  224.1 4.2 select_bitcast_fusion.1
  228.2 12.9 %convolution_convert_fusion.5.gate_ref = bf16[1536,1536]{1,0:T(8,128)(2,1)} fusion(bf16[1536,1536]{1,0:T(8,128)(2,1)} %all-gather.3.cloned.1.call-done, bf16[1536,1536]{1,0:T(8,128)(2,1)} %bitcast.133, f32[1536]{0:T(1024)S(1)} %mul.163, f32[1536]{0:T(1024)S(1)} %copy-done.29), kind=kOutput, calls=%fused_computation.20 | convolution fusion | flops 7259553792 | bytes 14168064 | tf_op jit(solution)/shard_map/dot_general | solution.py:20
  241.2 14.6 %gate_forward.1 = (bf16[1536,1536]{1,0:T(8,128)(2,1)}, bf16[1536,1536]{1,0:T(8,128)(2,1)}, f32[1536,128]{1,0:T(8,128)}) custom-call(bf16[1536,1536]{1,0:T(8,128)(2,1)} %get-tuple-element.62.y0_ref, bf16[1536,1536]{1,0:T(8,128)(2,1)} %convolution_convert_fusion.5.gate_ref, bf16[1536,256]{1,0:T(8,128)(2,1)} %get-tuple-element.63.bcs_ref, ...), custom_call_target="tpu_custom_call" | custom-call | flops 16099999744 | tf_op jit(solution)/shard_map/gate_forward/pallas_call | solution.py:1313
  255.8 1.6 slice_reduce_fusion
  258.6 1.5 copy-done.15
  260.1 9.7 %convolution_convert_fusion.4 = bf16[1536,1536]{1,0:T(8,128)(2,1)} fusion(bf16[1536,1536]{1,0:T(8,128)(2,1)S(1)} %bitcast.142, bf16[1536,1536]{1,0:T(8,128)(2,1)S(1)} %bitcast.174, f32[1536]{0:T(1024)S(1)} %mul.170, f32[1536]{0:T(1024)S(1)} %get-tuple-element.196), kind=kOutput, calls=%fused_computation.19 | convolution fusion | flops 7259553792 | bytes 14168064 | tf_op jit(solution)/shard_map/dot_general | solution.py:28
  269.8 11.0 %all-gather.5.cloned.1.call-done = bf16[1536,1536]{1,0:T(8,128)(2,1)} async-done(((bf16[384,1536]{1,0:T(8,128)(2,1)}), bf16[1536,1536]{1,0:T(8,128)(2,1)}) %all-gather.5.cloned.1.call-update) | async-done | bytes 4718608 | tf_op jit(solution)/shard_map/all_gather | solution.py:1024
  281.1 13.5 %fusion.7 = (f32[1536]{0:T(1024)S(1)}, f32[1536]{0:T(1024)S(1)}, bf16[1536,1536]{1,0:T(8,128)(2,1)}) fusion(bf16[1536,1536]{1,0:T(8,128)(2,1)} %get-tuple-element.68.gated_ref, f32[1536]{0:T(1024)S(1)} %get-tuple-element.196, f32[1536]{0:T(1024)S(1)} %mul.170, bf16[1536,1536]{1,0:T(8,128)(2,1)} %bitcast.143, bf16[1536,1536]{1,0:T(8,128)(2,1)} %all-gather.5.cloned.1.call-done), kind=kOutput, calls=%fused_computation.11 | convolution fusion | flops 7268987904 | bytes 18898944 | tf_op jit(solution)/shard_map/dot_general | solution.py:20
  297.9 19.4 %gate_backward.1 = (bf16[1536,1536]{1,0:T(8,128)(2,1)}, bf16[1536,1536]{1,0:T(8,128)(2,1)}, bf16[3,128,1536]{2,1,0:T(8,128)(2,1)}) custom-call(bf16[1536,1536]{1,0:T(8,128)(2,1)} %get-tuple-element.200.dno_ref, bf16[1536,1536]{1,0:T(8,128)(2,1)} %get-tuple-element.68.gated_ref, bf16[1536,1536]{1,0:T(8,128)(2,1)} %convolution_convert_fusion.5.gate_ref, ...), custom_call_target="tpu_custom_call" | custom-call | flops 21849999360 | tf_op jit(solution)/shard_map/gate_backward/pallas_call | solution.py:1345
  317.3 12.1 %convolution_convert_fusion.2 = bf16[1536,1536]{1,0:T(8,128)(2,1)} fusion(bf16[1536,1536]{1,0:T(8,128)(2,1)} %get-tuple-element.76, bf16[1536,1536]{1,0:T(8,128)(2,1)S(1)} %bitcast.138, f32[1536]{0:T(1024)S(1)} %mul.163, f32[1536]{0:T(1024)S(1)} %copy-done.29), kind=kOutput, calls=%fused_computation.17 | convolution fusion | flops 7259553792 | bytes 14168064 | tf_op jit(solution)/shard_map/dot_general | solution.py:28
  329.4 11.5 %reduce-scatter.3.cloned.1.call-done = bf16[384,1536]{1,0:T(8,128)(2,1)} async-done(((bf16[1536,1536]{1,0:T(8,128)(2,1)}), bf16[384,1536]{1,0:T(8,128)(2,1)}) %reduce-scatter.3.cloned.1.call-update) | async-done | bytes 1179664 | tf_op jit(solution)/shard_map/reduce_scatter | solution.py:1028
  341.3 11.0 %fusion.18 = f32[1536,1536]{1,0:T(8,128)S(1)} fusion(bf16[1536,1536]{1,0:T(8,128)(2,1)} %all-gather.5.cloned.1.call-done, bf16[1536,1536]{1,0:T(8,128)(2,1)} %get-tuple-element.68.gated_ref, f32[1536]{0:T(1024)S(1)} %mul.170, f32[1536]{0:T(1024)S(1)} %get-tuple-element.196), kind=kOutput, calls=%fused_computation.48 | convolution fusion | flops 7257194496 | bytes 18886656 | tf_op jit(solution)/shard_map/dot_general | solution.py:24
  352.4 4.0 copy-done.2
  356.3 1.8 fusion.17
  361.0 2.0 collective-permute-done.8
  363.0 7.7 fusion.16.refs_16_
  370.7 42.1 %states_back.1.refs_14_ = bf16[3,128,1536]{2,1,0:T(8,128)(2,1)} custom-call(bf16[3,128,1536]{2,1,0:T(8,128)(2,1)} %get-tuple-element.78.own_ref, f32[8,8,1536]{2,1,0:T(8,128)} %get-tuple-element.79.dec_ref), custom_call_target="tpu_custom_call" | custom-call | flops 40249999360 | tf_op jit(solution)/shard_map/states_back/pallas_call | solution.py:1170
  412.8 7.7 reduce-scatter.5.cloned.1.call-done
  420.5 75.4 %scan_backward.1 = (bf16[1536,1920]{1,0:T(8,128)(2,1)}, f32[3,8,1536]{2,1,0:T(8,128)}, f32[3,8,256]{2,1,0:T(8,128)}, f32[40,1536]{1,0:T(8,128)}, f32[40,256]{1,0...) custom-call(bf16[1536,1920]{1,0:T(8,128)(2,1)} %copy-done.8, f32[12,8,1536]{2,1,0:T(8,128)} %slice.274.xp_ref.refs_1_, ...), custom_call_target="tpu_custom_call" | custom-call | flops 80499998720 | tf_op jit(solution)/shard_map/scan_backward/pallas_call | solution.py:1416
  497.6 1.3 collective-permute-start.9
  501.1 2.7 collective-permute-done.9
  503.9 1.7 fusion.26
  505.7 16.1 %fusion.47 = f32[1536,1536]{1,0:T(8,128)} fusion(bf16[1536,1920]{1,0:T(8,128)(2,1)} %bitcast.165, bf16[1536,1920]{1,0:T(8,128)(2,1)} %bitcast.171), kind=kOutput, calls=%fused_computation.158 | convolution fusion | flops 9059696640 | bytes 21233664 | tf_op jit(solution)/shard_map/dot_general | solution.py:24
  521.7 14.1 %convolution_convert_fusion.g = bf16[1536,1920]{1,0:T(8,128)(2,1)} fusion(bf16[1536,1920]{1,0:T(8,128)(2,1)S(1)} %bitcast.166, bf16[1536,1536]{1,0:T(8,128)(2,1)} %bitcast.134, f32[1536]{0:T(1024)S(1)} %copy-done.22, f32[1536]{0:T(1024)S(1)} %copy-done.30), kind=kOutput, calls=%fused_computation.15 | convolution fusion | flops 9072082944 | bytes 16527360 | tf_op jit(solution)/shard_map/dot_general | solution.py:28
  535.8 14.3 %fusion.40 = (bf16[1536,1536]{1,0:T(8,128)(2,1)}, f32[1536]{0:T(1024)S(1)}) fusion(f32[1536]{0:T(1024)S(1)} %copy-done.30, bf16[1536,1536]{1,0:T(8,128)(2,1)S(1)} %bitcast.141, f32[1536,1536]{1,0:T(8,128)} %fusion.47, bf16[1536,1536]{1,0:T(8,128)(2,1)} %get-tuple-element.76, bf16[1536,1536]{1,0:T(8,128)(2,1)} %all-gather.3.cloned.1.call-done), kind=kOutput, calls=%fused_computation.151 | convolution fusion | flops 7261911552 | bytes 28323840 | tf_op jit(solution)/shard_map/dot_general | solution.py:24
  550.7 107.7 %tail.1 = (f32[192,3072]{1,0:T(8,128)}, f32[192,256]{1,0:T(8,128)}, f32[192,256]{1,0:T(8,128)}, f32[2,16,1536]{2,1,0:T(8,128)}, bf16[6,128,1536]{2,1,0:T(8,128)(2,1)}) custom-call(bf16[1536,1920]{1,0:T(8,128)(2,1)} %convolution_convert_fusion.g, f32[40,1536]{1,0:T(8,128)} %get-tuple-element.88.g_x, f32[40,256]{1,0:T(8,128)} %get-tuple-element.89.g_bc, ...), custom_call_target="tpu_custom_call" | custom-call | flops 103499997184 | tf_op jit(solution)/shard_map/tail/pallas_call | solution.py:986
  658.4 1.4 slice_reduce_fusion.4
  659.9 1.3 fusion.41
  661.2 1.5 slice.256
  662.7 1.3 reshape_squeeze.7
  665.3 1.3 reshape.243
  667.6 1.3 dynamic-slice_bitcast_fusion.1
  668.9 1.4 dynamic-slice_add_fusion
  670.2 1.3 constant_dynamic-slice_fusion.1
  672.3 1.4 fusion.43
  675.2 1.3 fusion.19
  677.7 1.3 fusion.35
  679.1 1.6 copy.63
  680.7 1.5 dynamic-slice_reduce_fusion
  682.2 1.3 slice_bitcast_fusion.6
  684.6 2.7 fusion.10
  687.4 5.2 fusion.13
  692.6 81.0 %all-reduce.9.cloned.1.call-done = (bf16[192,3072]{1,0:T(8,128)(2,1)}, bf16[192,3072]{1,0:T(8,128)(2,1)}) async-done(((bf16[192,3072]{1,0:T(8,128)(2,1)}, bf16[192,3072]{1,0:T(8,128)(2,1)}), (bf16[192,3072]{1,0:T(8,128)(2,1)}, bf16[192,3072]{1,0:T(8,128)(2,1)})) %all-reduce.9.cloned.1.call-update) | async-done | bytes 2359312 | tf_op jit(solution)/shard_map/psum | solution.py:1440
  773.6 2.9 convert_element_type.164
  776.5 3.0 convert_element_type.167
  779.5 1.4 copy.90
  (202 shorter events, 37.0 us)
Async XLA Ops:
  7.2 14.0 %copy-start.17 = (bf16[192,256]{1,0:T(8,128)(2,1)S(1)}, bf16[192,256]{1,0:T(8,128)(2,1)}, u32[]{:S(2)}) copy-start(bf16[192,256]{1,0:T(8,128)(2,1)} %param.20) | copy-start | bytes 294916
  7.2 221.0 %all-gather.3.cloned.1.call-start = ((), (), s32[]{:S(2)}) async-start(), calls=%async_computation.2 | async-start | bytes 5898240 | tf_op jit(solution)/shard_map/all_gather | solution.py:1024
  9.4 212.3 %collective-permute-start.6 = (bf16[192,1536]{1,0:T(8,128)(2,1)}, bf16[192,1536]{1,0:T(8,128)(2,1)}, u32[]{:S(2)}, u32[]{:S(2)}) collective-permute-start(bf16[192,1536]{1,0:T(8,128)(2,1)} %broadcast_select_fusion.4), channel_id=1, source_target_pairs={{0,4},{1,5},{2,6},{3,7},{4,0},{5,1},{6,2},{7,3},{8,12},{9,13},{10,... | collective-permute-start | bytes 1769480 | tf_op jit(solution)/shard_map/ppermute | solution.py:896
  11.9 116.0 %collective-permute-start.4 = (bf16[192,1536]{1,0:T(8,128)(2,1)}, bf16[192,1536]{1,0:T(8,128)(2,1)}, u32[]{:S(2)}, u32[]{:S(2)}) collective-permute-start(bf16[192,1536]{1,0:T(8,128)(2,1)} %broadcast_select_fusion.8), channel_id=1, source_target_pairs={{0,4},{1,5},{2,6},{3,7},{4,0},{5,1},{6,2},{7,3},{8,12},{9,13},{10,... | collective-permute-start | bytes 1769480 | tf_op jit(solution)/shard_map/ppermute | solution.py:896
  23.3 63.8 %copy-start.3 = (bf16[6,128,1536]{2,1,0:T(8,128)(2,1)S(1)}, bf16[6,128,1536]{2,1,0:T(8,128)(2,1)}, u32[]{:S(2)}) copy-start(bf16[6,128,1536]{2,1,0:T(8,128)(2,1)} %param.31) | copy-start | bytes 7077892
  87.1 14.4 %copy-start.14 = (bf16[3,4,128,1536]{3,2,1,0:T(8,128)(2,1)S(1)}, bf16[3,4,128,1536]{3,2,1,0:T(8,128)(2,1)}, u32[]{:S(2)}) copy-start(bf16[3,4,128,1536]{3,2,1,0:T(8,128)(2,1)} %get-tuple-element.57) | copy-start | bytes 14155780
  87.1 15.4 %copy-start.23 = (bf16[8,32,128]{2,1,0:T(8,128)(2,1)S(1)}, bf16[8,32,128]{2,1,0:T(8,128)(2,1)}, u32[]{:S(2)}) copy-start(bf16[8,32,128]{2,1,0:T(8,128)(2,1)} %get-tuple-element.59) | copy-start | bytes 196612
  88.7 74.4 %collective-permute-start.1 = (bf16[3,128,1536]{2,1,0:T(8,128)(2,1)}, bf16[3,128,1536]{2,1,0:T(8,128)(2,1)S(1)}, u32[]{:S(2)}, u32[]{:S(2)}) collective-permute-start(bf16[3,128,1536]{2,1,0:T(8,128)(2,1)} %get-tuple-element.165), channel_id=1, source_target_pairs={{0,2},{1,6},{2,0},{3,4},{4,3},{5,7},{6,1},{7,5},{8,10},{9,14},{10,... | collective-permute-start | bytes 3538952 | tf_op jit(solution)/shard_map/ppermute | solution.py:896
  91.1 71.9 %collective-permute-start.2 = (bf16[3,128,1536]{2,1,0:T(8,128)(2,1)}, bf16[3,128,1536]{2,1,0:T(8,128)(2,1)}, u32[]{:S(2)}, u32[]{:S(2)}) collective-permute-start(bf16[3,128,1536]{2,1,0:T(8,128)(2,1)} %get-tuple-element.166), channel_id=1, source_target_pairs={{0,0},{1,4},{2,2},{3,6},{4,1},{5,5},{6,3},{7,7},{8,8},{9,12},{10,1... | collective-permute-start | bytes 3538952 | tf_op jit(solution)/shard_map/ppermute | solution.py:896
  102.5 14.0 %copy-start.28 = (f32[1536]{0:T(1024)}, f32[1536]{0:T(1024)S(1)}, u32[]{:S(2)}) copy-start(f32[1536]{0:T(1024)S(1)} %add_rsqrt_fusion.1) | copy-start | bytes 18436
  102.7 214.6 %copy-start.21 = (f32[1536]{0:T(1024)}, f32[1536]{0:T(1024)S(1)}, u32[]{:S(2)}) copy-start(f32[1536]{0:T(1024)S(1)} %mul.163) | copy-start | bytes 18436
  116.5 2.5 copy-start.8
  119.0 9.0 %copy-start.9 = (bf16[192,3072]{1,0:T(8,128)(2,1)S(1)}, bf16[192,3072]{1,0:T(8,128)(2,1)}, u32[]{:S(2)}) copy-start(bf16[192,3072]{1,0:T(8,128)(2,1)} %param.18) | copy-start | bytes 3538948
  119.0 7.3 collective-permute-start
  121.1 9.1 %copy-start.25 = (f32[4,256]{1,0:T(4,128)}, f32[4,256]{1,0:T(4,128)S(1)}, u32[]{:S(2)}) copy-start(f32[4,256]{1,0:T(4,128)S(1)} %reshape.232) | copy-start | bytes 12292
  122.2 8.1 %copy-start.18 = (f32[1,4,4,384]{3,1,2,0:T(4,128)}, f32[1,4,4,384]{3,1,2,0:T(4,128)S(1)}, u32[]{:S(2)}) copy-start(f32[1,4,4,384]{3,1,2,0:T(4,128)S(1)} %copy.70) | copy-start | bytes 73732
  130.3 150.6 %all-gather.5.cloned.1.call-start = ((), (), s32[]{:S(2)}) async-start(), calls=%async_computation.3 | async-start | bytes 5898240 | tf_op jit(solution)/shard_map/all_gather | solution.py:1024
  166.3 57.8 %collective-permute-start.3 = (bf16[3,2,128,1536]{3,2,1,0:T(8,128)(2,1)}, bf16[3,2,128,1536]{3,2,1,0:T(8,128)(2,1)}, u32[]{:S(2)}, u32[]{:S(2)}) collective-permute-start(bf16[3,2,128,1536]{3,2,1,0:T(8,128)(2,1)} %pad_maximum_fusion.1), channel_id=1, source_target_pairs={{0,4},{1,5},{2,6},{3,7},{4,0},{5,1},{6,2},{7,3},{8,12},{9,13},{10,... | collective-permute-start | bytes 7077896 | tf_op jit(solution)/shard_map/ppermute | solution.py:896
  167.9 53.7 %copy-start.10 = (bf16[192,3072]{1,0:T(8,128)(2,1)S(1)}, bf16[192,3072]{1,0:T(8,128)(2,1)}, u32[]{:S(2)}) copy-start(bf16[192,3072]{1,0:T(8,128)(2,1)} %param.22) | copy-start | bytes 3538948
  224.0 4.2 copy-start.29
  224.0 117.0 %reduce-scatter.3.cloned.1.call-start = ((), (), s32[]{:S(2)}) async-start(), calls=%async_computation.4 | async-start | bytes 5898240 | tf_op jit(solution)/shard_map/reduce_scatter | solution.py:1028
  241.2 16.2 %copy-start.6 = (bf16[3,2,1,128,1536]{4,3,2,1,0:T(8,128)(2,1)S(1)}, bf16[3,2,1,128,1536]{4,3,2,1,0:T(8,128)(2,1)}, u32[]{:S(2)}) copy-start(bf16[3,2,1,128,1536]{4,3,2,1,0:T(8,128)(2,1)} %get-tuple-element.159) | copy-start | bytes 7077892
  241.2 16.2 %copy-start.7 = (bf16[3,2,1,128,1536]{4,3,2,1,0:T(8,128)(2,1)S(1)}, bf16[3,2,1,128,1536]{4,3,2,1,0:T(8,128)(2,1)}, u32[]{:S(2)}) copy-start(bf16[3,2,1,128,1536]{4,3,2,1,0:T(8,128)(2,1)} %get-tuple-element.160) | copy-start | bytes 7077892
  255.8 4.3 slice-start.4
  257.3 1.2 collective-permute-start.5
  257.4 2.6 slice-start.5
  257.9 2.2 copy-start.15
  280.9 139.6 %reduce-scatter.5.cloned.1.call-start = ((), (), s32[]{:S(2)}) async-start(), calls=%async_computation.5 | async-start | bytes 5898240 | tf_op jit(solution)/shard_map/reduce_scatter | solution.py:1028
  281.1 36.2 %slice-start = ((s8[4718592]{0:T(1024)(128)(4,1)}), s8[524288]{0:T(1024)(128)(4,1)S(1)}, s32[]{:S(2)}) async-start(s8[4718592]{0:T(1024)(128)(4,1)} %bitcast.136), calls=%async_computation.7 | async-start | bytes 1048576
  294.6 1.2 collective-permute-start.7
  297.9 19.5 %slice-start.1 = ((s8[4718592]{0:T(1024)(128)(4,1)}), s8[4194304]{0:T(1024)(128)(4,1)S(1)}, s32[]{:S(2)}) async-start(s8[4718592]{0:T(1024)(128)(4,1)} %bitcast.136), calls=%async_computation.8 | async-start | bytes 8388608
  341.0 432.6 %all-reduce.9.cloned.1.call-start = ((), (), s32[]{:S(2)}) async-start(), calls=%async_computation.6 | async-start | bytes 4718592 | tf_op jit(solution)/shard_map/psum | solution.py:1440
  352.3 4.0 copy-start.2
  352.3 5.8 copy-start.19
  352.3 5.8 copy-start.26
  352.3 5.9 copy-start
  358.1 4.9 collective-permute-start.8
  420.4 78.4 %copy-start.12 = (bf16[384,1536]{1,0:T(8,128)(2,1)S(1)}, bf16[384,1536]{1,0:T(8,128)(2,1)}, u32[]{:S(2)}) copy-start(bf16[384,1536]{1,0:T(8,128)(2,1)} %reduce-scatter.5.cloned.1.call-done) | copy-start | bytes 3538948
  420.5 79.3 %copy-start.11 = (bf16[384,1536]{1,0:T(8,128)(2,1)S(1)}, bf16[384,1536]{1,0:T(8,128)(2,1)}, u32[]{:S(2)}) copy-start(bf16[384,1536]{1,0:T(8,128)(2,1)} %reduce-scatter.3.cloned.1.call-done) | copy-start | bytes 3538948
  497.6 6.3 collective-permute-start.9
  498.9 36.9 %slice-start.2 = ((s8[4718592]{0:T(1024)(128)(4,1)}), s8[4194304]{0:T(1024)(128)(4,1)S(1)}, s32[]{:S(2)}) async-start(s8[4718592]{0:T(1024)(128)(4,1)} %bitcast.139), calls=%async_computation.9 | async-start | bytes 8388608
  499.8 173.9 %collective-permute-start.11 = (bf16[192,1536]{1,0:T(8,128)(2,1)S(1)}, bf16[192,1536]{1,0:T(8,128)(2,1)S(1)}, u32[]{:S(2)}, u32[]{:S(2)}) collective-permute-start(bf16[192,1536]{1,0:T(8,128)(2,1)S(1)} %select_convert_fusion.1), channel_id=1, source_target_pairs={{0,4},{1,5},{2,6},{3,7},{4,0},{5,1},{6,2},{7,3},{8,12},{9,13},{10,... | collective-permute-start | bytes 1769480 | tf_op jit(solution)/shard_map/ppermute | solution.py:896
  501.0 174.2 %collective-permute-start.10 = (bf16[192,1536]{1,0:T(8,128)(2,1)}, bf16[192,1536]{1,0:T(8,128)(2,1)}, u32[]{:S(2)}, u32[]{:S(2)}) collective-permute-start(bf16[192,1536]{1,0:T(8,128)(2,1)} %select_convert_fusion.2), channel_id=1, source_target_pairs={{0,4},{1,5},{2,6},{3,7},{4,0},{5,1},{6,2},{7,3},{8,12},{9,13},{10,... | collective-permute-start | bytes 1769480 | tf_op jit(solution)/shard_map/ppermute | solution.py:896
  505.7 16.1 %copy-start.22 = (f32[1536]{0:T(1024)S(1)}, f32[1536]{0:T(1024)}, u32[]{:S(2)}) copy-start(f32[1536]{0:T(1024)} %copy-done.21) | copy-start | bytes 18436
  505.7 16.1 %copy-start.30 = (f32[1536]{0:T(1024)S(1)}, f32[1536]{0:T(1024)}, u32[]{:S(2)}) copy-start(f32[1536]{0:T(1024)} %copy-done.28) | copy-start | bytes 18436
  505.7 16.1 %copy-start.31 = (bf16[3,512,1920]{2,1,0:T(8,128)(2,1)S(1)}, bf16[3,512,1920]{2,1,0:T(8,128)(2,1)}, u32[]{:S(2)}) copy-start(bf16[3,512,1920]{2,1,0:T(8,128)(2,1)} %fusion.26) | copy-start | bytes 17694724
  505.7 30.2 %slice-start.3 = ((s8[4718592]{0:T(1024)(128)(4,1)}), s8[524288]{0:T(1024)(128)(4,1)S(1)}, s32[]{:S(2)}) async-start(s8[4718592]{0:T(1024)(128)(4,1)} %bitcast.139), calls=%async_computation.10 | async-start | bytes 1048576
  658.4 16.8 %copy-start.13 = (bf16[384,1536]{1,0:T(8,128)(2,1)S(1)}, bf16[384,1536]{1,0:T(8,128)(2,1)}, u32[]{:S(2)}) copy-start(bf16[384,1536]{1,0:T(8,128)(2,1)} %reduce-scatter.5.cloned.1.call-done) | copy-start | bytes 3538948
  674.0 9.5 %copy-start.27 = (f32[1,5,32]{2,1,0:T(8,128)S(1)}, f32[1,5,32]{2,1,0:T(8,128)}, u32[]{:S(2)}) copy-start(f32[1,5,32]{2,1,0:T(8,128)} %dynamic-slice_add_fusion) | copy-start | bytes 1924
  674.0 10.6 %copy-start.1 = (bf16[6,128,1536]{2,1,0:T(8,128)(2,1)S(1)}, bf16[6,128,1536]{2,1,0:T(8,128)(2,1)}, u32[]{:S(2)}) copy-start(bf16[6,128,1536]{2,1,0:T(8,128)(2,1)} %hidden.1) | copy-start | bytes 7077892
  674.1 10.6 %copy-start.24 = (f32[6,128]{1,0:T(8,128)S(1)}, f32[6,128]{1,0:T(8,128)}, u32[]{:S(2)}) copy-start(f32[6,128]{1,0:T(8,128)} %add_rsqrt_fusion.2) | copy-start | bytes 9220
  680.7 6.7 copy-start.4
  680.7 6.7 copy-start.5
  692.6 86.9 %copy-start.16 = (f32[192,3072]{1,0:T(8,128)S(1)}, f32[192,3072]{1,0:T(8,128)}, u32[]{:S(2)}) copy-start(f32[192,3072]{1,0:T(8,128)} %get-tuple-element.223) | copy-start | bytes 7077892
  776.5 4.4 copy-start.20
Sparse Core Ops, SparseCore 0:
  130.4 89.2 all-gather.2
  224.1 56.6 all-gather.4
  283.8 57.1 reduce-scatter.2
  343.8 76.5 reduce-scatter.4
  677.8 95.6 all-reduce.8

commit v3 on v2

--- a/solution.py
+++ b/solution.py
@@ -162,9 +162,9 @@
 def pull_kernel(
     dno_ref, gated_ref, gate_ref, y_ref, stats_ref, gain_ref, bcs_ref, acum_ref,
     dy_ref, dgate_ref, pull_ref,
-    total,
+    total, chunk=None,
 ):
-    chunk = pl.program_id(1)
+    chunk = pl.program_id(1) if chunk is None else chunk
 
     @pl.when(chunk == 0)
     def _():
@@ -199,9 +199,9 @@
     x_ref, xp_ref, bc_ref, bcp_ref, step_ref, sig_ref, cx_ref, cbc_ref, hp_ref,
     dy_ref, y_ref, st_ref, in_ref, acum_ref, after_ref, pick_ref,
     dall_ref, head_ref, head_bc_ref, gx_ref, gbc_ref, gh_ref,
-    xe, be, adjoint, dpx, dpb, ends,
+    xe, be, adjoint, dpx, dpb, ends, place=None,
 ):
-    unit, chunk = pl.program_id(0), pl.program_id(1)
+    unit, chunk = (pl.program_id(0), pl.program_id(1)) if place is None else place
     inner = x_ref.shape[1]
 
     @pl.when((unit == 0) & (chunk == 0))
@@ -571,31 +571,186 @@
     keep_small.wait()
 
 
-PIECES = ((0, 512, "x"), (1024, 512, "y"), (512, 512, "x"), (1536, 384, "y"))
+class Reduction:
+    def __init__(self, pieces, sends, receives, base, special=None):
+        self.f, self.z, self.core, self.chip, self.by_x, self.by_y = places()
+        self.corner, self.bit = (self.by_x + 2) % 4, self.z % 2
+        self.sends, self.receives, self.base, self.special = sends, receives, base, special
+        self.pieces, z_start = [], 0
+        for n, (start, width, way) in enumerate(pieces):
+            wide = width + LANES if start == special else 2 * width
+            self.pieces.append((n, start, width, way, z_start, wide))
+            z_start += wide
+        self.wide = z_start
+        self.partner = (self.f + 1 - 2 * self.core, self.z)
+        self.over = {"x": (2 * self.by_x + self.core, self.z), "y": (2 * self.by_y + self.core, self.z)}
+        self.near, self.far = (self.f, self.z + 1 - 2 * self.bit), (self.f, (self.z + 2) % 4)
+
+    @staticmethod
+    def at(i, size):
+        return pl.ds(pl.multiple_of(i * size, size), size)
+
+    def copy(self, src, dst, n, k, device):
+        return remote(src, dst, self.sends, self.receives, self.base + 7 * n + k, device)
+
+    def over_chips(self, source, own, passed, r1, s2, r2, sp, rp, total):
+        self.source, self.own, self.passed = source, own, passed
+        self.r1, self.s2, self.r2, self.sp, self.rp, self.total = r1, s2, r2, sp, rp, total
+        self.rows = r2.shape[0]
+
+    def first_copies(self, piece):
+        n, start, width, way, _, _ = piece
+        columns = pl.ds(start, width)
+        to = self.by_x if way == "x" else self.by_y
+        return [
+            self.copy(self.source(i, columns), self.r1.at[k, :, columns], n, k, self.over[way])
+            for k, i in enumerate((to, self.corner))
+        ]
+
+    def second_copy(self, piece):
+        n, start, width, way, _, _ = piece
+        columns = pl.ds(start, width)
+        other = "y" if way == "x" else "x"
+        return self.copy(self.s2.at[:, columns], self.r2.at[:, columns], n, 2, self.over[other])
+
+    def pair_copy(self, piece):
+        n, start, width, _, _, _ = piece
+        columns = pl.ds(start, width)
+        return self.copy(self.sp.at[:, columns], self.rp.at[:, columns], n, 3, self.partner)
+
+    def start(self):
+        for piece in self.pieces:
+            for copy in self.first_copies(piece):
+                copy.start()
+
+    def after_first(self, piece):
+        _, start, width, way, _, _ = piece
+        if self.source is not None:
+            for copy in self.first_copies(piece):
+                copy.wait_recv()
+        columns = pl.ds(start, width)
+        passed = self.passed(self.by_y if way == "x" else self.by_x, columns)
+        self.s2[:, columns] = (passed.astype(F32) + self.r1[1, :, columns].astype(F32)).astype(BF16)
+        self.second_copy(piece).start()
+
+    def chip_sum(self, piece, side):
+        columns = pl.ds(piece[1], piece[2])
+        there = self.at(side, self.rows // 2)
+        own = self.own(side, columns).astype(F32)
+        return own + self.r1[0, there, columns].astype(F32) + self.r2[there, columns].astype(F32)
+
+    def lanes_at(self, start, side, width):
+        return pl.ds(pl.multiple_of(start + side * width, LANES), width)
+
+    def after_second(self, piece):
+        _, start, width, _, z_at, _ = piece
+        self.second_copy(piece).wait_recv()
+        self.sp[:, pl.ds(start, width)] = self.chip_sum(piece, 1 - self.core).astype(BF16)
+        self.pair_copy(piece).start()
+
+    def after_pair(self, piece):
+        _, start, width, _, z_at, _ = piece
+        self.pair_copy(piece).wait_recv()
+        own = self.chip_sum(piece, self.core)
+        came = self.rp[:, pl.ds(start, width)]
+        if start == self.special:
+            both = 2 * LANES
+            self.total[:, pl.ds(z_at, both)] = (own[:, :both] + came[:, :both].astype(F32)).astype(BF16)
+            self.total[:, self.lanes_at(z_at + both, self.core, LANES)] = own[:, both:].astype(BF16)
+            self.total[:, self.lanes_at(z_at + both, 1 - self.core, LANES)] = came[:, both:]
+        else:
+            self.total[:, self.lanes_at(z_at, self.core, width)] = own.astype(BF16)
+            self.total[:, self.lanes_at(z_at, 1 - self.core, width)] = came
+
+    def drain_chips(self):
+        for piece in self.pieces:
+            firsts = [] if self.source is None else self.first_copies(piece)
+            for copy in firsts + [self.second_copy(piece), self.pair_copy(piece)]:
+                copy.wait_send()
+
+    def over_members(self, total, came, sums, across, last, store):
+        self.total, self.store = total, store
+        self.came, self.sums, self.across, self.last = came, sums, across, last
+        self.half = total.shape[0] // 2
+
+    def z_copy(self, piece, k):
+        n, _, _, _, start, wide = piece
+        columns = pl.ds(start, wide)
+        src, dst, device = (
+            (self.total.at[self.at(1 - self.bit, self.half), columns], self.came, self.near),
+            (self.sums.at[0, :, columns], self.across, self.far),
+            (self.sums.at[1, :, columns], self.last, self.near),
+        )[k]
+        return self.copy(src, dst.at[:, columns], n, 4 + k, device)
+
+    def start_members(self, piece):
+        self.z_copy(piece, 0).start()
+
+    def after_near(self, piece):
+        columns = pl.ds(piece[4], piece[5])
+        self.z_copy(piece, 0).wait_recv()
+        own = self.total[self.at(self.bit, self.half), columns].astype(F32)
+        self.sums[0, :, columns] = (own + self.came[:, columns].astype(F32)).astype(BF16)
+        self.z_copy(piece, 1).start()
+
+    def after_far(self, piece):
+        columns = pl.ds(piece[4], piece[5])
+        self.z_copy(piece, 1).wait_recv()
+        total = self.sums[0, :, columns].astype(F32) + self.across[:, columns].astype(F32)
+        self.sums[1, :, columns] = total.astype(BF16)
+        self.z_copy(piece, 2).start()
+        self.store(piece, self.at(self.bit, self.half), total.astype(BF16).astype(F32))
+
+    def after_last(self, piece):
+        self.z_copy(piece, 2).wait_recv()
+        values = self.last[:, pl.ds(piece[4], piece[5])].astype(F32)
+        self.store(piece, self.at(1 - self.bit, self.half), values)
+
+    def drain_members(self):
+        for piece in self.pieces:
+            for k in range(3):
+                self.z_copy(piece, k).wait_send()
+
+
+def chip_scratch(rows, width):
+    return [
+        pltpu.VMEM((2, 2 * rows, width), BF16),
+        pltpu.VMEM((2 * rows, width), BF16),
+        pltpu.VMEM((2 * rows, width), BF16),
+        pltpu.VMEM((rows, width), BF16),
+        pltpu.VMEM((rows, width), BF16),
+    ]
+
+
+def member_scratch(rows, wide):
+    half = (rows // 2, wide)
+    return [
+        pltpu.VMEM(half, BF16), pltpu.VMEM((2,) + half, BF16),
+        pltpu.VMEM(half, BF16), pltpu.VMEM(half, BF16),
+    ]
+
+
+FIRST_PIECES = ((0, 512, "x"), (1024, 512, "y"), (512, 512, "x"), (1536, 384, "y"))
+HALF_PIECES = ((0, 768, "x"), (768, 768, "y"))
 
 
 def tail_kernel(
     g, g_x, g_bc, g_heads, g_gate, g_norm, d_part, out_x, out_bc, out_dt, vec_out, d_out,
-    d_came, d_sum, local, r1, s2, r2, sp, rp, total, z1s, z1r, z2s, z2r, z3s, z3r, vs, vr,
-    sends, receives, vec_sends, vec_receives,
+    d_came, d_sum, local, r1, s2, r2, sp, rp, total, came, sums, across, last,
+    vs, vr, sends, receives, vec_sends, vec_receives,
 ):
     f, z, core, chip, by_x, by_y = places()
-    corner = (by_x + 2) % 4
     rows = g.shape[0] // 4
-    half = rows // 2
-    quarter = half // 2
     inner = out_x.shape[1] // 2
-    bit = z % 2
-    partner = (f + 1 - 2 * core, z)
-    over = {"x": (2 * by_x + core, z), "y": (2 * by_y + core, z)}
-    near, far = (f, z + 1 - 2 * bit), (f, (z + 2) % 4)
-
-    upper, units = z // 2, d_part.shape[0]
+    bit, upper, units = z % 2, z // 2, d_part.shape[0]
+    first = Reduction(FIRST_PIECES, sends, receives, 0, inner)
+    slot = 7 * len(FIRST_PIECES)
+    partner, near, far = first.partner, first.near, first.far
     token_near, token_far = (2 * chip + bit, 2 * upper + core), (2 * chip + bit, 2 * (1 - upper) + core)
     stays = bit == core
 
     barrier = pltpu.get_barrier_semaphore()
-    for device in (partner, over["x"], over["y"], near, far, token_far):
+    for device in (partner, first.over["x"], first.over["y"], near, far, token_far):
         pl.semaphore_signal(barrier, inc=1, device_id=device, device_id_type=MESH)
 
     @pl.when(jnp.logical_not(stays))
@@ -603,8 +758,6 @@
         pl.semaphore_signal(barrier, inc=1, device_id=token_near, device_id_type=MESH)
 
     pl.semaphore_wait(barrier, 6 + (bit + core) % 2)
-
-    slot = 7 * len(PIECES)
 
     def d_pair(k, n):
         return remote(d_part.at[:, k, 1 - core], d_came.at[:, k], sends, receives, slot + n, partner)
@@ -622,8 +775,23 @@
     d_pair(upper, 1).start()
     d_keep = pltpu.make_async_copy(d_sum.at[:, upper], d_out.at[pl.ds(upper * units, units)], local.at[0])
 
-    def at(i, size):
-        return pl.ds(pl.multiple_of(i * size, size), size)
+    first.over_chips(
+        lambda i, columns: g.at[first.at(i, rows), columns],
+        lambda side, columns: g[pl.ds(pl.multiple_of(chip * rows + side * (rows // 2), rows // 2), rows // 2), columns],
+        lambda i, columns: g[first.at(i, rows), columns],
+        r1, s2, r2, sp, rp, total,
+    )
+
+    def store_first(piece, there, values):
+        _, start, width, _, _, _ = piece
+        if start == inner:
+            out_bc[there, :] = values[:, : 2 * LANES]
+            out_dt[there, :] = values[:, 2 * LANES :]
+        else:
+            out_x[there, pl.ds(start, width)] = values[:, :width]
+            out_x[there, pl.ds(inner + start, width)] = values[:, width:]
+
+    first.over_members(total, came, sums, across, last, store_first)
 
     vs[0] = jnp.zeros(vs.shape[1:], F32)
     for k in range(5):
@@ -635,116 +803,13 @@
         vs[0, 7:8, k * LANES : (k + 1) * LANES] = jnp.sum(
             g_heads[8 * k : 8 * k + 8], axis=0, keepdims=True
         )
-    vec_ways = [over["x"], over["y"], near, far]
+    vec_ways = [first.over["x"], first.over["y"], near, far]
 
     def vec_copy(k):
         return remote(vs.at[k], vr.at[k], vec_sends, vec_receives, k, vec_ways[k])
 
     def vec_last(side):
         return remote(vec_out.at[core], vec_out.at[side], vec_sends, vec_receives, 4, partner)
-
-    layout = []
-    z_start = 0
-    for n, (start, width, way) in enumerate(PIECES):
-        wide = 4 * LANES if start == inner else 2 * width
-        layout.append((n, start, width, way, "y" if way == "x" else "x", z_start, wide))
-        z_start += wide
-
-    def first_copies(piece):
-        n, start, width, way, _, _, _ = piece
-        columns = pl.ds(start, width)
-        to = by_x if way == "x" else by_y
-        return [
-            remote(g.at[at(i, rows), columns], r1.at[k, :, columns], sends, receives, 7 * n + k, over[way])
-            for k, i in enumerate((to, corner))
-        ]
-
-    def second_copy(piece):
-        n, start, width, _, other, _, _ = piece
-        columns = pl.ds(start, width)
-        return remote(s2.at[:, columns], r2.at[:, columns], sends, receives, 7 * n + 2, over[other])
-
-    def pair_copy(piece):
-        n, start, width, _, _, _, _ = piece
-        columns = pl.ds(start, width)
-        return remote(sp.at[:, columns], rp.at[:, columns], sends, receives, 7 * n + 3, partner)
-
-    def z_copy(piece, k):
-        n, _, _, _, _, start, wide = piece
-        columns = pl.ds(start, wide)
-        src, dst, device = ((z1s, z1r, near), (z2s, z2r, far), (z3s, z3r, near))[k]
-        return remote(src.at[:, columns], dst.at[:, columns], sends, receives, 7 * n + 4 + k, device)
-
-    def after_first(piece):
-        _, start, width, way, _, _, _ = piece
-        for copy in first_copies(piece):
-            copy.wait_recv()
-        columns = pl.ds(start, width)
-        to = by_y if way == "x" else by_x
-        s2[:, columns] = (g[at(to, rows), columns].astype(F32) + r1[1, :, columns].astype(F32)).astype(BF16)
-        second_copy(piece).start()
-
-    def chip_sum(piece, side):
-        _, start, width, _, _, _, _ = piece
-        columns = pl.ds(start, width)
-        own = g[pl.ds(pl.multiple_of(chip * rows + side * half, half), half), columns].astype(F32)
-        return own + r1[0, at(side, half), columns].astype(F32) + r2[at(side, half), columns].astype(F32)
-
-    def lanes_at(start, side, width):
-        return pl.ds(pl.multiple_of(start + side * width, LANES), width)
-
-    def after_second(piece):
-        _, start, width, _, _, z_at, _ = piece
-        second_copy(piece).wait_recv()
-        sp[:, pl.ds(start, width)] = chip_sum(piece, 1 - core).astype(BF16)
-        pair_copy(piece).start()
-        own = chip_sum(piece, core)
-        if start == inner:
-            total[:, pl.ds(z_at, 2 * LANES)] = own[:, : 2 * LANES]
-            total[:, lanes_at(z_at + 2 * LANES, core, LANES)] = own[:, 2 * LANES :]
-        else:
-            total[:, lanes_at(z_at, core, width)] = own
-
-    def after_pair(piece):
-        _, start, width, _, _, z_at, wide = piece
-        pair_copy(piece).wait_recv()
-        came = rp[:, pl.ds(start, width)].astype(F32)
-        if start == inner:
-            total[:, pl.ds(z_at, 2 * LANES)] += came[:, : 2 * LANES]
-            total[:, lanes_at(z_at + 2 * LANES, 1 - core, LANES)] = came[:, 2 * LANES :]
-        else:
-            total[:, lanes_at(z_at, 1 - core, width)] = came
-        columns = pl.ds(z_at, wide)
-        z1s[:, columns] = total[at(1 - bit, quarter), columns].astype(BF16)
-        z_copy(piece, 0).start()
-
-    def after_near(piece):
-        columns = pl.ds(piece[5], piece[6])
-        z_copy(piece, 0).wait_recv()
-        z2s[:, columns] = (total[at(bit, quarter), columns] + z1r[:, columns].astype(F32)).astype(BF16)
-        z_copy(piece, 1).start()
-
-    def store(piece, side, values):
-        _, start, width, _, _, _, _ = piece
-        there = at(side, quarter)
-        if start == inner:
-            out_bc[there, :] = values[:, : 2 * LANES]
-            out_dt[there, :] = values[:, 2 * LANES :]
-        else:
-            out_x[there, pl.ds(start, width)] = values[:, :width]
-            out_x[there, pl.ds(inner + start, width)] = values[:, width:]
-
-    def after_far(piece):
-        columns = pl.ds(piece[5], piece[6])
-        z_copy(piece, 1).wait_recv()
-        low = (z2s[:, columns].astype(F32) + z2r[:, columns].astype(F32)).astype(BF16)
-        z3s[:, columns] = low
-        z_copy(piece, 2).start()
-        store(piece, bit, low.astype(F32))
-
-    def after_last(piece):
-        z_copy(piece, 2).wait_recv()
-        store(piece, 1 - bit, z3r[:, pl.ds(piece[5], piece[6])].astype(F32))
 
     def vec_step(k):
         if k:
@@ -759,9 +824,7 @@
         else:
             vec_last(core).start()
 
-    for piece in layout:
-        for copy in first_copies(piece):
-            copy.start()
+    first.start()
     vec_step(0)
     d_pair(1 - upper, 0).wait_recv()
     d_add(1 - upper)
@@ -777,11 +840,18 @@
     def _():
         d_trade(upper, 1, token_near, upper).start()
 
-    early, late = layout[:2], layout[2:]
+    early, late = first.pieces[:2], first.pieces[2:]
+
+    def pair_on(piece):
+        first.after_pair(piece)
+        first.start_members(piece)
+
     order = (
-        (after_first, early), (1, ()), (after_first, late), (2, ()), (after_second, early), (3, ()),
-        (after_pair, early), (after_second, late), (4, ()), (after_near, early), (after_pair, late),
-        (after_far, early), (after_near, late), (after_last, early), (after_far, late), (after_last, late),
+        (first.after_first, early), (1, ()), (first.after_first, late), (2, ()),
+        (first.after_second, early), (3, ()), (pair_on, early), (first.after_second, late), (4, ()),
+        (first.after_near, early), (pair_on, late), (first.after_far, early),
+        (first.after_near, late), (first.after_last, early),
+        (first.after_far, late), (first.after_last, late),
     )
     for stage, pieces in order:
         if not pieces:
@@ -802,11 +872,8 @@
     d_trade(1 - upper, 0, token_far, upper).wait_send()
     d_pair(1 - upper, 0).wait_send()
     d_pair(upper, 1).wait_send()
-    for piece in layout:
-        for copy in first_copies(piece) + [second_copy(piece), pair_copy(piece)]:
-            copy.wait_send()
-        for k in range(3):
-            z_copy(piece, k).wait_send()
+    first.drain_chips()
+    first.drain_members()
     for k in range(4):
         vec_copy(k).wait_send()
     vec_last(core).wait_send()
@@ -825,14 +892,6 @@
     keep = pltpu.make_async_copy(source.at[:, upper], target.at[pl.ds(upper * units, units)], local.at[0])
 
     def start():
-        barrier = pltpu.get_barrier_semaphore()
-        pl.semaphore_signal(barrier, inc=1, device_id=far, device_id_type=MESH)
-
-        @pl.when(jnp.logical_not(stays))
-        def _():
-            pl.semaphore_signal(barrier, inc=1, device_id=near, device_id_type=MESH)
-
-        pl.semaphore_wait(barrier, 1 + (bit + core) % 2)
         copy(1 - upper, 0, far, upper).start()
 
         @pl.when(stays)
@@ -855,24 +914,223 @@
         def _():
             copy(upper, 1, near, upper).wait()
 
-    return start, finish
-
-
-def backward_sending_kernel(*refs):
-    inputs, source, outputs, target = refs[:16], refs[16], refs[17:23], refs[23]
-    scratch, sems = refs[24:30], refs[30:]
-    unit, chunk = pl.program_id(0), pl.program_id(1)
-    start, finish = trade_steps(source, target, *sems)
-
-    @pl.when((unit == 0) & (chunk == 0))
-    def _():
-        start()
-
-    backward_kernel(*inputs, *outputs, *scratch)
-
-    @pl.when((unit == pl.num_programs(0) - 1) & (chunk == PER_UNIT - 1))
-    def _():
-        finish()
+    return start, finish, far, near, stays
+
+
+class Segments:
+    def __init__(self):
+        self.f, self.z, self.core, self.chip, _, _ = places()
+        self.group = self.z // 2
+        self.me = self.chip * 2 + self.z % 2
+        self.count = 8
+
+    def peer(self, k):
+        other = (self.me + k) % self.count
+        return other, ((other // 2) * 2 + self.core, self.group * 2 + other % 2)
+
+
+def middle_kernel(
+    dno, gated, gate, y_pull, stats, gain, bcs, acum_pull, decays, normed, g_out, came_left, came_right, projected,
+    x, xp, bc, bcp, step, sig, cx, cbc, hp, y, st, incoming, acum, pick,
+    d_all, heads_x, heads_bc, g_x, g_bc, g_heads, d_gate_out, tokens_out, total_out, z_out,
+    dy_all, dgate_all, pulled, own, after, parts, results, blocks, g_z, out_own, out_passed,
+    o_r1, o_s2, o_r2, o_sp, o_rp, o_total, o_came, o_sums, o_across, o_last,
+    z_r1, z_s2, z_r2, z_sp, z_rp, z_total, z_came, z_sums, z_across, z_last,
+    xe, be, adjoint, dpx, dpb, ends,
+    local, block_sems, trade_local, trade_sends, trade_receives, sends, receives,
+    state_sends, state_receives, back_sends, back_receives,
+):
+    i = pl.program_id(0)
+    chunks = (pl.num_programs(0) - 1) // 2
+    f, z, core, chip, by_x, by_y = places()
+    segments = Segments()
+    me, count = segments.me, segments.count
+    units, share = own.shape[0], parts.shape[2]
+    rows = g_z.shape[0] // 4
+    half = rows // 2
+    inner = g_z.shape[1]
+
+    def at(k, size):
+        return pl.ds(pl.multiple_of(k * size, size), size)
+
+    start_trade, finish_trade, trade_far, trade_near, stays = trade_steps(
+        projected, tokens_out, trade_local, trade_sends, trade_receives
+    )
+    out = Reduction(HALF_PIECES, sends, receives, 0)
+    gz = Reduction(HALF_PIECES, sends, receives, 7 * len(HALF_PIECES))
+    out.over_chips(
+        None,
+        lambda side, columns: out_own[at(side, half), columns],
+        lambda k, columns: out_passed[:, columns],
+        o_r1, o_s2, o_r2, o_sp, o_rp, o_total,
+    )
+
+    def store_to(target):
+        def store(piece, there, values):
+            _, start, width, _, _, _ = piece
+            target[there, pl.ds(start, width)] = values[:, :width].astype(BF16)
+            target[there, pl.ds(inner + start, width)] = values[:, width:].astype(BF16)
+
+        return store
+
+    out.over_members(o_total, o_came, o_sums, o_across, o_last, store_to(total_out))
+    gz.over_chips(
+        lambda k, columns: g_z.at[at(k, rows), columns],
+        lambda side, columns: g_z[pl.ds(pl.multiple_of(chip * rows + side * half, half), half), columns],
+        lambda k, columns: g_z[at(k, rows), columns],
+        z_r1, z_s2, z_r2, z_sp, z_rp, z_total,
+    )
+    gz.over_members(z_total, z_came, z_sums, z_across, z_last, store_to(z_out))
+    left, right = (pl.ds(start, width) for start, width, _ in HALF_PIECES)
+    own_rows = pltpu.make_async_copy(g_out.at[at(chip, rows)], out_own, local.at[0])
+    pass_left = pltpu.make_async_copy(g_out.at[at(by_y, rows), left], out_passed.at[:, left], local.at[1])
+    pass_right = pltpu.make_async_copy(g_out.at[at(by_x, rows), right], out_passed.at[:, right], local.at[2])
+    keep_gate = pltpu.make_async_copy(dgate_all, d_gate_out, local.at[3])
+    take_left = pltpu.make_async_copy(came_left, o_r1.at[:, :, left], local.at[4])
+    take_right = pltpu.make_async_copy(came_right, o_r1.at[:, :, right], local.at[5])
+    taken = (own_rows, pass_left, pass_right, take_left, take_right)
+
+    def fetch(k):
+        columns = pl.ds(k * rows, rows) if isinstance(k, int) else at(k, rows)
+        return pltpu.make_async_copy(normed.at[:, columns], blocks.at[k % 2], block_sems.at[k % 2])
+
+    @pl.when(i == 0)
+    def _():
+        barrier = pltpu.get_barrier_semaphore()
+        for k in range(1, count):
+            pl.semaphore_signal(barrier, inc=1, device_id=segments.peer(k)[1], device_id_type=MESH)
+        for device in (out.partner, out.far, trade_far):
+            pl.semaphore_signal(barrier, inc=1, device_id=device, device_id_type=MESH)
+
+        @pl.when(jnp.logical_not(stays))
+        def _():
+            pl.semaphore_signal(barrier, inc=1, device_id=trade_near, device_id_type=MESH)
+
+        pl.semaphore_wait(barrier, count + 2 + (z + core) % 2)
+        for copy in taken:
+            copy.start()
+        start_trade()
+
+    @pl.when(i == 2)
+    def _():
+        for copy in taken:
+            copy.wait()
+        for piece in out.pieces:
+            out.after_first(piece)
+
+    @pl.when(i == chunks - 2)
+    def _():
+        for piece in out.pieces:
+            out.after_second(piece)
+
+    @pl.when(i < chunks)
+    def _():
+        place = at(i, CHUNK)
+        pull_kernel(
+            dno, gated, gate, y_pull, stats, gain, bcs, acum_pull,
+            dy_all.at[place], dgate_all.at[place], own.at[pl.ds(i // PER_UNIT, 1)],
+            pulled, chunk=i % PER_UNIT,
+        )
+
+    def state_copy(k, at_me):
+        other, device = segments.peer(k)
+        src, slot = (own.at[:, at(other, share)], me) if at_me else (own.at[:, at(me, share)], other)
+        return pltpu.make_async_remote_copy(
+            src_ref=src, dst_ref=parts.at[slot],
+            send_sem=state_sends.at[k], recv_sem=state_receives.at[slot],
+            device_id=device, device_id_type=MESH,
+        )
+
+    def back_copy(k, at_me):
+        other, device = segments.peer(k)
+        slot = me if at_me else other
+        return pltpu.make_async_remote_copy(
+            src_ref=results.at[other], dst_ref=after.at[:, at(slot, share)],
+            send_sem=back_sends.at[k], recv_sem=back_receives.at[slot],
+            device_id=device, device_id_type=MESH,
+        )
+
+    def multiply(k):
+        if k < 3:
+            fetch(k + 1).start()
+        fetch(k).wait()
+
+        def part(n, carry):
+            columns = pl.ds(pl.multiple_of(n * 256, 256), 256)
+            product = dot_tn(blocks[k % 2], dgate_all[:, columns])
+            g_z[pl.ds(k * rows, rows), columns] = product.astype(BF16)
+            return carry
+
+        lax.fori_loop(0, inner // 256, part, 0)
+
+    @pl.when(i == chunks)
+    def _():
+        for k in range(1, count):
+            state_copy(k, True).start()
+        fetch(0).start()
+        keep_gate.start()
+        parts[me] = own[:, at(me, share)]
+        multiply(0)
+        multiply(1)
+        for piece in out.pieces:
+            out.after_pair(piece)
+        for k in range(1, count):
+            state_copy(k, False).wait_recv()
+        running = [jnp.zeros((share, inner), F32) for _ in range(units)]
+        for n in range(count - 1, -1, -1):
+            for u in range(units):
+                results[n, u] = running[u].astype(BF16)
+                running[u] = running[u] * decays[n, u : u + 1] + parts[n, u].astype(F32)
+        after[:, at(me, share)] = results[me]
+        for k in range(1, count):
+            back_copy(k, True).start()
+        multiply(2)
+        multiply(3)
+        gz.start()
+        for k in range(1, count):
+            back_copy(k, False).wait_recv()
+        for k in range(1, count):
+            state_copy(k, True).wait_send()
+            back_copy(k, True).wait_send()
+        for piece in out.pieces:
+            out.start_members(piece)
+
+    def at_step(n, *stages):
+        @pl.when(i == chunks + 1 + n)
+        def _():
+            for stage, reduction in stages:
+                for piece in reduction.pieces:
+                    stage(piece)
+
+    @pl.when(i > chunks)
+    def _():
+        n = i - chunks - 1
+        unit, chunk = n // PER_UNIT, n % PER_UNIT
+        place = at(unit * PER_UNIT + PER_UNIT - 1 - chunk, CHUNK)
+        backward_kernel(
+            x, xp, bc, bcp, step, sig, cx, cbc, hp, dy_all.at[place], y, st, incoming, acum,
+            after.at[pl.ds(unit, 1)], pick, d_all, heads_x, heads_bc, g_x, g_bc, g_heads,
+            xe, be, adjoint, dpx, dpb, ends, place=(unit, chunk),
+        )
+
+    at_step(2, (out.after_near, out))
+    at_step(4, (gz.after_first, gz))
+    at_step(6, (out.after_far, out), (gz.after_second, gz))
+    at_step(7, (gz.after_pair, gz), (gz.start_members, gz))
+    at_step(8, (out.after_last, out))
+    at_step(9, (gz.after_near, gz))
+
+    @pl.when(i == 2 * chunks)
+    def _():
+        finish_trade()
+        out.drain_chips()
+        out.drain_members()
+        gz.drain_chips()
+        for stage in (gz.after_far, gz.after_last):
+            for piece in gz.pieces:
+                stage(piece)
+        gz.drain_members()
+        keep_gate.wait()
 
 
 class Plan:
@@ -980,9 +1238,11 @@
             d_rows = self.to_tokens(self.cores_sum(d_normed))
             return total[:, : 2 * inner], total[:, 2 * inner : cut], total[:, cut:], vec, d_rows
         width = g.shape[1]
-        half, whole = rows // 2, 2 * inner + 4 * LANES
+        wide = 2 * inner + 4 * LANES
         vmem = pl.BlockSpec(memory_space=pltpu.VMEM)
         vec = (16, inner)
+        d_shape = (self.units, 2, self.tokens, d_normed.shape[1])
+        slots = 7 * len(FIRST_PIECES) + 4
         return pl.pallas_call(
             tail_kernel,
             out_shape=[
@@ -994,20 +1254,13 @@
             ],
             in_specs=[vmem] * 7,
             out_specs=[vmem] * 5,
-            scratch_shapes=[
-                pltpu.VMEM((self.units, 2, self.tokens, d_normed.shape[1]), BF16),
-                pltpu.VMEM((self.units, 2, self.tokens, d_normed.shape[1]), BF16),
-                pltpu.SemaphoreType.DMA((1,)),
-                pltpu.VMEM((2, 2 * rows, width), BF16),
-                pltpu.VMEM((2 * rows, width), BF16),
-                pltpu.VMEM((2 * rows, width), BF16),
-                pltpu.VMEM((rows, width), BF16),
-                pltpu.VMEM((rows, width), BF16),
-                pltpu.VMEM((rows, whole), F32),
-            ]
-            + [pltpu.VMEM((half, whole), BF16)] * 6
+            scratch_shapes=[pltpu.VMEM(d_shape, BF16)] * 2
+            + [pltpu.SemaphoreType.DMA((1,))]
+            + chip_scratch(rows, width)
+            + [pltpu.VMEM((rows, wide), BF16)]
+            + member_scratch(rows, wide)
             + [pltpu.VMEM((4,) + vec, F32)] * 2
-            + [pltpu.SemaphoreType.DMA((7 * len(PIECES) + 4,))] * 2
+            + [pltpu.SemaphoreType.DMA((slots,))] * 2
             + [pltpu.SemaphoreType.DMA((5,))] * 2,
             compiler_params=pltpu.CompilerParams(
                 collective_id=3, has_side_effects=True, vmem_limit_bytes=VMEM_LIMIT
@@ -1018,6 +1271,18 @@
             g, g_x, g_bc, g_heads, g_gate, g_norm,
             d_normed.reshape(self.units, 2, 2, self.tokens, d_normed.shape[1]),
         )
+
+    def first_hop(self, g):
+        rows = g.shape[0] // 4
+        by_x, by_y = self.chip + 1 - 2 * (self.chip % 2), (self.chip + 2) % 4
+        corner = (by_x + 2) % 4
+        blocks = g.reshape(4, rows, g.shape[1])
+        found = []
+        for (start, width, _), to, df in zip(HALF_PIECES, (by_x, by_y), (2, 4)):
+            columns = blocks[:, :, start : start + width]
+            given = [lax.dynamic_index_in_dim(columns, k, 0, False) for k in (to, corner)]
+            found.append(self.swap(jnp.stack(given), df=df))
+        return found
 
     def gather(self, x):
         groups = [list(range(c, self.shards, 2)) for c in range(2)]
@@ -1342,89 +1607,150 @@
     stats = jnp.concatenate([scale_out, mean, jnp.zeros((rows, LANES - 2), F32)], axis=1)
     gain_rows = jnp.broadcast_to(gain_out[None], (8, inner))
 
-    dy, d_gate, pull = pl.pallas_call(
-        pull_kernel,
-        grid=(units, PER_UNIT),
-        in_specs=[
-            rows_spec(inner), rows_spec(inner), rows_spec(inner), rows_spec(inner), rows_spec(LANES),
-            whole_spec((8, inner)), rows_spec(2 * LANES), rows_spec(LANES),
-        ],
-        out_specs=[rows_spec(inner), rows_spec(inner), unit_spec(states)],
-        out_shape=[shaped(rows, inner), shaped(rows, inner), shaped(units, *states)],
-        scratch_shapes=[pltpu.VMEM(states, F32)],
-        compiler_params=params(),
-        cost_estimate=cost(19),
-        name="gate_backward",
-    )(d_normed_out, gated, gate_in, y, stats, gain_rows, shared, reach)
-
-    def both_halves(g):
-        half = g.shape[0] // 2
-        first_core = core == 0
-        mine = jnp.where(first_core, g[:half], g[half:])
-        other = jnp.where(first_core, g[half:], g[:half]).astype(BF16)
-        return mine, plan.swap(other, df=1)
-
-    g_z = dot_tn(normed, d_gate).astype(BF16)
-    pull, g_z, g_out = lax.optimization_barrier((pull, g_z, plan.reduce_chips(g_out)))
-    after, _ = exchange(plan, pull, all_decays, True)
-    after, projected, g_z, g_out = lax.optimization_barrier((after, projected, plan.reduce_chips(g_z), g_out))
-    g_out_mine, g_out_other = both_halves(g_out)
-    g_out = jnp.concatenate(plan.by_core(g_out_mine, g_out_other), axis=1).astype(BF16)
-    total_out = lax.psum(g_out, "sp")
-    g_z_mine, g_z_other = both_halves(g_z)
-    g_z = jnp.concatenate(plan.by_core(g_z_mine, g_z_other), axis=1).astype(BF16)
-
+    width = inner + 3 * LANES
     back = functools.partial(rows_spec, back=True)
-    width = inner + 3 * LANES
-    anywhere = pl.BlockSpec(memory_space=pl.ANY)
-    in_specs = [
-        back(inner), chunk_spec((8, inner), True),
-        back(2 * LANES, inner // (2 * LANES)), chunk_spec((8, 2 * LANES), True),
-        back(LANES), back(LANES), whole_spec(cx.shape), whole_spec(cbc.shape), whole_spec(hp.shape),
-        back(inner), back(inner), chunk_spec(states, True), unit_spec(states), back(LANES),
-        unit_spec(states), whole_spec(pick.shape),
-    ]
-    out_specs = [
-        back(width), unit_spec((8, inner)), unit_spec((8, 2 * LANES)),
-        whole_spec((40, inner)), whole_spec((40, 2 * LANES)), whole_spec((24, LANES)),
-    ]
-    out_shape = [
-        shaped(rows, width), shaped(units, 8, inner, dtype=F32), shaped(units, 8, 2 * LANES, dtype=F32),
-        shaped(40, inner, dtype=F32), shaped(40, 2 * LANES, dtype=F32), shaped(24, LANES, dtype=F32),
-    ]
-    scratch = [
-        pltpu.VMEM((CHUNK + 8, inner), F32), pltpu.VMEM((CHUNK + 8, 2 * LANES), F32),
-        pltpu.VMEM(states, F32),
-        pltpu.VMEM((CHUNK + 8, inner), F32), pltpu.VMEM((CHUNK + 8, 2 * LANES), F32),
-        pltpu.VMEM((8, inner), F32),
-    ]
-    operands = [
-        first, tail_x, first, tail_bc, step, slope_dt, cx, cbc, hp,
-        dy, y, starts, incoming, reach, after, pick,
-    ]
-    sending = params()
     if plan.fast:
-        in_specs, operands = in_specs + [anywhere], operands + [projected]
-        out_specs, out_shape = out_specs + [anywhere], out_shape + [shaped(batch, tokens, model)]
-        scratch = scratch + [
-            pltpu.SemaphoreType.DMA((1,)), pltpu.SemaphoreType.DMA((2,)), pltpu.SemaphoreType.DMA((2,)),
-        ]
-        sending = pltpu.CompilerParams(
-            dimension_semantics=("arbitrary", "arbitrary"), vmem_limit_bytes=VMEM_LIMIT,
-            collective_id=4, has_side_effects=True,
-        )
-    d_all, heads_x, heads_bc, g_x, g_bc, g_heads, *sent = pl.pallas_call(
-        backward_sending_kernel if plan.fast else backward_kernel,
-        grid=(units, PER_UNIT),
-        in_specs=in_specs,
-        out_specs=out_specs,
-        out_shape=out_shape,
-        scratch_shapes=scratch,
-        compiler_params=sending,
-        cost_estimate=cost(70),
-        name="scan_backward",
-    )(*operands)
-    projected = sent[0] if plan.fast else plan.to_tokens(projected)
+        came_left, came_right = plan.first_hop(g_out)
+        spots = 2 * chunks + 1
+        shard_rows = model // plan.shards
+        segments = plan.count
+        share = LANES // segments
+
+        def pulls(columns, column=0):
+            return pl.BlockSpec((CHUNK, columns), lambda i: (jnp.minimum(i, chunks - 1), column))
+
+        def scan_at(i):
+            n = jnp.maximum(i - chunks - 1, 0)
+            return n - n % PER_UNIT + PER_UNIT - 1 - n % PER_UNIT
+
+        def scans(columns, column=0):
+            return pl.BlockSpec((CHUNK, columns), lambda i: (scan_at(i), column))
+
+        def scan_chunk(shape):
+            return pl.BlockSpec((1,) + shape, lambda i: (scan_at(i), 0, 0))
+
+        def scan_unit(shape):
+            return pl.BlockSpec((1,) + shape, lambda i: (scan_at(i) // PER_UNIT, 0, 0))
+
+        def every(shape):
+            return pl.BlockSpec(shape, lambda i: (0,) * len(shape))
+
+        anywhere = pl.BlockSpec(memory_space=pl.ANY)
+        dma = pltpu.SemaphoreType.DMA
+        d_all, heads_x, heads_bc, g_x, g_bc, g_heads, d_gate, projected, total_out, total_z = pl.pallas_call(
+            middle_kernel,
+            grid=(spots,),
+            in_specs=[
+                pulls(inner), pulls(inner), pulls(inner), pulls(inner), pulls(LANES), every((8, inner)),
+                pulls(2 * LANES), pulls(LANES), every(all_decays.shape), anywhere, anywhere, anywhere, anywhere, anywhere,
+                scans(inner), scan_chunk((8, inner)),
+                scans(2 * LANES, inner // (2 * LANES)), scan_chunk((8, 2 * LANES)),
+                scans(LANES), scans(LANES), every(cx.shape), every(cbc.shape), every(hp.shape),
+                scans(inner), scan_chunk(states), scan_unit(states), scans(LANES), every(pick.shape),
+            ],
+            out_specs=[
+                scans(width), scan_unit((8, inner)), scan_unit((8, 2 * LANES)),
+                every((40, inner)), every((40, 2 * LANES)), every((24, LANES)),
+                anywhere, anywhere, every((shard_rows, 2 * inner)), every((shard_rows, 2 * inner)),
+            ],
+            out_shape=[
+                shaped(rows, width), shaped(units, 8, inner, dtype=F32), shaped(units, 8, 2 * LANES, dtype=F32),
+                shaped(40, inner, dtype=F32), shaped(40, 2 * LANES, dtype=F32), shaped(24, LANES, dtype=F32),
+                shaped(rows, inner), shaped(batch, tokens, model),
+                shaped(shard_rows, 2 * inner), shaped(shard_rows, 2 * inner),
+            ],
+            scratch_shapes=[
+                pltpu.VMEM((rows, inner), BF16), pltpu.VMEM((rows, inner), BF16), pltpu.VMEM(states, F32),
+                pltpu.VMEM((units,) + states, BF16), pltpu.VMEM((units,) + states, BF16),
+                pltpu.VMEM((segments, units, share, inner), BF16),
+                pltpu.VMEM((segments, units, share, inner), BF16),
+                pltpu.VMEM((2, rows, model // 4), BF16), pltpu.VMEM((model, inner), BF16),
+                pltpu.VMEM((model // 4, inner), BF16), pltpu.VMEM((model // 4, inner), BF16),
+            ]
+            + chip_scratch(shard_rows, inner)
+            + [pltpu.VMEM((shard_rows, 2 * inner), BF16)]
+            + member_scratch(shard_rows, 2 * inner)
+            + chip_scratch(shard_rows, inner)
+            + [pltpu.VMEM((shard_rows, 2 * inner), BF16)]
+            + member_scratch(shard_rows, 2 * inner)
+            + [
+                pltpu.VMEM((CHUNK + 8, inner), F32), pltpu.VMEM((CHUNK + 8, 2 * LANES), F32),
+                pltpu.VMEM(states, F32),
+                pltpu.VMEM((CHUNK + 8, inner), F32), pltpu.VMEM((CHUNK + 8, 2 * LANES), F32),
+                pltpu.VMEM((8, inner), F32),
+                dma((6,)), dma((2,)), dma((1,)), dma((2,)), dma((2,)),
+                dma((14 * len(HALF_PIECES),)), dma((14 * len(HALF_PIECES),)),
+                dma((segments,)), dma((segments,)), dma((segments,)), dma((segments,)),
+            ],
+            compiler_params=pltpu.CompilerParams(
+                dimension_semantics=("arbitrary",), vmem_limit_bytes=62 * 1024 * 1024,
+                collective_id=4, has_side_effects=True,
+            ),
+            cost_estimate=cost(125),
+            name="middle",
+        )(
+            d_normed_out, gated, gate_in, y, stats, gain_rows, shared, reach, all_decays, normed, g_out,
+            came_left, came_right, projected, first, tail_x, first, tail_bc, step, slope_dt, cx, cbc, hp, y, starts, incoming,
+            reach, pick,
+        )
+    else:
+        dy, d_gate, pull = pl.pallas_call(
+            pull_kernel,
+            grid=(units, PER_UNIT),
+            in_specs=[
+                rows_spec(inner), rows_spec(inner), rows_spec(inner), rows_spec(inner), rows_spec(LANES),
+                whole_spec((8, inner)), rows_spec(2 * LANES), rows_spec(LANES),
+            ],
+            out_specs=[rows_spec(inner), rows_spec(inner), unit_spec(states)],
+            out_shape=[shaped(rows, inner), shaped(rows, inner), shaped(units, *states)],
+            scratch_shapes=[pltpu.VMEM(states, F32)],
+            compiler_params=params(),
+            name="gate_backward",
+        )(d_normed_out, gated, gate_in, y, stats, gain_rows, shared, reach)
+        after, _ = exchange(plan, pull, all_decays, True)
+        d_all, heads_x, heads_bc, g_x, g_bc, g_heads = pl.pallas_call(
+            backward_kernel,
+            grid=(units, PER_UNIT),
+            in_specs=[
+                back(inner), chunk_spec((8, inner), True),
+                back(2 * LANES, inner // (2 * LANES)), chunk_spec((8, 2 * LANES), True),
+                back(LANES), back(LANES), whole_spec(cx.shape), whole_spec(cbc.shape), whole_spec(hp.shape),
+                back(inner), back(inner), chunk_spec(states, True), unit_spec(states), back(LANES),
+                unit_spec(states), whole_spec(pick.shape),
+            ],
+            out_specs=[
+                back(width), unit_spec((8, inner)), unit_spec((8, 2 * LANES)),
+                whole_spec((40, inner)), whole_spec((40, 2 * LANES)), whole_spec((24, LANES)),
+            ],
+            out_shape=[
+                shaped(rows, width), shaped(units, 8, inner, dtype=F32), shaped(units, 8, 2 * LANES, dtype=F32),
+                shaped(40, inner, dtype=F32), shaped(40, 2 * LANES, dtype=F32), shaped(24, LANES, dtype=F32),
+            ],
+            scratch_shapes=[
+                pltpu.VMEM((CHUNK + 8, inner), F32), pltpu.VMEM((CHUNK + 8, 2 * LANES), F32),
+                pltpu.VMEM(states, F32),
+                pltpu.VMEM((CHUNK + 8, inner), F32), pltpu.VMEM((CHUNK + 8, 2 * LANES), F32),
+                pltpu.VMEM((8, inner), F32),
+            ],
+            compiler_params=params(),
+            name="scan_backward",
+        )(
+            first, tail_x, first, tail_bc, step, slope_dt, cx, cbc, hp,
+            dy, y, starts, incoming, reach, after, pick,
+        )
+        projected = plan.to_tokens(projected)
+
+        def over_everything(g):
+            g = plan.reduce_chips(g)
+            half = g.shape[0] // 2
+            low = core == 0
+            mine, other = jnp.where(low, g[:half], g[half:]), jnp.where(low, g[half:], g[:half])
+            other = plan.swap(other.astype(BF16), df=1).astype(F32)
+            return plan.reduce_members(jnp.concatenate(plan.by_core(mine, other), axis=1))
+
+        total_out = over_everything(g_out)
+        total_z = over_everything(dot_tn(normed, d_gate).astype(BF16))
+    output = (hidden.astype(F32) + projected.astype(F32)).astype(BF16)
 
     later = plan.along(jnp.concatenate([heads_x, heads_bc], axis=2)[:, :3].astype(BF16), -1).astype(F32)
     taps = jnp.concatenate([cx[:4], cbc[:4]], axis=1)
@@ -1437,8 +1763,6 @@
     d_all = lax.dynamic_update_slice(d_all, (tail_rows + extra).astype(BF16), (0, 4 * tokens - 16, 0))
     d_all = d_all.reshape(rows, width)
 
-    total_z = lax.psum(g_z, "sp")
-    output = (hidden.astype(F32) + projected.astype(F32)).astype(BF16)
     g_first = dot_tn(normed, d_all).astype(BF16)
     d_normed = dot_nt(d_gate, weight_gate) + dot_nt(d_all, weight_first)
     g_norm_gain = jnp.sum(d_normed * unit_in, axis=0)

time: 798 us -> 728 us (0.912)
  waiting for transfers between devices: 118 us -> 28.2 us
  Pallas kernels: 408 us -> 440 us
  matrix products: 117 us -> 98.8 us
    pallas_call x2 -> x1, Pallas kernels: 94.9 us -> 177 us  [body(): pl.pallas_call(middle_kernel, grid=(spots,), in_specs=[pulls(inner), pull...]
    psum x1 -> x0, waiting for transfers between devices: 81 us -> none  [body(): total_z = lax.psum(g_z, 'sp')]
    pallas_call x2 -> x1, Pallas kernels: 95.8 us -> 44.4 us  [exchange(): pl.pallas_call(kernel, out_shape=out_shape, in_specs=[vmem, vmem], out_sp...]
    reduce_scatter x2 -> x0, waiting for transfers between devices: 19.2 us -> none  [reduce_chips(): lax.psum_scatter(g, 'fs', scatter_dimension=0, tiled=True, axis_index_gro...]
    dot_general x3 -> x2, matrix products: 35.9 us -> 22.8 us  [dot_tn(): lax.dot_general(a, b, (((0,), (0,)), ((), ())), preferred_element_type=F32)]
    ppermute x12, waiting for transfers between devices: 6.24 us -> 19.2 us  [send(): return lax.ppermute(x, ('fs', 'sp'), pairs)]
    unnamed x91 -> x85, local copies, waits for them, and re-layouts: 12.4 us -> 18.5 us
  transfers between devices with their start and end apart: 17 -> 14, of which waited for: 8 -> 3; matrix products, arithmetic and copies ran while one was open for 26% -> 13% of each run, Pallas kernels for 42% -> 13%
where the time goes in v3:
time: 728 us; the launch traced here: 718 us
  Pallas kernels  440 us (60%)
  matrix products  98.8 us (14%)
  other arithmetic  59.4 us (8%)
  local copies, waits for them, and re-layouts  55.1 us (8%)
  waiting for transfers between devices  28.2 us (4%)
  starting transfers between devices  21.3 us (3%)
  between operations  15 us (2%)
    pallas_call x1, Pallas kernels, body(): pl.pallas_call(middle_kernel, grid=(spots,), in_specs=[pulls(inner), pull...  177 us
    pallas_call x1, Pallas kernels, tail(): pl.pallas_call(tail_kernel, out_shape=[jax.ShapeDtypeStruct((rows, 2 * in...  109 us
    pallas_call x1, Pallas kernels, head(): pl.pallas_call(head_kernel, out_shape=[jax.ShapeDtypeStruct((self.units,...  63.8 us
    pallas_call x1, Pallas kernels, exchange(): pl.pallas_call(kernel, out_shape=out_shape, in_specs=[vmem, vmem], out_sp...  44.4 us
    dot_general x3, matrix products, dot_nt(): lax.dot_general(a, b, (((1,), (1,)), ((), ())), preferred_element_type=F32)  39.7 us
    dot_general x3, matrix products, dot(): return jnp.dot(a, b, preferred_element_type=F32)  36.4 us
    pallas_call x1, Pallas kernels, body(): pl.pallas_call(forward_kernel, grid=(units, PER_UNIT), in_specs=[rows_spe...  31 us
    dot_general x2, matrix products, dot_tn(): lax.dot_general(a, b, (((0,), (0,)), ((), ())), preferred_element_type=F32)  22.8 us
  transfers between devices with their start and end apart: 14, of which 3 were waited for; matrix products, arithmetic and copies ran while one was open for 13% of the time, Pallas kernels for 13%

profile of v3, /device:TPU:0, one launch (start us, length us, event | category | flops | bytes accessed | tf_op | source)
XLA Modules:
  0.0 717.7 jit_solution(5239819530820602083)
XLA Ops:
  9.7 4.8 concatenate.45
  15.1 1.3 broadcast_select_fusion.10
  16.4 1.8 concatenate.44.other
  18.2 1.8 concatenate.43.mine
  20.0 63.8 %head.1 = (bf16[3,4,128,1536]{3,2,1,0:T(8,128)(2,1)}, bf16[4,2,192,1920]{3,2,1,0:T(8,128)(2,1)}, bf16[8,32,128]{2,1,0:T(8,128)(2,1)}) custom-call(bf16[6,128,1536]{2,1,0:T(8,128)(2,1)} %hidden.1, bf16[192,1920]{1,0:T(8,128)(2,1)} %concatenate.43.mine, bf16[192,1920]{1,0:T(8,128)(2,1)} %concatenate.44.other, bf16[32,128]{1,0:T(8,128)(2,1)} %pad_bitcast_fusion.small), custom_call_target="tpu_custom_call" | custom-call | flops 63250001920 | tf_op jit(solution)/shard_map/head/pallas_call | solution.py:1185
  85.5 3.5 fusion.4
  89.3 1.1 fusion.2.normed
  90.4 2.2 copy-done.10
  92.6 12.4 %convolution_convert_fusion.1.x_ref.bc_ref.x.bc = bf16[1536,1920]{1,0:T(8,128)(2,1)S(1)} fusion(bf16[1536,1536]{1,0:T(8,128)(2,1)S(1)} %fusion.2.normed, bf16[1536,1920]{1,0:T(8,128)(2,1)} %bitcast.174), kind=kOutput, calls=%fused_computation.16 | convolution fusion | flops 9062645760 | bytes 16515072 | tf_op jit(solution)/shard_map/dot_general | solution.py:20
  105.4 2.4 copy-done.6
  107.8 2.7 copy-done.5
  111.1 1.9 collective-permute-start.3
  113.9 1.9 collective-permute-start.4
  115.8 0.9 broadcast_select_fusion.4
  116.8 3.2 broadcast_select_fusion.1
  120.0 2.6 collective-permute-start
  122.6 10.4 %collective-permute-start.1 = (bf16[3,128,1536]{2,1,0:T(8,128)(2,1)}, bf16[3,128,1536]{2,1,0:T(8,128)(2,1)}, u32[]{:S(2)}, u32[]{:S(2)}) collective-permute-start(bf16[3,128,1536]{2,1,0:T(8,128)(2,1)} %get-tuple-element.156), channel_id=1, source_target_pairs={{0,0},{1,4},{2,2},{3,6},{4,1},{5,5},{6,3},{7,7},{8,8},{9,12},{10,1... | collective-permute-start | bytes 3538952 | tf_op jit(solution)/shard_map/ppermute | solution.py:1154
  133.0 1.5 fusion.39
  134.4 1.3 fusion.38
  143.1 1.2 broadcast_select_fusion.7
  144.3 1.1 pad_maximum_fusion.2
  146.0 1.0 slice.261
  149.4 1.0 fusion.19.pick
  150.4 2.8 add_divide_fusion
  153.2 0.9 pad_maximum_fusion.6
  154.2 0.9 slice.262.xp_ref.xp
  155.7 31.0 %scan_forward.1 = (bf16[1536,1536]{1,0:T(8,128)(2,1)}, bf16[12,128,1536]{2,1,0:T(8,128)(2,1)}, bf16[3,128,1536]{2,1,0:T(8,128)(2,1)}, f32[3,8,1536]{2,1,0:T(8,12...) custom-call(bf16[1536,1920]{1,0:T(8,128)(2,1)} %copy-done.6, f32[12,8,1536]{2,1,0:T(8,128)} %slice.262.xp_ref.xp, ...), custom_call_target="tpu_custom_call" | custom-call | flops 35649998848 | tf_op jit(solution)/shard_map/scan_forward/pallas_call | solution.py:1549
  186.7 1.0 copy.57
  188.4 1.2 broadcast_select_fusion.3
  189.6 1.2 pad_maximum_fusion.3
  190.8 1.8 select_bitcast_fusion.3
  192.9 44.4 %states.1 = (bf16[3,128,1536]{2,1,0:T(8,128)(2,1)}, f32[8,8,1536]{2,1,0:T(8,128)}) custom-call(bf16[3,128,1536]{2,1,0:T(8,128)(2,1)} %get-tuple-element.58.own_ref, f32[8,1536]{1,0:T(8,128)} %concatenate.51.dec_ref), custom_call_target="tpu_custom_call" | custom-call | flops 40249999360 | tf_op jit(solution)/shard_map/states/pallas_call | solution.py:1435
  237.2 3.4 select_bitcast_fusion.1
  240.6 12.3 %convolution_convert_fusion.4.gate_ref.gate = bf16[1536,1536]{1,0:T(8,128)(2,1)} fusion(bf16[1536,1536]{1,0:T(8,128)(2,1)} %copy-done.10, bf16[1536,1536]{1,0:T(8,128)(2,1)} %all-gather.3.cloned.1.call-done), kind=kOutput, calls=%fused_computation.19 | convolution fusion | flops 7250116608 | bytes 14155776 | tf_op jit(solution)/shard_map/dot_general | solution.py:20
  252.9 14.5 %gate_forward.1 = (bf16[1536,1536]{1,0:T(8,128)(2,1)}, bf16[1536,1536]{1,0:T(8,128)(2,1)}, f32[1536,128]{1,0:T(8,128)}) custom-call(bf16[1536,1536]{1,0:T(8,128)(2,1)} %get-tuple-element.55.y0_ref, bf16[1536,1536]{1,0:T(8,128)(2,1)} %convolution_convert_fusion.4.gate_ref.gate, bf16[1536,256]{1,0:T(8,128)(2,1)} %get-tuple-element.56.bcs_ref.bcs, ...), custom_call_target="tpu_custom_call" | custom-call | flops 16099999744 | tf_op jit(solution)/shard_map/gate_forward/pallas_call | solution.py:1578
  267.4 1.4 slice_reduce_fusion
  268.9 2.6 pad_maximum_fusion
  271.5 8.9 %all-gather.5.cloned.1.call-done = bf16[1536,1536]{1,0:T(8,128)(2,1)} async-done(((bf16[384,1536]{1,0:T(8,128)(2,1)}), bf16[1536,1536]{1,0:T(8,128)(2,1)}) %all-gather.5.cloned.1.call-update) | async-done | bytes 4718608 | tf_op jit(solution)/shard_map/all_gather | solution.py:1289
  280.4 11.1 %fusion.18 = f32[1536,1536]{1,0:T(8,128)S(1)} fusion(bf16[1536,1536]{1,0:T(8,128)(2,1)} %all-gather.5.cloned.1.call-done, bf16[1536,1536]{1,0:T(8,128)(2,1)} %get-tuple-element.61.gated, f32[1536]{0:T(1024)S(1)} %mul.173, f32[1536]{0:T(1024)S(1)} %get-tuple-element.182), kind=kOutput, calls=%fused_computation.43 | convolution fusion | flops 7257194496 | bytes 18886656 | tf_op jit(solution)/shard_map/dot_general | solution.py:24
  291.6 1.8 fusion.17
  293.4 4.0 copy-done.12
  297.4 10.8 %convolution_convert_fusion.3.g_out = bf16[1536,1536]{1,0:T(8,128)(2,1)S(1)} fusion(bf16[1536,1536]{1,0:T(8,128)(2,1)S(1)} %bitcast.143, bf16[1536,1536]{1,0:T(8,128)(2,1)} %get-tuple-element.61.gated, f32[1536]{0:T(1024)S(1)} %mul.173, f32[1536]{0:T(1024)S(1)} %get-tuple-element.182), kind=kOutput, calls=%fused_computation.18 | convolution fusion | flops 7259553792 | bytes 14168064 | tf_op jit(solution)/shard_map/dot_general | solution.py:28
  308.5 1.8 copy-done.11
  310.5 1.5 collective-permute-start.9
  312.0 11.7 %fusion.7 = (f32[1536]{0:T(1024)}, f32[1536]{0:T(1024)S(1)}, bf16[1536,1536]{1,0:T(8,128)(2,1)}) fusion(bf16[1536,1536]{1,0:T(8,128)(2,1)} %get-tuple-element.61.gated, f32[1536]{0:T(1024)S(1)} %get-tuple-element.182, f32[1536]{0:T(1024)S(1)} %mul.173, bf16[1536,1536]{1,0:T(8,128)(2,1)S(1)} %bitcast.144, bf16[1536,1536]{1,0:T(8,128)(2,1)S(1)} %bitcast.172), kind=kOutput, calls=%fused_computation.11 | convolution fusion | flops 7268987904 | bytes 18898944 | tf_op jit(solution)/shard_map/dot_general | solution.py:20
  323.8 1.1 pad_maximum_fusion.4
  326.1 1.2 maximum_maximum_fusion.stats
  327.3 7.1 fusion.16.projected
  334.4 3.9 collective-permute-done.9.came_right
  338.3 15.3 %collective-permute-done.8.came_left = bf16[2,384,768]{2,1,0:T(8,128)(2,1)} collective-permute-done((bf16[2,384,768]{2,1,0:T(8,128)(2,1)}, bf16[2,384,768]{2,1,0:T(8,128)(2,1)}, u32[]{:S(2)}, u32[]{:S(2)}) %collective-permute-start.8) | collective-permute-done | bytes 1179680 | tf_op jit(solution)/shard_map/ppermute | solution.py:1154
  354.2 177.0 %middle.1 = (bf16[1536,1920]{1,0:T(8,128)(2,1)}, f32[3,8,1536]{2,1,0:T(8,128)}, f32[3,8,256]{2,1,0:T(8,128)}, f32[40,1536]{1,0:T(8,128)}, f32[40,256]{1,0:T(8,12...) custom-call(bf16[1536,1536]{1,0:T(8,128)(2,1)} %get-tuple-element.18, ...), custom_call_target="tpu_custom_call" | custom-call | flops 143750004736 | tf_op jit(solution)/shard_map/middle/pallas_call | solution.py:1640
  531.2 1.0 convert.9
  533.0 1.7 collective-permute-start.11
  535.4 3.2 convert_element_type.132
  538.6 1.7 convert_element_type.133
  540.6 14.8 %fusion.41 = f32[1536,1536]{1,0:T(8,128)} fusion(bf16[1536,1920]{1,0:T(8,128)(2,1)S(1)} %bitcast.165, bf16[1536,1920]{1,0:T(8,128)(2,1)} %bitcast.175), kind=kOutput, calls=%fused_computation.152 | convolution fusion | flops 9059696640 | bytes 21233664 | tf_op jit(solution)/shard_map/dot_general | solution.py:24
  555.4 12.0 %convolution_convert_fusion.g = bf16[1536,1920]{1,0:T(8,128)(2,1)} fusion(bf16[1536,1536]{1,0:T(8,128)(2,1)S(1)} %bitcast.141, bf16[1536,1920]{1,0:T(8,128)(2,1)S(1)} %bitcast.166), kind=kOutput, calls=%fused_computation.15 | convolution fusion | flops 9062645760 | bytes 16515072 | tf_op jit(solution)/shard_map/dot_general | solution.py:28
  567.4 13.8 %fusion.33 = (bf16[1536,1536]{1,0:T(8,128)(2,1)}, f32[1536]{0:T(1024)S(1)}) fusion(f32[1536]{0:T(1024)S(1)} %copy-done.23, bf16[1536,1536]{1,0:T(8,128)(2,1)S(1)} %bitcast.137, f32[1536,1536]{1,0:T(8,128)} %fusion.41, bf16[1536,1536]{1,0:T(8,128)(2,1)} %get-tuple-element.76, bf16[1536,1536]{1,0:T(8,128)(2,1)S(1)} %bitcast.170), kind=kOutput, calls=%fused_computation.144 | convolution fusion | flops 7261911552 | bytes 28323840 | tf_op jit(solution)/shard_map/dot_general | solution.py:24
  581.8 109.2 %tail.1 = (f32[192,3072]{1,0:T(8,128)}, f32[192,256]{1,0:T(8,128)}, f32[192,256]{1,0:T(8,128)}, f32[2,16,1536]{2,1,0:T(8,128)}, bf16[6,128,1536]{2,1,0:T(8,128)(2,1)}) custom-call(bf16[1536,1920]{1,0:T(8,128)(2,1)} %convolution_convert_fusion.g, f32[40,1536]{1,0:T(8,128)} %get-tuple-element.73.g_x, f32[40,256]{1,0:T(8,128)} %get-tuple-element.74.g_bc, ...), custom_call_target="tpu_custom_call" | custom-call | flops 103499997184 | tf_op jit(solution)/shard_map/tail/pallas_call | solution.py:1246
  693.8 0.9 slice.244
  695.4 1.0 fusion.36
  697.2 2.7 fusion.10
  700.6 6.1 fusion.13
  708.6 1.4 copy.88
  (185 shorter events, 31.2 us)
Async XLA Ops:
  7.2 233.4 %all-gather.3.cloned.1.call-start = ((), (), s32[]{:S(2)}) async-start(), calls=%async_computation | async-start | bytes 5898240 | tf_op jit(solution)/shard_map/all_gather | solution.py:1289
  84.8 0.7 copy-start.15
  85.5 4.9 copy-start.17
  85.5 3.8 copy-start.3
  89.3 1.2 copy-start.22
  90.4 2.2 copy-start.10
  105.0 2.8 copy-start.6
  105.0 8.0 %copy-start.7 = (bf16[192,3072]{1,0:T(8,128)(2,1)S(1)}, bf16[192,3072]{1,0:T(8,128)(2,1)}, u32[]{:S(2)}) copy-start(bf16[192,3072]{1,0:T(8,128)(2,1)} %param.18) | copy-start | bytes 3538948
  105.0 10.8 %copy-start.8 = (bf16[192,3072]{1,0:T(8,128)(2,1)S(1)}, bf16[192,3072]{1,0:T(8,128)(2,1)}, u32[]{:S(2)}) copy-start(bf16[192,3072]{1,0:T(8,128)(2,1)} %param.22) | copy-start | bytes 3538948
  107.8 2.7 copy-start.5
  107.8 27.9 %copy-start = (bf16[6,128,1536]{2,1,0:T(8,128)(2,1)S(1)}, bf16[6,128,1536]{2,1,0:T(8,128)(2,1)}, u32[]{:S(2)}) copy-start(bf16[6,128,1536]{2,1,0:T(8,128)(2,1)} %hidden.1) | copy-start | bytes 7077892
  111.1 42.1 %collective-permute-start.3 = (bf16[3,8,1792]{2,1,0:T(8,128)(2,1)}, bf16[3,8,1792]{2,1,0:T(8,128)(2,1)}, u32[]{:S(2)}, u32[]{:S(2)}) collective-permute-start(bf16[3,8,1792]{2,1,0:T(8,128)(2,1)} %slice_bitcast_fusion.2), channel_id=1, source_target_pairs={{0,1},{1,8},{2,3},{3,10},{4,5},{5,12},{6,7},{7,14},{8,9},{9,16},{1... | collective-permute-start | bytes 258056 | tf_op jit(solution)/shard_map/ppermute | solution.py:1154
  113.9 29.2 %collective-permute-start.4 = (bf16[192,1536]{1,0:T(8,128)(2,1)}, bf16[192,1536]{1,0:T(8,128)(2,1)}, u32[]{:S(2)}, u32[]{:S(2)}) collective-permute-start(bf16[192,1536]{1,0:T(8,128)(2,1)} %broadcast_select_fusion.8), channel_id=1, source_target_pairs={{0,4},{1,5},{2,6},{3,7},{4,0},{5,1},{6,2},{7,3},{8,12},{9,13},{10,... | collective-permute-start | bytes 1769480 | tf_op jit(solution)/shard_map/ppermute | solution.py:1154
  116.8 71.6 %collective-permute-start.6 = (bf16[192,1536]{1,0:T(8,128)(2,1)}, bf16[192,1536]{1,0:T(8,128)(2,1)}, u32[]{:S(2)}, u32[]{:S(2)}) collective-permute-start(bf16[192,1536]{1,0:T(8,128)(2,1)} %broadcast_select_fusion.4), channel_id=1, source_target_pairs={{0,4},{1,5},{2,6},{3,7},{4,0},{5,1},{6,2},{7,3},{8,12},{9,13},{10,... | collective-permute-start | bytes 1769480 | tf_op jit(solution)/shard_map/ppermute | solution.py:1154
  120.0 70.8 %collective-permute-start = (bf16[3,128,1536]{2,1,0:T(8,128)(2,1)}, bf16[3,128,1536]{2,1,0:T(8,128)(2,1)}, u32[]{:S(2)}, u32[]{:S(2)}) collective-permute-start(bf16[3,128,1536]{2,1,0:T(8,128)(2,1)} %get-tuple-element.155), channel_id=1, source_target_pairs={{0,2},{1,6},{2,0},{3,4},{4,3},{5,7},{6,1},{7,5},{8,10},{9,14},{10,... | collective-permute-start | bytes 3538952 | tf_op jit(solution)/shard_map/ppermute | solution.py:1154
  122.6 68.2 %collective-permute-start.1 = (bf16[3,128,1536]{2,1,0:T(8,128)(2,1)}, bf16[3,128,1536]{2,1,0:T(8,128)(2,1)}, u32[]{:S(2)}, u32[]{:S(2)}) collective-permute-start(bf16[3,128,1536]{2,1,0:T(8,128)(2,1)} %get-tuple-element.156), channel_id=1, source_target_pairs={{0,0},{1,4},{2,2},{3,6},{4,1},{5,5},{6,3},{7,7},{8,8},{9,12},{10,1... | collective-permute-start | bytes 3538952 | tf_op jit(solution)/shard_map/ppermute | solution.py:1154
  145.4 135.0 %all-gather.5.cloned.1.call-start = ((), (), s32[]{:S(2)}) async-start(), calls=%async_computation.1 | async-start | bytes 5898240 | tf_op jit(solution)/shard_map/all_gather | solution.py:1289
  153.2 2.5 copy-start.19
  155.7 32.6 %copy-start.9 = (bf16[192,3072]{1,0:T(8,128)(2,1)S(1)}, bf16[192,3072]{1,0:T(8,128)(2,1)}, u32[]{:S(2)}) copy-start(bf16[192,3072]{1,0:T(8,128)(2,1)} %param.22) | copy-start | bytes 3538948
  192.8 44.5 %collective-permute-start.2 = (bf16[3,2,128,1536]{3,2,1,0:T(8,128)(2,1)S(1)}, bf16[3,2,128,1536]{3,2,1,0:T(8,128)(2,1)}, u32[]{:S(2)}, u32[]{:S(2)}) collective-permute-start(bf16[3,2,128,1536]{3,2,1,0:T(8,128)(2,1)S(1)} %pad_maximum_fusion.1), channel_id=1, source_target_pairs={{0,4},{1,5},{2,6},{3,7},{4,0},{5,1},{6,2},{7,3},{8,12},{9,13},{10,... | collective-permute-start | bytes 7077896 | tf_op jit(solution)/shard_map/ppermute | solution.py:1154
  252.9 16.0 %copy-start.4 = (bf16[3,2,1,128,1536]{4,3,2,1,0:T(8,128)(2,1)S(1)}, bf16[3,2,1,128,1536]{4,3,2,1,0:T(8,128)(2,1)}, u32[]{:S(2)}) copy-start(bf16[3,2,1,128,1536]{4,3,2,1,0:T(8,128)(2,1)} %get-tuple-element.146) | copy-start | bytes 7077892
  268.8 2.6 collective-permute-start.5
  291.5 16.6 %copy-start.2 = (f32[1536,1536]{1,0:T(8,128)}, f32[1536,1536]{1,0:T(8,128)S(1)}, u32[]{:S(2)}) copy-start(f32[1536,1536]{1,0:T(8,128)S(1)} %fusion.18) | copy-start | bytes 28311556
  291.6 5.8 copy-start.12
  291.6 20.4 %slice-start.6 = ((s8[4718592]{0:T(1024)(128)(4,1)}), s8[4194304]{0:T(1024)(128)(4,1)S(1)}, s32[]{:S(2)}) async-start(s8[4718592]{0:T(1024)(128)(4,1)} %bitcast.171), calls=%async_computation.8 | async-start | bytes 8388608
  293.4 33.9 %collective-permute-start.10 = (bf16[3,2,128,1536]{3,2,1,0:T(8,128)(2,1)}, bf16[3,2,128,1536]{3,2,1,0:T(8,128)(2,1)}, u32[]{:S(2)}, u32[]{:S(2)}) collective-permute-start(bf16[3,2,128,1536]{3,2,1,0:T(8,128)(2,1)} %fusion.17), channel_id=1, source_target_pairs={{0,4},{1,5},{2,6},{3,7},{4,0},{5,1},{6,2},{7,3},{8,12},{9,13},{10,... | collective-permute-start | bytes 7077896 | tf_op jit(solution)/shard_map/ppermute | solution.py:1154
  297.4 14.6 %slice-start.7 = ((s8[4718592]{0:T(1024)(128)(4,1)}), s8[524288]{0:T(1024)(128)(4,1)S(1)}, s32[]{:S(2)}) async-start(s8[4718592]{0:T(1024)(128)(4,1)} %bitcast.171), calls=%async_computation.9 | async-start | bytes 1048576
  308.2 2.1 copy-start.11
  310.5 27.9 %collective-permute-start.9 = (bf16[2,384,768]{2,1,0:T(8,128)(2,1)S(1)}, bf16[2,384,768]{2,1,0:T(8,128)(2,1)}, u32[]{:S(2)}, u32[]{:S(2)}) collective-permute-start(bf16[2,384,768]{2,1,0:T(8,128)(2,1)S(1)} %pad_maximum_fusion.5), channel_id=1, source_target_pairs={{0,16},{1,17},{2,18},{3,19},{4,20},{5,21},{6,22},{7,23},{8,24},{9,... | collective-permute-start | bytes 3538952 | tf_op jit(solution)/shard_map/ppermute | solution.py:1154
  323.7 2.4 copy-start.26
  323.7 2.1 collective-permute-start.7
  324.9 28.7 %collective-permute-start.8 = (bf16[2,384,768]{2,1,0:T(8,128)(2,1)}, bf16[2,384,768]{2,1,0:T(8,128)(2,1)}, u32[]{:S(2)}, u32[]{:S(2)}) collective-permute-start(bf16[2,384,768]{2,1,0:T(8,128)(2,1)} %pad_maximum_fusion.4), channel_id=1, source_target_pairs={{0,8},{1,9},{2,10},{3,11},{4,12},{5,13},{6,14},{7,15},{8,0},{9,1},... | collective-permute-start | bytes 3538952 | tf_op jit(solution)/shard_map/ppermute | solution.py:1154
  354.2 180.5 %copy-start.20 = (f32[4,1792]{1,0:T(4,128)S(1)}, f32[4,1792]{1,0:T(4,128)}, u32[]{:S(2)}) copy-start(f32[4,1792]{1,0:T(4,128)} %copy-done.19) | copy-start | bytes 86020
  354.2 180.6 %copy-start.24 = (f32[1536]{0:T(1024)S(1)}, f32[1536]{0:T(1024)}, u32[]{:S(2)}) copy-start(f32[1536]{0:T(1024)} %get-tuple-element.132) | copy-start | bytes 18436
  531.2 7.4 %copy-start.14 = (bf16[192,3072]{1,0:T(8,128)(2,1)S(1)}, bf16[192,3072]{1,0:T(8,128)(2,1)}, u32[]{:S(2)}) copy-start(bf16[192,3072]{1,0:T(8,128)(2,1)} %get-tuple-element.83) | copy-start | bytes 3538948
  533.0 7.3 %collective-permute-start.11 = (bf16[3,3,1792]{2,1,0:T(4,128)(2,1)S(1)}, bf16[3,3,1792]{2,1,0:T(4,128)(2,1)S(1)}, u32[]{:S(2)}, u32[]{:S(2)}) collective-permute-start(bf16[3,3,1792]{2,1,0:T(4,128)(2,1)S(1)} %pad_maximum_fusion.8), channel_id=1, source_target_pairs={{1,0},{3,2},{5,4},{7,6},{8,1},{9,8},{10,3},{11,10},{12,5},{13,12},... | collective-permute-start | bytes 96776 | tf_op jit(solution)/shard_map/ppermute | solution.py:1154
  534.8 5.6 copy-start.25
  538.6 28.8 %slice-start = ((s8[4718592]{0:T(1024)(128)(4,1)}), s8[4194304]{0:T(1024)(128)(4,1)S(1)}, s32[]{:S(2)}) async-start(s8[4718592]{0:T(1024)(128)(4,1)} %bitcast.135), calls=%async_computation.2 | async-start | bytes 8388608
  538.6 28.8 %slice-start.4 = ((s8[4718592]{0:T(1024)(128)(4,1)}), s8[524288]{0:T(1024)(128)(4,1)S(1)}, s32[]{:S(2)}) async-start(s8[4718592]{0:T(1024)(128)(4,1)} %bitcast.169), calls=%async_computation.6 | async-start | bytes 1048576
  540.3 15.1 %slice-start.2 = ((s8[4718592]{0:T(1024)(128)(4,1)}), s8[4194304]{0:T(1024)(128)(4,1)S(1)}, s32[]{:S(2)}) async-start(s8[4718592]{0:T(1024)(128)(4,1)} %bitcast.140), calls=%async_computation.4 | async-start | bytes 8388608
  540.6 14.8 %slice-start.3 = ((s8[4718592]{0:T(1024)(128)(4,1)}), s8[524288]{0:T(1024)(128)(4,1)S(1)}, s32[]{:S(2)}) async-start(s8[4718592]{0:T(1024)(128)(4,1)} %bitcast.140), calls=%async_computation.5 | async-start | bytes 1048576
  540.6 26.8 %slice-start.1 = ((s8[4718592]{0:T(1024)(128)(4,1)}), s8[524288]{0:T(1024)(128)(4,1)S(1)}, s32[]{:S(2)}) async-start(s8[4718592]{0:T(1024)(128)(4,1)} %bitcast.135), calls=%async_computation.3 | async-start | bytes 1048576
  540.6 26.8 %slice-start.5 = ((s8[4718592]{0:T(1024)(128)(4,1)}), s8[4194304]{0:T(1024)(128)(4,1)S(1)}, s32[]{:S(2)}) async-start(s8[4718592]{0:T(1024)(128)(4,1)} %bitcast.169), calls=%async_computation.7 | async-start | bytes 8388608
  555.4 12.0 %copy-start.23 = (f32[1536]{0:T(1024)S(1)}, f32[1536]{0:T(1024)}, u32[]{:S(2)}) copy-start(f32[1536]{0:T(1024)} %copy-done.22) | copy-start | bytes 18436
  581.8 115.4 %copy-start.1 = (bf16[6,128,1536]{2,1,0:T(8,128)(2,1)S(1)}, bf16[6,128,1536]{2,1,0:T(8,128)(2,1)}, u32[]{:S(2)}) copy-start(bf16[6,128,1536]{2,1,0:T(8,128)(2,1)} %hidden.1) | copy-start | bytes 7077892
  581.8 115.4 %copy-start.18 = (f32[1536]{0:T(1024)S(1)}, f32[1536]{0:T(1024)}, u32[]{:S(2)}) copy-start(f32[1536]{0:T(1024)} %copy-done.17) | copy-start | bytes 18436
  581.8 115.4 %copy-start.21 = (f32[6,128]{1,0:T(8,128)S(1)}, f32[6,128]{1,0:T(8,128)}, u32[]{:S(2)}) copy-start(f32[6,128]{1,0:T(8,128)} %add_rsqrt_fusion.2) | copy-start | bytes 9220
  700.6 8.0 %copy-start.13 = (f32[192,3072]{1,0:T(8,128)S(1)}, f32[192,3072]{1,0:T(8,128)}, u32[]{:S(2)}) copy-start(f32[192,3072]{1,0:T(8,128)} %get-tuple-element.209) | copy-start | bytes 7077892
  706.7 3.3 copy-start.16
Sparse Core Ops, SparseCore 0:
  145.5 69.4 all-gather.2
  216.9 63.4 all-gather.4

commit v4 on v3

--- a/solution.py
+++ b/solution.py
@@ -13,7 +13,9 @@
 CHUNK = 128
 LANES = 128
 PER_UNIT = 4
-VMEM_LIMIT = 56 * 1024 * 1024
+VMEM_LIMIT = 24 * 1024 * 1024
+TAIL_LIMIT = 44 * 1024 * 1024
+MIDDLE_LIMIT = 55 * 1024 * 1024
 
 
 def dot(a, b):
@@ -64,22 +66,32 @@
     return total
 
 
+def step_of(dt_ref, hp_ref):
+    shifted = dt_ref[...].astype(F32) + hp_ref[1:2]
+    return shifted, jnp.maximum(shifted, 0.0) + jnp.log1p(jnp.exp(-jnp.abs(shifted)))
+
+
 def forward_kernel(
-    x_ref, xp_ref, bc_ref, bcp_ref, step_ref, cx_ref, cbc_ref, hp_ref,
+    x_ref, bc_ref, dt_ref, halo_ref, cx_ref, cbc_ref, hp_ref,
     y_ref, st_ref, own_ref, dec_ref, bcs_ref, acum_ref,
     xe, be, state, base,
 ):
-    chunk = pl.program_id(1)
+    unit, chunk = pl.program_id(0), pl.program_id(1)
     inner = x_ref.shape[1]
 
     @pl.when(chunk == 0)
     def _():
         state[...] = jnp.zeros_like(state)
         base[...] = jnp.zeros_like(base)
-
-    xe[0:8] = xp_ref[0]
+        xe[0:8] = halo_ref[unit, :, :inner].astype(F32)[8:]
+        be[0:8] = halo_ref[unit, :, inner:].astype(F32)[8:]
+
+    @pl.when(chunk != 0)
+    def _():
+        xe[0:8] = xe[CHUNK:]
+        be[0:8] = be[CHUNK:]
+
     xe[8:] = x_ref[...].astype(F32)
-    be[0:8] = bcp_ref[0]
     be[8:] = bc_ref[...].astype(F32)
     shared = []
     for k in range(2):
@@ -92,7 +104,7 @@
     keys, reads = keys.astype(BF16), reads.astype(BF16)
     rows, columns = grid_iotas()
     causal = rows >= columns
-    step = step_ref[...]
+    _, step = step_of(dt_ref, hp_ref)
     running = exact_left(jnp.where(causal, 1.0, 0.0).astype(BF16), -step * hp_ref[0:1])
     acum_ref[...] = base[0:1] + running
     total = running[CHUNK - 1 : CHUNK]
@@ -196,7 +208,7 @@
 
 
 def backward_kernel(
-    x_ref, xp_ref, bc_ref, bcp_ref, step_ref, sig_ref, cx_ref, cbc_ref, hp_ref,
+    x_ref, xp_ref, bc_ref, bcp_ref, dt_ref, halo_ref, cx_ref, cbc_ref, hp_ref,
     dy_ref, y_ref, st_ref, in_ref, acum_ref, after_ref, pick_ref,
     dall_ref, head_ref, head_bc_ref, gx_ref, gbc_ref, gh_ref,
     xe, be, adjoint, dpx, dpb, ends, place=None,
@@ -216,9 +228,10 @@
         dpx[CHUNK:] = jnp.zeros((8, inner), F32)
         dpb[CHUNK:] = jnp.zeros((8, 2 * LANES), F32)
 
-    xe[0:8] = xp_ref[0]
+    inside = chunk != PER_UNIT - 1
+    xe[0:8] = jnp.where(inside, xp_ref[...].astype(F32)[8:], halo_ref[unit, :, :inner].astype(F32)[8:])
     xe[8:] = x_ref[...].astype(F32)
-    be[0:8] = bcp_ref[0]
+    be[0:8] = jnp.where(inside, bcp_ref[...].astype(F32)[8:], halo_ref[unit, :, inner:].astype(F32)[8:])
     be[8:] = bc_ref[...].astype(F32)
     shared, slopes = [], []
     for k in range(2):
@@ -231,7 +244,7 @@
     keys, reads = keys.astype(BF16), reads.astype(BF16)
     rows, columns = grid_iotas()
     causal = rows >= columns
-    step = step_ref[...]
+    shifted_dt, step = step_of(dt_ref, hp_ref)
     rate = hp_ref[0:1]
     log_decay = -step * rate
     running = exact_left(jnp.where(causal, 1.0, 0.0).astype(BF16), log_decay)
@@ -335,7 +348,7 @@
     at_end = exact_right(ends[...], pick_ref[...])[0:1]
     d_log = exact_left(jnp.where(rows <= columns, 1.0, 0.0).astype(BF16), sums[:CHUNK]) + at_end
     d_step = sums[CHUNK : 2 * CHUNK] - d_log * rate
-    d_dt = d_step * sig_ref[...]
+    d_dt = d_step * sigmoid(shifted_dt)
     dall_ref[:, inner + 2 * LANES :] = d_dt.astype(BF16)
     for k, part in enumerate((d_dt, d_log * log_decay, sums[2 * CHUNK :])):
         gh_ref[8 * k : 8 * k + 8] += jnp.sum(part.reshape(CHUNK // 8, 8, LANES), axis=0)
@@ -349,9 +362,12 @@
 
 
 def exchange_kernel(
-    count, joints, back, own_ref, dec_ref, out_ref, dec_out_ref,
+    own_ref, dec_ref, cot, near_ref, far_ref, out_ref, dec_out_ref, rows_out,
     parts, decs, results, sends, receives, dec_sends, dec_receives, back_sends, back_receives,
+    row_sends, row_receives, local,
 ):
+    count, joints, back = 8, 2, False
+    trade = Trade(cot, row_sends, row_receives)
     f, z = lax.axis_index("fs"), lax.axis_index("sp")
     core, group = f % 2, z // joints
     me = (f // 2) * joints + z % joints
@@ -364,7 +380,21 @@
     barrier = pltpu.get_barrier_semaphore()
     for k in range(1, count):
         pl.semaphore_signal(barrier, inc=1, device_id=peer(k)[1], device_id_type=MESH)
-    pl.semaphore_wait(barrier, count - 1)
+    for device in (trade.partner, trade.far):
+        pl.semaphore_signal(barrier, inc=1, device_id=device, device_id_type=MESH)
+    pl.semaphore_wait(barrier, count + 1)
+    early = far_ref.shape[0]
+    near_at, far_at = trade.near_at, trade.far_at
+    last = trade.send(trade.rows_for(trade.far_group, early, units), rows_out.at[early:, z], 0, trade.far)
+    last.start()
+    near_on = trade.send(near_ref, rows_out.at[:, near_at], 1, trade.partner)
+    near_on.start()
+    far_on = trade.send(far_ref, rows_out.at[:early, far_at], 2, trade.partner)
+    far_on.start()
+    near_keep = pltpu.make_async_copy(near_ref, rows_out.at[:, near_at], local.at[0])
+    near_keep.start()
+    far_keep = pltpu.make_async_copy(far_ref, rows_out.at[:early, far_at], local.at[1])
+    far_keep.start()
 
     def rows_of(i):
         return pl.ds(pl.multiple_of(i * share, share), share)
@@ -425,6 +455,9 @@
     out_ref[:, rows_of(me)] = results[me]
     for k in range(1, count):
         back_copy(k).start()
+    trade.send(trade.rows_for(trade.far_group, early, units), rows_out.at[early:, far_at], 0, trade.far).wait_recv()
+    last_on = trade.send(rows_out.at[early:, far_at], rows_out.at[early:, far_at], 3, trade.partner)
+    last_on.start()
     for k in range(1, count):
         other = (me + k) % count
         pltpu.make_async_remote_copy(
@@ -437,6 +470,14 @@
             dec_copy(k).wait_send()
         out_copy(k).wait_send()
         back_copy(k).wait_send()
+    other_near, other_far = trade.swapped(near_at), trade.swapped(far_at)
+    trade.send(near_ref, rows_out.at[:, other_near], 1, trade.partner).wait_recv()
+    trade.send(far_ref, rows_out.at[:early, other_far], 2, trade.partner).wait_recv()
+    trade.send(rows_out.at[early:, far_at], rows_out.at[early:, other_far], 3, trade.partner).wait_recv()
+    for copy in (last, near_on, far_on, last_on):
+        copy.wait_send()
+    near_keep.wait()
+    far_keep.wait()
 
 
 def places():
@@ -453,16 +494,131 @@
     )
 
 
+class Trade:
+    def __init__(self, source, sends, receives):
+        self.f, self.z, self.core, self.chip, _, _ = places()
+        self.source, self.sends, self.receives = source, sends, receives
+        self.units = source.shape[0] // 2
+        self.near_group, self.far_group = self.z // 2, 1 - self.z // 2
+        across = 2 * self.chip + self.z % 2
+        self.near, self.far = (across, 2 * self.near_group + self.core), (across, 2 * self.far_group + self.core)
+        self.near_at, self.far_at = 2 * self.near_group + self.core, 2 * self.far_group + self.core
+        self.partner = (self.f + 1 - 2 * self.core, self.z)
+        self.stays = self.z % 2 == self.core
+        self.moves = (self.z + self.core) % 2
+
+    def rows_for(self, group, first, last):
+        return self.source.at[pl.ds(group * self.units + first, last - first)]
+
+    def swapped(self, at):
+        return at + 1 - 2 * (at % 2)
+
+    def send(self, src, dst, slot, device):
+        return remote(src, dst, self.sends, self.receives, slot, device)
+
+
+EARLY_UNITS = 2
+
+
+def scan_forward_kernel(
+    x, bc, dt, first, cot, cx, cbc, hp,
+    y, st, own, dec, bcs, acum, halo_out, near_out, far_out,
+    xe, be, state, base, halo, halo_sends, halo_receives, sends, receives, local,
+):
+    unit, chunk = pl.program_id(0), pl.program_id(1)
+    segments, trade = Segments(), Trade(cot, sends, receives)
+    me, last = segments.me, segments.count - 1
+    units, depth, width = halo.shape
+
+    def halo_copy():
+        at = pl.ds(first.shape[1] - depth, depth)
+        device = segments.device((me + 1) % segments.count)
+        return remote(first.at[:, at, pl.ds(0, width)], halo, halo_sends, halo_receives, 0, device)
+
+    far_copy = trade.send(trade.rows_for(trade.far_group, 0, EARLY_UNITS), far_out, 0, trade.far)
+    near_copy = trade.send(trade.rows_for(trade.near_group, 0, units), near_out, 1, trade.near)
+    keep = pltpu.make_async_copy(trade.rows_for(trade.near_group, 0, units), near_out, local.at[0])
+
+    @pl.when((unit == 0) & (chunk == 0))
+    def _():
+        barrier = pltpu.get_barrier_semaphore()
+        pl.semaphore_signal(barrier, inc=1, device_id=trade.far, device_id_type=MESH)
+
+        @pl.when(jnp.logical_not(trade.stays))
+        def _():
+            pl.semaphore_signal(barrier, inc=1, device_id=trade.near, device_id_type=MESH)
+
+        @pl.when(me > 0)
+        def _():
+            pl.semaphore_signal(
+                barrier, inc=1, device_id=segments.device((me + last) % segments.count), device_id_type=MESH
+            )
+
+        pl.semaphore_wait(barrier, 1 + trade.moves + jnp.where(me < last, 1, 0))
+
+        @pl.when(me < last)
+        def _():
+            halo_copy().start()
+
+        far_copy.start()
+
+        @pl.when(trade.stays)
+        def _():
+            keep.start()
+
+        @pl.when(jnp.logical_not(trade.stays))
+        def _():
+            near_copy.start()
+
+        @pl.when(me > 0)
+        def _():
+            halo_copy().wait_recv()
+
+        @pl.when(me == 0)
+        def _():
+            halo[...] = jnp.zeros_like(halo)
+
+        halo_out[...] = halo[...]
+
+    forward_kernel(x, bc, dt, halo, cx, cbc, hp, y, st, own, dec, bcs, acum, xe, be, state, base)
+
+    @pl.when((unit == units - 1) & (chunk == PER_UNIT - 1))
+    def _():
+        @pl.when(me < last)
+        def _():
+            halo_copy().wait_send()
+
+        far_copy.wait()
+
+        @pl.when(trade.stays)
+        def _():
+            keep.wait()
+
+        @pl.when(jnp.logical_not(trade.stays))
+        def _():
+            near_copy.wait()
+
+
+def one_hot(rows, columns, offset):
+    i = lax.broadcasted_iota(jnp.int32, (rows, columns), 0)
+    j = lax.broadcasted_iota(jnp.int32, (rows, columns), 1)
+    return jnp.where(j == i + offset, 1.0, 0.0).astype(BF16)
+
+
+SMALL_ROWS = 32
+
+
 def head_kernel(
-    hidden, mine, other, small, rows_out, first_out, small_out, local, sends, receives, small_sends, small_receives
+    hidden, w_x, w_bc, w_dt, conv_x, conv_x_bias, gate_gain, norm_gain, conv_bc, conv_bc_bias, dt_bias, a_log, skip_d,
+    rows_out, first_out, cx, cbc, hp, gain_in, gain_rows,
+    dt_mine, dt_other, small, small_all, local, sends, receives, small_sends, small_receives,
 ):
     f, z, core, chip, by_x, by_y = places()
-    units = rows_out.shape[0]
-    partner, over_x, over_y = (f + 1 - 2 * core, z), (2 * by_x + core, z), (2 * by_y + core, z)
-    near_group, far_group = z // 2, 1 - z // 2
-    near, far = (2 * chip + z % 2, 2 * near_group + core), (2 * chip + z % 2, 2 * far_group + core)
-    stays = z % 2 == core
-    shards = small_out.shape[0]
+    trade = Trade(hidden, sends, receives)
+    partner, over_x, over_y = trade.partner, (2 * by_x + core, z), (2 * by_y + core, z)
+    far, near, stays = trade.far, trade.near, trade.stays
+    units, inner, shards = rows_out.shape[0], cx.shape[1], small_all.shape[0]
+    heads = w_dt.shape[1] // 2
 
     barrier = pltpu.get_barrier_semaphore()
     for k in range(1, shards):
@@ -473,10 +629,7 @@
     def _():
         pl.semaphore_signal(barrier, inc=1, device_id=near, device_id_type=MESH)
 
-    pl.semaphore_wait(barrier, shards + (z + core) % 2)
-
-    def group_of(g):
-        return hidden.at[pl.ds(g * units, units)]
+    pl.semaphore_wait(barrier, shards + trade.moves)
 
     def part(chip_at, core_at):
         return first_out.at[chip_at, core_at]
@@ -484,16 +637,37 @@
     def copy(src, dst, slot, device):
         return remote(src, dst, sends, receives, slot, device)
 
-    to_far = copy(group_of(far_group), rows_out.at[:, z], 0, far)
+    class Thirds:
+        def __init__(self, side, slot, device):
+            columns = pl.ds(pl.multiple_of(side * inner, inner), inner)
+            self.whole = copy(part(chip, core), part(chip, core), slot, device)
+            dst, wide = part(chip, core), 2 * LANES
+            dt = dt_mine if device is not partner else dt_other
+            self.copies = [
+                copy(w_x.at[:, columns], dst.at[:, pl.ds(0, inner)], slot, device),
+                copy(w_bc, dst.at[:, pl.ds(inner, wide)], slot, device),
+                copy(dt, dst.at[:, pl.ds(inner + wide, LANES)], slot, device),
+            ]
+
+        def start(self):
+            for one in self.copies:
+                one.start()
+
+        def wait_send(self):
+            self.whole.wait_send()
+
+    to_far = copy(trade.rows_for(trade.far_group, 0, units), rows_out.at[:, z], 0, far)
     to_far.start()
-    to_partner = copy(other, part(chip, core), 1, partner)
-    to_partner.start()
-    to_x = copy(mine, part(chip, core), 2, over_x)
-    to_x.start()
-    to_y = copy(mine, part(chip, core), 3, over_y)
-    to_y.start()
-    to_near = copy(group_of(near_group), rows_out.at[:, z], 4, near)
-    keep_rows = pltpu.make_async_copy(group_of(near_group), rows_out.at[:, z], local.at[0])
+    i = lax.broadcasted_iota(jnp.int32, (2 * heads, LANES), 0)
+    j = lax.broadcasted_iota(jnp.int32, (2 * heads, LANES), 1)
+    for side, kept in ((core, dt_mine), (1 - core, dt_other)):
+        chosen = jnp.where((i == j + side * heads) & (j < heads), 1.0, 0.0).astype(BF16)
+        kept[...] = dot(w_dt[...], chosen).astype(BF16)
+    to_partner, to_x, to_y = Thirds(1 - core, 1, partner), Thirds(core, 2, over_x), Thirds(core, 3, over_y)
+    for one in (to_partner, to_x, to_y):
+        one.start()
+    to_near = copy(trade.rows_for(trade.near_group, 0, units), rows_out.at[:, z], 4, near)
+    keep_rows = pltpu.make_async_copy(trade.rows_for(trade.near_group, 0, units), rows_out.at[:, z], local.at[0])
 
     @pl.when(stays)
     def _():
@@ -503,29 +677,56 @@
     def _():
         to_near.start()
 
-    keep_first = pltpu.make_async_copy(mine, part(chip, core), local.at[1])
-    keep_first.start()
-    keep_small = pltpu.make_async_copy(small, small_out.at[f], local.at[2])
-    keep_small.start()
+    own = part(chip, core)
+    keeps = [
+        pltpu.make_async_copy(
+            w_x.at[:, pl.ds(pl.multiple_of(core * inner, inner), inner)], own.at[:, pl.ds(0, inner)], local.at[1]
+        ),
+        pltpu.make_async_copy(w_bc, own.at[:, pl.ds(inner, 2 * LANES)], local.at[2]),
+        pltpu.make_async_copy(dt_mine, own.at[:, pl.ds(inner + 2 * LANES, LANES)], local.at[3]),
+    ]
+    for keep in keeps:
+        keep.start()
+
+    share = conv_x.shape[0]
+    per_norm, per_bc, per_head = norm_gain.shape[1], conv_bc.shape[0], dt_bias.shape[1]
+    built = jnp.zeros((SMALL_ROWS, share), F32)
+    taps = dot_tn(conv_x[...], one_hot(share, share, 0))
+    gains = dot(norm_gain[...], one_hot(per_norm, share, per_norm * (f % 2)))
+    spread_bc = one_hot(per_bc, 2 * LANES, per_bc * f)
+    taps_bc, bias_bc = dot_tn(conv_bc[...], spread_bc), dot(conv_bc_bias[...], spread_bc)
+    spread_heads = one_hot(per_head, LANES, per_head * (f % 4))
+    by_head = [dot(v[...], spread_heads) for v in (dt_bias, a_log, skip_d)]
+    small[...] = built
+    small[0:4] = taps
+    small[4:5] = conv_x_bias[...].astype(F32)
+    small[5:6] = gate_gain[...].astype(F32)
+    for k in range(4):
+        small[6 + k : 7 + k] = jnp.where(f // 2 == k, gains, 0.0)
+    small[10:14, : 2 * LANES] = taps_bc
+    small[14:15, : 2 * LANES] = bias_bc
+    for side in range(2):
+        for n, values in enumerate(by_head):
+            small[15 + side : 16 + side, n * LANES : (n + 1) * LANES] = jnp.where(f // 4 == side, values, 0.0)
 
     def small_copy(k, at):
         return pltpu.make_async_remote_copy(
-            src_ref=small, dst_ref=small_out.at[at],
+            src_ref=small, dst_ref=small_all.at[at],
             send_sem=small_sends.at[k], recv_sem=small_receives.at[at],
             device_id=((f + k) % shards, z), device_id_type=MESH,
         )
 
     for k in range(1, shards):
         small_copy(k, f).start()
-
-    from_partner = copy(other, part(chip, 1 - core), 1, partner)
-    from_partner.wait_recv()
+    small_all[f] = small[...]
+
+    copy(part(chip, core), part(chip, 1 - core), 1, partner).wait_recv()
     again_x = copy(part(chip, 1 - core), part(chip, 1 - core), 5, over_x)
     again_x.start()
     again_y = copy(part(chip, 1 - core), part(chip, 1 - core), 6, over_y)
     again_y.start()
 
-    near_at, far_at = 2 * near_group + core, 2 * far_group + core
+    near_at, far_at = trade.near_at, trade.far_at
 
     @pl.when(stays)
     def _():
@@ -533,31 +734,53 @@
 
     @pl.when(jnp.logical_not(stays))
     def _():
-        copy(group_of(near_group), rows_out.at[:, near_at], 4, near).wait_recv()
+        copy(trade.rows_for(trade.near_group, 0, units), rows_out.at[:, near_at], 4, near).wait_recv()
 
     near_on = copy(rows_out.at[:, near_at], rows_out.at[:, near_at], 7, partner)
     near_on.start()
 
-    copy(mine, part(by_x, core), 2, over_x).wait_recv()
+    for k in range(1, shards):
+        small_copy(k, (f + k) % shards).wait_recv()
+    cx[...] = jnp.zeros_like(cx)
+    for k in range(4):
+        block = small_all[4 * core + k]
+        lanes = slice(k * share, (k + 1) * share)
+        cx[0:5, lanes] = block[0:5]
+        gain_rows[:, lanes] = jnp.broadcast_to(block[5:6], (8, share))
+    summed = small_all[0]
+    for k in range(1, shards):
+        summed = summed + small_all[k]
+    for k in range(4):
+        gain_in[:, k * share : (k + 1) * share] = jnp.broadcast_to(summed[6 + k : 7 + k], (8, share))
+    cbc[...] = jnp.zeros_like(cbc)
+    cbc[0:5] = summed[10:15, : 2 * LANES]
+    ours = jnp.where(core == 0, summed[15:16], summed[16:17])
+    lane = lax.broadcasted_iota(jnp.int32, (1, LANES), 1)
+    hp[...] = jnp.zeros_like(hp)
+    hp[0:1] = jnp.where(lane < heads, jnp.exp(ours[:, LANES : 2 * LANES]), 0.0)
+    hp[1:2] = ours[:, :LANES]
+    skips = ours[:, 2 * LANES :]
+    for pair in range(inner // LANES):
+        cx[5:6, pair * LANES : (pair + 1) * LANES] = two_heads(skips, pair, lane < LANES // 2)
+
+    copy(part(by_x, core), part(by_x, core), 2, over_x).wait_recv()
     on_y = copy(part(by_x, core), part(by_x, core), 8, over_y)
     on_y.start()
-    copy(mine, part(by_y, core), 3, over_y).wait_recv()
-    copy(mine, part(by_x, 1 - core), 5, over_x).wait_recv()
-    copy(mine, part(by_y, 1 - core), 6, over_y).wait_recv()
+    copy(part(by_y, core), part(by_y, core), 3, over_y).wait_recv()
+    copy(part(by_x, 1 - core), part(by_x, 1 - core), 5, over_x).wait_recv()
+    copy(part(by_y, 1 - core), part(by_y, 1 - core), 6, over_y).wait_recv()
     on_x = copy(part(by_y, 1 - core), part(by_y, 1 - core), 9, over_x)
     on_x.start()
 
-    copy(group_of(far_group), rows_out.at[:, far_at], 0, far).wait_recv()
+    copy(trade.rows_for(trade.far_group, 0, units), rows_out.at[:, far_at], 0, far).wait_recv()
     far_on = copy(rows_out.at[:, far_at], rows_out.at[:, far_at], 10, partner)
     far_on.start()
 
     corner = (by_x + 2) % 4
-    for k in range(1, shards):
-        small_copy(k, (f + k) % shards).wait_recv()
-    copy(mine, part(corner, core), 8, over_y).wait_recv()
-    copy(mine, part(corner, 1 - core), 9, over_x).wait_recv()
-    copy(rows_out.at[:, near_at], rows_out.at[:, 2 * near_group + 1 - core], 7, partner).wait_recv()
-    copy(rows_out.at[:, far_at], rows_out.at[:, 2 * far_group + 1 - core], 10, partner).wait_recv()
+    copy(part(corner, core), part(corner, core), 8, over_y).wait_recv()
+    copy(part(corner, 1 - core), part(corner, 1 - core), 9, over_x).wait_recv()
+    copy(rows_out.at[:, near_at], rows_out.at[:, trade.swapped(near_at)], 7, partner).wait_recv()
+    copy(rows_out.at[:, far_at], rows_out.at[:, trade.swapped(far_at)], 10, partner).wait_recv()
     for sent in (to_far, to_partner, to_x, to_y, again_x, again_y, near_on, on_y, on_x, far_on):
         sent.wait_send()
 
@@ -567,8 +790,8 @@
 
     for k in range(1, shards):
         small_copy(k, f).wait_send()
-    keep_first.wait()
-    keep_small.wait()
+    for keep in keeps:
+        keep.wait()
 
 
 class Reduction:
@@ -924,18 +1147,21 @@
         self.me = self.chip * 2 + self.z % 2
         self.count = 8
 
+    def device(self, i):
+        return ((i // 2) * 2 + self.core, self.group * 2 + i % 2)
+
     def peer(self, k):
         other = (self.me + k) % self.count
-        return other, ((other // 2) * 2 + self.core, self.group * 2 + other % 2)
+        return other, self.device(other)
 
 
 def middle_kernel(
     dno, gated, gate, y_pull, stats, gain, bcs, acum_pull, decays, normed, g_out, came_left, came_right, projected,
-    x, xp, bc, bcp, step, sig, cx, cbc, hp, y, st, incoming, acum, pick,
+    x, xp, bc, bcp, dt, halo, cx, cbc, hp, y, st, incoming, acum, pick,
     d_all, heads_x, heads_bc, g_x, g_bc, g_heads, d_gate_out, tokens_out, total_out, z_out,
-    dy_all, dgate_all, pulled, own, after, parts, results, blocks, g_z, out_own, out_passed,
-    o_r1, o_s2, o_r2, o_sp, o_rp, o_total, o_came, o_sums, o_across, o_last,
-    z_r1, z_s2, z_r2, z_sp, z_rp, z_total, z_came, z_sums, z_across, z_last,
+    dy_all, dgate_all, pulled, own, after, parts, results, blocks, g_z, out_own,
+    o_r1, o_s2, o_r2, o_sp, o_rp, o_total, o_came, o_sums, o_across, o_last, o_final,
+    z_rp, z_total, z_came, z_sums, z_across, z_last, z_final,
     xe, be, adjoint, dpx, dpb, ends,
     local, block_sems, trade_local, trade_sends, trade_receives, sends, receives,
     state_sends, state_receives, back_sends, back_receives,
@@ -961,7 +1187,7 @@
     out.over_chips(
         None,
         lambda side, columns: out_own[at(side, half), columns],
-        lambda k, columns: out_passed[:, columns],
+        lambda k, columns: o_s2[:, columns],
         o_r1, o_s2, o_r2, o_sp, o_rp, o_total,
     )
 
@@ -973,25 +1199,27 @@
 
         return store
 
-    out.over_members(o_total, o_came, o_sums, o_across, o_last, store_to(total_out))
+    out.over_members(o_total, o_came, o_sums, o_across, o_last, store_to(o_final))
     gz.over_chips(
         lambda k, columns: g_z.at[at(k, rows), columns],
         lambda side, columns: g_z[pl.ds(pl.multiple_of(chip * rows + side * half, half), half), columns],
         lambda k, columns: g_z[at(k, rows), columns],
-        z_r1, z_s2, z_r2, z_sp, z_rp, z_total,
+        o_r1, o_s2, o_r2, o_sp, z_rp, z_total,
     )
-    gz.over_members(z_total, z_came, z_sums, z_across, z_last, store_to(z_out))
+    gz.over_members(z_total, z_came, z_sums, z_across, z_last, store_to(z_final))
     left, right = (pl.ds(start, width) for start, width, _ in HALF_PIECES)
     own_rows = pltpu.make_async_copy(g_out.at[at(chip, rows)], out_own, local.at[0])
-    pass_left = pltpu.make_async_copy(g_out.at[at(by_y, rows), left], out_passed.at[:, left], local.at[1])
-    pass_right = pltpu.make_async_copy(g_out.at[at(by_x, rows), right], out_passed.at[:, right], local.at[2])
+    pass_left = pltpu.make_async_copy(g_out.at[at(by_y, rows), left], o_s2.at[:, left], local.at[1])
+    pass_right = pltpu.make_async_copy(g_out.at[at(by_x, rows), right], o_s2.at[:, right], local.at[2])
     keep_gate = pltpu.make_async_copy(dgate_all, d_gate_out, local.at[3])
     take_left = pltpu.make_async_copy(came_left, o_r1.at[:, :, left], local.at[4])
     take_right = pltpu.make_async_copy(came_right, o_r1.at[:, :, right], local.at[5])
+    keep_out = pltpu.make_async_copy(o_final, total_out, local.at[6])
+    keep_z = pltpu.make_async_copy(z_final, z_out, local.at[7])
     taken = (own_rows, pass_left, pass_right, take_left, take_right)
 
     def fetch(k):
-        columns = pl.ds(k * rows, rows) if isinstance(k, int) else at(k, rows)
+        columns = pl.ds(k * 256, 256)
         return pltpu.make_async_copy(normed.at[:, columns], blocks.at[k % 2], block_sems.at[k % 2])
 
     @pl.when(i == 0)
@@ -1051,14 +1279,14 @@
         )
 
     def multiply(k):
-        if k < 3:
+        if k < 5:
             fetch(k + 1).start()
         fetch(k).wait()
 
         def part(n, carry):
             columns = pl.ds(pl.multiple_of(n * 256, 256), 256)
             product = dot_tn(blocks[k % 2], dgate_all[:, columns])
-            g_z[pl.ds(k * rows, rows), columns] = product.astype(BF16)
+            g_z[pl.ds(k * 256, 256), columns] = product.astype(BF16)
             return carry
 
         lax.fori_loop(0, inner // 256, part, 0)
@@ -1070,8 +1298,8 @@
         fetch(0).start()
         keep_gate.start()
         parts[me] = own[:, at(me, share)]
-        multiply(0)
-        multiply(1)
+        for k in range(3):
+            multiply(k)
         for piece in out.pieces:
             out.after_pair(piece)
         for k in range(1, count):
@@ -1084,11 +1312,12 @@
         after[:, at(me, share)] = results[me]
         for k in range(1, count):
             back_copy(k, True).start()
-        multiply(2)
-        multiply(3)
-        gz.start()
+        for k in range(3, 6):
+            multiply(k)
         for k in range(1, count):
             back_copy(k, False).wait_recv()
+        out.drain_chips()
+        gz.start()
         for k in range(1, count):
             state_copy(k, True).wait_send()
             back_copy(k, True).wait_send()
@@ -1108,7 +1337,7 @@
         unit, chunk = n // PER_UNIT, n % PER_UNIT
         place = at(unit * PER_UNIT + PER_UNIT - 1 - chunk, CHUNK)
         backward_kernel(
-            x, xp, bc, bcp, step, sig, cx, cbc, hp, dy_all.at[place], y, st, incoming, acum,
+            x, xp, bc, bcp, dt, halo, cx, cbc, hp, dy_all.at[place], y, st, incoming, acum,
             after.at[pl.ds(unit, 1)], pick, d_all, heads_x, heads_bc, g_x, g_bc, g_heads,
             xe, be, adjoint, dpx, dpb, ends, place=(unit, chunk),
         )
@@ -1123,14 +1352,17 @@
     @pl.when(i == 2 * chunks)
     def _():
         finish_trade()
-        out.drain_chips()
         out.drain_members()
+        keep_out.start()
         gz.drain_chips()
         for stage in (gz.after_far, gz.after_last):
             for piece in gz.pieces:
                 stage(piece)
+        keep_z.start()
         gz.drain_members()
         keep_gate.wait()
+        keep_out.wait()
+        keep_z.wait()
 
 
 class Plan:
@@ -1177,36 +1409,38 @@
         first = self.core == 0
         return jnp.where(first, mine, other), jnp.where(first, other, mine)
 
-    def head(self, hidden, mine, other, small):
-        if not self.fast:
-            both = jnp.concatenate(self.by_core(mine, self.swap(other, df=1)), axis=0)
-            return self.to_units(hidden), self.gather(both), lax.all_gather(small, "fs")
-        anywhere = pl.BlockSpec(memory_space=pl.ANY)
-        rows, first, everyone = pl.pallas_call(
+    def head(self, hidden, w_x, w_bc, w_dt, conv_x, conv_bc, *vectors):
+        anywhere, vmem = pl.BlockSpec(memory_space=pl.ANY), pl.BlockSpec(memory_space=pltpu.VMEM)
+        conv_x_bias, gate_gain, norm_gain, conv_bc_bias, dt_bias, a_log, skip_d = (v[None] for v in vectors)
+        rows, inner = w_x.shape[0], w_x.shape[1] // 2
+        small = (SMALL_ROWS, conv_x.shape[0])
+        dma = pltpu.SemaphoreType.DMA
+        shape = jax.ShapeDtypeStruct
+        units, first, *params = pl.pallas_call(
             head_kernel,
             out_shape=[
-                jax.ShapeDtypeStruct((self.units, 4, self.tokens, hidden.shape[-1]), BF16),
-                jax.ShapeDtypeStruct((4, 2) + mine.shape, BF16),
-                jax.ShapeDtypeStruct((self.shards,) + small.shape, BF16),
+                shape((self.units, 4, self.tokens, hidden.shape[-1]), BF16),
+                shape((4, 2, rows, inner + 3 * LANES), BF16),
+                shape((8, inner), F32), shape((8, 2 * LANES), F32), shape((8, LANES), F32),
+                shape((8, hidden.shape[-1]), F32), shape((8, inner), F32),
             ],
-            in_specs=[anywhere] * 4,
-            out_specs=[anywhere] * 3,
+            in_specs=[anywhere] * 3 + [vmem] * 10,
+            out_specs=[anywhere] * 2 + [vmem] * 5,
             scratch_shapes=[
-                pltpu.SemaphoreType.DMA((3,)),
-                pltpu.SemaphoreType.DMA((11,)),
-                pltpu.SemaphoreType.DMA((11,)),
-                pltpu.SemaphoreType.DMA((self.shards,)),
-                pltpu.SemaphoreType.DMA((self.shards,)),
+                pltpu.VMEM((rows, LANES), BF16), pltpu.VMEM((rows, LANES), BF16),
+                pltpu.VMEM(small, F32), pltpu.VMEM((self.shards,) + small, F32),
+                dma((4,)), dma((11,)), dma((11,)), dma((self.shards,)), dma((self.shards,)),
             ],
-            compiler_params=pltpu.CompilerParams(collective_id=2, has_side_effects=True),
+            compiler_params=pltpu.CompilerParams(
+                collective_id=2, has_side_effects=True, vmem_limit_bytes=VMEM_LIMIT
+            ),
             cost_estimate=cost(55),
             name="head",
-        )(hidden, mine, other, small)
-        return (
-            rows.reshape(-1, rows.shape[-1]),
-            first.reshape(-1, first.shape[-1]),
-            everyone,
-        )
+        )(
+            hidden, w_x, w_bc, w_dt, conv_x, conv_x_bias, gate_gain, norm_gain, conv_bc, conv_bc_bias,
+            dt_bias, a_log, skip_d,
+        )
+        return units.reshape(-1, hidden.shape[-1]), first.reshape(-1, inner + 3 * LANES), *params
 
     def tail(self, g, g_x, g_bc, g_heads, g_gate, g_norm, d_normed):
         rows, inner = g.shape[0] // self.shards, g_x.shape[1]
@@ -1263,7 +1497,7 @@
             + [pltpu.SemaphoreType.DMA((slots,))] * 2
             + [pltpu.SemaphoreType.DMA((5,))] * 2,
             compiler_params=pltpu.CompilerParams(
-                collective_id=3, has_side_effects=True, vmem_limit_bytes=VMEM_LIMIT
+                collective_id=3, has_side_effects=True, vmem_limit_bytes=TAIL_LIMIT
             ),
             cost_estimate=cost(90),
             name="tail",
@@ -1404,47 +1638,46 @@
     )
 
 
-def exchange(plan, own, decays, back):
+def slow_exchange(plan, own, decays, back):
+    count, units = plan.count, own.shape[0]
+    rates, pieces = decays[:units, None], own.astype(F32)
+
+    def hop(_, before):
+        return plan.along((before * rates + pieces).astype(BF16), -1 if back else 1).astype(F32)
+
+    return lax.fori_loop(0, count - 1, hop, jnp.zeros(own.shape, F32)).astype(BF16)
+
+
+def exchange(plan, own, decays, cot, near, far):
     units, depth, width = own.shape
-    count = plan.count
-    if depth % (16 * count):
-        rates, pieces = decays[:units, None], own.astype(F32)
-
-        def hop(_, before):
-            return plan.along((before * rates + pieces).astype(BF16), -1 if back else 1).astype(F32)
-
-        found = lax.fori_loop(0, count - 1, hop, jnp.zeros(own.shape, F32))
-        return found.astype(BF16), decays
-    share = depth // count
+    count, share = plan.count, depth // plan.count
     dec_shape = (count, 8, width)
-    vmem = pl.BlockSpec(memory_space=pltpu.VMEM)
-    scratch = [
-        pltpu.VMEM((count, units, share, width), BF16),
-        pltpu.VMEM(dec_shape, F32),
-        pltpu.VMEM((count, units, share, width), BF16),
-    ] + [pltpu.SemaphoreType.DMA((count,))] * 6
-    out_shape = [jax.ShapeDtypeStruct(own.shape, BF16)]
-    if not back:
-        out_shape.append(jax.ShapeDtypeStruct(dec_shape, F32))
-        kernel = functools.partial(exchange_kernel, count, plan.joints, False)
-    else:
-
-        def kernel(own_ref, dec_ref, out_ref, *rest):
-            exchange_kernel(count, plan.joints, True, own_ref, dec_ref, out_ref, None, *rest)
-
-    outs = pl.pallas_call(
-        kernel,
-        out_shape=out_shape,
-        in_specs=[vmem, vmem],
-        out_specs=[vmem] * len(out_shape),
-        scratch_shapes=scratch,
+    vmem, anywhere = pl.BlockSpec(memory_space=pltpu.VMEM), pl.BlockSpec(memory_space=pl.ANY)
+    dma = pltpu.SemaphoreType.DMA
+    rows_shape = (units, 4, plan.tokens, cot.shape[-1])
+    incoming, all_decays, rows = pl.pallas_call(
+        exchange_kernel,
+        out_shape=[
+            jax.ShapeDtypeStruct(own.shape, BF16),
+            jax.ShapeDtypeStruct(dec_shape, F32),
+            jax.ShapeDtypeStruct(rows_shape, BF16),
+        ],
+        in_specs=[vmem, vmem, anywhere, anywhere, anywhere],
+        out_specs=[vmem, vmem, anywhere],
+        scratch_shapes=[
+            pltpu.VMEM((count, units, share, width), BF16),
+            pltpu.VMEM(dec_shape, F32),
+            pltpu.VMEM((count, units, share, width), BF16),
+        ]
+        + [dma((count,))] * 6
+        + [dma((4,)), dma((4,)), dma((2,))],
         compiler_params=pltpu.CompilerParams(
-            collective_id=1 if back else 0, has_side_effects=True, vmem_limit_bytes=VMEM_LIMIT
+            collective_id=0, has_side_effects=True, vmem_limit_bytes=VMEM_LIMIT
         ),
         cost_estimate=cost(35),
-        name="states_back" if back else "states",
-    )(own, decays)
-    return (outs[0], decays) if back else (outs[0], outs[1])
+        name="states",
+    )(own, decays, cot, near, far)
+    return incoming, all_decays, rows.reshape(-1, cot.shape[-1])
 
 
 def body(
@@ -1465,66 +1698,52 @@
         half = w.shape[1] // 2
         return jnp.where(core == 0, w[:, :half], w[:, half:]), jnp.where(core == 0, w[:, half:], w[:, :half])
 
-    misc = jnp.concatenate([conv_bc_bias, dt_bias, a_log, skip_d])
-    flat = jnp.concatenate(
-        [conv_x.T.reshape(-1), conv_x_bias, gate_gain, norm_gain, conv_bc.T.reshape(-1), misc]
-    )
-    length = flat.shape[0]
-    padded = -(-length // (16 * LANES)) * 16 * LANES
-    flat = jnp.pad(flat, (0, padded - length)).reshape(padded // LANES, LANES)
-
-    x_mine, x_other = halves(w_x)
-    dt_mine, dt_other = halves(w_dt)
     z_mine, z_other = halves(w_z)
     o_mine, o_other = halves(w_out)
-    fill = jnp.zeros((w_dt.shape[0], LANES - heads), BF16)
-    first_mine = jnp.concatenate([x_mine, w_bc, dt_mine, fill], axis=1)
-    first_other = jnp.concatenate([x_other, w_bc, dt_other, fill], axis=1)
 
     def rows_of_chip(mine, other):
         return jnp.concatenate(plan.by_core(mine, plan.swap(other, df=1)), axis=0)
 
-    rows_gate, rows_out = rows_of_chip(z_mine, z_other), rows_of_chip(o_mine, o_other)
-    weight_gate, weight_out = plan.gather(rows_gate), plan.gather(rows_out)
-    hidden_rows, weight_first, everyone = plan.head(hidden, first_mine, first_other, flat)
-    everyone = everyone.reshape(plan.shards, padded).astype(F32)
-
-    parts, start = [], 0
-    for shape in (
-        conv_x.shape[::-1], conv_x_bias.shape, gate_gain.shape, norm_gain.shape, conv_bc.shape[::-1],
-        conv_bc_bias.shape, dt_bias.shape, a_log.shape, skip_d.shape,
-    ):
-        size = shape[0] * (shape[1] if len(shape) > 1 else 1)
-        parts.append(everyone[:, start : start + size].reshape((plan.shards,) + shape))
-        start += size
-    taps_x, bias_x, gain_out, gain_in, taps_bc, bias_bc, shift, rate_log, skip = parts
-    gain_in = gain_in.reshape(-1)
-
-    def mine_of(v):
-        half = v.shape[0] // 2
-        return lax.dynamic_slice_in_dim(v, core * half, half, 0)
-
-    def flat_taps(v):
-        return jnp.moveaxis(v, 0, 1).reshape(v.shape[1], -1)
-
-    bias_x, gain_out, skip_mine = (mine_of(v).reshape(-1) for v in (bias_x, gain_out, skip))
-    shift, rate_log = mine_of(shift).reshape(-1), mine_of(rate_log).reshape(-1)
-    cx = jnp.concatenate(
-        [
-            flat_taps(mine_of(taps_x)), bias_x[None],
-            jnp.repeat(skip_mine, head_size)[None], jnp.zeros((2, inner), F32),
-        ]
-    )
-    cbc = jnp.concatenate(
-        [flat_taps(taps_bc), bias_bc.reshape(1, -1), jnp.zeros((3, bias_bc.size), F32)]
-    )
-    pad_heads = (0, LANES - heads)
-    rate = jnp.pad(jnp.exp(rate_log), pad_heads)
-    hp = jnp.concatenate([rate[None], jnp.zeros((7, LANES), F32)])
+    vectors = (conv_x_bias, gate_gain, norm_gain, conv_bc_bias, dt_bias, a_log, skip_d)
+    if plan.fast:
+        hidden_rows, weight_first, cx, cbc, hp, gain_in, gain_rows = plan.head(
+            hidden, w_x, w_bc, w_dt, conv_x, conv_bc, *vectors
+        )
+        gain_in, gain_out = gain_in[0], gain_rows[0]
+    else:
+        x_mine, x_other = halves(w_x)
+        dt_mine, dt_other = halves(w_dt)
+        fill = jnp.zeros((w_dt.shape[0], LANES - heads), BF16)
+        weight_first = plan.gather(
+            rows_of_chip(
+                jnp.concatenate([x_mine, w_bc, dt_mine, fill], axis=1),
+                jnp.concatenate([x_other, w_bc, dt_other, fill], axis=1),
+            )
+        )
+        hidden_rows, cot_rows = plan.to_units(hidden), plan.to_units(cotangent)
+
+        def whole_of(v):
+            return lax.all_gather(v.astype(F32), "fs", axis=0, tiled=True)
+
+        def mine_of(v):
+            half = v.shape[0] // 2
+            return lax.dynamic_slice_in_dim(v, core * half, half, 0)
+
+        bias_x, gain_out, gain_in, bias_bc, shift, rate_log, skip = (whole_of(v) for v in vectors)
+        taps_x, taps_bc = mine_of(whole_of(conv_x)), whole_of(conv_bc)
+        bias_x, gain_out, skip, shift, rate_log = (
+            mine_of(v) for v in (bias_x, gain_out, skip, shift, rate_log)
+        )
+        nothing = jnp.zeros((2, inner), F32)
+        cx = jnp.concatenate([taps_x.T, bias_x[None], jnp.repeat(skip, head_size)[None], nothing])
+        cbc = jnp.concatenate([taps_bc.T, bias_bc[None], jnp.zeros((3, bias_bc.size), F32)])
+        pad_heads = (0, LANES - heads)
+        hp = jnp.stack([jnp.pad(jnp.exp(rate_log), pad_heads), jnp.pad(shift, pad_heads)])
+        hp = jnp.pad(hp, ((0, 6), (0, 0)))
+        gain_rows = jnp.broadcast_to(gain_out[None], (8, inner))
+    weight_gate = plan.gather(rows_of_chip(z_mine, z_other))
+    weight_out = plan.gather(rows_of_chip(o_mine, o_other))
     pick = (jnp.arange(inner)[:, None] // head_size == jnp.arange(LANES)[None, :]).astype(BF16)
-
-    hidden_rows, cot_late = lax.optimization_barrier((hidden_rows, cotangent))
-    cot_rows = plan.to_units(cot_late)
 
     hidden_rows = hidden_rows.astype(F32)
     scale_in = row_scale(hidden_rows)
@@ -1532,47 +1751,66 @@
     normed = (unit_in * gain_in[None]).astype(BF16)
 
     first = dot(normed, weight_first).astype(BF16)
-    dt_shifted = first[:, inner + 2 * LANES :].astype(F32) + jnp.pad(shift, pad_heads)[None]
-    step = jax.nn.softplus(dt_shifted)
-    slope_dt = jax.nn.sigmoid(dt_shifted)
-
-    tails = first[:, : inner + 2 * LANES].reshape(units, PER_UNIT, CHUNK, inner + 2 * LANES)[:, :, CHUNK - 8 :]
-    before = plan.along(tails[:, PER_UNIT - 1], 1)
-    tails = jnp.concatenate([before[:, None], tails[:, : PER_UNIT - 1]], axis=1).astype(F32)
-    tails = tails.reshape(chunks, 8, inner + 2 * LANES)
-    tail_x, tail_bc = tails[..., :inner], tails[..., inner:]
-
     def shaped(*shape, dtype=BF16):
         return jax.ShapeDtypeStruct(shape, dtype)
 
     states = (LANES, inner)
-    y_own, starts, own, decays, shared, reach = pl.pallas_call(
-        forward_kernel,
-        grid=(units, PER_UNIT),
-        in_specs=[
-            rows_spec(inner), chunk_spec((8, inner)),
-            rows_spec(2 * LANES, inner // (2 * LANES)), chunk_spec((8, 2 * LANES)),
-            rows_spec(LANES), whole_spec(cx.shape), whole_spec(cbc.shape), whole_spec(hp.shape),
-        ],
-        out_specs=[
-            rows_spec(inner), chunk_spec(states), unit_spec(states), unit_spec((8, inner)),
-            rows_spec(2 * LANES), rows_spec(LANES),
-        ],
-        out_shape=[
-            shaped(rows, inner), shaped(chunks, *states), shaped(units, *states),
-            shaped(units, 8, inner, dtype=F32), shaped(rows, 2 * LANES), shaped(rows, LANES, dtype=F32),
-        ],
-        scratch_shapes=[
-            pltpu.VMEM((CHUNK + 8, inner), F32), pltpu.VMEM((CHUNK + 8, 2 * LANES), F32),
-            pltpu.VMEM(states, F32), pltpu.VMEM((8, LANES), F32),
-        ],
-        compiler_params=params(),
-        cost_estimate=cost(31),
-        name="scan_forward",
-    )(first, tail_x, first, tail_bc, step, cx, cbc, hp)
+    edge = (units, 16, inner + 2 * LANES)
+    in_specs = [
+        rows_spec(inner), rows_spec(2 * LANES, inner // (2 * LANES)),
+        rows_spec(LANES, (inner + 2 * LANES) // LANES),
+    ]
+    consts = [whole_spec(cx.shape), whole_spec(cbc.shape), whole_spec(hp.shape)]
+    out_specs = [
+        rows_spec(inner), chunk_spec(states), unit_spec(states), unit_spec((8, inner)),
+        rows_spec(2 * LANES), rows_spec(LANES),
+    ]
+    out_shape = [
+        shaped(rows, inner), shaped(chunks, *states), shaped(units, *states),
+        shaped(units, 8, inner, dtype=F32), shaped(rows, 2 * LANES), shaped(rows, LANES, dtype=F32),
+    ]
+    scratch = [
+        pltpu.VMEM((CHUNK + 8, inner), F32), pltpu.VMEM((CHUNK + 8, 2 * LANES), F32),
+        pltpu.VMEM(states, F32), pltpu.VMEM((8, LANES), F32),
+    ]
+    by_unit = first.reshape(units, 4 * tokens, first.shape[1])
+    if plan.fast:
+        anywhere = pl.BlockSpec(memory_space=pl.ANY)
+        dma = pltpu.SemaphoreType.DMA
+        y_own, starts, own, decays, shared, reach, halo, near, far = pl.pallas_call(
+            scan_forward_kernel,
+            grid=(units, PER_UNIT),
+            in_specs=in_specs + [anywhere, anywhere] + consts,
+            out_specs=out_specs + [whole_spec(edge), anywhere, anywhere],
+            out_shape=out_shape
+            + [shaped(*edge), shaped(units, tokens, model), shaped(EARLY_UNITS, tokens, model)],
+            scratch_shapes=scratch
+            + [pltpu.VMEM(edge, BF16), dma((1,)), dma((1,)), dma((2,)), dma((2,)), dma((1,))],
+            compiler_params=pltpu.CompilerParams(
+                dimension_semantics=("arbitrary", "arbitrary"), vmem_limit_bytes=VMEM_LIMIT,
+                collective_id=1, has_side_effects=True,
+            ),
+            cost_estimate=cost(31),
+            name="scan_forward",
+        )(first, first, first, by_unit, cotangent, cx, cbc, hp)
+    else:
+        halo = plan.along(by_unit[:, 4 * tokens - 16 :, : inner + 2 * LANES], 1)
+        y_own, starts, own, decays, shared, reach = pl.pallas_call(
+            forward_kernel,
+            grid=(units, PER_UNIT),
+            in_specs=in_specs + [whole_spec(edge)] + consts,
+            out_specs=out_specs,
+            out_shape=out_shape,
+            scratch_shapes=scratch,
+            compiler_params=params(),
+            name="scan_forward",
+        )(first, first, first, halo, cx, cbc, hp)
 
     decay_rows = jnp.concatenate([decays[:, 0], jnp.zeros((8 - units, inner), F32)])
-    incoming, all_decays = exchange(plan, own, decay_rows, False)
+    if plan.fast:
+        incoming, all_decays, cot_rows = exchange(plan, own, decay_rows, cotangent, near, far)
+    else:
+        incoming = slow_exchange(plan, own, decay_rows, False)
     gate_in = dot(normed, weight_gate).astype(BF16)
 
     y, gated, squares = pl.pallas_call(
@@ -1605,7 +1843,6 @@
     mean = pair_sum(jnp.sum(wide * gain_out[None] * unit_out, axis=1).reshape(chunks, CHUNK))
     mean = (mean / (2 * inner)).reshape(rows, 1)
     stats = jnp.concatenate([scale_out, mean, jnp.zeros((rows, LANES - 2), F32)], axis=1)
-    gain_rows = jnp.broadcast_to(gain_out[None], (8, inner))
 
     width = inner + 3 * LANES
     back = functools.partial(rows_spec, back=True)
@@ -1626,6 +1863,9 @@
         def scans(columns, column=0):
             return pl.BlockSpec((CHUNK, columns), lambda i: (scan_at(i), column))
 
+        def edges(columns, column=0):
+            return pl.BlockSpec((16, columns), lambda i: (jnp.maximum(scan_at(i) * 8 - 1, 0), column))
+
         def scan_chunk(shape):
             return pl.BlockSpec((1,) + shape, lambda i: (scan_at(i), 0, 0))
 
@@ -1633,6 +1873,9 @@
             return pl.BlockSpec((1,) + shape, lambda i: (scan_at(i) // PER_UNIT, 0, 0))
 
         def every(shape):
+            return pl.BlockSpec(shape, lambda i: (0,) * len(shape), pipeline_mode=pl.Buffered(1))
+
+        def whole(shape):
             return pl.BlockSpec(shape, lambda i: (0,) * len(shape))
 
         anywhere = pl.BlockSpec(memory_space=pl.ANY)
@@ -1643,15 +1886,15 @@
             in_specs=[
                 pulls(inner), pulls(inner), pulls(inner), pulls(inner), pulls(LANES), every((8, inner)),
                 pulls(2 * LANES), pulls(LANES), every(all_decays.shape), anywhere, anywhere, anywhere, anywhere, anywhere,
-                scans(inner), scan_chunk((8, inner)),
-                scans(2 * LANES, inner // (2 * LANES)), scan_chunk((8, 2 * LANES)),
-                scans(LANES), scans(LANES), every(cx.shape), every(cbc.shape), every(hp.shape),
+                scans(inner), edges(inner),
+                scans(2 * LANES, inner // (2 * LANES)), edges(2 * LANES, inner // (2 * LANES)),
+                scans(LANES, (inner + 2 * LANES) // LANES), every(edge), every(cx.shape), every(cbc.shape), every(hp.shape),
                 scans(inner), scan_chunk(states), scan_unit(states), scans(LANES), every(pick.shape),
             ],
             out_specs=[
                 scans(width), scan_unit((8, inner)), scan_unit((8, 2 * LANES)),
-                every((40, inner)), every((40, 2 * LANES)), every((24, LANES)),
-                anywhere, anywhere, every((shard_rows, 2 * inner)), every((shard_rows, 2 * inner)),
+                whole((40, inner)), whole((40, 2 * LANES)), whole((24, LANES)),
+                anywhere, anywhere, anywhere, anywhere,
             ],
             out_shape=[
                 shaped(rows, width), shaped(units, 8, inner, dtype=F32), shaped(units, 8, 2 * LANES, dtype=F32),
@@ -1664,36 +1907,44 @@
                 pltpu.VMEM((units,) + states, BF16), pltpu.VMEM((units,) + states, BF16),
                 pltpu.VMEM((segments, units, share, inner), BF16),
                 pltpu.VMEM((segments, units, share, inner), BF16),
-                pltpu.VMEM((2, rows, model // 4), BF16), pltpu.VMEM((model, inner), BF16),
-                pltpu.VMEM((model // 4, inner), BF16), pltpu.VMEM((model // 4, inner), BF16),
+                pltpu.VMEM((2, rows, 256), BF16), pltpu.VMEM((model, inner), BF16),
+                pltpu.VMEM((model // 4, inner), BF16),
             ]
             + chip_scratch(shard_rows, inner)
             + [pltpu.VMEM((shard_rows, 2 * inner), BF16)]
             + member_scratch(shard_rows, 2 * inner)
-            + chip_scratch(shard_rows, inner)
             + [pltpu.VMEM((shard_rows, 2 * inner), BF16)]
+            + [pltpu.VMEM((shard_rows, inner), BF16), pltpu.VMEM((shard_rows, 2 * inner), BF16)]
             + member_scratch(shard_rows, 2 * inner)
+            + [pltpu.VMEM((shard_rows, 2 * inner), BF16)]
             + [
                 pltpu.VMEM((CHUNK + 8, inner), F32), pltpu.VMEM((CHUNK + 8, 2 * LANES), F32),
                 pltpu.VMEM(states, F32),
                 pltpu.VMEM((CHUNK + 8, inner), F32), pltpu.VMEM((CHUNK + 8, 2 * LANES), F32),
                 pltpu.VMEM((8, inner), F32),
-                dma((6,)), dma((2,)), dma((1,)), dma((2,)), dma((2,)),
+                dma((8,)), dma((2,)), dma((1,)), dma((2,)), dma((2,)),
                 dma((14 * len(HALF_PIECES),)), dma((14 * len(HALF_PIECES),)),
                 dma((segments,)), dma((segments,)), dma((segments,)), dma((segments,)),
             ],
             compiler_params=pltpu.CompilerParams(
-                dimension_semantics=("arbitrary",), vmem_limit_bytes=62 * 1024 * 1024,
+                dimension_semantics=("arbitrary",), vmem_limit_bytes=MIDDLE_LIMIT,
                 collective_id=4, has_side_effects=True,
             ),
             cost_estimate=cost(125),
             name="middle",
         )(
             d_normed_out, gated, gate_in, y, stats, gain_rows, shared, reach, all_decays, normed, g_out,
-            came_left, came_right, projected, first, tail_x, first, tail_bc, step, slope_dt, cx, cbc, hp, y, starts, incoming,
+            came_left, came_right, projected, first, first, first, first, first, halo, cx, cbc, hp, y, starts, incoming,
             reach, pick,
         )
     else:
+
+        def edges(columns, column=0):
+            def place(u, c):
+                return (jnp.maximum((u * PER_UNIT + PER_UNIT - 1 - c) * 8 - 1, 0), column)
+
+            return pl.BlockSpec((16, columns), place)
+
         dy, d_gate, pull = pl.pallas_call(
             pull_kernel,
             grid=(units, PER_UNIT),
@@ -1707,14 +1958,14 @@
             compiler_params=params(),
             name="gate_backward",
         )(d_normed_out, gated, gate_in, y, stats, gain_rows, shared, reach)
-        after, _ = exchange(plan, pull, all_decays, True)
+        after = slow_exchange(plan, pull, decay_rows, True)
         d_all, heads_x, heads_bc, g_x, g_bc, g_heads = pl.pallas_call(
             backward_kernel,
             grid=(units, PER_UNIT),
             in_specs=[
-                back(inner), chunk_spec((8, inner), True),
-                back(2 * LANES, inner // (2 * LANES)), chunk_spec((8, 2 * LANES), True),
-                back(LANES), back(LANES), whole_spec(cx.shape), whole_spec(cbc.shape), whole_spec(hp.shape),
+                back(inner), edges(inner),
+                back(2 * LANES, inner // (2 * LANES)), edges(2 * LANES, inner // (2 * LANES)),
+                back(LANES, (inner + 2 * LANES) // LANES), whole_spec(edge), whole_spec(cx.shape), whole_spec(cbc.shape), whole_spec(hp.shape),
                 back(inner), back(inner), chunk_spec(states, True), unit_spec(states), back(LANES),
                 unit_spec(states), whole_spec(pick.shape),
             ],
@@ -1735,7 +1986,7 @@
             compiler_params=params(),
             name="scan_backward",
         )(
-            first, tail_x, first, tail_bc, step, slope_dt, cx, cbc, hp,
+            first, first, first, first, first, halo, cx, cbc, hp,
             dy, y, starts, incoming, reach, after, pick,
         )
         projected = plan.to_tokens(projected)

time: 728 us -> 684 us (0.940)
  starting transfers between devices: 21.3 us -> 5.07 us
  other arithmetic: 59.4 us -> 47.4 us
  waiting for transfers between devices: 28.2 us -> 20.4 us
    unnamed x85 -> x150, local copies, waits for them, and re-layouts: 18.5 us -> 48.1 us
    ppermute x12 -> x8, starting transfers between devices: 20.7 us -> 4.81 us  [send(): return lax.ppermute(x, ('fs', 'sp'), pairs)]
    pallas_call x3, Pallas kernels: 139 us -> 148 us  [the longest x1 61.8 us: head(): pl.pallas_call(head_kernel, out_shape=[shape((self.units, 4, self.tokens,...]
    concatenate x7 -> x0, local copies, waits for them, and re-layouts: 9.09 us -> none  [the longest x1 4.8 us: body(): jnp.concatenate([conv_x.T.reshape(-1), conv_x_bias, gate_gain, norm_gain,...]
    all_gather x2, waiting for transfers between devices: 8.91 us -> 0.01 us  [gather(): return lax.all_gather(x, 'fs', axis=0, tiled=True, axis_index_groups=groups)]
    slice x12 -> x4, local copies, waits for them, and re-layouts: 8.76 us -> 0.05 us  [the longest x2 0.04 us: body(): gain_in, gain_out = (gain_in[0], gain_rows[0])]
    another operation x6 -> x2, other arithmetic: 9.69 us -> 1.76 us  [the longest x2 5.93 us: to_units(): block = jnp.stack(pair, axis=2)]
    ppermute x12 -> x8, waiting for transfers between devices: 19.2 us -> 20.4 us  [send(): return lax.ppermute(x, ('fs', 'sp'), pairs)]
  transfers between devices with their start and end apart: 14 -> 10, of which waited for: 3 -> 3; matrix products, arithmetic and copies ran while one was open for 13% -> 12% of each run, Pallas kernels for 13% -> 23%
where the time goes in v4:
time: 684 us; the launch traced here: 679 us
  Pallas kernels  439 us (64%)
  matrix products  97.4 us (14%)
  local copies, waits for them, and re-layouts  54.3 us (8%)
  other arithmetic  47.4 us (7%)
  waiting for transfers between devices  20.4 us (3%)
  between operations  15.2 us (2%)
    pallas_call x1, Pallas kernels, body(): pl.pallas_call(middle_kernel, grid=(spots,), in_specs=[pulls(inner), pull...  175 us
    pallas_call x1, Pallas kernels, tail(): pl.pallas_call(tail_kernel, out_shape=[jax.ShapeDtypeStruct((rows, 2 * in...  107 us
    pallas_call x1, Pallas kernels, head(): pl.pallas_call(head_kernel, out_shape=[shape((self.units, 4, self.tokens,...  61.8 us
    pallas_call x1, Pallas kernels, exchange(): pl.pallas_call(exchange_kernel, out_shape=[jax.ShapeDtypeStruct(own.shape...  49.7 us
    unnamed x150, local copies, waits for them, and re-layouts  48.1 us
    dot_general x3, matrix products, dot(): return jnp.dot(a, b, preferred_element_type=F32)  39.2 us
    dot_general x3, matrix products, dot_nt(): lax.dot_general(a, b, (((1,), (1,)), ((), ())), preferred_element_type=F32)  37.6 us
    pallas_call x1, Pallas kernels, body(): pl.pallas_call(scan_forward_kernel, grid=(units, PER_UNIT), in_specs=in_s...  36.9 us
  transfers between devices with their start and end apart: 10, of which 3 were waited for; matrix products, arithmetic and copies ran while one was open for 12% of the time, Pallas kernels for 23%

profile of v4, /device:TPU:0, one launch (start us, length us, event | category | flops | bytes accessed | tf_op | source)
XLA Modules:
  0.0 678.9 jit_solution(13049236808756550560)
XLA Ops:
  7.2 1.3 broadcast_select_fusion.6
  9.1 2.1 broadcast_select_fusion.2
  11.2 0.9 copy.48.conv_x
  12.1 0.9 copy.47.w_dt
  13.0 0.8 copy.49.conv_bc
  15.8 1.7 copy-done.1
  17.4 1.3 copy-done.13
  18.7 0.9 copy-done.14
  22.2 61.8 %head.1 = (bf16[3,4,128,1536]{3,2,1,0:T(8,128)(2,1)S(1)}, bf16[4,2,192,1920]{3,2,1,0:T(8,128)(2,1)S(1)}, f32[8,1536]{1,0:T(8,128)S(1)}, f32[8,256]{1,0:T(8,128)S...) custom-call(bf16[6,128,1536]{2,1,0:T(8,128)(2,1)S(1)} %copy-done.1, ...), custom_call_target="tpu_custom_call" | custom-call | flops 63250001920 | tf_op jit(solution)/shard_map/head/pallas_call | solution.py:1419
  84.1 2.5 copy-done.19
  86.6 1.0 multiply_reduce_fusion.1
  87.6 3.3 multiply_convert_fusion.2
  91.1 1.1 pad_maximum_fusion
  92.5 15.2 %convolution_convert_fusion.1.x.bc.dt.xp.bcp = bf16[1536,1920]{1,0:T(8,128)(2,1)} fusion(bf16[1536,1536]{1,0:T(8,128)(2,1)} %bitcast.117, bf16[1536,1920]{1,0:T(8,128)(2,1)} %bitcast.108), kind=kOutput, calls=%fused_computation.14 | convolution fusion | flops 9062645760 | bytes 16515072 | tf_op jit(solution)/shard_map/dot_general | solution.py:22
  107.8 2.7 copy-done.21
  110.4 36.9 %scan_forward.1 = (bf16[1536,1536]{1,0:T(8,128)(2,1)S(1)}, bf16[12,128,1536]{2,1,0:T(8,128)(2,1)S(1)}, bf16[3,128,1536]{2,1,0:T(8,128)(2,1)S(1)}, f32[3,8,1536]{...) custom-call(bf16[1536,1920]{1,0:T(8,128)(2,1)S(1)} %copy-done.21, ...), custom_call_target="tpu_custom_call" | custom-call | flops 35649998848 | tf_op jit(solution)/shard_map/scan_forward/pallas_call | solution.py:1780
  147.3 2.2 copy-done.28
  149.5 2.2 copy-done.32
  151.6 1.0 copy-done.37
  152.7 1.0 copy-done.39
  153.9 3.5 multiply_convert_fusion.1.normed
  157.4 1.1 fusion.10
  158.5 1.1 fusion.14.pick
  159.6 1.2 broadcast_select_fusion.1
  160.7 1.1 pad_maximum_fusion.1
  161.9 1.3 copy-done.38
  163.1 1.3 copy-done.40
  164.4 1.1 copy-done.42
  165.5 49.7 %states.1 = (bf16[3,128,1536]{2,1,0:T(8,128)(2,1)S(1)}, f32[8,8,1536]{2,1,0:T(8,128)S(1)}, bf16[3,4,128,1536]{3,2,1,0:T(8,128)(2,1)S(1)}) custom-call(bf16[3,128,1536]{2,1,0:T(8,128)(2,1)S(1)} %copy-done.38, f32[8,1536]{1,0:T(8,128)S(1)} %concatenate.22.dec_ref, bf16[6,128,1536]{2,1,0:T(8,128)(2,1)S(1)} %copy-done.5, bf16[3,128,1536]{2,1,0:T(8,128)(2,1)S(1)} %copy-done.40, ...), custom_call_target="tpu_custom_call" | custom-call | flops 40249999360 | tf_op jit(solution)/shard_map/states/pallas_call | solution.py:1658
  215.2 2.1 copy-done.22
  217.4 1.0 copy-done.30
  219.1 11.0 %convolution_convert_fusion.4.gate_ref.gate = bf16[1536,1536]{1,0:T(8,128)(2,1)S(1)} fusion(bf16[1536,1536]{1,0:T(8,128)(2,1)} %multiply_convert_fusion.1.normed, bf16[1536,1536]{1,0:T(8,128)(2,1)} %all-gather.3.cloned.1.call-done), kind=kOutput, calls=%fused_computation.17 | convolution fusion | flops 7250116608 | bytes 14155776 | tf_op jit(solution)/shard_map/dot_general | solution.py:22
  230.2 4.0 copy-done.29
  234.2 8.6 %gate_forward.1 = (bf16[1536,1536]{1,0:T(8,128)(2,1)S(1)}, bf16[1536,1536]{1,0:T(8,128)(2,1)S(1)}, f32[1536,128]{1,0:T(8,128)S(1)}) custom-call(bf16[1536,1536]{1,0:T(8,128)(2,1)S(1)} %copy-done.29, bf16[1536,1536]{1,0:T(8,128)(2,1)S(1)} %convolution_convert_fusion.4.gate_ref.gate, bf16[1536,256]{1,0:T(8,128)(2,1)S(1)} %copy-done.34, ...), custom_call_target="tpu_custom_call" | custom-call | flops 16099999744 | tf_op jit(solution)/shard_map/gate_forward/pallas_call | solution.py:1816
  242.9 2.2 copy-done.27
  245.4 1.9 copy-done.24
  247.5 0.9 collective-permute-done.1
  248.5 11.2 %fusion.13 = f32[1536,1536]{1,0:T(8,128)S(1)} fusion(bf16[1536,1536]{1,0:T(8,128)(2,1)} %all-gather.5.cloned.1.call-done, bf16[1536,1536]{1,0:T(8,128)(2,1)} %copy-done.24, f32[1536]{0:T(1024)S(1)} %slice_reduce_fusion.1, f32[1536]{0:T(1024)S(1)} %get-tuple-element.175), kind=kOutput, calls=%fused_computation.36 | convolution fusion | flops 7257194496 | bytes 18886656 | tf_op jit(solution)/shard_map/dot_general | solution.py:26
  259.7 1.8 fusion.12
  261.7 3.8 copy-done.23
  265.5 8.6 %convolution_convert_fusion.3.g_out = bf16[1536,1536]{1,0:T(8,128)(2,1)S(1)} fusion(bf16[1536,1536]{1,0:T(8,128)(2,1)S(1)} %bitcast.111, bf16[1536,1536]{1,0:T(8,128)(2,1)S(1)} %copy-done.25, f32[1536]{0:T(1024)S(1)} %slice_reduce_fusion.1, f32[1536]{0:T(1024)S(1)} %get-tuple-element.175), kind=kOutput, calls=%fused_computation.16 | convolution fusion | flops 7259553792 | bytes 14168064 | tf_op jit(solution)/shard_map/dot_general | solution.py:30
  274.4 1.8 copy-done.52
  276.4 2.4 collective-permute-start.5
  278.9 12.9 %fusion.2 = (f32[1536]{0:T(1024)}, f32[1536]{0:T(1024)S(1)}, bf16[1536,1536]{1,0:T(8,128)(2,1)}) fusion(bf16[1536,1536]{1,0:T(8,128)(2,1)S(1)} %copy-done.25, f32[1536]{0:T(1024)S(1)} %get-tuple-element.175, f32[1536]{0:T(1024)S(1)} %slice_reduce_fusion.1, bf16[1536,1536]{1,0:T(8,128)(2,1)S(1)} %bitcast.112, bf16[1536,1536]{1,0:T(8,128)(2,1)} %all-gather.5.cloned.1.call-done), kind=kOutput, calls=%fused_computation.4 | convolution fusion | flops 7268987904 | bytes 18898944 | tf_op jit(solution)/shard_map/dot_general | solution.py:22
  291.8 1.1 pad_maximum_fusion.2
  293.9 1.2 maximum_maximum_fusion.stats
  295.0 7.1 %fusion.11.projected = bf16[3,2,128,1536]{3,2,1,0:T(8,128)(2,1)} fusion(bf16[3,2,128,1536]{3,2,1,0:T(8,128)(2,1)} %collective-permute-done.6, f32[3,2,2,128,1536]{4,3,2,1,0:T(8,128)} %bitcast.115, pred[]{:T(512)S(6)} %eq.13), kind=kLoop, calls=%fused_computation.32 | loop fusion | flops 4718592 | bytes 14155777 | tf_op jit(solution)/shard_map/convert_element_type | solution.py:1571
  302.1 3.1 collective-permute-done.5.came_right
  305.3 16.4 %collective-permute-done.4.came_left = bf16[2,384,768]{2,1,0:T(8,128)(2,1)} collective-permute-done((bf16[2,384,768]{2,1,0:T(8,128)(2,1)}, bf16[2,384,768]{2,1,0:T(8,128)(2,1)}, u32[]{:S(2)}, u32[]{:S(2)}) %collective-permute-start.4) | collective-permute-done | bytes 1179680 | tf_op jit(solution)/shard_map/ppermute | solution.py:1386
  321.6 174.7 %middle.1 = (bf16[1536,1920]{1,0:T(8,128)(2,1)}, f32[3,8,1536]{2,1,0:T(8,128)}, f32[3,8,256]{2,1,0:T(8,128)}, f32[40,1536]{1,0:T(8,128)}, f32[40,256]{1,0:T(8,12...) custom-call(bf16[1536,1536]{1,0:T(8,128)(2,1)} %get-tuple-element.17, ...), custom_call_target="tpu_custom_call" | custom-call | flops 143750004736 | tf_op jit(solution)/shard_map/middle/pallas_call | solution.py:1883
  496.4 1.0 convert.8
  498.1 1.3 collective-permute-start.7
  500.2 3.1 convert_element_type.122
  503.3 1.7 convert_element_type.123
  505.0 2.3 fusion.17
  507.4 13.9 %fusion.32 = f32[1536,1536]{1,0:T(8,128)} fusion(bf16[1536,1920]{1,0:T(8,128)(2,1)} %bitcast.130, bf16[1536,1920]{1,0:T(8,128)(2,1)S(1)} %bitcast.109), kind=kOutput, calls=%fused_computation.114 | convolution fusion | flops 9059696640 | bytes 21233664 | tf_op jit(solution)/shard_map/dot_general | solution.py:26
  521.3 12.0 %convolution_convert_fusion.g = bf16[1536,1920]{1,0:T(8,128)(2,1)} fusion(bf16[1536,1536]{1,0:T(8,128)(2,1)S(1)} %bitcast.120, bf16[1536,1920]{1,0:T(8,128)(2,1)S(1)} %bitcast.131), kind=kOutput, calls=%fused_computation.13 | convolution fusion | flops 9062645760 | bytes 16515072 | tf_op jit(solution)/shard_map/dot_general | solution.py:30
  533.4 12.5 %fusion.27 = (bf16[1536,1536]{1,0:T(8,128)(2,1)S(1)}, f32[1536]{0:T(1024)S(1)}) fusion(f32[1536]{0:T(1024)S(1)} %copy-done.58, bf16[3,4,128,1536]{3,2,1,0:T(8,128)(2,1)S(1)} %bitcast.103, f32[1536,1536]{1,0:T(8,128)} %fusion.32, bf16[1536,1536]{1,0:T(8,128)(2,1)} %get-tuple-element.88, bf16[1536,1536]{1,0:T(8,128)(2,1)S(1)} %bitcast.134), kind=kOutput, calls=%fused_computation.109 | convolution fusion | flops 7261911552 | bytes 28323840 | tf_op jit(solution)/shard_map/dot_general | solution.py:26
  546.0 107.4 %tail.1 = (f32[192,3072]{1,0:T(8,128)S(1)}, f32[192,256]{1,0:T(8,128)S(1)}, f32[192,256]{1,0:T(8,128)S(1)}, f32[2,16,1536]{2,1,0:T(8,128)S(1)}, bf16[6,128,1536]{2,1,0:T(8,128)(2,1)S(1)}) custom-call(bf16[1536,1920]{1,0:T(8,128)(2,1)} %convolution_convert_fusion.g, f32[40,1536]{1,0:T(8,128)S(1)} %copy-done.45, f32[40,256]{1,0:T(8,128)S(1)} %copy-done.47, ...), custom_call_target="tpu_custom_call" | custom-call | flops 103499997184 | tf_op jit(solution)/shard_map/tail/pallas_call | solution.py:1480
  653.4 1.4 copy-done.4
  654.8 1.4 copy-done.6
  658.2 2.7 fusion.5
  661.7 6.1 fusion.8
  669.7 1.4 copy.72
  (195 shorter events, 15.7 us)
Async XLA Ops:
  7.2 212.0 %all-gather.3.cloned.1.call-start = ((), (), s32[]{:S(2)}) async-start(), calls=%async_computation | async-start | bytes 5898240 | tf_op jit(solution)/shard_map/all_gather | solution.py:1523
  8.6 82.4 %collective-permute-start = (bf16[192,1536]{1,0:T(8,128)(2,1)S(1)}, bf16[192,1536]{1,0:T(8,128)(2,1)S(1)}, u32[]{:S(2)}, u32[]{:S(2)}) collective-permute-start(bf16[192,1536]{1,0:T(8,128)(2,1)S(1)} %broadcast_select_fusion.6), channel_id=1, source_target_pairs={{0,4},{1,5},{2,6},{3,7},{4,0},{5,1},{6,2},{7,3},{8,12},{9,13},{10,... | collective-permute-start | bytes 1769480 | tf_op jit(solution)/shard_map/ppermute | solution.py:1386
  11.2 148.4 %collective-permute-start.2 = (bf16[192,1536]{1,0:T(8,128)(2,1)}, bf16[192,1536]{1,0:T(8,128)(2,1)}, u32[]{:S(2)}, u32[]{:S(2)}) collective-permute-start(bf16[192,1536]{1,0:T(8,128)(2,1)} %broadcast_select_fusion.2), channel_id=1, source_target_pairs={{0,4},{1,5},{2,6},{3,7},{4,0},{5,1},{6,2},{7,3},{8,12},{9,13},{10,... | collective-permute-start | bytes 1769480 | tf_op jit(solution)/shard_map/ppermute | solution.py:1386
  84.1 2.5 copy-start.19
  86.5 4.4 copy-start
  86.5 21.2 %copy-start.8 = (f32[8,1536]{1,0:T(8,128)}, f32[8,1536]{1,0:T(8,128)S(1)}, u32[]{:S(2)}) copy-start(f32[8,1536]{1,0:T(8,128)S(1)} %get-tuple-element.59.cx) | copy-start | bytes 147460
  86.5 21.2 %copy-start.10 = (f32[8,256]{1,0:T(8,128)}, f32[8,256]{1,0:T(8,128)S(1)}, u32[]{:S(2)}) copy-start(f32[8,256]{1,0:T(8,128)S(1)} %get-tuple-element.60.cbc) | copy-start | bytes 24580
  86.5 21.2 %copy-start.46 = (f32[8,128]{1,0:T(8,128)}, f32[8,128]{1,0:T(8,128)S(1)}, u32[]{:S(2)}) copy-start(f32[8,128]{1,0:T(8,128)S(1)} %get-tuple-element.61.hp) | copy-start | bytes 12292
  86.6 160.8 %copy-start.12 = (f32[8,1536]{1,0:T(8,128)}, f32[8,1536]{1,0:T(8,128)S(1)}, u32[]{:S(2)}) copy-start(f32[8,1536]{1,0:T(8,128)S(1)} %get-tuple-element.73.gain) | copy-start | bytes 147460
  87.6 66.2 %copy-start.54 = (f32[1536]{0:T(1024)}, f32[1536]{0:T(1024)S(1)}, u32[]{:S(2)}) copy-start(f32[1536]{0:T(1024)S(1)} %slice_reduce_fusion.2) | copy-start | bytes 18436
  87.6 3.4 copy-start.50
  92.2 156.2 %all-gather.5.cloned.1.call-start = ((), (), s32[]{:S(2)}) async-start(), calls=%async_computation.1 | async-start | bytes 5898240 | tf_op jit(solution)/shard_map/all_gather | solution.py:1523
  92.4 15.3 %copy-start.5 = (bf16[6,128,1536]{2,1,0:T(8,128)(2,1)S(1)}, bf16[6,128,1536]{2,1,0:T(8,128)(2,1)}, u32[]{:S(2)}) copy-start(bf16[6,128,1536]{2,1,0:T(8,128)(2,1)} %cot.3) | copy-start | bytes 7077892
  92.4 61.4 %slice-start = ((s8[4718592]{0:T(1024)(128)(4,1)}), s8[524288]{0:T(1024)(128)(4,1)S(1)}, s32[]{:S(2)}) async-start(s8[4718592]{0:T(1024)(128)(4,1)} %bitcast.100), calls=%async_computation.2 | async-start | bytes 1048576
  107.7 46.1 %copy-start.57 = (f32[1536]{0:T(1024)}, f32[1536]{0:T(1024)S(1)}, u32[]{:S(2)}) copy-start(f32[1536]{0:T(1024)S(1)} %rsqrt.24) | copy-start | bytes 18436
  107.8 2.7 copy-start.21
  110.4 43.4 %slice-start.1 = ((s8[4718592]{0:T(1024)(128)(4,1)}), s8[4194304]{0:T(1024)(128)(4,1)S(1)}, s32[]{:S(2)}) async-start(s8[4718592]{0:T(1024)(128)(4,1)} %bitcast.100), calls=%async_computation.3 | async-start | bytes 8388608
  147.3 2.2 copy-start.28
  149.5 2.2 copy-start.32
  153.7 3.7 copy-start.33
  153.7 3.7 copy-start.35
  153.7 3.7 copy-start.41
  153.7 3.7 copy-start.44
  153.9 3.5 copy-start.2
  153.9 5.7 copy-start.51
  215.2 2.1 copy-start.22
  219.1 11.0 %copy-start.34 = (bf16[1536,256]{1,0:T(8,128)(2,1)S(1)}, bf16[1536,256]{1,0:T(8,128)(2,1)}, u32[]{:S(2)}) copy-start(bf16[1536,256]{1,0:T(8,128)(2,1)} %copy-done.33) | copy-start | bytes 2359300
  219.1 11.0 %copy-start.36 = (f32[1536,128]{1,0:T(8,128)S(1)}, f32[1536,128]{1,0:T(8,128)}, u32[]{:S(2)}) copy-start(f32[1536,128]{1,0:T(8,128)} %copy-done.35) | copy-start | bytes 2359300
  219.1 11.0 %copy-start.31 = (bf16[3,128,1536]{2,1,0:T(8,128)(2,1)S(1)}, bf16[3,128,1536]{2,1,0:T(8,128)(2,1)}, u32[]{:S(2)}) copy-start(bf16[3,128,1536]{2,1,0:T(8,128)(2,1)} %copy-done.30) | copy-start | bytes 3538948
  230.1 12.7 %copy-start.26 = (bf16[1536,1536]{1,0:T(8,128)(2,1)}, bf16[1536,1536]{1,0:T(8,128)(2,1)S(1)}, u32[]{:S(2)}) copy-start(bf16[1536,1536]{1,0:T(8,128)(2,1)S(1)} %convolution_convert_fusion.4.gate_ref.gate) | copy-start | bytes 14155780
  230.2 4.0 copy-start.29
  242.9 2.2 copy-start.27
  245.1 2.2 copy-start.24
  247.2 1.2 collective-permute-start.1
  248.4 13.2 %copy-start.25 = (bf16[1536,1536]{1,0:T(8,128)(2,1)S(1)}, bf16[1536,1536]{1,0:T(8,128)(2,1)}, u32[]{:S(2)}) copy-start(bf16[1536,1536]{1,0:T(8,128)(2,1)} %copy-done.24) | copy-start | bytes 14155780
  259.7 14.4 %copy-start.49 = (f32[1536,1536]{1,0:T(8,128)}, f32[1536,1536]{1,0:T(8,128)S(1)}, u32[]{:S(2)}) copy-start(f32[1536,1536]{1,0:T(8,128)S(1)} %fusion.13) | copy-start | bytes 28311556
  259.7 5.8 copy-start.23
  261.5 33.5 %collective-permute-start.6 = (bf16[3,2,128,1536]{3,2,1,0:T(8,128)(2,1)}, bf16[3,2,128,1536]{3,2,1,0:T(8,128)(2,1)}, u32[]{:S(2)}, u32[]{:S(2)}) collective-permute-start(bf16[3,2,128,1536]{3,2,1,0:T(8,128)(2,1)} %fusion.12), channel_id=1, source_target_pairs={{0,4},{1,5},{2,6},{3,7},{4,0},{5,1},{6,2},{7,3},{8,12},{9,13},{10,... | collective-permute-start | bytes 7077896 | tf_op jit(solution)/shard_map/ppermute | solution.py:1386
  274.1 2.1 copy-start.52
  276.4 28.8 %collective-permute-start.5 = (bf16[2,384,768]{2,1,0:T(8,128)(2,1)S(1)}, bf16[2,384,768]{2,1,0:T(8,128)(2,1)}, u32[]{:S(2)}, u32[]{:S(2)}) collective-permute-start(bf16[2,384,768]{2,1,0:T(8,128)(2,1)S(1)} %pad_maximum_fusion.3), channel_id=1, source_target_pairs={{0,16},{1,17},{2,18},{3,19},{4,20},{5,21},{6,22},{7,23},{8,24},{9,... | collective-permute-start | bytes 3538952 | tf_op jit(solution)/shard_map/ppermute | solution.py:1386
  291.8 1.7 collective-permute-start.3
  292.9 28.7 %collective-permute-start.4 = (bf16[2,384,768]{2,1,0:T(8,128)(2,1)}, bf16[2,384,768]{2,1,0:T(8,128)(2,1)}, u32[]{:S(2)}, u32[]{:S(2)}) collective-permute-start(bf16[2,384,768]{2,1,0:T(8,128)(2,1)} %pad_maximum_fusion.2), channel_id=1, source_target_pairs={{0,8},{1,9},{2,10},{3,11},{4,12},{5,13},{6,14},{7,15},{8,0},{9,1},... | collective-permute-start | bytes 3538952 | tf_op jit(solution)/shard_map/ppermute | solution.py:1386
  321.6 177.8 %copy-start.59 = (f32[6,128]{1,0:T(8,128)S(1)}, f32[6,128]{1,0:T(8,128)}, u32[]{:S(2)}) copy-start(f32[6,128]{1,0:T(8,128)} %fusion.10) | copy-start | bytes 9220
  321.6 178.4 %copy-start.9 = (f32[8,1536]{1,0:T(8,128)S(1)}, f32[8,1536]{1,0:T(8,128)}, u32[]{:S(2)}) copy-start(f32[8,1536]{1,0:T(8,128)} %copy-done.8) | copy-start | bytes 147460
  321.6 178.4 %copy-start.11 = (f32[8,256]{1,0:T(8,128)S(1)}, f32[8,256]{1,0:T(8,128)}, u32[]{:S(2)}) copy-start(f32[8,256]{1,0:T(8,128)} %copy-done.10) | copy-start | bytes 24580
  321.6 178.5 %copy-start.60 = (f32[1536]{0:T(1024)S(1)}, f32[1536]{0:T(1024)}, u32[]{:S(2)}) copy-start(f32[1536]{0:T(1024)} %get-tuple-element.144) | copy-start | bytes 18436
  496.3 6.9 %copy-start.53 = (bf16[192,3072]{1,0:T(8,128)(2,1)S(1)}, bf16[192,3072]{1,0:T(8,128)(2,1)}, u32[]{:S(2)}) copy-start(bf16[192,3072]{1,0:T(8,128)(2,1)} %get-tuple-element.95) | copy-start | bytes 3538948
  498.1 6.8 %collective-permute-start.7 = (bf16[3,3,1792]{2,1,0:T(4,128)(2,1)S(1)}, bf16[3,3,1792]{2,1,0:T(4,128)(2,1)S(1)}, u32[]{:S(2)}, u32[]{:S(2)}) collective-permute-start(bf16[3,3,1792]{2,1,0:T(4,128)(2,1)S(1)} %pad_maximum_fusion.5), channel_id=1, source_target_pairs={{1,0},{3,2},{5,4},{7,6},{8,1},{9,8},{10,3},{11,10},{12,5},{13,12},... | collective-permute-start | bytes 96776 | tf_op jit(solution)/shard_map/ppermute | solution.py:1386
  500.1 7.3 %copy-start.20 = (bf16[4,2,192,1920]{3,2,1,0:T(8,128)(2,1)S(1)}, bf16[4,2,192,1920]{3,2,1,0:T(8,128)(2,1)}, u32[]{:S(2)}) copy-start(bf16[4,2,192,1920]{3,2,1,0:T(8,128)(2,1)} %copy-done.19) | copy-start | bytes 17694724
  503.3 30.1 %slice-start.2 = ((s8[4718592]{0:T(1024)(128)(4,1)}), s8[4194304]{0:T(1024)(128)(4,1)S(1)}, s32[]{:S(2)}) async-start(s8[4718592]{0:T(1024)(128)(4,1)} %bitcast.102), calls=%async_computation.4 | async-start | bytes 8388608
  503.3 30.1 %slice-start.6 = ((s8[4718592]{0:T(1024)(128)(4,1)}), s8[524288]{0:T(1024)(128)(4,1)S(1)}, s32[]{:S(2)}) async-start(s8[4718592]{0:T(1024)(128)(4,1)} %bitcast.133), calls=%async_computation.8 | async-start | bytes 1048576
  504.9 16.3 %slice-start.4 = ((s8[4718592]{0:T(1024)(128)(4,1)}), s8[4194304]{0:T(1024)(128)(4,1)S(1)}, s32[]{:S(2)}) async-start(s8[4718592]{0:T(1024)(128)(4,1)} %bitcast.118), calls=%async_computation.6 | async-start | bytes 8388608
  507.3 13.9 %slice-start.5 = ((s8[4718592]{0:T(1024)(128)(4,1)}), s8[524288]{0:T(1024)(128)(4,1)S(1)}, s32[]{:S(2)}) async-start(s8[4718592]{0:T(1024)(128)(4,1)} %bitcast.118), calls=%async_computation.7 | async-start | bytes 1048576
  507.3 13.9 %copy-start.61 = (bf16[3,512,1920]{2,1,0:T(8,128)(2,1)S(1)}, bf16[3,512,1920]{2,1,0:T(8,128)(2,1)}, u32[]{:S(2)}) copy-start(bf16[3,512,1920]{2,1,0:T(8,128)(2,1)} %fusion.17) | copy-start | bytes 17694724
  507.3 26.0 %slice-start.3 = ((s8[4718592]{0:T(1024)(128)(4,1)}), s8[524288]{0:T(1024)(128)(4,1)S(1)}, s32[]{:S(2)}) async-start(s8[4718592]{0:T(1024)(128)(4,1)} %bitcast.102), calls=%async_computation.5 | async-start | bytes 1048576
  507.3 26.0 %slice-start.7 = ((s8[4718592]{0:T(1024)(128)(4,1)}), s8[4194304]{0:T(1024)(128)(4,1)S(1)}, s32[]{:S(2)}) async-start(s8[4718592]{0:T(1024)(128)(4,1)} %bitcast.133), calls=%async_computation.9 | async-start | bytes 8388608
  521.3 12.1 %copy-start.58 = (f32[1536]{0:T(1024)S(1)}, f32[1536]{0:T(1024)}, u32[]{:S(2)}) copy-start(f32[1536]{0:T(1024)} %copy-done.57) | copy-start | bytes 18436
  533.4 12.5 %copy-start.45 = (f32[40,1536]{1,0:T(8,128)S(1)}, f32[40,1536]{1,0:T(8,128)}, u32[]{:S(2)}) copy-start(f32[40,1536]{1,0:T(8,128)} %get-tuple-element.85.g_x) | copy-start | bytes 737284
  533.4 12.5 %copy-start.47 = (f32[40,256]{1,0:T(8,128)S(1)}, f32[40,256]{1,0:T(8,128)}, u32[]{:S(2)}) copy-start(f32[40,256]{1,0:T(8,128)} %get-tuple-element.86.g_bc) | copy-start | bytes 122884
  533.4 12.5 %copy-start.48 = (f32[24,128]{1,0:T(8,128)S(1)}, f32[24,128]{1,0:T(8,128)}, u32[]{:S(2)}) copy-start(f32[24,128]{1,0:T(8,128)} %get-tuple-element.87.g_heads) | copy-start | bytes 36868
  545.9 112.3 %copy-start.3 = (bf16[6,128,1536]{2,1,0:T(8,128)(2,1)S(1)}, bf16[6,128,1536]{2,1,0:T(8,128)(2,1)}, u32[]{:S(2)}) copy-start(bf16[6,128,1536]{2,1,0:T(8,128)(2,1)} %hidden.1) | copy-start | bytes 7077892
  545.9 112.3 %copy-start.55 = (f32[1536]{0:T(1024)S(1)}, f32[1536]{0:T(1024)}, u32[]{:S(2)}) copy-start(f32[1536]{0:T(1024)} %copy-done.54) | copy-start | bytes 18436
  545.9 112.3 %copy-start.56 = (f32[6,128]{1,0:T(8,128)S(1)}, f32[6,128]{1,0:T(8,128)}, u32[]{:S(2)}) copy-start(f32[6,128]{1,0:T(8,128)} %add_rsqrt_fusion.2) | copy-start | bytes 9220
  661.7 8.0 %copy-start.7 = (f32[192,3072]{1,0:T(8,128)S(1)}, f32[192,3072]{1,0:T(8,128)}, u32[]{:S(2)}) copy-start(f32[192,3072]{1,0:T(8,128)} %copy-done.6) | copy-start | bytes 7077892
  (16 other events, 16.7 us)
Sparse Core Ops, SparseCore 0:
  92.3 57.1 all-gather.2
  162.0 84.2 all-gather.4

commit v5 on v4

--- a/solution.py
+++ b/solution.py
@@ -13,9 +13,9 @@
 CHUNK = 128
 LANES = 128
 PER_UNIT = 4
-VMEM_LIMIT = 24 * 1024 * 1024
-TAIL_LIMIT = 44 * 1024 * 1024
-MIDDLE_LIMIT = 55 * 1024 * 1024
+VMEM_LIMIT = 56 * 1024 * 1024
+TAIL_LIMIT = 56 * 1024 * 1024
+MIDDLE_LIMIT = 58 * 1024 * 1024
 
 
 def dot(a, b):
@@ -361,125 +361,6 @@
         head_bc_ref[0] = dpb[0:8]
 
 
-def exchange_kernel(
-    own_ref, dec_ref, cot, near_ref, far_ref, out_ref, dec_out_ref, rows_out,
-    parts, decs, results, sends, receives, dec_sends, dec_receives, back_sends, back_receives,
-    row_sends, row_receives, local,
-):
-    count, joints, back = 8, 2, False
-    trade = Trade(cot, row_sends, row_receives)
-    f, z = lax.axis_index("fs"), lax.axis_index("sp")
-    core, group = f % 2, z // joints
-    me = (f // 2) * joints + z % joints
-    units, share = own_ref.shape[0], parts.shape[2]
-
-    def peer(k):
-        other = (me + k) % count
-        return other, ((other // joints) * 2 + core, group * joints + other % joints)
-
-    barrier = pltpu.get_barrier_semaphore()
-    for k in range(1, count):
-        pl.semaphore_signal(barrier, inc=1, device_id=peer(k)[1], device_id_type=MESH)
-    for device in (trade.partner, trade.far):
-        pl.semaphore_signal(barrier, inc=1, device_id=device, device_id_type=MESH)
-    pl.semaphore_wait(barrier, count + 1)
-    early = far_ref.shape[0]
-    near_at, far_at = trade.near_at, trade.far_at
-    last = trade.send(trade.rows_for(trade.far_group, early, units), rows_out.at[early:, z], 0, trade.far)
-    last.start()
-    near_on = trade.send(near_ref, rows_out.at[:, near_at], 1, trade.partner)
-    near_on.start()
-    far_on = trade.send(far_ref, rows_out.at[:early, far_at], 2, trade.partner)
-    far_on.start()
-    near_keep = pltpu.make_async_copy(near_ref, rows_out.at[:, near_at], local.at[0])
-    near_keep.start()
-    far_keep = pltpu.make_async_copy(far_ref, rows_out.at[:early, far_at], local.at[1])
-    far_keep.start()
-
-    def rows_of(i):
-        return pl.ds(pl.multiple_of(i * share, share), share)
-
-    def out_copy(k):
-        other, device = peer(k)
-        return pltpu.make_async_remote_copy(
-            src_ref=own_ref.at[:, rows_of(other)], dst_ref=parts.at[me],
-            send_sem=sends.at[k], recv_sem=receives.at[me], device_id=device, device_id_type=MESH,
-        )
-
-    def dec_copy(k):
-        return pltpu.make_async_remote_copy(
-            src_ref=dec_ref, dst_ref=decs.at[me],
-            send_sem=dec_sends.at[k], recv_sem=dec_receives.at[me],
-            device_id=peer(k)[1], device_id_type=MESH,
-        )
-
-    def back_copy(k):
-        other, device = peer(k)
-        return pltpu.make_async_remote_copy(
-            src_ref=results.at[other], dst_ref=out_ref.at[:, rows_of(me)],
-            send_sem=back_sends.at[k], recv_sem=back_receives.at[me],
-            device_id=device, device_id_type=MESH,
-        )
-
-    for k in range(1, count):
-        if not back:
-            dec_copy(k).start()
-        out_copy(k).start()
-    parts[me] = own_ref[:, rows_of(me)]
-    if not back:
-        decs[me] = dec_ref[...]
-    else:
-        decs[...] = dec_ref[...]
-    for k in range(1, count):
-        other = (me + k) % count
-        if not back:
-            pltpu.make_async_remote_copy(
-                src_ref=dec_ref, dst_ref=decs.at[other],
-                send_sem=dec_sends.at[k], recv_sem=dec_receives.at[other],
-                device_id=peer(k)[1], device_id_type=MESH,
-            ).wait_recv()
-        pltpu.make_async_remote_copy(
-            src_ref=own_ref.at[:, rows_of(other)], dst_ref=parts.at[other],
-            send_sem=sends.at[k], recv_sem=receives.at[other],
-            device_id=peer(k)[1], device_id_type=MESH,
-        ).wait_recv()
-    if not back:
-        dec_out_ref[...] = decs[...]
-    order = range(count - 1, -1, -1) if back else range(count)
-    width = own_ref.shape[2]
-    running = [jnp.zeros((share, width), F32) for _ in range(units)]
-    for i in order:
-        for u in range(units):
-            results[i, u] = running[u].astype(BF16)
-            running[u] = running[u] * decs[i, u : u + 1] + parts[i, u].astype(F32)
-    out_ref[:, rows_of(me)] = results[me]
-    for k in range(1, count):
-        back_copy(k).start()
-    trade.send(trade.rows_for(trade.far_group, early, units), rows_out.at[early:, far_at], 0, trade.far).wait_recv()
-    last_on = trade.send(rows_out.at[early:, far_at], rows_out.at[early:, far_at], 3, trade.partner)
-    last_on.start()
-    for k in range(1, count):
-        other = (me + k) % count
-        pltpu.make_async_remote_copy(
-            src_ref=results.at[other], dst_ref=out_ref.at[:, rows_of(other)],
-            send_sem=back_sends.at[k], recv_sem=back_receives.at[other],
-            device_id=peer(k)[1], device_id_type=MESH,
-        ).wait_recv()
-    for k in range(1, count):
-        if not back:
-            dec_copy(k).wait_send()
-        out_copy(k).wait_send()
-        back_copy(k).wait_send()
-    other_near, other_far = trade.swapped(near_at), trade.swapped(far_at)
-    trade.send(near_ref, rows_out.at[:, other_near], 1, trade.partner).wait_recv()
-    trade.send(far_ref, rows_out.at[:early, other_far], 2, trade.partner).wait_recv()
-    trade.send(rows_out.at[early:, far_at], rows_out.at[early:, other_far], 3, trade.partner).wait_recv()
-    for copy in (last, near_on, far_on, last_on):
-        copy.wait_send()
-    near_keep.wait()
-    far_keep.wait()
-
-
 def places():
     f, z = lax.axis_index("fs"), lax.axis_index("sp")
     core, chip = f % 2, f // 2
@@ -517,14 +398,83 @@
         return remote(src, dst, self.sends, self.receives, slot, device)
 
 
+class Gather:
+    def __init__(self, weight, target, sends, receives, local):
+        f, z, self.core, self.chip, self.by_x, self.by_y = places()
+        self.weight, self.target, self.sends, self.receives = weight, target, sends, receives
+        self.partner = (f + 1 - 2 * self.core, z)
+        self.over_x, self.over_y = (2 * self.by_x + self.core, z), (2 * self.by_y + self.core, z)
+        self.keep = pltpu.make_async_copy(self.columns(self.core), self.part(self.chip, self.core), local.at[0])
+
+    def columns(self, side):
+        width = self.weight.shape[1] // 2
+        return self.weight.at[:, pl.ds(pl.multiple_of(side * width, width), width)]
+
+    def part(self, chip, core):
+        return self.target.at[chip, core]
+
+    def copy(self, src, dst, slot, device):
+        return remote(src, dst, self.sends, self.receives, slot, device)
+
+    def sent(self, slot):
+        own, other = (self.chip, self.core), (self.chip, 1 - self.core)
+        src, dst, device = (
+            (self.columns(1 - self.core), own, self.partner),
+            (self.columns(self.core), own, self.over_x),
+            (self.columns(self.core), own, self.over_y),
+            (self.part(*other), other, self.over_x),
+            (self.part(*other), other, self.over_y),
+            (self.part(self.by_x, self.core), (self.by_x, self.core), self.over_y),
+            (self.part(self.by_y, 1 - self.core), (self.by_y, 1 - self.core), self.over_x),
+        )[slot]
+        return self.copy(src, self.part(*dst), slot, device)
+
+    def arrives(self, slot):
+        corner = (self.by_x + 2) % 4
+        chip, core = (
+            (self.chip, 1 - self.core), (self.by_x, self.core), (self.by_y, self.core),
+            (self.by_x, 1 - self.core), (self.by_y, 1 - self.core), (corner, self.core), (corner, 1 - self.core),
+        )[slot]
+        device = (self.partner, self.over_x, self.over_y, self.over_x, self.over_y, self.over_y, self.over_x)[slot]
+        there = self.part(chip, core)
+        self.copy(there, there, slot, device).wait_recv()
+
+    def start(self):
+        for slot in range(3):
+            self.sent(slot).start()
+        self.keep.start()
+
+    def second(self):
+        self.arrives(0)
+        for slot in (3, 4):
+            self.sent(slot).start()
+
+    def third(self):
+        self.arrives(1)
+        self.sent(5).start()
+
+    def fourth(self):
+        self.arrives(4)
+        self.sent(6).start()
+
+    def finish(self):
+        for slot in (2, 3, 5, 6):
+            self.arrives(slot)
+        for slot in range(7):
+            self.sent(slot).wait_send()
+        self.keep.wait()
+
+
 EARLY_UNITS = 2
 
 
 def scan_forward_kernel(
-    x, bc, dt, first, cot, cx, cbc, hp,
-    y, st, own, dec, bcs, acum, halo_out, near_out, far_out,
+    x, bc, dt, first, cot, weight, cx, cbc, hp,
+    y, st, own, dec, bcs, acum, halo_out, near_out, far_out, gathered,
     xe, be, state, base, halo, halo_sends, halo_receives, sends, receives, local,
+    w_sends, w_receives, w_local,
 ):
+    gather = Gather(weight, gathered, w_sends, w_receives, w_local)
     unit, chunk = pl.program_id(0), pl.program_id(1)
     segments, trade = Segments(), Trade(cot, sends, receives)
     me, last = segments.me, segments.count - 1
@@ -554,12 +504,15 @@
                 barrier, inc=1, device_id=segments.device((me + last) % segments.count), device_id_type=MESH
             )
 
-        pl.semaphore_wait(barrier, 1 + trade.moves + jnp.where(me < last, 1, 0))
+        for device in (gather.partner, gather.over_x, gather.over_y):
+            pl.semaphore_signal(barrier, inc=1, device_id=device, device_id_type=MESH)
+        pl.semaphore_wait(barrier, 4 + trade.moves + jnp.where(me < last, 1, 0))
 
         @pl.when(me < last)
         def _():
             halo_copy().start()
 
+        gather.start()
         far_copy.start()
 
         @pl.when(trade.stays)
@@ -582,8 +535,16 @@
 
     forward_kernel(x, bc, dt, halo, cx, cbc, hp, y, st, own, dec, bcs, acum, xe, be, state, base)
 
+    for at_unit, at_chunk, stage in ((0, 0, gather.second), (1, 1, gather.third), (1, 3, gather.fourth)):
+
+        @pl.when((unit == at_unit) & (chunk == at_chunk))
+        def _(stage=stage):
+            stage()
+
     @pl.when((unit == units - 1) & (chunk == PER_UNIT - 1))
     def _():
+        gather.finish()
+
         @pl.when(me < last)
         def _():
             halo_copy().wait_send()
@@ -794,6 +755,159 @@
         keep.wait()
 
 
+def states_kernel(
+    own, dec, cot, near_rows, far_rows, normed, w_gate, w_out, y0, bcs, acum,
+    dec_out, rows_out, gathered, gate_out, incoming_out, y, gated, squares,
+    incoming, parts, decs, results, weight, gate, blocks,
+    sends, receives, dec_sends, dec_receives, back_sends, back_receives,
+    row_sends, row_receives, w_sends, w_receives, local, w_local, block_sems,
+):
+    i = pl.program_id(0)
+    chunks = pl.num_programs(0) - 1
+    segments, trade = Segments(), Trade(cot, row_sends, row_receives)
+    gather = Gather(w_out, gathered, w_sends, w_receives, w_local)
+    me, count, z = segments.me, segments.count, segments.z
+    units, share = own.shape[0], parts.shape[2]
+    early = far_rows.shape[0]
+    near_at, far_at = trade.near_at, trade.far_at
+    block = blocks.shape[1]
+    count_blocks = gate.shape[0] // block
+
+    def rows_of(k):
+        return pl.ds(pl.multiple_of(k * share, share), share)
+
+    def out_copy(k, at_me):
+        other, device = segments.peer(k)
+        src, slot = (own.at[:, rows_of(other)], me) if at_me else (own.at[:, rows_of(me)], other)
+        return pltpu.make_async_remote_copy(
+            src_ref=src, dst_ref=parts.at[slot], send_sem=sends.at[k], recv_sem=receives.at[slot],
+            device_id=device, device_id_type=MESH,
+        )
+
+    def dec_copy(k, at_me):
+        other, device = segments.peer(k)
+        slot = me if at_me else other
+        return pltpu.make_async_remote_copy(
+            src_ref=dec, dst_ref=decs.at[slot], send_sem=dec_sends.at[k], recv_sem=dec_receives.at[slot],
+            device_id=device, device_id_type=MESH,
+        )
+
+    def back_copy(k, at_me):
+        other, device = segments.peer(k)
+        slot = me if at_me else other
+        return pltpu.make_async_remote_copy(
+            src_ref=results.at[other], dst_ref=incoming.at[:, rows_of(slot)],
+            send_sem=back_sends.at[k], recv_sem=back_receives.at[slot],
+            device_id=device, device_id_type=MESH,
+        )
+
+    def fetch(k):
+        return pltpu.make_async_copy(normed.at[pl.ds(k * block, block)], blocks.at[k % 2], block_sems.at[k % 2])
+
+    def multiply(k):
+        if k + 1 < count_blocks:
+            fetch(k + 1).start()
+        fetch(k).wait()
+
+        def part(n, carry):
+            columns = pl.ds(pl.multiple_of(n * 384, 384), 384)
+            gate[pl.ds(k * block, block), columns] = dot(blocks[k % 2], weight[:, columns]).astype(BF16)
+            return carry
+
+        lax.fori_loop(0, gate.shape[1] // 384, part, 0)
+
+    last = trade.send(trade.rows_for(trade.far_group, early, units), rows_out.at[early:, z], 0, trade.far)
+    last_came = trade.send(
+        trade.rows_for(trade.far_group, early, units), rows_out.at[early:, far_at], 0, trade.far
+    )
+    near_on = trade.send(near_rows, rows_out.at[:, near_at], 1, trade.partner)
+    far_on = trade.send(far_rows, rows_out.at[:early, far_at], 2, trade.partner)
+    last_on = trade.send(rows_out.at[early:, far_at], rows_out.at[early:, far_at], 3, trade.partner)
+    near_keep = pltpu.make_async_copy(near_rows, rows_out.at[:, near_at], local.at[0])
+    far_keep = pltpu.make_async_copy(far_rows, rows_out.at[:early, far_at], local.at[1])
+    take_weight = pltpu.make_async_copy(w_gate, weight, local.at[2])
+    keep_gate = pltpu.make_async_copy(gate, gate_out, local.at[3])
+    keep_states = pltpu.make_async_copy(incoming, incoming_out, local.at[4])
+
+    @pl.when(i == 0)
+    def _():
+        barrier = pltpu.get_barrier_semaphore()
+        for k in range(1, count):
+            pl.semaphore_signal(barrier, inc=1, device_id=segments.peer(k)[1], device_id_type=MESH)
+        for device in (trade.partner, trade.far):
+            pl.semaphore_signal(barrier, inc=1, device_id=device, device_id_type=MESH)
+        pl.semaphore_wait(barrier, count + 1)
+        for k in range(1, count):
+            dec_copy(k, True).start()
+            out_copy(k, True).start()
+        take_weight.start()
+        fetch(0).start()
+        last.start()
+        near_on.start()
+        far_on.start()
+        near_keep.start()
+        far_keep.start()
+        parts[me] = own[:, rows_of(me)]
+        decs[me] = dec[...]
+        take_weight.wait()
+        for k in range(count_blocks // 2):
+            multiply(k)
+        for k in range(1, count):
+            dec_copy(k, False).wait_recv()
+            out_copy(k, False).wait_recv()
+        dec_out[...] = decs[...]
+        running = [jnp.zeros((share, own.shape[2]), F32) for _ in range(units)]
+        for n in range(count):
+            for u in range(units):
+                results[n, u] = running[u].astype(BF16)
+                running[u] = running[u] * decs[n, u : u + 1] + parts[n, u].astype(F32)
+        incoming[:, rows_of(me)] = results[me]
+        for k in range(1, count):
+            back_copy(k, True).start()
+        gather.start()
+        multiply(count_blocks // 2)
+        gather.second()
+        for k in range(count_blocks // 2 + 1, count_blocks):
+            multiply(k)
+        keep_gate.start()
+        last_came.wait_recv()
+        last_on.start()
+        for k in range(1, count):
+            back_copy(k, False).wait_recv()
+        keep_states.start()
+
+    @pl.when(i > 0)
+    def _():
+        place = pl.ds(pl.multiple_of((i - 1) * CHUNK, CHUNK), CHUNK)
+        gate_kernel(
+            y0, gate.at[place], bcs, acum, incoming.at[pl.ds((i - 1) // PER_UNIT, 1)], y, gated, squares
+        )
+
+    @pl.when(i == 3)
+    def _():
+        gather.third()
+
+    @pl.when(i == 6)
+    def _():
+        gather.fourth()
+
+    @pl.when(i == chunks)
+    def _():
+        other_near, other_far = trade.swapped(near_at), trade.swapped(far_at)
+        trade.send(near_rows, rows_out.at[:, other_near], 1, trade.partner).wait_recv()
+        trade.send(far_rows, rows_out.at[:early, other_far], 2, trade.partner).wait_recv()
+        trade.send(rows_out.at[early:, far_at], rows_out.at[early:, other_far], 3, trade.partner).wait_recv()
+        for copy in (last, near_on, far_on, last_on):
+            copy.wait_send()
+        for k in range(1, count):
+            dec_copy(k, True).wait_send()
+            out_copy(k, True).wait_send()
+            back_copy(k, True).wait_send()
+        for copy in (near_keep, far_keep, keep_gate, keep_states):
+            copy.wait()
+        gather.finish()
+
+
 class Reduction:
     def __init__(self, pieces, sends, receives, base, special=None):
         self.f, self.z, self.core, self.chip, self.by_x, self.by_y = places()
@@ -841,8 +955,8 @@
         columns = pl.ds(start, width)
         return self.copy(self.sp.at[:, columns], self.rp.at[:, columns], n, 3, self.partner)
 
-    def start(self):
-        for piece in self.pieces:
+    def start(self, pieces=None):
+        for piece in self.pieces if pieces is None else pieces:
             for copy in self.first_copies(piece):
                 copy.start()
 
@@ -958,45 +1072,39 @@
 
 
 def tail_kernel(
-    g, g_x, g_bc, g_heads, g_gate, g_norm, d_part, out_x, out_bc, out_dt, vec_out, d_out,
-    d_came, d_sum, local, r1, s2, r2, sp, rp, total, came, sums, across, last,
-    vs, vr, sends, receives, vec_sends, vec_receives,
+    normed, d_all, d_base, w_first, unit_rows, g_x, g_bc, g_heads, g_gate, z_total,
+    out_x, out_bc, out_dt, vec_out, d_out, out_z,
+    turned, g, d_part, d_came, local, r1, s2, r2, sp, rp, total, came, sums, across, last,
+    z_came, z_sums, z_across, z_last, end_x, end_bc, end_dt, end_z,
+    vs, vr, vec_all, sends, receives, vec_sends, vec_receives,
 ):
+    i = pl.program_id(0)
+    steps = pl.num_programs(0) // 2
     f, z, core, chip, by_x, by_y = places()
     rows = g.shape[0] // 4
     inner = out_x.shape[1] // 2
+    wide = normed.shape[1]
     bit, upper, units = z % 2, z // 2, d_part.shape[0]
     first = Reduction(FIRST_PIECES, sends, receives, 0, inner)
-    slot = 7 * len(FIRST_PIECES)
+    gate = Reduction(HALF_PIECES, sends, receives, 7 * len(FIRST_PIECES))
+    slot = 7 * (len(FIRST_PIECES) + len(HALF_PIECES))
     partner, near, far = first.partner, first.near, first.far
     token_near, token_far = (2 * chip + bit, 2 * upper + core), (2 * chip + bit, 2 * (1 - upper) + core)
     stays = bit == core
 
-    barrier = pltpu.get_barrier_semaphore()
-    for device in (partner, first.over["x"], first.over["y"], near, far, token_far):
-        pl.semaphore_signal(barrier, inc=1, device_id=device, device_id_type=MESH)
-
-    @pl.when(jnp.logical_not(stays))
-    def _():
-        pl.semaphore_signal(barrier, inc=1, device_id=token_near, device_id_type=MESH)
-
-    pl.semaphore_wait(barrier, 6 + (bit + core) % 2)
-
     def d_pair(k, n):
         return remote(d_part.at[:, k, 1 - core], d_came.at[:, k], sends, receives, slot + n, partner)
 
     def d_trade(k, n, device, group):
         return remote(
-            d_sum.at[:, k], d_out.at[pl.ds(group * units, units)], sends, receives, slot + 2 + n, device
+            d_part.at[:, k, core], d_out.at[pl.ds(group * units, units)], sends, receives, slot + 2 + n, device
         )
 
     def d_add(k):
         for u in range(units):
-            d_sum[u, k] = (d_part[u, k, core].astype(F32) + d_came[u, k].astype(F32)).astype(BF16)
-
-    d_pair(1 - upper, 0).start()
-    d_pair(upper, 1).start()
-    d_keep = pltpu.make_async_copy(d_sum.at[:, upper], d_out.at[pl.ds(upper * units, units)], local.at[0])
+            d_part[u, k, core] = (d_part[u, k, core].astype(F32) + d_came[u, k].astype(F32)).astype(BF16)
+
+    d_keep = pltpu.make_async_copy(d_part.at[:, upper, core], d_out.at[pl.ds(upper * units, units)], local.at[0])
 
     first.over_chips(
         lambda i, columns: g.at[first.at(i, rows), columns],
@@ -1008,31 +1116,27 @@
     def store_first(piece, there, values):
         _, start, width, _, _, _ = piece
         if start == inner:
-            out_bc[there, :] = values[:, : 2 * LANES]
-            out_dt[there, :] = values[:, 2 * LANES :]
+            end_bc[there, :] = values[:, : 2 * LANES]
+            end_dt[there, :] = values[:, 2 * LANES :]
         else:
-            out_x[there, pl.ds(start, width)] = values[:, :width]
-            out_x[there, pl.ds(inner + start, width)] = values[:, width:]
-
+            end_x[there, pl.ds(start, width)] = values[:, :width]
+            end_x[there, pl.ds(inner + start, width)] = values[:, width:]
+
+    def store_gate(piece, there, values):
+        _, start, width, _, _, _ = piece
+        end_z[there, pl.ds(start, width)] = values[:, :width]
+        end_z[there, pl.ds(inner + start, width)] = values[:, width:]
+
+    gate.over_members(z_total, z_came, z_sums, z_across, z_last, store_gate)
     first.over_members(total, came, sums, across, last, store_first)
 
-    vs[0] = jnp.zeros(vs.shape[1:], F32)
-    for k in range(5):
-        vs[0, k : k + 1] = jnp.sum(g_x[8 * k : 8 * k + 8], axis=0, keepdims=True)
-        vs[0, 8 + k : 9 + k, : 2 * LANES] = jnp.sum(g_bc[8 * k : 8 * k + 8], axis=0, keepdims=True)
-    vs[0, 5:6] = g_gate[...]
-    vs[0, 6:7] = g_norm[...]
-    for k in range(3):
-        vs[0, 7:8, k * LANES : (k + 1) * LANES] = jnp.sum(
-            g_heads[8 * k : 8 * k + 8], axis=0, keepdims=True
-        )
     vec_ways = [first.over["x"], first.over["y"], near, far]
 
     def vec_copy(k):
         return remote(vs.at[k], vr.at[k], vec_sends, vec_receives, k, vec_ways[k])
 
     def vec_last(side):
-        return remote(vec_out.at[core], vec_out.at[side], vec_sends, vec_receives, 4, partner)
+        return remote(vec_all.at[core], vec_all.at[side], vec_sends, vec_receives, 4, partner)
 
     def vec_step(k):
         if k:
@@ -1041,65 +1145,142 @@
             if k < 4:
                 vs[k] = summed
             else:
-                vec_out[core] = summed
+                vec_all[core] = summed
         if k < 4:
             vec_copy(k).start()
         else:
             vec_last(core).start()
 
-    first.start()
-    vec_step(0)
-    d_pair(1 - upper, 0).wait_recv()
-    d_add(1 - upper)
-    d_trade(1 - upper, 0, token_far, upper).start()
-    d_pair(upper, 1).wait_recv()
-    d_add(upper)
-
-    @pl.when(stays)
-    def _():
-        d_keep.start()
-
-    @pl.when(jnp.logical_not(stays))
-    def _():
-        d_trade(upper, 1, token_near, upper).start()
-
     early, late = first.pieces[:2], first.pieces[2:]
 
     def pair_on(piece):
         first.after_pair(piece)
         first.start_members(piece)
 
-    order = (
-        (first.after_first, early), (1, ()), (first.after_first, late), (2, ()),
-        (first.after_second, early), (3, ()), (pair_on, early), (first.after_second, late), (4, ()),
-        (first.after_near, early), (pair_on, late), (first.after_far, early),
-        (first.after_near, late), (first.after_last, early),
-        (first.after_far, late), (first.after_last, late),
-    )
-    for stage, pieces in order:
-        if not pieces:
-            vec_step(stage)
-        for piece in pieces:
-            stage(piece)
-    vec_last(1 - core).wait_recv()
-    d_trade(1 - upper, 0, token_far, 1 - upper).wait_recv()
-
-    @pl.when(stays)
-    def _():
-        d_keep.wait()
-
-    @pl.when(jnp.logical_not(stays))
-    def _():
-        d_trade(upper, 1, token_near, upper).wait()
-
-    d_trade(1 - upper, 0, token_far, upper).wait_send()
-    d_pair(1 - upper, 0).wait_send()
-    d_pair(upper, 1).wait_send()
-    first.drain_chips()
-    first.drain_members()
-    for k in range(4):
-        vec_copy(k).wait_send()
-    vec_last(core).wait_send()
+    @pl.when(i == 0)
+    def _():
+        barrier = pltpu.get_barrier_semaphore()
+        for device in (partner, first.over["x"], first.over["y"], near, far, token_far):
+            pl.semaphore_signal(barrier, inc=1, device_id=device, device_id_type=MESH)
+
+        @pl.when(jnp.logical_not(stays))
+        def _():
+            pl.semaphore_signal(barrier, inc=1, device_id=token_near, device_id_type=MESH)
+
+        pl.semaphore_wait(barrier, 6 + (bit + core) % 2)
+        for piece in gate.pieces:
+            gate.start_members(piece)
+        vs[0] = jnp.zeros(vs.shape[1:], F32)
+
+    @pl.when(i < steps)
+    def _():
+        def part(n, carry):
+            columns = pl.ds(pl.multiple_of(n * 384, 384), 384)
+            g[pl.ds(pl.multiple_of(i * wide, wide), wide), columns] = dot(
+                turned[...], d_all[:, columns]
+            ).astype(BF16)
+            return carry
+
+        turned[...] = normed[...].T
+        lax.fori_loop(0, g.shape[1] // 384, part, 0)
+
+    @pl.when(i == steps - 1)
+    def _():
+        first.start(early)
+
+    @pl.when(i == steps + 4)
+    def _():
+        for piece in early:
+            first.after_first(piece)
+        first.start(late)
+
+    @pl.when(i >= steps)
+    def _():
+        columns = pl.ds(pl.multiple_of((i - steps) * wide, wide), wide)
+        per = d_all.shape[0] // units
+
+        def part(u, carry):
+            there = pl.ds(pl.multiple_of(u * per, per), per)
+            product = d_base[there, :].astype(F32) + dot_nt(d_all[there, :], w_first[...])
+            d_part[u, :, :, :, columns] = product.astype(BF16).reshape(2, 2, per // 4, wide)
+            return carry + jnp.sum(product * unit_rows[there, :].astype(F32), axis=0, keepdims=True)
+
+        vs[0, 6:7, columns] = lax.fori_loop(0, units, part, jnp.zeros((1, wide), F32))
+
+    @pl.when(i == steps)
+    def _():
+        for piece in gate.pieces:
+            gate.after_near(piece)
+
+    @pl.when(i == 2 * steps - 1)
+    def _():
+        d_pair(1 - upper, 0).start()
+        d_pair(upper, 1).start()
+        for k in range(5):
+            vs[0, k : k + 1] = jnp.sum(g_x[8 * k : 8 * k + 8], axis=0, keepdims=True)
+            vs[0, 8 + k : 9 + k, : 2 * LANES] = jnp.sum(g_bc[8 * k : 8 * k + 8], axis=0, keepdims=True)
+        vs[0, 5:6] = g_gate[...]
+        for k in range(3):
+            vs[0, 7:8, k * LANES : (k + 1) * LANES] = jnp.sum(
+                g_heads[8 * k : 8 * k + 8], axis=0, keepdims=True
+            )
+        vec_step(0)
+        d_pair(1 - upper, 0).wait_recv()
+        d_add(1 - upper)
+        d_trade(1 - upper, 0, token_far, upper).start()
+        d_pair(upper, 1).wait_recv()
+        d_add(upper)
+
+        @pl.when(stays)
+        def _():
+            d_keep.start()
+
+        @pl.when(jnp.logical_not(stays))
+        def _():
+            d_trade(upper, 1, token_near, upper).start()
+
+        order = (
+            (first.after_second, early), (1, ()), (pair_on, early), (2, ()), (first.after_first, late),
+            (gate.after_far, gate.pieces), (3, ()), (first.after_second, late), (4, ()),
+            (first.after_near, early), (pair_on, late), (gate.after_last, gate.pieces), (first.after_far, early),
+            (first.after_near, late), (first.after_last, early), (first.after_far, late), (first.after_last, late),
+        )
+        for stage, pieces in order:
+            if not pieces:
+                vec_step(stage)
+            for piece in pieces:
+                stage(piece)
+        ends = [
+            pltpu.make_async_copy(src, dst, local.at[1 + n])
+            for n, (src, dst) in enumerate(
+                ((end_x, out_x), (end_bc, out_bc), (end_dt, out_dt), (end_z, out_z))
+            )
+        ]
+        for end in ends:
+            end.start()
+        vec_last(1 - core).wait_recv()
+        vec_out[...] = vec_all[...]
+        d_trade(1 - upper, 0, token_far, 1 - upper).wait_recv()
+
+        @pl.when(stays)
+        def _():
+            d_keep.wait()
+
+        @pl.when(jnp.logical_not(stays))
+        def _():
+            d_trade(upper, 1, token_near, upper).wait()
+
+        d_trade(1 - upper, 0, token_far, upper).wait_send()
+        d_pair(1 - upper, 0).wait_send()
+        d_pair(upper, 1).wait_send()
+        first.drain_chips()
+        first.drain_members()
+        gate.drain_members()
+        for k in range(4):
+            vec_copy(k).wait_send()
+        vec_last(core).wait_send()
+        for end in ends:
+            end.wait()
 
 
 def trade_steps(source, target, local, sends, receives):
@@ -1156,14 +1337,14 @@
 
 
 def middle_kernel(
-    dno, gated, gate, y_pull, stats, gain, bcs, acum_pull, decays, normed, g_out, came_left, came_right, projected,
+    dno, gated, gate, y_pull, stats, gain, bcs, acum_pull, decays, normed, w_gate, g_out, projected,
     x, xp, bc, bcp, dt, halo, cx, cbc, hp, y, st, incoming, acum, pick,
-    d_all, heads_x, heads_bc, g_x, g_bc, g_heads, d_gate_out, tokens_out, total_out, z_out,
-    dy_all, dgate_all, pulled, own, after, parts, results, blocks, g_z, out_own,
-    o_r1, o_s2, o_r2, o_sp, o_rp, o_total, o_came, o_sums, o_across, o_last, o_final,
-    z_rp, z_total, z_came, z_sums, z_across, z_last, z_final,
+    d_all, heads_x, heads_bc, g_x, g_bc, g_heads, d_base_out, tokens_out, total_out, z_out,
+    dy_all, dgate_all, pulled, own, after, parts, results, blocks, turned, w_blocks, products, g_z, out_own,
+    o_r1, o_s2, o_r2, o_sp, o_rp, o_total, o_came, o_sums, o_across, o_last,
+    z_r1, z_r2, z_rp, z_total,
     xe, be, adjoint, dpx, dpb, ends,
-    local, block_sems, trade_local, trade_sends, trade_receives, sends, receives,
+    local, keep_sems, block_sems, w_sems, product_sems, trade_local, trade_sends, trade_receives, sends, receives,
     state_sends, state_receives, back_sends, back_receives,
 ):
     i = pl.program_id(0)
@@ -1185,38 +1366,42 @@
     out = Reduction(HALF_PIECES, sends, receives, 0)
     gz = Reduction(HALF_PIECES, sends, receives, 7 * len(HALF_PIECES))
     out.over_chips(
-        None,
+        lambda k, columns: g_out.at[at(k, rows), columns],
         lambda side, columns: out_own[at(side, half), columns],
         lambda k, columns: o_s2[:, columns],
         o_r1, o_s2, o_r2, o_sp, o_rp, o_total,
     )
 
-    def store_to(target):
-        def store(piece, there, values):
-            _, start, width, _, _, _ = piece
-            target[there, pl.ds(start, width)] = values[:, :width].astype(BF16)
-            target[there, pl.ds(inner + start, width)] = values[:, width:].astype(BF16)
-
-        return store
-
-    out.over_members(o_total, o_came, o_sums, o_across, o_last, store_to(o_final))
+    out.over_members(o_total, o_came, o_sums, o_across, o_last, lambda piece, there, values: None)
     gz.over_chips(
         lambda k, columns: g_z.at[at(k, rows), columns],
         lambda side, columns: g_z[pl.ds(pl.multiple_of(chip * rows + side * half, half), half), columns],
         lambda k, columns: g_z[at(k, rows), columns],
-        o_r1, o_s2, o_r2, o_sp, z_rp, z_total,
+        z_r1, o_s2, z_r2, o_sp, z_rp, z_total,
     )
-    gz.over_members(z_total, z_came, z_sums, z_across, z_last, store_to(z_final))
     left, right = (pl.ds(start, width) for start, width, _ in HALF_PIECES)
     own_rows = pltpu.make_async_copy(g_out.at[at(chip, rows)], out_own, local.at[0])
     pass_left = pltpu.make_async_copy(g_out.at[at(by_y, rows), left], o_s2.at[:, left], local.at[1])
     pass_right = pltpu.make_async_copy(g_out.at[at(by_x, rows), right], o_s2.at[:, right], local.at[2])
-    keep_gate = pltpu.make_async_copy(dgate_all, d_gate_out, local.at[3])
-    take_left = pltpu.make_async_copy(came_left, o_r1.at[:, :, left], local.at[4])
-    take_right = pltpu.make_async_copy(came_right, o_r1.at[:, :, right], local.at[5])
-    keep_out = pltpu.make_async_copy(o_final, total_out, local.at[6])
-    keep_z = pltpu.make_async_copy(z_final, z_out, local.at[7])
-    taken = (own_rows, pass_left, pass_right, take_left, take_right)
+
+    def keep_out():
+        copies = []
+        for piece in out.pieces:
+            n, start, width, _, z_at, _ = piece
+            for side, (src, half_at) in enumerate(((o_sums.at[1], out.bit), (o_last, 1 - out.bit))):
+                for part in range(2):
+                    slot = 4 * n + 2 * side + part
+                    copies.append(
+                        pltpu.make_async_copy(
+                            src.at[:, pl.ds(z_at + part * width, width)],
+                            total_out.at[out.at(half_at, out.half), pl.ds(part * inner + start, width)],
+                            keep_sems.at[slot],
+                        )
+                    )
+        return copies
+
+    keep_z = pltpu.make_async_copy(z_total, z_out, local.at[7])
+    taken = (own_rows, pass_left, pass_right)
 
     def fetch(k):
         columns = pl.ds(k * 256, 256)
@@ -1235,21 +1420,10 @@
             pl.semaphore_signal(barrier, inc=1, device_id=trade_near, device_id_type=MESH)
 
         pl.semaphore_wait(barrier, count + 2 + (z + core) % 2)
+        out.start()
         for copy in taken:
             copy.start()
         start_trade()
-
-    @pl.when(i == 2)
-    def _():
-        for copy in taken:
-            copy.wait()
-        for piece in out.pieces:
-            out.after_first(piece)
-
-    @pl.when(i == chunks - 2)
-    def _():
-        for piece in out.pieces:
-            out.after_second(piece)
 
     @pl.when(i < chunks)
     def _():
@@ -1283,25 +1457,49 @@
             fetch(k + 1).start()
         fetch(k).wait()
 
+        turned[...] = blocks[k % 2].T
+
         def part(n, carry):
             columns = pl.ds(pl.multiple_of(n * 256, 256), 256)
-            product = dot_tn(blocks[k % 2], dgate_all[:, columns])
+            product = dot(turned[...], dgate_all[:, columns])
             g_z[pl.ds(k * 256, 256), columns] = product.astype(BF16)
             return carry
 
         lax.fori_loop(0, inner // 256, part, 0)
+
+    def fetch_w(k):
+        return pltpu.make_async_copy(w_gate.at[pl.ds(k * 256, 256)], w_blocks.at[k % 2], w_sems.at[k % 2])
+
+    def put(k):
+        return pltpu.make_async_copy(
+            products.at[k % 2], d_base_out.at[:, pl.ds(k * 256, 256)], product_sems.at[k % 2]
+        )
+
+    def project(k):
+        if k < 5:
+            fetch_w(k + 1).start()
+        fetch_w(k).wait()
+        if k > 1:
+            put(k - 2).wait()
+        per = dgate_all.shape[0] // units
+
+        def part(n, carry):
+            there = pl.ds(pl.multiple_of(n * per, per), per)
+            products[k % 2, there, :] = dot_nt(dgate_all[there, :], w_blocks[k % 2]).astype(BF16)
+            return carry
+
+        lax.fori_loop(0, units, part, 0)
+        put(k).start()
 
     @pl.when(i == chunks)
     def _():
         for k in range(1, count):
             state_copy(k, True).start()
         fetch(0).start()
-        keep_gate.start()
+        fetch_w(0).start()
         parts[me] = own[:, at(me, share)]
-        for k in range(3):
+        for k in range(6):
             multiply(k)
-        for piece in out.pieces:
-            out.after_pair(piece)
         for k in range(1, count):
             state_copy(k, False).wait_recv()
         running = [jnp.zeros((share, inner), F32) for _ in range(units)]
@@ -1312,17 +1510,20 @@
         after[:, at(me, share)] = results[me]
         for k in range(1, count):
             back_copy(k, True).start()
-        for k in range(3, 6):
-            multiply(k)
+        for k in range(6):
+            project(k)
+        put(4).wait()
+        put(5).wait()
         for k in range(1, count):
             back_copy(k, False).wait_recv()
-        out.drain_chips()
-        gz.start()
         for k in range(1, count):
             state_copy(k, True).wait_send()
             back_copy(k, True).wait_send()
+        for copy in taken:
+            copy.wait()
         for piece in out.pieces:
-            out.start_members(piece)
+            out.after_first(piece)
+        gz.start()
 
     def at_step(n, *stages):
         @pl.when(i == chunks + 1 + n)
@@ -1342,26 +1543,34 @@
             xe, be, adjoint, dpx, dpb, ends, place=(unit, chunk),
         )
 
-    at_step(2, (out.after_near, out))
-    at_step(4, (gz.after_first, gz))
-    at_step(6, (out.after_far, out), (gz.after_second, gz))
-    at_step(7, (gz.after_pair, gz), (gz.start_members, gz))
-    at_step(8, (out.after_last, out))
-    at_step(9, (gz.after_near, gz))
+    at_step(2, (out.after_second, out))
+    at_step(3, (out.after_pair, out), (out.start_members, out))
+    at_step(5, (out.after_near, out))
+
+    @pl.when(i == chunks + 1 + 6)
+    def _():
+        for piece in out.pieces:
+            out.second_copy(piece).wait_send()
+            out.pair_copy(piece).wait_send()
+            gz.after_first(piece)
+
+    at_step(8, (gz.after_second, gz))
+    at_step(9, (out.after_far, out), (gz.after_pair, gz))
 
     @pl.when(i == 2 * chunks)
     def _():
         finish_trade()
+        for piece in out.pieces:
+            out.after_last(piece)
+            for copy in out.first_copies(piece):
+                copy.wait_send()
         out.drain_members()
-        keep_out.start()
+        for copy in keep_out():
+            copy.start()
+        keep_z.start()
         gz.drain_chips()
-        for stage in (gz.after_far, gz.after_last):
-            for piece in gz.pieces:
-                stage(piece)
-        keep_z.start()
-        gz.drain_members()
-        keep_gate.wait()
-        keep_out.wait()
+        for copy in keep_out():
+            copy.wait()
         keep_z.wait()
 
 
@@ -1442,81 +1651,94 @@
         )
         return units.reshape(-1, hidden.shape[-1]), first.reshape(-1, inner + 3 * LANES), *params
 
-    def tail(self, g, g_x, g_bc, g_heads, g_gate, g_norm, d_normed):
+    def slow_tail(self, g, g_x, g_bc, g_heads, g_gate, g_norm, d_normed):
         rows, inner = g.shape[0] // self.shards, g_x.shape[1]
-        if not self.fast:
-            g = self.reduce_chips(g)
-            low = self.core == 0
-            kept, given = jnp.where(low, g[:rows], g[rows:]), jnp.where(low, g[rows:], g[:rows])
-            came = self.swap(given.astype(BF16), df=1).astype(F32)
-            total = self.reduce_members(
-                jnp.concatenate(
-                    list(self.by_core(kept[:, :inner], came[:, :inner]))
-                    + [kept[:, inner : inner + 2 * LANES] + came[:, inner : inner + 2 * LANES]]
-                    + list(self.by_core(kept[:, inner + 2 * LANES :], came[:, inner + 2 * LANES :])),
-                    axis=1,
-                )
+        g = self.reduce_chips(g)
+        low = self.core == 0
+        kept, given = jnp.where(low, g[:rows], g[rows:]), jnp.where(low, g[rows:], g[:rows])
+        came = self.swap(given.astype(BF16), df=1).astype(F32)
+        total = self.reduce_members(
+            jnp.concatenate(
+                list(self.by_core(kept[:, :inner], came[:, :inner]))
+                + [kept[:, inner : inner + 2 * LANES] + came[:, inner : inner + 2 * LANES]]
+                + list(self.by_core(kept[:, inner + 2 * LANES :], came[:, inner + 2 * LANES :])),
+                axis=1,
             )
-            wide = ((0, 0), (0, inner - 2 * LANES))
-            heads = g_heads.reshape(3, 8, LANES).sum(axis=1).reshape(1, -1)
-            vec = jnp.concatenate(
-                [
-                    g_x.reshape(5, 8, inner).sum(axis=1), g_gate, g_norm,
-                    jnp.pad(heads, ((0, 0), (0, inner - 3 * LANES))),
-                    jnp.pad(g_bc.reshape(5, 8, 2 * LANES).sum(axis=1), wide),
-                ]
-            )
-            vec = self.sum_all(jnp.pad(vec, ((0, 3), (0, 0))))
-            vec = jnp.stack(self.by_core(vec, self.swap(vec, df=1)))
-            cut = 2 * inner + 2 * LANES
-            d_rows = self.to_tokens(self.cores_sum(d_normed))
-            return total[:, : 2 * inner], total[:, 2 * inner : cut], total[:, cut:], vec, d_rows
-        width = g.shape[1]
-        wide = 2 * inner + 4 * LANES
-        vmem = pl.BlockSpec(memory_space=pltpu.VMEM)
+        )
+        wide = ((0, 0), (0, inner - 2 * LANES))
+        heads = g_heads.reshape(3, 8, LANES).sum(axis=1).reshape(1, -1)
+        vec = jnp.concatenate(
+            [
+                g_x.reshape(5, 8, inner).sum(axis=1), g_gate, g_norm,
+                jnp.pad(heads, ((0, 0), (0, inner - 3 * LANES))),
+                jnp.pad(g_bc.reshape(5, 8, 2 * LANES).sum(axis=1), wide),
+            ]
+        )
+        vec = self.sum_all(jnp.pad(vec, ((0, 3), (0, 0))))
+        vec = jnp.stack(self.by_core(vec, self.swap(vec, df=1)))
+        cut = 2 * inner + 2 * LANES
+        d_rows = self.to_tokens(self.cores_sum(d_normed))
+        return total[:, : 2 * inner], total[:, 2 * inner : cut], total[:, cut:], vec, d_rows
+    def tail(self, normed, d_all, d_base, w_first, unit_rows, g_x, g_bc, g_heads, g_gate, z_total):
+        model, inner, width = normed.shape[1], g_x.shape[1], d_all.shape[1]
+        rows, count = model // self.shards, normed.shape[0]
+        wide, block = 2 * inner + 4 * LANES, 256
+        steps = model // block
         vec = (16, inner)
-        d_shape = (self.units, 2, self.tokens, d_normed.shape[1])
-        slots = 7 * len(FIRST_PIECES) + 4
+        slots = 7 * (len(FIRST_PIECES) + len(HALF_PIECES)) + 4
+        anywhere, dma, shape = pl.BlockSpec(memory_space=pl.ANY), pltpu.SemaphoreType.DMA, jax.ShapeDtypeStruct
+
+        def whole(v):
+            return pl.BlockSpec(v.shape, lambda i: (0,) * v.ndim, pipeline_mode=pl.Buffered(1))
+
+        def early(i):
+            return jnp.minimum(i, steps - 1)
+
+        def late(i):
+            return jnp.maximum(i - steps, 0)
+
         return pl.pallas_call(
             tail_kernel,
+            grid=(2 * steps,),
+            in_specs=[
+                pl.BlockSpec((count, block), lambda i: (0, early(i))), whole(d_all),
+                pl.BlockSpec((count, block), lambda i: (0, late(i))),
+                pl.BlockSpec((block, width), lambda i: (late(i), 0)),
+                pl.BlockSpec((count, block), lambda i: (0, late(i))),
+                whole(g_x), whole(g_bc), whole(g_heads), whole(g_gate), whole(z_total),
+            ],
+            out_specs=[anywhere] * 3
+            + [pl.BlockSpec((2,) + vec, lambda i: (0, 0, 0))]
+            + [anywhere] * 2,
             out_shape=[
-                jax.ShapeDtypeStruct((rows, 2 * inner), F32),
-                jax.ShapeDtypeStruct((rows, 2 * LANES), F32),
-                jax.ShapeDtypeStruct((rows, 2 * LANES), F32),
-                jax.ShapeDtypeStruct((2,) + vec, F32),
-                jax.ShapeDtypeStruct((self.batch, self.tokens, d_normed.shape[1]), BF16),
+                shape((rows, 2 * inner), F32), shape((rows, 2 * LANES), F32), shape((rows, 2 * LANES), F32),
+                shape((2,) + vec, F32), shape((self.batch, self.tokens, model), BF16),
+                shape((rows, 2 * inner), F32),
             ],
-            in_specs=[vmem] * 7,
-            out_specs=[vmem] * 5,
-            scratch_shapes=[pltpu.VMEM(d_shape, BF16)] * 2
-            + [pltpu.SemaphoreType.DMA((1,))]
+            scratch_shapes=[
+                pltpu.VMEM((block, count), BF16),
+                pltpu.VMEM((model, width), BF16),
+                pltpu.VMEM((self.units, 2, 2, self.tokens, model), BF16),
+                pltpu.VMEM((self.units, 2, self.tokens, model), BF16),
+                dma((5,)),
+            ]
             + chip_scratch(rows, width)
             + [pltpu.VMEM((rows, wide), BF16)]
             + member_scratch(rows, wide)
-            + [pltpu.VMEM((4,) + vec, F32)] * 2
-            + [pltpu.SemaphoreType.DMA((slots,))] * 2
-            + [pltpu.SemaphoreType.DMA((5,))] * 2,
+            + member_scratch(rows, 2 * inner)
+            + [
+                pltpu.VMEM((rows, 2 * inner), F32), pltpu.VMEM((rows, 2 * LANES), F32),
+                pltpu.VMEM((rows, 2 * LANES), F32), pltpu.VMEM((rows, 2 * inner), F32),
+                pltpu.VMEM((4,) + vec, F32), pltpu.VMEM((4,) + vec, F32), pltpu.VMEM((2,) + vec, F32),
+                dma((slots,)), dma((slots,)), dma((5,)), dma((5,)),
+            ],
             compiler_params=pltpu.CompilerParams(
-                collective_id=3, has_side_effects=True, vmem_limit_bytes=TAIL_LIMIT
+                dimension_semantics=("arbitrary",), collective_id=3, has_side_effects=True,
+                vmem_limit_bytes=TAIL_LIMIT,
             ),
-            cost_estimate=cost(90),
+            cost_estimate=cost(130),
             name="tail",
-        )(
-            g, g_x, g_bc, g_heads, g_gate, g_norm,
-            d_normed.reshape(self.units, 2, 2, self.tokens, d_normed.shape[1]),
-        )
-
-    def first_hop(self, g):
-        rows = g.shape[0] // 4
-        by_x, by_y = self.chip + 1 - 2 * (self.chip % 2), (self.chip + 2) % 4
-        corner = (by_x + 2) % 4
-        blocks = g.reshape(4, rows, g.shape[1])
-        found = []
-        for (start, width, _), to, df in zip(HALF_PIECES, (by_x, by_y), (2, 4)):
-            columns = blocks[:, :, start : start + width]
-            given = [lax.dynamic_index_in_dim(columns, k, 0, False) for k in (to, corner)]
-            found.append(self.swap(jnp.stack(given), df=df))
-        return found
+        )(normed, d_all, d_base, w_first, unit_rows, g_x, g_bc, g_heads, g_gate, z_total)
 
     def gather(self, x):
         groups = [list(range(c, self.shards, 2)) for c in range(2)]
@@ -1648,36 +1870,51 @@
     return lax.fori_loop(0, count - 1, hop, jnp.zeros(own.shape, F32)).astype(BF16)
 
 
-def exchange(plan, own, decays, cot, near, far):
+def exchange(plan, own, decays, cot, near, far, normed, w_gate, w_out, y0, bcs, acum):
     units, depth, width = own.shape
     count, share = plan.count, depth // plan.count
-    dec_shape = (count, 8, width)
-    vmem, anywhere = pl.BlockSpec(memory_space=pltpu.VMEM), pl.BlockSpec(memory_space=pl.ANY)
-    dma = pltpu.SemaphoreType.DMA
-    rows_shape = (units, 4, plan.tokens, cot.shape[-1])
-    incoming, all_decays, rows = pl.pallas_call(
-        exchange_kernel,
+    dec_shape, rows, model = (count, 8, width), normed.shape[0], normed.shape[1]
+    chunks = rows // CHUNK
+    anywhere, dma, shape = pl.BlockSpec(memory_space=pl.ANY), pltpu.SemaphoreType.DMA, jax.ShapeDtypeStruct
+
+    def whole(v):
+        return pl.BlockSpec(v.shape, lambda i: (0,) * v.ndim, pipeline_mode=pl.Buffered(1))
+
+    def chunk(columns):
+        return pl.BlockSpec((CHUNK, columns), lambda i: (jnp.maximum(i - 1, 0), 0))
+
+    all_decays, cot_rows, weight_out, gate, incoming, y, gated, squares = pl.pallas_call(
+        states_kernel,
+        grid=(chunks + 1,),
+        in_specs=[whole(own), whole(decays)]
+        + [anywhere] * 6
+        + [chunk(width), chunk(2 * LANES), chunk(LANES)],
+        out_specs=[pl.BlockSpec(dec_shape, lambda i: (0, 0, 0))]
+        + [anywhere] * 4
+        + [chunk(width), chunk(width), chunk(LANES)],
         out_shape=[
-            jax.ShapeDtypeStruct(own.shape, BF16),
-            jax.ShapeDtypeStruct(dec_shape, F32),
-            jax.ShapeDtypeStruct(rows_shape, BF16),
+            shape(dec_shape, F32), shape((units, 4, plan.tokens, model), BF16),
+            shape((4, 2, w_out.shape[0], width), BF16), shape((rows, width), BF16), shape(own.shape, BF16),
+            shape((rows, width), BF16), shape((rows, width), BF16), shape((rows, LANES), F32),
         ],
-        in_specs=[vmem, vmem, anywhere, anywhere, anywhere],
-        out_specs=[vmem, vmem, anywhere],
         scratch_shapes=[
-            pltpu.VMEM((count, units, share, width), BF16),
-            pltpu.VMEM(dec_shape, F32),
-            pltpu.VMEM((count, units, share, width), BF16),
+            pltpu.VMEM(own.shape, BF16), pltpu.VMEM((count, units, share, width), BF16),
+            pltpu.VMEM(dec_shape, F32), pltpu.VMEM((count, units, share, width), BF16),
+            pltpu.VMEM(w_gate.shape, BF16), pltpu.VMEM((rows, width), BF16), pltpu.VMEM((2, 256, model), BF16),
         ]
         + [dma((count,))] * 6
-        + [dma((4,)), dma((4,)), dma((2,))],
+        + [dma((4,)), dma((4,)), dma((7,)), dma((7,)), dma((5,)), dma((1,)), dma((2,))],
         compiler_params=pltpu.CompilerParams(
-            collective_id=0, has_side_effects=True, vmem_limit_bytes=VMEM_LIMIT
+            dimension_semantics=("arbitrary",), collective_id=0, has_side_effects=True,
+            vmem_limit_bytes=VMEM_LIMIT,
         ),
-        cost_estimate=cost(35),
+        cost_estimate=cost(60),
         name="states",
-    )(own, decays, cot, near, far)
-    return incoming, all_decays, rows.reshape(-1, cot.shape[-1])
+    )(own, decays, cot, near, far, normed, w_gate, w_out, y0, bcs, acum)
+    return (
+        all_decays, cot_rows.reshape(rows, model), weight_out.reshape(model, width), gate, incoming,
+        y, gated, squares,
+    )
 
 
 def body(
@@ -1698,9 +1935,6 @@
         half = w.shape[1] // 2
         return jnp.where(core == 0, w[:, :half], w[:, half:]), jnp.where(core == 0, w[:, half:], w[:, :half])
 
-    z_mine, z_other = halves(w_z)
-    o_mine, o_other = halves(w_out)
-
     def rows_of_chip(mine, other):
         return jnp.concatenate(plan.by_core(mine, plan.swap(other, df=1)), axis=0)
 
@@ -1741,14 +1975,16 @@
         hp = jnp.stack([jnp.pad(jnp.exp(rate_log), pad_heads), jnp.pad(shift, pad_heads)])
         hp = jnp.pad(hp, ((0, 6), (0, 0)))
         gain_rows = jnp.broadcast_to(gain_out[None], (8, inner))
-    weight_gate = plan.gather(rows_of_chip(z_mine, z_other))
-    weight_out = plan.gather(rows_of_chip(o_mine, o_other))
+        weight_gate = plan.gather(rows_of_chip(*halves(w_z)))
+        weight_out = plan.gather(rows_of_chip(*halves(w_out)))
     pick = (jnp.arange(inner)[:, None] // head_size == jnp.arange(LANES)[None, :]).astype(BF16)
 
     hidden_rows = hidden_rows.astype(F32)
     scale_in = row_scale(hidden_rows)
     unit_in = hidden_rows * scale_in
     normed = (unit_in * gain_in[None]).astype(BF16)
+    unit_low = unit_in.astype(BF16)
+    normed, unit_low = lax.optimization_barrier((normed, unit_low))
 
     first = dot(normed, weight_first).astype(BF16)
     def shaped(*shape, dtype=BF16):
@@ -1777,22 +2013,25 @@
     if plan.fast:
         anywhere = pl.BlockSpec(memory_space=pl.ANY)
         dma = pltpu.SemaphoreType.DMA
-        y_own, starts, own, decays, shared, reach, halo, near, far = pl.pallas_call(
+        y_own, starts, own, decays, shared, reach, halo, near, far, weight_gate = pl.pallas_call(
             scan_forward_kernel,
             grid=(units, PER_UNIT),
-            in_specs=in_specs + [anywhere, anywhere] + consts,
-            out_specs=out_specs + [whole_spec(edge), anywhere, anywhere],
+            in_specs=in_specs + [anywhere, anywhere, anywhere] + consts,
+            out_specs=out_specs + [whole_spec(edge), anywhere, anywhere, anywhere],
             out_shape=out_shape
-            + [shaped(*edge), shaped(units, tokens, model), shaped(EARLY_UNITS, tokens, model)],
+            + [
+                shaped(*edge), shaped(units, tokens, model), shaped(EARLY_UNITS, tokens, model),
+                shaped(4, 2, w_z.shape[0], inner),
+            ],
             scratch_shapes=scratch
-            + [pltpu.VMEM(edge, BF16), dma((1,)), dma((1,)), dma((2,)), dma((2,)), dma((1,))],
+            + [pltpu.VMEM(edge, BF16), dma((1,)), dma((1,)), dma((2,)), dma((2,)), dma((1,)), dma((7,)), dma((7,)), dma((1,))],
             compiler_params=pltpu.CompilerParams(
                 dimension_semantics=("arbitrary", "arbitrary"), vmem_limit_bytes=VMEM_LIMIT,
                 collective_id=1, has_side_effects=True,
             ),
             cost_estimate=cost(31),
             name="scan_forward",
-        )(first, first, first, by_unit, cotangent, cx, cbc, hp)
+        )(first, first, first, by_unit, cotangent, w_z, cx, cbc, hp)
     else:
         halo = plan.along(by_unit[:, 4 * tokens - 16 :, : inner + 2 * LANES], 1)
         y_own, starts, own, decays, shared, reach = pl.pallas_call(
@@ -1808,23 +2047,24 @@
 
     decay_rows = jnp.concatenate([decays[:, 0], jnp.zeros((8 - units, inner), F32)])
     if plan.fast:
-        incoming, all_decays, cot_rows = exchange(plan, own, decay_rows, cotangent, near, far)
+        weight_gate = weight_gate.reshape(model, inner)
+        all_decays, cot_rows, weight_out, gate_in, incoming, y, gated, squares = exchange(
+            plan, own, decay_rows, cotangent, near, far, normed, weight_gate, w_out, y_own, shared, reach
+        )
     else:
         incoming = slow_exchange(plan, own, decay_rows, False)
-    gate_in = dot(normed, weight_gate).astype(BF16)
-
-    y, gated, squares = pl.pallas_call(
-        gate_kernel,
-        grid=(units, PER_UNIT),
-        in_specs=[
-            rows_spec(inner), rows_spec(inner), rows_spec(2 * LANES), rows_spec(LANES), unit_spec(states),
-        ],
-        out_specs=[rows_spec(inner), rows_spec(inner), rows_spec(LANES)],
-        out_shape=[shaped(rows, inner), shaped(rows, inner), shaped(rows, LANES, dtype=F32)],
-        compiler_params=params(),
-        cost_estimate=cost(14),
-        name="gate_forward",
-    )(y_own, gate_in, shared, reach, incoming)
+        gate_in = dot(normed, weight_gate).astype(BF16)
+        y, gated, squares = pl.pallas_call(
+            gate_kernel,
+            grid=(units, PER_UNIT),
+            in_specs=[
+                rows_spec(inner), rows_spec(inner), rows_spec(2 * LANES), rows_spec(LANES), unit_spec(states),
+            ],
+            out_specs=[rows_spec(inner), rows_spec(inner), rows_spec(LANES)],
+            out_shape=[shaped(rows, inner), shaped(rows, inner), shaped(rows, LANES, dtype=F32)],
+            compiler_params=params(),
+            name="gate_forward",
+        )(y_own, gate_in, shared, reach, incoming)
 
     def pair_sum(v):
         return v + plan.swap(v, df=1)
@@ -1833,10 +2073,9 @@
     scale_out = lax.rsqrt(squares / (2 * inner) + EPSILON).reshape(rows, 1)
     unit_out = gated.astype(F32) * scale_out
     normed_out = (unit_out * gain_out[None]).astype(BF16)
-    projected = plan.cores_sum(dot_nt(normed_out, weight_out))
-
     g_out = dot_tn(cot_rows, normed_out).astype(BF16)
-    g_out, weight_out, cot_rows = lax.optimization_barrier((g_out, weight_out, cot_rows))
+    projected = plan.cores_sum(dot_nt(normed_out, weight_out).astype(BF16))
+
     d_normed_out = dot(cot_rows, weight_out).astype(BF16)
     wide = d_normed_out.astype(F32)
     g_gate_gain = jnp.sum(wide * unit_out, axis=0)
@@ -1847,7 +2086,6 @@
     width = inner + 3 * LANES
     back = functools.partial(rows_spec, back=True)
     if plan.fast:
-        came_left, came_right = plan.first_hop(g_out)
         spots = 2 * chunks + 1
         shard_rows = model // plan.shards
         segments = plan.count
@@ -1880,12 +2118,12 @@
 
         anywhere = pl.BlockSpec(memory_space=pl.ANY)
         dma = pltpu.SemaphoreType.DMA
-        d_all, heads_x, heads_bc, g_x, g_bc, g_heads, d_gate, projected, total_out, total_z = pl.pallas_call(
+        d_all, heads_x, heads_bc, g_x, g_bc, g_heads, d_base, projected, total_out, total_z = pl.pallas_call(
             middle_kernel,
             grid=(spots,),
             in_specs=[
                 pulls(inner), pulls(inner), pulls(inner), pulls(inner), pulls(LANES), every((8, inner)),
-                pulls(2 * LANES), pulls(LANES), every(all_decays.shape), anywhere, anywhere, anywhere, anywhere, anywhere,
+                pulls(2 * LANES), pulls(LANES), every(all_decays.shape), anywhere, anywhere, anywhere, anywhere,
                 scans(inner), edges(inner),
                 scans(2 * LANES, inner // (2 * LANES)), edges(2 * LANES, inner // (2 * LANES)),
                 scans(LANES, (inner + 2 * LANES) // LANES), every(edge), every(cx.shape), every(cbc.shape), every(hp.shape),
@@ -1899,7 +2137,7 @@
             out_shape=[
                 shaped(rows, width), shaped(units, 8, inner, dtype=F32), shaped(units, 8, 2 * LANES, dtype=F32),
                 shaped(40, inner, dtype=F32), shaped(40, 2 * LANES, dtype=F32), shaped(24, LANES, dtype=F32),
-                shaped(rows, inner), shaped(batch, tokens, model),
+                shaped(rows, model), shaped(batch, tokens, model),
                 shaped(shard_rows, 2 * inner), shaped(shard_rows, 2 * inner),
             ],
             scratch_shapes=[
@@ -1907,22 +2145,24 @@
                 pltpu.VMEM((units,) + states, BF16), pltpu.VMEM((units,) + states, BF16),
                 pltpu.VMEM((segments, units, share, inner), BF16),
                 pltpu.VMEM((segments, units, share, inner), BF16),
-                pltpu.VMEM((2, rows, 256), BF16), pltpu.VMEM((model, inner), BF16),
+                pltpu.VMEM((2, rows, 256), BF16), pltpu.VMEM((256, rows), BF16),
+                pltpu.VMEM((2, 256, inner), BF16), pltpu.VMEM((2, rows, 256), BF16),
+                pltpu.VMEM((model, inner), BF16),
                 pltpu.VMEM((model // 4, inner), BF16),
             ]
             + chip_scratch(shard_rows, inner)
             + [pltpu.VMEM((shard_rows, 2 * inner), BF16)]
             + member_scratch(shard_rows, 2 * inner)
-            + [pltpu.VMEM((shard_rows, 2 * inner), BF16)]
-            + [pltpu.VMEM((shard_rows, inner), BF16), pltpu.VMEM((shard_rows, 2 * inner), BF16)]
-            + member_scratch(shard_rows, 2 * inner)
-            + [pltpu.VMEM((shard_rows, 2 * inner), BF16)]
+            + [
+                pltpu.VMEM((2, 2 * shard_rows, inner), BF16), pltpu.VMEM((2 * shard_rows, inner), BF16),
+                pltpu.VMEM((shard_rows, inner), BF16), pltpu.VMEM((shard_rows, 2 * inner), BF16),
+            ]
             + [
                 pltpu.VMEM((CHUNK + 8, inner), F32), pltpu.VMEM((CHUNK + 8, 2 * LANES), F32),
                 pltpu.VMEM(states, F32),
                 pltpu.VMEM((CHUNK + 8, inner), F32), pltpu.VMEM((CHUNK + 8, 2 * LANES), F32),
                 pltpu.VMEM((8, inner), F32),
-                dma((8,)), dma((2,)), dma((1,)), dma((2,)), dma((2,)),
+                dma((8,)), dma((8,)), dma((2,)), dma((2,)), dma((2,)), dma((1,)), dma((2,)), dma((2,)),
                 dma((14 * len(HALF_PIECES),)), dma((14 * len(HALF_PIECES),)),
                 dma((segments,)), dma((segments,)), dma((segments,)), dma((segments,)),
             ],
@@ -1933,8 +2173,8 @@
             cost_estimate=cost(125),
             name="middle",
         )(
-            d_normed_out, gated, gate_in, y, stats, gain_rows, shared, reach, all_decays, normed, g_out,
-            came_left, came_right, projected, first, first, first, first, first, halo, cx, cbc, hp, y, starts, incoming,
+            d_normed_out, gated, gate_in, y, stats, gain_rows, shared, reach, all_decays, normed, weight_gate, g_out,
+            projected, first, first, first, first, first, halo, cx, cbc, hp, y, starts, incoming,
             reach, pick,
         )
     else:
@@ -2014,13 +2254,17 @@
     d_all = lax.dynamic_update_slice(d_all, (tail_rows + extra).astype(BF16), (0, 4 * tokens - 16, 0))
     d_all = d_all.reshape(rows, width)
 
-    g_first = dot_tn(normed, d_all).astype(BF16)
-    d_normed = dot_nt(d_gate, weight_gate) + dot_nt(d_all, weight_first)
-    g_norm_gain = jnp.sum(d_normed * unit_in, axis=0)
-
-    total_x, total_bc, total_dt, vec, grad_rows = plan.tail(
-        g_first, g_x, g_bc, g_heads, g_gate_gain[None], g_norm_gain[None], d_normed.astype(BF16)
-    )
+    if plan.fast:
+        total_x, total_bc, total_dt, vec, grad_rows, total_z = plan.tail(
+            normed, d_all, d_base, weight_first, unit_low, g_x, g_bc, g_heads, g_gate_gain[None], total_z
+        )
+    else:
+        g_first = dot_tn(normed, d_all).astype(BF16)
+        d_normed = dot_nt(d_gate, weight_gate) + dot_nt(d_all, weight_first)
+        g_norm_gain = jnp.sum(d_normed * unit_in, axis=0)
+        total_x, total_bc, total_dt, vec, grad_rows = plan.slow_tail(
+            g_first, g_x, g_bc, g_heads, g_gate_gain[None], g_norm_gain[None], d_normed.astype(BF16)
+        )
     grad_rows = grad_rows.astype(F32)
     resid = hidden.astype(F32)
     own_scale = row_scale(resid)

time: 684 us -> 642 us (0.939)
  Pallas kernels: 439 us -> 524 us
  matrix products: 97.4 us -> 48.4 us
  local copies, waits for them, and re-layouts: 54.3 us -> 25.5 us
  waiting for transfers between devices: 20.4 us -> 0.38 us
  between operations: 15.2 us -> 1.18 us
  other arithmetic: 47.4 us -> 36.5 us
    pallas_call x3 -> x2, Pallas kernels: 166 us -> 246 us  [the longest x1 159 us: tail(): pl.pallas_call(tail_kernel, grid=(2 * steps,), in_specs=[pl.BlockSpec((co...]
    unnamed x150 -> x49, local copies, waits for them, and re-layouts: 48.1 us -> 9.16 us
    dot_general x3 -> x1, matrix products: 37.6 us -> 11.3 us  [dot_nt(): lax.dot_general(a, b, (((1,), (1,)), ((), ())), preferred_element_type=F32)]
    pallas_call x1, Pallas kernels: 36.9 us -> 59.4 us  [body(): pl.pallas_call(scan_forward_kernel, grid=(units, PER_UNIT), in_specs=in_s...]
    pallas_call x1, Pallas kernels: 175 us -> 154 us  [body(): pl.pallas_call(middle_kernel, grid=(spots,), in_specs=[pulls(inner), pull...]
    ppermute x8 -> x4, waiting for transfers between devices: 20.4 us -> 0.38 us  [send(): return lax.ppermute(x, ('fs', 'sp'), pairs)]
    dot_general x3 -> x2, matrix products: 39.2 us -> 27.6 us  [dot(): return jnp.dot(a, b, preferred_element_type=F32)]
    dot_general x2 -> x1, matrix products: 20.6 us -> 9.58 us  [dot_tn(): lax.dot_general(a, b, (((0,), (0,)), ((), ())), preferred_element_type=F32)]
  transfers between devices with their start and end apart: 10 -> 4, of which waited for: 3 -> 1; matrix products, arithmetic and copies ran while one was open for 12% -> 5% of each run, Pallas kernels for 23% -> 0%
where the time goes in v5:
time: 642 us; the launch traced here: 638 us
  Pallas kernels  524 us (82%)
  matrix products  48.4 us (8%)
  other arithmetic  36.5 us (6%)
  local copies, waits for them, and re-layouts  25.5 us (4%)
    pallas_call x1, Pallas kernels, tail(): pl.pallas_call(tail_kernel, grid=(2 * steps,), in_specs=[pl.BlockSpec((co...  159 us
    pallas_call x1, Pallas kernels, body(): pl.pallas_call(middle_kernel, grid=(spots,), in_specs=[pulls(inner), pull...  154 us
    pallas_call x1, Pallas kernels, exchange(): pl.pallas_call(states_kernel, grid=(chunks + 1,), in_specs=[whole(own), w...  87.5 us
    pallas_call x1, Pallas kernels, head(): pl.pallas_call(head_kernel, out_shape=[shape((self.units, 4, self.tokens,...  64 us
    pallas_call x1, Pallas kernels, body(): pl.pallas_call(scan_forward_kernel, grid=(units, PER_UNIT), in_specs=in_s...  59.4 us
    dot_general x2, matrix products, dot(): return jnp.dot(a, b, preferred_element_type=F32)  27.6 us
  transfers between devices with their start and end apart: 4, of which 1 were waited for; matrix products, arithmetic and copies ran while one was open for 5% of the time, Pallas kernels for 0%

profile of v5, /device:TPU:0, one launch (start us, length us, event | category | flops | bytes accessed | tf_op | source)
XLA Modules:
  0.0 637.7 jit_solution(5065191539426749998)
XLA Ops:
  0.6 1.5 copy.48.conv_x
  2.1 1.5 copy.47.w_dt
  3.6 1.4 copy.49.conv_bc
  4.9 1.2 broadcast_in_dim.33.conv_x_bias
  6.2 1.2 broadcast_in_dim.34.gate_gain
  7.4 1.2 broadcast_in_dim.35.norm_gain
  8.7 64.0 %head.1 = (bf16[3,4,128,1536]{3,2,1,0:T(8,128)(2,1)}, bf16[4,2,192,1920]{3,2,1,0:T(8,128)(2,1)}, f32[8,1536]{1,0:T(8,128)}, f32[8,256]{1,0:T(8,128)}, f32[8,128]...) custom-call(bf16[6,128,1536]{2,1,0:T(8,128)(2,1)} %hidden.1, bf16[192,3072]{1,0:T(8,128)(2,1)} %w_x.1, ...), custom_call_target="tpu_custom_call" | custom-call | flops 63250001920 | tf_op jit(solution)/shard_map/head/pallas_call | solution.py:1628
  72.7 0.8 slice_reduce_fusion.2
  73.5 3.3 multiply_reduce_fusion
  76.9 6.0 fusion.3
  82.9 11.7 %convolution_convert_fusion.x.bc.dt.xp.bcp = bf16[1536,1920]{1,0:T(8,128)(2,1)} fusion(bf16[1536,1536]{1,0:T(8,128)(2,1)S(1)} %get-tuple-element.61.normed, bf16[1536,1920]{1,0:T(8,128)(2,1)S(1)} %bitcast.104), kind=kOutput, calls=%fused_computation.11 | convolution fusion | flops 9062645760 | bytes 16515072 | tf_op jit(solution)/shard_map/dot_general | solution.py:22
  94.6 59.4 %scan_forward.1 = (bf16[1536,1536]{1,0:T(8,128)(2,1)}, bf16[12,128,1536]{2,1,0:T(8,128)(2,1)}, bf16[3,128,1536]{2,1,0:T(8,128)(2,1)}, f32[3,8,1536]{2,1,0:T(8,12...) custom-call(bf16[1536,1920]{1,0:T(8,128)(2,1)} %convolution_convert_, ...), custom_call_target="tpu_custom_call" | custom-call | flops 35649998848 | tf_op jit(solution)/shard_map/scan_forward/pallas_call | solution.py:2016
  154.0 1.0 copy.50
  155.1 0.6 concatenate.16.dec
  155.7 87.5 %states.1 = (f32[8,8,1536]{2,1,0:T(8,128)}, bf16[3,4,128,1536]{3,2,1,0:T(8,128)(2,1)}, bf16[4,2,192,1536]{3,2,1,0:T(8,128)(2,1)}, bf16[1536,1536]{1,0:T(8,128)(2...) custom-call(bf16[3,128,1536]{2,1,0:T(8,128)(2,1)} %get-tuple-element, ...), custom_call_target="tpu_custom_call" | custom-call | flops 69000003584 | tf_op jit(solution)/shard_map/states/pallas_call | solution.py:1886
  243.2 1.4 slice_reduce_fusion
  244.6 0.1 collective-permute-start
  244.7 1.1 fusion.11
  245.8 1.0 fusion.13.pick
  246.8 0.8 slice_reduce_fusion.1
  247.7 0.1 pad.17.clone
  247.8 11.3 %convolution_convert_fusion.1 = bf16[1536,1536]{1,0:T(8,128)(2,1)S(1)} fusion(bf16[1536,1536]{1,0:T(8,128)(2,1)} %bitcast.112, bf16[1536,1536]{1,0:T(8,128)(2,1)} %get-tuple-element.76.gated, f32[1536]{0:T(1024)S(1)} %get-tuple-element.171, f32[1536]{0:T(1024)S(1)} %slice_reduce_fusion.1), kind=kOutput, calls=%fused_computation.12 | convolution fusion | flops 7259553792 | bytes 14168064 | tf_op jit(solution)/shard_map/dot_general | solution.py:26
  259.1 1.7 select_bitcast_fusion
  260.7 0.5 collective-permute-start.2
  261.2 15.9 %fusion.2 = (f32[1536]{0:T(1024)}, f32[1536]{0:T(1024)S(1)}, bf16[1536,1536]{1,0:T(8,128)(2,1)}) fusion(bf16[1536,1536]{1,0:T(8,128)(2,1)} %get-tuple-element.76.gated, f32[1536]{0:T(1024)S(1)} %get-tuple-element.171, f32[1536]{0:T(1024)S(1)} %slice_reduce_fusion.1, bf16[1536,1536]{1,0:T(8,128)(2,1)} %bitcast.108, bf16[1536,1536]{1,0:T(8,128)(2,1)} %bitcast.113), kind=kOutput, calls=%fused_computation.4 | convolution fusion | flops 7268987904 | bytes 18898944 | tf_op jit(solution)/shard_map/dot_general | solution.py:22
  277.1 0.4 collective-permute-start.1
  277.4 9.6 %convolution_convert_fusion.2.g_out = bf16[1536,1536]{1,0:T(8,128)(2,1)} fusion(bf16[1536,1536]{1,0:T(8,128)(2,1)S(1)} %bitcast.111, bf16[1536,1536]{1,0:T(8,128)(2,1)S(1)} %bitcast.115, f32[1536]{0:T(1024)S(1)} %get-tuple-element.171, f32[1536]{0:T(1024)S(1)} %slice_reduce_fusion.1), kind=kOutput, calls=%fused_computation.13 | convolution fusion | flops 7259553792 | bytes 14168064 | tf_op jit(solution)/shard_map/dot_general | solution.py:30
  287.0 0.3 copy.61
  287.4 0.3 copy.63
  287.7 1.2 maximum_maximum_fusion.stats
  288.8 5.5 fusion.12.projected
  294.4 154.0 %middle.1 = (bf16[1536,1920]{1,0:T(8,128)(2,1)}, f32[3,8,1536]{2,1,0:T(8,128)}, f32[3,8,256]{2,1,0:T(8,128)}, f32[40,1536]{1,0:T(8,128)}, f32[40,256]{1,0:T(8,12...) custom-call(bf16[1536,1536]{1,0:T(8,128)(2,1)} %get-tuple-element.17, ...), custom_call_target="tpu_custom_call" | custom-call | flops 143750004736 | tf_op jit(solution)/shard_map/middle/pallas_call | solution.py:2121
  448.4 0.9 convert.9
  449.3 0.7 convert.10
  450.1 1.3 collective-permute-start.3
  451.4 0.6 add_rsqrt_fusion.2
  452.0 0.1 maximum_reduce_fusion.1
  452.1 0.6 broadcast_in_dim.41.g_gate
  452.7 2.9 convert_element_type.107
  455.7 0.4 collective-permute-done.3
  456.0 0.1 multiply_add_fusion
  456.1 1.7 fusion.16
  457.8 158.5 %tail.1 = (f32[192,3072]{1,0:T(8,128)}, f32[192,256]{1,0:T(8,128)}, f32[192,256]{1,0:T(8,128)}, f32[2,16,1536]{2,1,0:T(8,128)}, bf16[6,128,1536]{2,1,0:T(8,128)(2,1)}, /*index=5*/f32[192,3072]{1,0:T(8,128)}) custom-call(bf16[1536,1536]{1,0:T(8,128)(2,1)} %copy-done.3, bf16[1536,1920]{1,0:T(8,128)(2,1)} %bitcast.97, ...), custom_call_target="tpu_custom_call" | custom-call | flops 149500002304 | tf_op jit(solution)/shard_map/tail/pallas_call | solution.py:1700
  616.4 0.7 fusion.26
  617.1 0.1 dynamic-slice_add_fusion
  617.2 0.6 slice_bitcast_fusion.4
  617.8 0.5 slice_bitcast_fusion.8
  618.3 0.8 fusion.28
  619.1 0.9 slice.141
  620.0 0.8 slice_reduce_fusion.3
  620.8 1.0 fusion.27
  621.7 0.1 pad_maximum_fusion
  621.8 0.7 copy.56
  622.5 2.7 fusion.6
  625.3 0.1 reshape.204
  625.4 0.1 constant_dynamic-slice_fusion.1
  625.4 0.5 slice_bitcast_fusion.5
  626.0 6.1 fusion.9
  632.1 0.6 dynamic-slice_bitcast_fusion
  632.7 0.7 dynamic-slice_reduce_fusion
  633.3 0.6 fusion.25
  634.0 1.4 copy.73
  635.4 1.4 copy.74
  636.8 0.7 copy.75
  (60 shorter events, 0.2 us)
Async XLA Ops:
  73.5 9.3 %copy-start.7 = (f32[1536]{0:T(1024)}, f32[1536]{0:T(1024)S(1)}, u32[]{:S(2)}) copy-start(f32[1536]{0:T(1024)S(1)} %slice_reduce_fusion.2) | copy-start | bytes 18436
  76.9 6.0 copy-start.14
  82.9 11.7 %copy-start.3 = (bf16[1536,1536]{1,0:T(8,128)(2,1)}, bf16[1536,1536]{1,0:T(8,128)(2,1)S(1)}, u32[]{:S(2)}) copy-start(bf16[1536,1536]{1,0:T(8,128)(2,1)S(1)} %get-tuple-element.61.normed) | copy-start | bytes 14155780
  155.7 89.0 %copy-start = (bf16[6,128,1536]{2,1,0:T(8,128)(2,1)S(1)}, bf16[6,128,1536]{2,1,0:T(8,128)(2,1)}, u32[]{:S(2)}) copy-start(bf16[6,128,1536]{2,1,0:T(8,128)(2,1)} %hidden.1) | copy-start | bytes 7077892
  244.6 3.2 collective-permute-start
  259.0 18.0 %copy-start.2 = (bf16[1536,1536]{1,0:T(8,128)(2,1)}, bf16[1536,1536]{1,0:T(8,128)(2,1)S(1)}, u32[]{:S(2)}) copy-start(bf16[1536,1536]{1,0:T(8,128)(2,1)S(1)} %convolution_convert_fusion.1) | copy-start | bytes 14155780
  259.0 18.4 %slice-start = ((s8[4718592]{0:T(1024)(128)(4,1)}), s8[4194304]{0:T(1024)(128)(4,1)S(1)}, s32[]{:S(2)}) async-start(s8[4718592]{0:T(1024)(128)(4,1)} %bitcast.109), calls=%async_computation | async-start | bytes 8388608
  259.0 18.4 %slice-start.2 = ((s8[4718592]{0:T(1024)(128)(4,1)}), s8[4194304]{0:T(1024)(128)(4,1)S(1)}, s32[]{:S(2)}) async-start(s8[4718592]{0:T(1024)(128)(4,1)} %bitcast.114), calls=%async_computation.2 | async-start | bytes 8388608
  260.7 28.1 %collective-permute-start.2 = (bf16[3,2,128,1536]{3,2,1,0:T(8,128)(2,1)}, bf16[3,2,128,1536]{3,2,1,0:T(8,128)(2,1)}, u32[]{:S(2)}, u32[]{:S(2)}) collective-permute-start(bf16[3,2,128,1536]{3,2,1,0:T(8,128)(2,1)} %select_bitcast_fusion), channel_id=1, source_target_pairs={{0,4},{1,5},{2,6},{3,7},{4,0},{5,1},{6,2},{7,3},{8,12},{9,13},{10,... | collective-permute-start | bytes 7077896 | tf_op jit(solution)/shard_map/ppermute | solution.py:1595
  261.2 16.2 %slice-start.1 = ((s8[4718592]{0:T(1024)(128)(4,1)}), s8[524288]{0:T(1024)(128)(4,1)S(1)}, s32[]{:S(2)}) async-start(s8[4718592]{0:T(1024)(128)(4,1)} %bitcast.109), calls=%async_computation.1 | async-start | bytes 1048576
  261.2 16.2 %slice-start.3 = ((s8[4718592]{0:T(1024)(128)(4,1)}), s8[524288]{0:T(1024)(128)(4,1)S(1)}, s32[]{:S(2)}) async-start(s8[4718592]{0:T(1024)(128)(4,1)} %bitcast.114), calls=%async_computation.3 | async-start | bytes 1048576
  277.1 10.3 %collective-permute-start.1 = (f32[12,128]{1,0:T(8,128)S(1)}, f32[12,128]{1,0:T(8,128)S(1)}, u32[]{:S(2)}, u32[]{:S(2)}) collective-permute-start(f32[12,128]{1,0:T(8,128)S(1)} %bitcast.95), channel_id=1, source_target_pairs={{0,4},{1,5},{2,6},{3,7},{4,0},{5,1},{6,2},{7,3},{8,12},{9,13},{10,... | collective-permute-start | bytes 18440 | tf_op jit(solution)/shard_map/ppermute | solution.py:1595
  294.4 157.0 %copy-start.10 = (f32[6,128]{1,0:T(8,128)S(1)}, f32[6,128]{1,0:T(8,128)}, u32[]{:S(2)}) copy-start(f32[6,128]{1,0:T(8,128)} %fusion.11) | copy-start | bytes 9220
  294.4 157.7 %copy-start.11 = (f32[8,1536]{1,0:T(8,128)S(1)}, f32[8,1536]{1,0:T(8,128)}, u32[]{:S(2)}) copy-start(f32[8,1536]{1,0:T(8,128)} %get-tuple-element.63.cx) | copy-start | bytes 147460
  294.4 157.7 %copy-start.13 = (f32[8,256]{1,0:T(8,128)S(1)}, f32[8,256]{1,0:T(8,128)}, u32[]{:S(2)}) copy-start(f32[8,256]{1,0:T(8,128)} %get-tuple-element.64.cbc) | copy-start | bytes 24580
  294.4 157.7 %copy-start.12 = (f32[1536]{0:T(1024)S(1)}, f32[1536]{0:T(1024)}, u32[]{:S(2)}) copy-start(f32[1536]{0:T(1024)} %get-tuple-element.150) | copy-start | bytes 18436
  450.1 5.9 collective-permute-start.3
  457.8 164.7 %copy-start.1 = (bf16[6,128,1536]{2,1,0:T(8,128)(2,1)S(1)}, bf16[6,128,1536]{2,1,0:T(8,128)(2,1)}, u32[]{:S(2)}) copy-start(bf16[6,128,1536]{2,1,0:T(8,128)(2,1)} %hidden.1) | copy-start | bytes 7077892
  457.8 164.7 %copy-start.8 = (f32[1536]{0:T(1024)S(1)}, f32[1536]{0:T(1024)}, u32[]{:S(2)}) copy-start(f32[1536]{0:T(1024)} %copy-done.7) | copy-start | bytes 18436
  457.8 164.7 %copy-start.9 = (f32[6,128]{1,0:T(8,128)S(1)}, f32[6,128]{1,0:T(8,128)}, u32[]{:S(2)}) copy-start(f32[6,128]{1,0:T(8,128)} %add_rsqrt_fusion.2) | copy-start | bytes 9220
  626.0 8.0 %copy-start.5 = (f32[192,3072]{1,0:T(8,128)S(1)}, f32[192,3072]{1,0:T(8,128)}, u32[]{:S(2)}) copy-start(f32[192,3072]{1,0:T(8,128)} %get-tuple-element.195) | copy-start | bytes 7077892
  632.1 3.3 copy-start.4
  634.0 2.8 copy-start.6

commit v6 on v5

--- a/solution.py
+++ b/solution.py
@@ -375,6 +375,22 @@
     )
 
 
+class Bounce:
+    def __init__(self, src, buffer, dst, sems, n):
+        self.into = pltpu.make_async_copy(src, buffer, sems.at[2 * n])
+        self.out = pltpu.make_async_copy(buffer, dst, sems.at[2 * n + 1])
+
+    def start(self):
+        self.into.start()
+
+    def relay(self):
+        self.into.wait()
+        self.out.start()
+
+    def wait(self):
+        self.out.wait()
+
+
 class Trade:
     def __init__(self, source, sends, receives):
         self.f, self.z, self.core, self.chip, _, _ = places()
@@ -399,12 +415,12 @@
 
 
 class Gather:
-    def __init__(self, weight, target, sends, receives, local):
+    def __init__(self, weight, target, sends, receives, local, buffer):
         f, z, self.core, self.chip, self.by_x, self.by_y = places()
         self.weight, self.target, self.sends, self.receives = weight, target, sends, receives
         self.partner = (f + 1 - 2 * self.core, z)
         self.over_x, self.over_y = (2 * self.by_x + self.core, z), (2 * self.by_y + self.core, z)
-        self.keep = pltpu.make_async_copy(self.columns(self.core), self.part(self.chip, self.core), local.at[0])
+        self.keep = Bounce(self.columns(self.core), buffer, self.part(self.chip, self.core), local, 0)
 
     def columns(self, side):
         width = self.weight.shape[1] // 2
@@ -445,6 +461,7 @@
         self.keep.start()
 
     def second(self):
+        self.keep.relay()
         self.arrives(0)
         for slot in (3, 4):
             self.sent(slot).start()
@@ -472,9 +489,9 @@
     x, bc, dt, first, cot, weight, cx, cbc, hp,
     y, st, own, dec, bcs, acum, halo_out, near_out, far_out, gathered,
     xe, be, state, base, halo, halo_sends, halo_receives, sends, receives, local,
-    w_sends, w_receives, w_local,
+    w_sends, w_receives, w_local, w_buffer, row_buffer,
 ):
-    gather = Gather(weight, gathered, w_sends, w_receives, w_local)
+    gather = Gather(weight, gathered, w_sends, w_receives, w_local, w_buffer)
     unit, chunk = pl.program_id(0), pl.program_id(1)
     segments, trade = Segments(), Trade(cot, sends, receives)
     me, last = segments.me, segments.count - 1
@@ -487,7 +504,7 @@
 
     far_copy = trade.send(trade.rows_for(trade.far_group, 0, EARLY_UNITS), far_out, 0, trade.far)
     near_copy = trade.send(trade.rows_for(trade.near_group, 0, units), near_out, 1, trade.near)
-    keep = pltpu.make_async_copy(trade.rows_for(trade.near_group, 0, units), near_out, local.at[0])
+    keep = Bounce(trade.rows_for(trade.near_group, 0, units), row_buffer, near_out, local, 0)
 
     @pl.when((unit == 0) & (chunk == 0))
     def _():
@@ -535,6 +552,10 @@
 
     forward_kernel(x, bc, dt, halo, cx, cbc, hp, y, st, own, dec, bcs, acum, xe, be, state, base)
 
+    @pl.when((unit == 0) & (chunk == 1) & trade.stays)
+    def _():
+        keep.relay()
+
     for at_unit, at_chunk, stage in ((0, 0, gather.second), (1, 1, gather.third), (1, 3, gather.fourth)):
 
         @pl.when((unit == at_unit) & (chunk == at_chunk))
@@ -572,7 +593,8 @@
 def head_kernel(
     hidden, w_x, w_bc, w_dt, conv_x, conv_x_bias, gate_gain, norm_gain, conv_bc, conv_bc_bias, dt_bias, a_log, skip_d,
     rows_out, first_out, cx, cbc, hp, gain_in, gain_rows,
-    dt_mine, dt_other, small, small_all, local, sends, receives, small_sends, small_receives,
+    dt_mine, dt_other, small, small_all, row_buffer, x_buffer, bc_buffer,
+    local, sends, receives, small_sends, small_receives,
 ):
     f, z, core, chip, by_x, by_y = places()
     trade = Trade(hidden, sends, receives)
@@ -628,7 +650,7 @@
     for one in (to_partner, to_x, to_y):
         one.start()
     to_near = copy(trade.rows_for(trade.near_group, 0, units), rows_out.at[:, z], 4, near)
-    keep_rows = pltpu.make_async_copy(trade.rows_for(trade.near_group, 0, units), rows_out.at[:, z], local.at[0])
+    keep_rows = Bounce(trade.rows_for(trade.near_group, 0, units), row_buffer, rows_out.at[:, z], local, 0)
 
     @pl.when(stays)
     def _():
@@ -640,14 +662,16 @@
 
     own = part(chip, core)
     keeps = [
-        pltpu.make_async_copy(
-            w_x.at[:, pl.ds(pl.multiple_of(core * inner, inner), inner)], own.at[:, pl.ds(0, inner)], local.at[1]
+        Bounce(
+            w_x.at[:, pl.ds(pl.multiple_of(core * inner, inner), inner)], x_buffer,
+            own.at[:, pl.ds(0, inner)], local, 1,
         ),
-        pltpu.make_async_copy(w_bc, own.at[:, pl.ds(inner, 2 * LANES)], local.at[2]),
-        pltpu.make_async_copy(dt_mine, own.at[:, pl.ds(inner + 2 * LANES, LANES)], local.at[3]),
+        Bounce(w_bc, bc_buffer, own.at[:, pl.ds(inner, 2 * LANES)], local, 2),
     ]
+    keep_dt = pltpu.make_async_copy(dt_mine, own.at[:, pl.ds(inner + 2 * LANES, LANES)], local.at[6])
     for keep in keeps:
         keep.start()
+    keep_dt.start()
 
     share = conv_x.shape[0]
     per_norm, per_bc, per_head = norm_gain.shape[1], conv_bc.shape[0], dt_bias.shape[1]
@@ -680,6 +704,13 @@
     for k in range(1, shards):
         small_copy(k, f).start()
     small_all[f] = small[...]
+
+    for keep in keeps:
+        keep.relay()
+
+    @pl.when(stays)
+    def _():
+        keep_rows.relay()
 
     copy(part(chip, core), part(chip, 1 - core), 1, partner).wait_recv()
     again_x = copy(part(chip, 1 - core), part(chip, 1 - core), 5, over_x)
@@ -753,6 +784,7 @@
         small_copy(k, f).wait_send()
     for keep in keeps:
         keep.wait()
+    keep_dt.wait()
 
 
 def states_kernel(
@@ -761,11 +793,12 @@
     incoming, parts, decs, results, weight, gate, blocks,
     sends, receives, dec_sends, dec_receives, back_sends, back_receives,
     row_sends, row_receives, w_sends, w_receives, local, w_local, block_sems,
+    w_buffer, near_buffer, far_buffer, row_local,
 ):
     i = pl.program_id(0)
     chunks = pl.num_programs(0) - 1
     segments, trade = Segments(), Trade(cot, row_sends, row_receives)
-    gather = Gather(w_out, gathered, w_sends, w_receives, w_local)
+    gather = Gather(w_out, gathered, w_sends, w_receives, w_local, w_buffer)
     me, count, z = segments.me, segments.count, segments.z
     units, share = own.shape[0], parts.shape[2]
     early = far_rows.shape[0]
@@ -823,8 +856,8 @@
     near_on = trade.send(near_rows, rows_out.at[:, near_at], 1, trade.partner)
     far_on = trade.send(far_rows, rows_out.at[:early, far_at], 2, trade.partner)
     last_on = trade.send(rows_out.at[early:, far_at], rows_out.at[early:, far_at], 3, trade.partner)
-    near_keep = pltpu.make_async_copy(near_rows, rows_out.at[:, near_at], local.at[0])
-    far_keep = pltpu.make_async_copy(far_rows, rows_out.at[:early, far_at], local.at[1])
+    near_keep = Bounce(near_rows, near_buffer, rows_out.at[:, near_at], row_local, 0)
+    far_keep = Bounce(far_rows, far_buffer, rows_out.at[:early, far_at], row_local, 1)
     take_weight = pltpu.make_async_copy(w_gate, weight, local.at[2])
     keep_gate = pltpu.make_async_copy(gate, gate_out, local.at[3])
     keep_states = pltpu.make_async_copy(incoming, incoming_out, local.at[4])
@@ -852,6 +885,8 @@
         take_weight.wait()
         for k in range(count_blocks // 2):
             multiply(k)
+        near_keep.relay()
+        far_keep.relay()
         for k in range(1, count):
             dec_copy(k, False).wait_recv()
             out_copy(k, False).wait_recv()
@@ -1283,7 +1318,7 @@
             end.wait()
 
 
-def trade_steps(source, target, local, sends, receives):
+def trade_steps(source, target, buffer, local, sends, receives):
     f, z, core, chip, _, _ = places()
     units = source.shape[0]
     bit, upper = z % 2, z // 2
@@ -1293,14 +1328,33 @@
     def copy(k, n, device, group):
         return remote(source.at[:, k], target.at[pl.ds(group * units, units)], sends, receives, n, device)
 
-    keep = pltpu.make_async_copy(source.at[:, upper], target.at[pl.ds(upper * units, units)], local.at[0])
+    tokens = source.shape[2]
+    keeps = [
+        Bounce(
+            source.at[u, upper], buffer.at[pl.ds(u * tokens, tokens)], target.at[upper * units + u], local, u
+        )
+        for u in range(units)
+    ]
+
+    def relay():
+        @pl.when(stays)
+        def _():
+            for keep in keeps:
+                keep.relay()
+
+    def settle():
+        @pl.when(stays)
+        def _():
+            for keep in keeps:
+                keep.wait()
 
     def start():
         copy(1 - upper, 0, far, upper).start()
 
         @pl.when(stays)
         def _():
-            keep.start()
+            for keep in keeps:
+                keep.start()
 
         @pl.when(jnp.logical_not(stays))
         def _():
@@ -1310,15 +1364,11 @@
         copy(1 - upper, 0, far, 1 - upper).wait_recv()
         copy(1 - upper, 0, far, upper).wait_send()
 
-        @pl.when(stays)
-        def _():
-            keep.wait()
-
         @pl.when(jnp.logical_not(stays))
         def _():
             copy(upper, 1, near, upper).wait()
 
-    return start, finish, far, near, stays
+    return start, relay, settle, finish, far, near, stays
 
 
 class Segments:
@@ -1360,8 +1410,8 @@
     def at(k, size):
         return pl.ds(pl.multiple_of(k * size, size), size)
 
-    start_trade, finish_trade, trade_far, trade_near, stays = trade_steps(
-        projected, tokens_out, trade_local, trade_sends, trade_receives
+    start_trade, relay_trade, settle_trade, finish_trade, trade_far, trade_near, stays = trade_steps(
+        projected, tokens_out, g_z, trade_local, trade_sends, trade_receives
     )
     out = Reduction(HALF_PIECES, sends, receives, 0)
     gz = Reduction(HALF_PIECES, sends, receives, 7 * len(HALF_PIECES))
@@ -1425,6 +1475,10 @@
             copy.start()
         start_trade()
 
+    @pl.when(i == 3)
+    def _():
+        relay_trade()
+
     @pl.when(i < chunks)
     def _():
         place = at(i, CHUNK)
@@ -1497,6 +1551,7 @@
             state_copy(k, True).start()
         fetch(0).start()
         fetch_w(0).start()
+        settle_trade()
         parts[me] = own[:, at(me, share)]
         for k in range(6):
             multiply(k)
@@ -1638,7 +1693,9 @@
             scratch_shapes=[
                 pltpu.VMEM((rows, LANES), BF16), pltpu.VMEM((rows, LANES), BF16),
                 pltpu.VMEM(small, F32), pltpu.VMEM((self.shards,) + small, F32),
-                dma((4,)), dma((11,)), dma((11,)), dma((self.shards,)), dma((self.shards,)),
+                pltpu.VMEM((self.units, self.tokens, hidden.shape[-1]), BF16),
+                pltpu.VMEM((rows, inner), BF16), pltpu.VMEM((rows, 2 * LANES), BF16),
+                dma((7,)), dma((11,)), dma((11,)), dma((self.shards,)), dma((self.shards,)),
             ],
             compiler_params=pltpu.CompilerParams(
                 collective_id=2, has_side_effects=True, vmem_limit_bytes=VMEM_LIMIT
@@ -1903,7 +1960,11 @@
             pltpu.VMEM(w_gate.shape, BF16), pltpu.VMEM((rows, width), BF16), pltpu.VMEM((2, 256, model), BF16),
         ]
         + [dma((count,))] * 6
-        + [dma((4,)), dma((4,)), dma((7,)), dma((7,)), dma((5,)), dma((1,)), dma((2,))],
+        + [dma((4,)), dma((4,)), dma((7,)), dma((7,)), dma((5,)), dma((2,)), dma((2,))]
+        + [
+            pltpu.VMEM((w_out.shape[0], width), BF16), pltpu.VMEM(near.shape, BF16),
+            pltpu.VMEM(far.shape, BF16), dma((4,)),
+        ],
         compiler_params=pltpu.CompilerParams(
             dimension_semantics=("arbitrary",), collective_id=0, has_side_effects=True,
             vmem_limit_bytes=VMEM_LIMIT,
@@ -2024,7 +2085,8 @@
                 shaped(4, 2, w_z.shape[0], inner),
             ],
             scratch_shapes=scratch
-            + [pltpu.VMEM(edge, BF16), dma((1,)), dma((1,)), dma((2,)), dma((2,)), dma((1,)), dma((7,)), dma((7,)), dma((1,))],
+            + [pltpu.VMEM(edge, BF16), dma((1,)), dma((1,)), dma((2,)), dma((2,)), dma((2,)), dma((7,)), dma((7,)), dma((2,))]
+            + [pltpu.VMEM((w_z.shape[0], inner), BF16), pltpu.VMEM((units, tokens, model), BF16)],
             compiler_params=pltpu.CompilerParams(
                 dimension_semantics=("arbitrary", "arbitrary"), vmem_limit_bytes=VMEM_LIMIT,
                 collective_id=1, has_side_effects=True,
@@ -2162,7 +2224,7 @@
                 pltpu.VMEM(states, F32),
                 pltpu.VMEM((CHUNK + 8, inner), F32), pltpu.VMEM((CHUNK + 8, 2 * LANES), F32),
                 pltpu.VMEM((8, inner), F32),
-                dma((8,)), dma((8,)), dma((2,)), dma((2,)), dma((2,)), dma((1,)), dma((2,)), dma((2,)),
+                dma((8,)), dma((8,)), dma((2,)), dma((2,)), dma((2,)), dma((6,)), dma((2,)), dma((2,)),
                 dma((14 * len(HALF_PIECES),)), dma((14 * len(HALF_PIECES),)),
                 dma((segments,)), dma((segments,)), dma((segments,)), dma((segments,)),
             ],

time: 642 us -> 636 us (level)
  Pallas kernels: 524 us -> 517 us
    pallas_call x1, Pallas kernels: 59.4 us -> 47.3 us  [body(): pl.pallas_call(scan_forward_kernel, grid=(units, PER_UNIT), in_specs=in_s...]
where the time goes in v6:
time: 636 us; the launch traced here: 631 us
  Pallas kernels  517 us (81%)
  matrix products  48.4 us (8%)
  other arithmetic  36.5 us (6%)
  local copies, waits for them, and re-layouts  25.5 us (4%)
    pallas_call x1, Pallas kernels, tail(): pl.pallas_call(tail_kernel, grid=(2 * steps,), in_specs=[pl.BlockSpec((co...  159 us
    pallas_call x1, Pallas kernels, body(): pl.pallas_call(middle_kernel, grid=(spots,), in_specs=[pulls(inner), pull...  158 us
    pallas_call x1, Pallas kernels, exchange(): pl.pallas_call(states_kernel, grid=(chunks + 1,), in_specs=[whole(own), w...  88.2 us
    pallas_call x1, Pallas kernels, head(): pl.pallas_call(head_kernel, out_shape=[shape((self.units, 4, self.tokens,...  64.2 us
    pallas_call x1, Pallas kernels, body(): pl.pallas_call(scan_forward_kernel, grid=(units, PER_UNIT), in_specs=in_s...  47.3 us
    dot_general x2, matrix products, dot(): return jnp.dot(a, b, preferred_element_type=F32)  27.6 us
  transfers between devices with their start and end apart: 4, of which 1 were waited for; matrix products, arithmetic and copies ran while one was open for 5% of the time, Pallas kernels for 0%

profile of v6, /device:TPU:0, one launch (start us, length us, event | category | flops | bytes accessed | tf_op | source)
XLA Modules:
  0.0 631.1 jit_solution(8431864882745222156)
XLA Ops:
  0.6 1.5 copy.48.conv_x
  2.1 1.5 copy.47.w_dt
  3.6 1.4 copy.49.conv_bc
  4.9 1.2 broadcast_in_dim.33.conv_x_bias
  6.2 1.2 broadcast_in_dim.34.gate_gain
  7.4 1.2 broadcast_in_dim.35.norm_gain
  8.7 64.2 %head.1 = (bf16[3,4,128,1536]{3,2,1,0:T(8,128)(2,1)}, bf16[4,2,192,1920]{3,2,1,0:T(8,128)(2,1)}, f32[8,1536]{1,0:T(8,128)}, f32[8,256]{1,0:T(8,128)}, f32[8,128]...) custom-call(bf16[6,128,1536]{2,1,0:T(8,128)(2,1)} %hidden.1, bf16[192,3072]{1,0:T(8,128)(2,1)} %w_x.1, ...), custom_call_target="tpu_custom_call" | custom-call | flops 63250001920 | tf_op jit(solution)/shard_map/head/pallas_call | solution.py:1683
  72.8 0.8 slice_reduce_fusion.2
  73.6 3.3 multiply_reduce_fusion
  77.0 6.0 fusion.3
  83.0 11.7 %convolution_convert_fusion.x.bc.dt.xp.bcp = bf16[1536,1920]{1,0:T(8,128)(2,1)} fusion(bf16[1536,1536]{1,0:T(8,128)(2,1)S(1)} %get-tuple-element.61.normed, bf16[1536,1920]{1,0:T(8,128)(2,1)S(1)} %bitcast.104), kind=kOutput, calls=%fused_computation.11 | convolution fusion | flops 9062645760 | bytes 16515072 | tf_op jit(solution)/shard_map/dot_general | solution.py:22
  94.7 47.3 %scan_forward.1 = (bf16[1536,1536]{1,0:T(8,128)(2,1)}, bf16[12,128,1536]{2,1,0:T(8,128)(2,1)}, bf16[3,128,1536]{2,1,0:T(8,128)(2,1)}, f32[3,8,1536]{2,1,0:T(8,12...) custom-call(bf16[1536,1920]{1,0:T(8,128)(2,1)} %convolution_convert_, ...), custom_call_target="tpu_custom_call" | custom-call | flops 35649998848 | tf_op jit(solution)/shard_map/scan_forward/pallas_call | solution.py:2077
  142.0 1.0 copy.50
  143.0 0.6 concatenate.16.dec
  143.6 88.2 %states.1 = (f32[8,8,1536]{2,1,0:T(8,128)}, bf16[3,4,128,1536]{3,2,1,0:T(8,128)(2,1)}, bf16[4,2,192,1536]{3,2,1,0:T(8,128)(2,1)}, bf16[1536,1536]{1,0:T(8,128)(2...) custom-call(bf16[3,128,1536]{2,1,0:T(8,128)(2,1)} %get-tuple-element, ...), custom_call_target="tpu_custom_call" | custom-call | flops 69000003584 | tf_op jit(solution)/shard_map/states/pallas_call | solution.py:1943
  231.9 1.4 slice_reduce_fusion
  233.3 0.1 collective-permute-start
  233.4 1.1 fusion.11
  234.5 1.0 fusion.13.pick
  235.5 0.8 slice_reduce_fusion.1
  236.4 0.1 pad.17.clone
  236.5 11.3 %convolution_convert_fusion.1 = bf16[1536,1536]{1,0:T(8,128)(2,1)S(1)} fusion(bf16[1536,1536]{1,0:T(8,128)(2,1)} %bitcast.112, bf16[1536,1536]{1,0:T(8,128)(2,1)} %get-tuple-element.76.gated, f32[1536]{0:T(1024)S(1)} %get-tuple-element.171, f32[1536]{0:T(1024)S(1)} %slice_reduce_fusion.1), kind=kOutput, calls=%fused_computation.12 | convolution fusion | flops 7259553792 | bytes 14168064 | tf_op jit(solution)/shard_map/dot_general | solution.py:26
  247.7 1.7 select_bitcast_fusion
  249.4 0.5 collective-permute-start.2
  249.9 15.9 %fusion.2 = (f32[1536]{0:T(1024)}, f32[1536]{0:T(1024)S(1)}, bf16[1536,1536]{1,0:T(8,128)(2,1)}) fusion(bf16[1536,1536]{1,0:T(8,128)(2,1)} %get-tuple-element.76.gated, f32[1536]{0:T(1024)S(1)} %get-tuple-element.171, f32[1536]{0:T(1024)S(1)} %slice_reduce_fusion.1, bf16[1536,1536]{1,0:T(8,128)(2,1)} %bitcast.108, bf16[1536,1536]{1,0:T(8,128)(2,1)} %bitcast.113), kind=kOutput, calls=%fused_computation.4 | convolution fusion | flops 7268987904 | bytes 18898944 | tf_op jit(solution)/shard_map/dot_general | solution.py:22
  265.8 0.4 collective-permute-start.1
  266.1 9.6 %convolution_convert_fusion.2.g_out = bf16[1536,1536]{1,0:T(8,128)(2,1)} fusion(bf16[1536,1536]{1,0:T(8,128)(2,1)S(1)} %bitcast.111, bf16[1536,1536]{1,0:T(8,128)(2,1)S(1)} %bitcast.115, f32[1536]{0:T(1024)S(1)} %get-tuple-element.171, f32[1536]{0:T(1024)S(1)} %slice_reduce_fusion.1), kind=kOutput, calls=%fused_computation.13 | convolution fusion | flops 7259553792 | bytes 14168064 | tf_op jit(solution)/shard_map/dot_general | solution.py:30
  275.7 0.3 copy.61
  276.1 0.3 copy.63
  276.4 1.2 maximum_maximum_fusion.stats
  277.5 5.5 fusion.12.projected
  283.1 158.3 %middle.1 = (bf16[1536,1920]{1,0:T(8,128)(2,1)}, f32[3,8,1536]{2,1,0:T(8,128)}, f32[3,8,256]{2,1,0:T(8,128)}, f32[40,1536]{1,0:T(8,128)}, f32[40,256]{1,0:T(8,12...) custom-call(bf16[1536,1536]{1,0:T(8,128)(2,1)} %get-tuple-element.17, ...), custom_call_target="tpu_custom_call" | custom-call | flops 143750004736 | tf_op jit(solution)/shard_map/middle/pallas_call | solution.py:2183
  441.4 0.9 convert.9
  442.3 0.7 convert.10
  443.0 1.3 collective-permute-start.3
  444.4 0.6 add_rsqrt_fusion.2
  445.0 0.1 maximum_reduce_fusion.1
  445.1 0.6 broadcast_in_dim.41.g_gate
  445.7 2.9 convert_element_type.107
  448.6 0.8 collective-permute-done.3
  449.4 0.1 multiply_add_fusion
  449.5 1.7 fusion.16
  451.2 158.6 %tail.1 = (f32[192,3072]{1,0:T(8,128)}, f32[192,256]{1,0:T(8,128)}, f32[192,256]{1,0:T(8,128)}, f32[2,16,1536]{2,1,0:T(8,128)}, bf16[6,128,1536]{2,1,0:T(8,128)(2,1)}, /*index=5*/f32[192,3072]{1,0:T(8,128)}) custom-call(bf16[1536,1536]{1,0:T(8,128)(2,1)} %copy-done.3, bf16[1536,1920]{1,0:T(8,128)(2,1)} %bitcast.97, ...), custom_call_target="tpu_custom_call" | custom-call | flops 149500002304 | tf_op jit(solution)/shard_map/tail/pallas_call | solution.py:1757
  609.8 0.7 fusion.26
  610.6 0.1 dynamic-slice_add_fusion
  610.6 0.6 slice_bitcast_fusion.4
  611.2 0.5 slice_bitcast_fusion.8
  611.7 0.8 fusion.28
  612.6 0.9 slice.141
  613.5 0.8 slice_reduce_fusion.3
  614.2 1.0 fusion.27
  615.2 0.1 pad_maximum_fusion
  615.3 0.7 copy.56
  616.0 2.7 fusion.6
  618.7 0.1 reshape.204
  618.8 0.1 constant_dynamic-slice_fusion.1
  618.9 0.5 slice_bitcast_fusion.5
  619.4 6.1 fusion.9
  625.5 0.6 dynamic-slice_bitcast_fusion
  626.1 0.7 dynamic-slice_reduce_fusion
  626.8 0.6 fusion.25
  627.4 1.4 copy.73
  628.8 1.4 copy.74
  630.3 0.7 copy.75
  (60 shorter events, 0.2 us)
Async XLA Ops:
  73.6 9.3 %copy-start.7 = (f32[1536]{0:T(1024)}, f32[1536]{0:T(1024)S(1)}, u32[]{:S(2)}) copy-start(f32[1536]{0:T(1024)S(1)} %slice_reduce_fusion.2) | copy-start | bytes 18436
  77.0 6.0 copy-start.14
  83.0 11.7 %copy-start.3 = (bf16[1536,1536]{1,0:T(8,128)(2,1)}, bf16[1536,1536]{1,0:T(8,128)(2,1)S(1)}, u32[]{:S(2)}) copy-start(bf16[1536,1536]{1,0:T(8,128)(2,1)S(1)} %get-tuple-element.61.normed) | copy-start | bytes 14155780
  143.6 89.8 %copy-start = (bf16[6,128,1536]{2,1,0:T(8,128)(2,1)S(1)}, bf16[6,128,1536]{2,1,0:T(8,128)(2,1)}, u32[]{:S(2)}) copy-start(bf16[6,128,1536]{2,1,0:T(8,128)(2,1)} %hidden.1) | copy-start | bytes 7077892
  233.3 3.2 collective-permute-start
  247.7 18.0 %copy-start.2 = (bf16[1536,1536]{1,0:T(8,128)(2,1)}, bf16[1536,1536]{1,0:T(8,128)(2,1)S(1)}, u32[]{:S(2)}) copy-start(bf16[1536,1536]{1,0:T(8,128)(2,1)S(1)} %convolution_convert_fusion.1) | copy-start | bytes 14155780
  247.7 18.4 %slice-start = ((s8[4718592]{0:T(1024)(128)(4,1)}), s8[4194304]{0:T(1024)(128)(4,1)S(1)}, s32[]{:S(2)}) async-start(s8[4718592]{0:T(1024)(128)(4,1)} %bitcast.109), calls=%async_computation | async-start | bytes 8388608
  247.7 18.4 %slice-start.2 = ((s8[4718592]{0:T(1024)(128)(4,1)}), s8[4194304]{0:T(1024)(128)(4,1)S(1)}, s32[]{:S(2)}) async-start(s8[4718592]{0:T(1024)(128)(4,1)} %bitcast.114), calls=%async_computation.2 | async-start | bytes 8388608
  249.4 28.1 %collective-permute-start.2 = (bf16[3,2,128,1536]{3,2,1,0:T(8,128)(2,1)}, bf16[3,2,128,1536]{3,2,1,0:T(8,128)(2,1)}, u32[]{:S(2)}, u32[]{:S(2)}) collective-permute-start(bf16[3,2,128,1536]{3,2,1,0:T(8,128)(2,1)} %select_bitcast_fusion), channel_id=1, source_target_pairs={{0,4},{1,5},{2,6},{3,7},{4,0},{5,1},{6,2},{7,3},{8,12},{9,13},{10,... | collective-permute-start | bytes 7077896 | tf_op jit(solution)/shard_map/ppermute | solution.py:1650
  249.9 16.2 %slice-start.1 = ((s8[4718592]{0:T(1024)(128)(4,1)}), s8[524288]{0:T(1024)(128)(4,1)S(1)}, s32[]{:S(2)}) async-start(s8[4718592]{0:T(1024)(128)(4,1)} %bitcast.109), calls=%async_computation.1 | async-start | bytes 1048576
  249.9 16.2 %slice-start.3 = ((s8[4718592]{0:T(1024)(128)(4,1)}), s8[524288]{0:T(1024)(128)(4,1)S(1)}, s32[]{:S(2)}) async-start(s8[4718592]{0:T(1024)(128)(4,1)} %bitcast.114), calls=%async_computation.3 | async-start | bytes 1048576
  265.8 10.3 %collective-permute-start.1 = (f32[12,128]{1,0:T(8,128)S(1)}, f32[12,128]{1,0:T(8,128)S(1)}, u32[]{:S(2)}, u32[]{:S(2)}) collective-permute-start(f32[12,128]{1,0:T(8,128)S(1)} %bitcast.95), channel_id=1, source_target_pairs={{0,4},{1,5},{2,6},{3,7},{4,0},{5,1},{6,2},{7,3},{8,12},{9,13},{10,... | collective-permute-start | bytes 18440 | tf_op jit(solution)/shard_map/ppermute | solution.py:1650
  283.0 161.3 %copy-start.10 = (f32[6,128]{1,0:T(8,128)S(1)}, f32[6,128]{1,0:T(8,128)}, u32[]{:S(2)}) copy-start(f32[6,128]{1,0:T(8,128)} %fusion.11) | copy-start | bytes 9220
  283.0 161.9 %copy-start.11 = (f32[8,1536]{1,0:T(8,128)S(1)}, f32[8,1536]{1,0:T(8,128)}, u32[]{:S(2)}) copy-start(f32[8,1536]{1,0:T(8,128)} %get-tuple-element.63.cx) | copy-start | bytes 147460
  283.0 161.9 %copy-start.13 = (f32[8,256]{1,0:T(8,128)S(1)}, f32[8,256]{1,0:T(8,128)}, u32[]{:S(2)}) copy-start(f32[8,256]{1,0:T(8,128)} %get-tuple-element.64.cbc) | copy-start | bytes 24580
  283.0 162.0 %copy-start.12 = (f32[1536]{0:T(1024)S(1)}, f32[1536]{0:T(1024)}, u32[]{:S(2)}) copy-start(f32[1536]{0:T(1024)} %get-tuple-element.150) | copy-start | bytes 18436
  443.0 6.3 %collective-permute-start.3 = (bf16[3,3,1792]{2,1,0:T(4,128)(2,1)S(1)}, bf16[3,3,1792]{2,1,0:T(4,128)(2,1)S(1)}, u32[]{:S(2)}, u32[]{:S(2)}) collective-permute-start(bf16[3,3,1792]{2,1,0:T(4,128)(2,1)S(1)} %pad_maximum_fusion.1), channel_id=1, source_target_pairs={{1,0},{3,2},{5,4},{7,6},{8,1},{9,8},{10,3},{11,10},{12,5},{13,12},... | collective-permute-start | bytes 96776 | tf_op jit(solution)/shard_map/ppermute | solution.py:1650
  451.2 164.8 %copy-start.1 = (bf16[6,128,1536]{2,1,0:T(8,128)(2,1)S(1)}, bf16[6,128,1536]{2,1,0:T(8,128)(2,1)}, u32[]{:S(2)}) copy-start(bf16[6,128,1536]{2,1,0:T(8,128)(2,1)} %hidden.1) | copy-start | bytes 7077892
  451.2 164.8 %copy-start.8 = (f32[1536]{0:T(1024)S(1)}, f32[1536]{0:T(1024)}, u32[]{:S(2)}) copy-start(f32[1536]{0:T(1024)} %copy-done.7) | copy-start | bytes 18436
  451.2 164.8 %copy-start.9 = (f32[6,128]{1,0:T(8,128)S(1)}, f32[6,128]{1,0:T(8,128)}, u32[]{:S(2)}) copy-start(f32[6,128]{1,0:T(8,128)} %add_rsqrt_fusion.2) | copy-start | bytes 9220
  619.4 8.0 %copy-start.5 = (f32[192,3072]{1,0:T(8,128)S(1)}, f32[192,3072]{1,0:T(8,128)}, u32[]{:S(2)}) copy-start(f32[192,3072]{1,0:T(8,128)} %get-tuple-element.195) | copy-start | bytes 7077892
  625.5 3.3 copy-start.4
  627.4 2.8 copy-start.6

commit v7 on v6

--- a/solution.py
+++ b/solution.py
@@ -873,6 +873,7 @@
         for k in range(1, count):
             dec_copy(k, True).start()
             out_copy(k, True).start()
+        gather.start()
         take_weight.start()
         fetch(0).start()
         last.start()
@@ -883,7 +884,9 @@
         parts[me] = own[:, rows_of(me)]
         decs[me] = dec[...]
         take_weight.wait()
-        for k in range(count_blocks // 2):
+        multiply(0)
+        gather.second()
+        for k in range(1, count_blocks // 2):
             multiply(k)
         near_keep.relay()
         far_keep.relay()
@@ -899,10 +902,8 @@
         incoming[:, rows_of(me)] = results[me]
         for k in range(1, count):
             back_copy(k, True).start()
-        gather.start()
-        multiply(count_blocks // 2)
-        gather.second()
-        for k in range(count_blocks // 2 + 1, count_blocks):
+        gather.third()
+        for k in range(count_blocks // 2, count_blocks):
             multiply(k)
         keep_gate.start()
         last_came.wait_recv()
@@ -918,11 +919,7 @@
             y0, gate.at[place], bcs, acum, incoming.at[pl.ds((i - 1) // PER_UNIT, 1)], y, gated, squares
         )
 
-    @pl.when(i == 3)
-    def _():
-        gather.third()
-
-    @pl.when(i == 6)
+    @pl.when(i == 1)
     def _():
         gather.fourth()
 
@@ -1207,11 +1204,11 @@
             gate.start_members(piece)
         vs[0] = jnp.zeros(vs.shape[1:], F32)
 
-    @pl.when(i < steps)
+    @pl.when(i >= steps)
     def _():
         def part(n, carry):
             columns = pl.ds(pl.multiple_of(n * 384, 384), 384)
-            g[pl.ds(pl.multiple_of(i * wide, wide), wide), columns] = dot(
+            g[pl.ds(pl.multiple_of((i - steps) * wide, wide), wide), columns] = dot(
                 turned[...], d_all[:, columns]
             ).astype(BF16)
             return carry
@@ -1219,19 +1216,13 @@
         turned[...] = normed[...].T
         lax.fori_loop(0, g.shape[1] // 384, part, 0)
 
-    @pl.when(i == steps - 1)
+    @pl.when(i == 2 * steps - 1)
     def _():
         first.start(early)
 
-    @pl.when(i == steps + 4)
-    def _():
-        for piece in early:
-            first.after_first(piece)
-        first.start(late)
-
-    @pl.when(i >= steps)
-    def _():
-        columns = pl.ds(pl.multiple_of((i - steps) * wide, wide), wide)
+    @pl.when(i < steps)
+    def _():
+        columns = pl.ds(pl.multiple_of(i * wide, wide), wide)
         per = d_all.shape[0] // units
 
         def part(u, carry):
@@ -1242,15 +1233,31 @@
 
         vs[0, 6:7, columns] = lax.fori_loop(0, units, part, jnp.zeros((1, wide), F32))
 
-    @pl.when(i == steps)
+    @pl.when(i == steps - 1)
     def _():
         for piece in gate.pieces:
             gate.after_near(piece)
-
-    @pl.when(i == 2 * steps - 1)
-    def _():
         d_pair(1 - upper, 0).start()
         d_pair(upper, 1).start()
+
+    @pl.when(i == steps + 2)
+    def _():
+        d_pair(1 - upper, 0).wait_recv()
+        d_add(1 - upper)
+        d_trade(1 - upper, 0, token_far, upper).start()
+        d_pair(upper, 1).wait_recv()
+        d_add(upper)
+
+        @pl.when(stays)
+        def _():
+            d_keep.start()
+
+        @pl.when(jnp.logical_not(stays))
+        def _():
+            d_trade(upper, 1, token_near, upper).start()
+
+    @pl.when(i == 2 * steps - 1)
+    def _():
         for k in range(5):
             vs[0, k : k + 1] = jnp.sum(g_x[8 * k : 8 * k + 8], axis=0, keepdims=True)
             vs[0, 8 + k : 9 + k, : 2 * LANES] = jnp.sum(g_bc[8 * k : 8 * k + 8], axis=0, keepdims=True)
@@ -1260,20 +1267,9 @@
                 g_heads[8 * k : 8 * k + 8], axis=0, keepdims=True
             )
         vec_step(0)
-        d_pair(1 - upper, 0).wait_recv()
-        d_add(1 - upper)
-        d_trade(1 - upper, 0, token_far, upper).start()
-        d_pair(upper, 1).wait_recv()
-        d_add(upper)
-
-        @pl.when(stays)
-        def _():
-            d_keep.start()
-
-        @pl.when(jnp.logical_not(stays))
-        def _():
-            d_trade(upper, 1, token_near, upper).start()
-
+        for piece in early:
+            first.after_first(piece)
+        first.start(late)
         order = (
             (first.after_second, early), (1, ()), (pair_on, early), (2, ()), (first.after_first, late),
             (gate.after_far, gate.pieces), (3, ()), (first.after_second, late), (4, ()),
@@ -1758,10 +1754,10 @@
             tail_kernel,
             grid=(2 * steps,),
             in_specs=[
-                pl.BlockSpec((count, block), lambda i: (0, early(i))), whole(d_all),
-                pl.BlockSpec((count, block), lambda i: (0, late(i))),
-                pl.BlockSpec((block, width), lambda i: (late(i), 0)),
-                pl.BlockSpec((count, block), lambda i: (0, late(i))),
+                pl.BlockSpec((count, block), lambda i: (0, late(i))), whole(d_all),
+                pl.BlockSpec((count, block), lambda i: (0, early(i))),
+                pl.BlockSpec((block, width), lambda i: (early(i), 0)),
+                pl.BlockSpec((count, block), lambda i: (0, early(i))),
                 whole(g_x), whole(g_bc), whole(g_heads), whole(g_gate), whole(z_total),
             ],
             out_specs=[anywhere] * 3

time: 636 us -> 621 us (0.976)
  Pallas kernels: 517 us -> 502 us
    pallas_call x1, Pallas kernels: 88.2 us -> 81.5 us  [exchange(): pl.pallas_call(states_kernel, grid=(chunks + 1,), in_specs=[whole(own), w...]
  transfers between devices with their start and end apart: 4 -> 4, of which waited for: 1 -> 1; matrix products, arithmetic and copies ran while one was open for 5% -> 6% of each run, Pallas kernels for 0% -> 0%
where the time goes in v7:
time: 621 us; the launch traced here: 616 us
  Pallas kernels  502 us (81%)
  matrix products  48.4 us (8%)
  other arithmetic  36.5 us (6%)
  local copies, waits for them, and re-layouts  25.5 us (4%)
    pallas_call x1, Pallas kernels, body(): pl.pallas_call(middle_kernel, grid=(spots,), in_specs=[pulls(inner), pull...  156 us
    pallas_call x1, Pallas kernels, tail(): pl.pallas_call(tail_kernel, grid=(2 * steps,), in_specs=[pl.BlockSpec((co...  153 us
    pallas_call x1, Pallas kernels, exchange(): pl.pallas_call(states_kernel, grid=(chunks + 1,), in_specs=[whole(own), w...  81.5 us
    pallas_call x1, Pallas kernels, head(): pl.pallas_call(head_kernel, out_shape=[shape((self.units, 4, self.tokens,...  64.2 us
    pallas_call x1, Pallas kernels, body(): pl.pallas_call(scan_forward_kernel, grid=(units, PER_UNIT), in_specs=in_s...  47.3 us
    dot_general x2, matrix products, dot(): return jnp.dot(a, b, preferred_element_type=F32)  27.6 us
  transfers between devices with their start and end apart: 4, of which 1 were waited for; matrix products, arithmetic and copies ran while one was open for 6% of the time, Pallas kernels for 0%

profile of v7, /device:TPU:0, one launch (start us, length us, event | category | flops | bytes accessed | tf_op | source)
XLA Modules:
  0.0 615.7 jit_solution(6659139020840979696)
XLA Ops:
  0.6 1.5 copy.48.conv_x
  2.1 1.5 copy.47.w_dt
  3.6 1.4 copy.49.conv_bc
  4.9 1.2 broadcast_in_dim.33.conv_x_bias
  6.2 1.2 broadcast_in_dim.34.gate_gain
  7.4 1.2 broadcast_in_dim.35.norm_gain
  8.7 64.2 %head.1 = (bf16[3,4,128,1536]{3,2,1,0:T(8,128)(2,1)}, bf16[4,2,192,1920]{3,2,1,0:T(8,128)(2,1)}, f32[8,1536]{1,0:T(8,128)}, f32[8,256]{1,0:T(8,128)}, f32[8,128]...) custom-call(bf16[6,128,1536]{2,1,0:T(8,128)(2,1)} %hidden.1, bf16[192,3072]{1,0:T(8,128)(2,1)} %w_x.1, ...), custom_call_target="tpu_custom_call" | custom-call | flops 63250001920 | tf_op jit(solution)/shard_map/head/pallas_call | solution.py:1679
  72.8 0.8 slice_reduce_fusion.2
  73.6 3.3 multiply_reduce_fusion
  77.0 6.0 fusion.3
  83.0 11.7 %convolution_convert_fusion.x.bc.dt.xp.bcp = bf16[1536,1920]{1,0:T(8,128)(2,1)} fusion(bf16[1536,1536]{1,0:T(8,128)(2,1)S(1)} %get-tuple-element.61.normed, bf16[1536,1920]{1,0:T(8,128)(2,1)S(1)} %bitcast.104), kind=kOutput, calls=%fused_computation.11 | convolution fusion | flops 9062645760 | bytes 16515072 | tf_op jit(solution)/shard_map/dot_general | solution.py:22
  94.7 47.3 %scan_forward.1 = (bf16[1536,1536]{1,0:T(8,128)(2,1)}, bf16[12,128,1536]{2,1,0:T(8,128)(2,1)}, bf16[3,128,1536]{2,1,0:T(8,128)(2,1)}, f32[3,8,1536]{2,1,0:T(8,12...) custom-call(bf16[1536,1920]{1,0:T(8,128)(2,1)} %convolution_convert_, ...), custom_call_target="tpu_custom_call" | custom-call | flops 35649998848 | tf_op jit(solution)/shard_map/scan_forward/pallas_call | solution.py:2073
  142.0 1.0 copy.50
  143.0 0.6 concatenate.16.dec
  143.6 81.5 %states.1 = (f32[8,8,1536]{2,1,0:T(8,128)}, bf16[3,4,128,1536]{3,2,1,0:T(8,128)(2,1)}, bf16[4,2,192,1536]{3,2,1,0:T(8,128)(2,1)}, bf16[1536,1536]{1,0:T(8,128)(2...) custom-call(bf16[3,128,1536]{2,1,0:T(8,128)(2,1)} %get-tuple-element, ...), custom_call_target="tpu_custom_call" | custom-call | flops 69000003584 | tf_op jit(solution)/shard_map/states/pallas_call | solution.py:1939
  225.1 1.4 slice_reduce_fusion
  226.5 0.1 collective-permute-start
  226.6 1.1 fusion.11
  227.7 1.0 fusion.13.pick
  228.7 0.8 slice_reduce_fusion.1
  229.6 0.1 pad.17.clone
  229.7 11.3 %convolution_convert_fusion.1 = bf16[1536,1536]{1,0:T(8,128)(2,1)S(1)} fusion(bf16[1536,1536]{1,0:T(8,128)(2,1)} %bitcast.112, bf16[1536,1536]{1,0:T(8,128)(2,1)} %get-tuple-element.76.gated, f32[1536]{0:T(1024)S(1)} %get-tuple-element.171, f32[1536]{0:T(1024)S(1)} %slice_reduce_fusion.1), kind=kOutput, calls=%fused_computation.12 | convolution fusion | flops 7259553792 | bytes 14168064 | tf_op jit(solution)/shard_map/dot_general | solution.py:26
  241.0 1.7 select_bitcast_fusion
  242.6 0.5 collective-permute-start.2
  243.1 15.9 %fusion.2 = (f32[1536]{0:T(1024)}, f32[1536]{0:T(1024)S(1)}, bf16[1536,1536]{1,0:T(8,128)(2,1)}) fusion(bf16[1536,1536]{1,0:T(8,128)(2,1)} %get-tuple-element.76.gated, f32[1536]{0:T(1024)S(1)} %get-tuple-element.171, f32[1536]{0:T(1024)S(1)} %slice_reduce_fusion.1, bf16[1536,1536]{1,0:T(8,128)(2,1)} %bitcast.108, bf16[1536,1536]{1,0:T(8,128)(2,1)} %bitcast.113), kind=kOutput, calls=%fused_computation.4 | convolution fusion | flops 7268987904 | bytes 18898944 | tf_op jit(solution)/shard_map/dot_general | solution.py:22
  259.0 0.4 collective-permute-start.1
  259.3 9.6 %convolution_convert_fusion.2.g_out = bf16[1536,1536]{1,0:T(8,128)(2,1)} fusion(bf16[1536,1536]{1,0:T(8,128)(2,1)S(1)} %bitcast.111, bf16[1536,1536]{1,0:T(8,128)(2,1)S(1)} %bitcast.115, f32[1536]{0:T(1024)S(1)} %get-tuple-element.171, f32[1536]{0:T(1024)S(1)} %slice_reduce_fusion.1), kind=kOutput, calls=%fused_computation.13 | convolution fusion | flops 7259553792 | bytes 14168064 | tf_op jit(solution)/shard_map/dot_general | solution.py:30
  268.9 0.3 copy.61
  269.3 0.3 copy.63
  269.6 1.2 maximum_maximum_fusion.stats
  270.7 5.5 fusion.12.projected
  276.2 155.7 %middle.1 = (bf16[1536,1920]{1,0:T(8,128)(2,1)}, f32[3,8,1536]{2,1,0:T(8,128)}, f32[3,8,256]{2,1,0:T(8,128)}, f32[40,1536]{1,0:T(8,128)}, f32[40,256]{1,0:T(8,12...) custom-call(bf16[1536,1536]{1,0:T(8,128)(2,1)} %get-tuple-element.17, ...), custom_call_target="tpu_custom_call" | custom-call | flops 143750004736 | tf_op jit(solution)/shard_map/middle/pallas_call | solution.py:2179
  431.9 0.9 convert.9
  432.8 0.7 convert.10
  433.6 1.3 collective-permute-start.3
  434.9 0.6 add_rsqrt_fusion.2
  435.5 0.1 maximum_reduce_fusion.1
  435.6 0.6 broadcast_in_dim.41.g_gate
  436.2 2.9 convert_element_type.107
  439.1 0.4 collective-permute-done.3
  439.5 0.1 multiply_add_fusion
  439.6 1.7 fusion.16
  441.3 153.1 %tail.1 = (f32[192,3072]{1,0:T(8,128)}, f32[192,256]{1,0:T(8,128)}, f32[192,256]{1,0:T(8,128)}, f32[2,16,1536]{2,1,0:T(8,128)}, bf16[6,128,1536]{2,1,0:T(8,128)(2,1)}, /*index=5*/f32[192,3072]{1,0:T(8,128)}) custom-call(bf16[1536,1536]{1,0:T(8,128)(2,1)} %copy-done.3, bf16[1536,1920]{1,0:T(8,128)(2,1)} %bitcast.97, ...), custom_call_target="tpu_custom_call" | custom-call | flops 149500002304 | tf_op jit(solution)/shard_map/tail/pallas_call | solution.py:1753
  594.5 0.7 fusion.26
  595.2 0.1 dynamic-slice_add_fusion
  595.3 0.6 slice_bitcast_fusion.4
  595.8 0.5 slice_bitcast_fusion.8
  596.4 0.8 fusion.28
  597.2 0.9 slice.141
  598.1 0.8 slice_reduce_fusion.3
  598.9 1.0 fusion.27
  599.8 0.1 pad_maximum_fusion
  599.9 0.7 copy.56
  600.6 2.7 fusion.6
  603.4 0.1 reshape.204
  603.5 0.1 constant_dynamic-slice_fusion.1
  603.5 0.5 slice_bitcast_fusion.5
  604.1 6.1 fusion.9
  610.2 0.6 dynamic-slice_bitcast_fusion
  610.7 0.7 dynamic-slice_reduce_fusion
  611.4 0.6 fusion.25
  612.1 1.4 copy.73
  613.5 1.4 copy.74
  614.9 0.7 copy.75
  (60 shorter events, 0.2 us)
Async XLA Ops:
  73.6 9.3 %copy-start.7 = (f32[1536]{0:T(1024)}, f32[1536]{0:T(1024)S(1)}, u32[]{:S(2)}) copy-start(f32[1536]{0:T(1024)S(1)} %slice_reduce_fusion.2) | copy-start | bytes 18436
  77.0 6.0 copy-start.14
  83.0 11.7 %copy-start.3 = (bf16[1536,1536]{1,0:T(8,128)(2,1)}, bf16[1536,1536]{1,0:T(8,128)(2,1)S(1)}, u32[]{:S(2)}) copy-start(bf16[1536,1536]{1,0:T(8,128)(2,1)S(1)} %get-tuple-element.61.normed) | copy-start | bytes 14155780
  143.6 83.0 %copy-start = (bf16[6,128,1536]{2,1,0:T(8,128)(2,1)S(1)}, bf16[6,128,1536]{2,1,0:T(8,128)(2,1)}, u32[]{:S(2)}) copy-start(bf16[6,128,1536]{2,1,0:T(8,128)(2,1)} %hidden.1) | copy-start | bytes 7077892
  226.5 3.2 collective-permute-start
  240.9 18.0 %copy-start.2 = (bf16[1536,1536]{1,0:T(8,128)(2,1)}, bf16[1536,1536]{1,0:T(8,128)(2,1)S(1)}, u32[]{:S(2)}) copy-start(bf16[1536,1536]{1,0:T(8,128)(2,1)S(1)} %convolution_convert_fusion.1) | copy-start | bytes 14155780
  240.9 18.4 %slice-start = ((s8[4718592]{0:T(1024)(128)(4,1)}), s8[4194304]{0:T(1024)(128)(4,1)S(1)}, s32[]{:S(2)}) async-start(s8[4718592]{0:T(1024)(128)(4,1)} %bitcast.109), calls=%async_computation | async-start | bytes 8388608
  241.0 18.4 %slice-start.2 = ((s8[4718592]{0:T(1024)(128)(4,1)}), s8[4194304]{0:T(1024)(128)(4,1)S(1)}, s32[]{:S(2)}) async-start(s8[4718592]{0:T(1024)(128)(4,1)} %bitcast.114), calls=%async_computation.2 | async-start | bytes 8388608
  242.6 28.1 %collective-permute-start.2 = (bf16[3,2,128,1536]{3,2,1,0:T(8,128)(2,1)}, bf16[3,2,128,1536]{3,2,1,0:T(8,128)(2,1)}, u32[]{:S(2)}, u32[]{:S(2)}) collective-permute-start(bf16[3,2,128,1536]{3,2,1,0:T(8,128)(2,1)} %select_bitcast_fusion), channel_id=1, source_target_pairs={{0,4},{1,5},{2,6},{3,7},{4,0},{5,1},{6,2},{7,3},{8,12},{9,13},{10,... | collective-permute-start | bytes 7077896 | tf_op jit(solution)/shard_map/ppermute | solution.py:1646
  243.1 16.2 %slice-start.1 = ((s8[4718592]{0:T(1024)(128)(4,1)}), s8[524288]{0:T(1024)(128)(4,1)S(1)}, s32[]{:S(2)}) async-start(s8[4718592]{0:T(1024)(128)(4,1)} %bitcast.109), calls=%async_computation.1 | async-start | bytes 1048576
  243.1 16.2 %slice-start.3 = ((s8[4718592]{0:T(1024)(128)(4,1)}), s8[524288]{0:T(1024)(128)(4,1)S(1)}, s32[]{:S(2)}) async-start(s8[4718592]{0:T(1024)(128)(4,1)} %bitcast.114), calls=%async_computation.3 | async-start | bytes 1048576
  259.0 10.3 %collective-permute-start.1 = (f32[12,128]{1,0:T(8,128)S(1)}, f32[12,128]{1,0:T(8,128)S(1)}, u32[]{:S(2)}, u32[]{:S(2)}) collective-permute-start(f32[12,128]{1,0:T(8,128)S(1)} %bitcast.95), channel_id=1, source_target_pairs={{0,4},{1,5},{2,6},{3,7},{4,0},{5,1},{6,2},{7,3},{8,12},{9,13},{10,... | collective-permute-start | bytes 18440 | tf_op jit(solution)/shard_map/ppermute | solution.py:1646
  276.2 158.7 %copy-start.10 = (f32[6,128]{1,0:T(8,128)S(1)}, f32[6,128]{1,0:T(8,128)}, u32[]{:S(2)}) copy-start(f32[6,128]{1,0:T(8,128)} %fusion.11) | copy-start | bytes 9220
  276.2 159.3 %copy-start.11 = (f32[8,1536]{1,0:T(8,128)S(1)}, f32[8,1536]{1,0:T(8,128)}, u32[]{:S(2)}) copy-start(f32[8,1536]{1,0:T(8,128)} %get-tuple-element.63.cx) | copy-start | bytes 147460
  276.2 159.3 %copy-start.13 = (f32[8,256]{1,0:T(8,128)S(1)}, f32[8,256]{1,0:T(8,128)}, u32[]{:S(2)}) copy-start(f32[8,256]{1,0:T(8,128)} %get-tuple-element.64.cbc) | copy-start | bytes 24580
  276.2 159.4 %copy-start.12 = (f32[1536]{0:T(1024)S(1)}, f32[1536]{0:T(1024)}, u32[]{:S(2)}) copy-start(f32[1536]{0:T(1024)} %get-tuple-element.150) | copy-start | bytes 18436
  433.6 5.9 collective-permute-start.3
  441.3 159.3 %copy-start.1 = (bf16[6,128,1536]{2,1,0:T(8,128)(2,1)S(1)}, bf16[6,128,1536]{2,1,0:T(8,128)(2,1)}, u32[]{:S(2)}) copy-start(bf16[6,128,1536]{2,1,0:T(8,128)(2,1)} %hidden.1) | copy-start | bytes 7077892
  441.3 159.3 %copy-start.8 = (f32[1536]{0:T(1024)S(1)}, f32[1536]{0:T(1024)}, u32[]{:S(2)}) copy-start(f32[1536]{0:T(1024)} %copy-done.7) | copy-start | bytes 18436
  441.3 159.3 %copy-start.9 = (f32[6,128]{1,0:T(8,128)S(1)}, f32[6,128]{1,0:T(8,128)}, u32[]{:S(2)}) copy-start(f32[6,128]{1,0:T(8,128)} %add_rsqrt_fusion.2) | copy-start | bytes 9220
  604.1 8.0 %copy-start.5 = (f32[192,3072]{1,0:T(8,128)S(1)}, f32[192,3072]{1,0:T(8,128)}, u32[]{:S(2)}) copy-start(f32[192,3072]{1,0:T(8,128)} %get-tuple-element.195) | copy-start | bytes 7077892
  610.1 3.3 copy-start.4
  612.1 2.8 copy-start.6
